TPU v7x, 256 devices: a whole 4x4x8 slice. The times are simulated.
256 devices in a mesh: gx: 8 (over x_hi, y), gy: 32 (over x_lo, z, core).
Axes of the slice: x: 4 (x_hi: 2, x_lo: 2; x = x_hi * 2 + x_lo), y: 4, z: 8, core: 2. Of those that a mesh axis runs over, the one named last changes fastest.
Arguments:
- images: bfloat16 [256, 14, 14, 512], P(('gx', 'gy')), may hold values from -6 to 6
- conv_weight: bfloat16 [4608, 512], replicated, may hold values from -0.09375 to 0.09375
- fc6_weight: bfloat16 [25088, 4096], P('gx', 'gy'), may hold values from -0.0390625 to 0.0390625
- fc7_weight: bfloat16 [4096, 4096], P(None, ('gx', 'gy')), may hold values from -0.09375 to 0.09375
- cotangent: bfloat16 [256, 4096], P(None, ('gx', 'gy')), may hold values from -12 to 12
Outputs:
- grad_conv: float32 [4608, 512], P('gy', 'gx')
- grad_fc6: float32 [25088, 4096], P('gx', 'gy')
- grad_fc7: float32 [4096, 4096], P(None, ('gx', 'gy'))
- grad_images: float32 [256, 14, 14, 512], P(('gx', 'gy'))
All inputs are finite; a program needn't handle non-finite values.
Results may differ from a plain program's by a relative error of at most 0.012.
Values may be sent and summed in bfloat16 or wider, within the bound.
No kernel may reach another device: no remote copies, remote signals or barrier semaphores. Data moves between devices by JAX's collectives and lax.ppermute only.
A program may use at most 128 MiB of HBM per device.

v0:
```python
import jax
import jax.numpy as jnp
from jax import lax
from jax.sharding import PartitionSpec as P


def shifted(arr, row, col, side):
    return arr[:, row : row + side, col : col + side, :].reshape(-1, arr.shape[3])


def activate(value):
    return value * jax.nn.sigmoid(value)


def slope(value):
    sig = jax.nn.sigmoid(value)
    return sig * (1.0 + value * (1.0 - sig))


def on_device(images, conv_weight, fc6_weight, fc7_weight, cotangent):
    count = images.shape[0]
    side = images.shape[1]
    chans = images.shape[3]
    half = side // 2
    padded = jnp.pad(images, ((0, 0), (1, 1), (1, 1), (0, 0)))
    conv_pre = jnp.zeros((count * side * side, chans), jnp.float32)
    for row in range(3):
        for col in range(3):
            kernel = conv_weight[(3 * row + col) * chans : (3 * row + col + 1) * chans]
            conv_pre = conv_pre + jnp.dot(
                shifted(padded, row, col, side), kernel, preferred_element_type=jnp.float32
            )
    active = activate(conv_pre).reshape(count, half, 2, half, 2, chans)
    feat = (0.25 * active.sum(axis=(2, 4))).reshape(count, -1).astype(jnp.bfloat16)
    group_rows = lax.all_gather(feat, "gy", axis=0, tiled=True)
    inputs = lax.all_to_all(group_rows, "gx", split_axis=1, concat_axis=0, tiled=True)
    partial_value = jnp.dot(inputs, fc6_weight, preferred_element_type=jnp.float32)
    h6_pre = lax.psum(partial_value, "gx")
    own_block = activate(h6_pre).astype(jnp.bfloat16)
    hidden = lax.all_gather(own_block, "gy", axis=1, tiled=True)
    y7_pre = jnp.dot(hidden, fc7_weight, preferred_element_type=jnp.float32)
    g_seven = (cotangent.astype(jnp.float32) * slope(y7_pre)).astype(jnp.bfloat16)
    grad_fc7 = jnp.dot(hidden.T, g_seven, preferred_element_type=jnp.float32)
    hidden_terms = jnp.dot(g_seven, fc7_weight.T, preferred_element_type=jnp.float32)
    column_sums = lax.psum_scatter(hidden_terms, "gy", scatter_dimension=1, tiled=True)
    grad_hidden = lax.psum(column_sums, "gx")
    g_six = (grad_hidden * slope(h6_pre)).astype(jnp.bfloat16)
    grad_fc6 = jnp.dot(inputs.T, g_six, preferred_element_type=jnp.float32)
    feat_terms = jnp.dot(g_six, fc6_weight.T, preferred_element_type=jnp.float32)
    returned = lax.all_to_all(feat_terms, "gx", split_axis=0, concat_axis=1, tiled=True)
    dfeat = lax.psum_scatter(returned, "gy", scatter_dimension=0, tiled=True).astype(jnp.bfloat16)
    spread = dfeat.astype(jnp.float32).reshape(count, half, 1, half, 1, chans)
    spread = jnp.broadcast_to(spread, (count, half, 2, half, 2, chans)).reshape(
        count * side * side, chans
    )
    g_conv = (0.25 * spread * slope(conv_pre)).astype(jnp.bfloat16)
    g_padded = jnp.pad(g_conv.reshape(count, side, side, chans), ((0, 0), (1, 1), (1, 1), (0, 0)))
    blocks = []
    grad_in = jnp.zeros((count * side * side, chans), jnp.float32)
    for row in range(3):
        for col in range(3):
            kernel = conv_weight[(3 * row + col) * chans : (3 * row + col + 1) * chans]
            blocks.append(
                jnp.dot(
                    shifted(padded, row, col, side).T, g_conv, preferred_element_type=jnp.float32
                )
            )
            grad_in = grad_in + jnp.dot(
                shifted(g_padded, 2 - row, 2 - col, side),
                kernel.T,
                preferred_element_type=jnp.float32,
            )
    kernel_terms = jnp.concatenate(blocks, axis=0)
    grad_images = grad_in.reshape(count, side, side, chans)
    section = lax.psum_scatter(kernel_terms, "gy", scatter_dimension=0, tiled=True)
    grad_conv = lax.psum_scatter(section, "gx", scatter_dimension=1, tiled=True)
    return (grad_conv, grad_fc6, grad_fc7, grad_images)


def solution(mesh):
    placed = (
        P(("gx", "gy"), None, None, None),
        P(),
        P("gx", "gy"),
        P(None, ("gx", "gy")),
        P(None, ("gx", "gy")),
    )
    return jax.shard_map(
        on_device,
        mesh=mesh,
        in_specs=placed,
        out_specs=(
            P("gy", "gx"),
            P("gx", "gy"),
            P(None, ("gx", "gy")),
            P(("gx", "gy"), None, None, None),
        ),
        check_vma=False,
    )
```

profile of v0, /device:TPU:1, one launch (start us, length us, event | category | flops | bytes accessed | tf_op | source)
XLA Modules:
  0.0 913.7 jit_solution(3866566167579939608)
XLA Ops:
  7.2 1.1 reshape.123
  8.3 2.4 pad_slice_fusion.8
  10.7 0.7 reshape.127
  12.0 1.4 fusion.19
  13.5 1.5 convolution_add_fusion.15
  15.0 1.3 convolution_add_fusion.14
  16.3 1.3 convolution_add_fusion.13
  17.6 0.3 convolution_add_fusion.12
  17.9 0.3 convolution_add_fusion.11
  18.2 0.3 convolution_add_fusion.10
  18.5 0.3 convolution_add_fusion.9
  18.8 1.0 fusion.21
  20.1 0.3 reduce_sum.9
  20.4 0.7 reshape.139
  21.3 70.2 %all-gather.6.cloned.1.call-done = bf16[32,1,25088]{2,1,0:T(2,128)(2,1)} async-done(((bf16[1,1,25088]{2,1,0:T(2,128)(2,1)}), bf16[32,1,25088]{2,1,0:T(2,128)(2,1)}) %all-gather.6.cloned.1.call-update) | async-done | bytes 1605648 | tf_op jit(solution)/shard_map/all_gather | solution.py:35
  91.6 11.9 %reduce.1 = bf16[32,25088]{1,0:T(8,128)(2,1)} reduce(bf16[32,1,25088]{2,1,0:T(2,128)(2,1)} %all-gather.6.cloned.1.call-done, bf16[]{:T(256)} %constant.23), dimensions={1}, to_apply=%all-gather.reduce_sub_computation | reduce | bytes 3211266 | tf_op jit(solution)/shard_map/all_gather | solution.py:35
  103.5 2.5 all_to_all.28
  106.2 28.9 %all_to_all.38 = bf16[32,8,3136]{2,0,1:T(8,128)(2,1)S(1)} all-to-all(bf16[32,8,3136]{2,0,1:T(8,128)(2,1)S(1)} %copy.16), channel_id=1, replica_groups=mesh['gx'=8,'gy'=32] {'gx'}, dimensions={1} | all-to-all | bytes 3211264 | tf_op jit(solution)/shard_map/all_to_all | solution.py:36
  135.1 1.2 fusion.33
  136.5 80.4 %all-reduce.7.cloned.1.call-done = f32[256,128]{1,0:T(8,128)} async-done(((f32[256,128]{1,0:T(8,128)}), f32[256,128]{1,0:T(8,128)}) %all-reduce.7.cloned.1.call-update) | async-done | bytes 131088 | tf_op jit(solution)/shard_map/psum | solution.py:38
  216.9 1.6 multiply_convert_fusion.2
  218.8 70.5 %all-gather.4.cloned.1.call-done = bf16[256,4096]{1,0:T(8,128)(2,1)} async-done(((bf16[256,128]{1,0:T(8,128)(2,1)}), bf16[256,4096]{1,0:T(8,128)(2,1)}) %all-gather.4.cloned.1.call-update) | async-done | bytes 2097168 | tf_op jit(solution)/shard_map/all_gather | solution.py:40
  289.3 2.2 fusion.34
  291.5 2.7 fusion.26
  294.3 116.1 %reduce-scatter.6.cloned.1.call-done = f32[256,128]{1,0:T(8,128)} async-done(((f32[256,4096]{1,0:T(8,128)}), f32[256,128]{1,0:T(8,128)}) %reduce-scatter.6.cloned.1.call-update) | async-done | bytes 131088 | tf_op jit(solution)/shard_map/reduce_scatter | solution.py:45
  410.5 85.9 %all-reduce.9.cloned.1.call-done = f32[256,128]{1,0:T(8,128)} async-done(((f32[256,128]{1,0:T(8,128)}), f32[256,128]{1,0:T(8,128)}) %all-reduce.9.cloned.1.call-update) | async-done | bytes 131088 | tf_op jit(solution)/shard_map/psum | solution.py:46
  496.4 1.0 multiply_convert_fusion.1
  497.4 2.3 fusion.35
  499.7 4.5 all-to-all-start.1
  504.2 0.6 dynamic-slice
  504.8 33.6 %all-to-all-done.1 = f32[8,32,3136]{2,1,0:T(8,128)} async-done(((f32[8,32,3136]{2,1,0:T(8,128)}), f32[8,32,3136]{2,1,0:T(8,128)}, u32[]{:S(2)}, u32[]{:S(2)}) %all-to-all-start.1) | async-done | bytes 3211296 | tf_op jit(solution)/shard_map/all_to_all | solution.py:50
  538.4 5.5 copy.18
  544.0 3.6 all_to_all.35
  547.6 129.5 %all-reduce.10 = bf16[32,25088]{1,0:T(8,128)(2,1)} all-reduce(f32[32,25088]{1,0:T(8,128)} %all_to_all.35), channel_id=3, replica_groups=mesh['gx'=8,'gy'=32] {'gy'}, use_global_device_ids=true, to_apply=%region_4.5.clone | all-reduce | flops 802816 | bytes 4816896
  677.1 2.6 fusion.24
  679.7 0.9 mul.75
  680.6 0.9 broadcast_in_dim.2
  681.4 2.0 mul.76
  683.5 1.3 multiply_convert_fusion
  684.7 2.2 convolution_dynamic-update-slice_fusion.7
  687.0 2.3 convolution_dynamic-update-slice_fusion.6
  689.3 2.3 convolution_dynamic-update-slice_fusion.5
  691.6 2.3 convolution_dynamic-update-slice_fusion.4
  693.8 1.3 fusion
  695.1 1.3 convolution_dynamic-update-slice_fusion.3
  696.5 1.3 convolution_dynamic-update-slice_fusion.2
  697.8 1.4 convolution_dynamic-update-slice_fusion.1
  699.2 1.4 convolution_dynamic-update-slice_fusion
  700.7 2.7 fusion.25
  703.4 1.8 fusion.36
  705.4 0.7 reshape.131
  706.5 1.4 fusion.17
  707.9 1.5 convolution_add_fusion.7
  709.3 1.4 convolution_add_fusion.6
  710.7 1.4 convolution_add_fusion.5
  712.1 1.4 convolution_add_fusion.4
  713.5 1.4 convolution_add_fusion.3
  714.9 114.2 %reduce-scatter.8.cloned.1.call-done = f32[144,512]{1,0:T(8,128)} async-done(((f32[4608,512]{1,0:T(8,128)}), f32[144,512]{1,0:T(8,128)}) %reduce-scatter.8.cloned.1.call-update) | async-done | bytes 294928 | tf_op jit(solution)/shard_map/reduce_scatter | solution.py:75
  829.1 2.0 copy.22
  831.1 1.4 convolution_add_fusion.2
  832.6 1.4 convolution_add_fusion.1
  834.0 1.4 convolution_add_fusion
  835.4 1.2 reshape.143
  836.6 70.2 %reduce-scatter.10.cloned.1.call-done = f32[64,144]{1,0:T(8,128)} async-done(((f32[512,144]{1,0:T(8,128)}), f32[64,144]{1,0:T(8,128)}) %reduce-scatter.10.cloned.1.call-update) | async-done | bytes 36880
  (55 shorter events, 2.4 us)
Async XLA Ops:
  7.2 128.0 %copy-start = (bf16[3136,128]{1,0:T(8,128)(2,1)S(1)}, bf16[3136,128]{1,0:T(8,128)(2,1)}, u32[]{:S(2)}) copy-start(bf16[3136,128]{1,0:T(8,128)(2,1)} %param.7) | copy-start | bytes 2408452
  7.2 84.4 %all-gather.6.cloned.1.call-start = ((), (), s32[]{:S(2)}) async-start(), calls=%async_computation.10 | async-start | bytes 3311616 | tf_op jit(solution)/shard_map/all_gather | solution.py:35
  11.5 6.4 copy-start.4
  11.6 6.3 copy-start.3
  11.7 6.5 copy-start.2
  12.0 6.5 copy-start.5
  12.0 5.6 copy-start.1
  15.0 3.8 copy-start.6
  21.1 195.8 %all-reduce.7.cloned.1.call-start = ((), (), s32[]{:S(2)}) async-start(), calls=%async_computation.5 | async-start | bytes 262144 | tf_op jit(solution)/shard_map/psum | solution.py:38
  106.0 183.2 %copy-start.8 = (bf16[4096,16]{0,1:T(8,128)(2,1)S(1)}, bf16[4096,16]{0,1:T(8,128)(2,1)}, u32[]{:S(2)}) copy-start(bf16[4096,16]{0,1:T(8,128)(2,1)} %param.8) | copy-start | bytes 393220
  106.2 185.3 %copy-start.9 = (bf16[256,16]{0,1:T(8,128)(2,1)S(1)}, bf16[256,16]{0,1:T(8,128)(2,1)}, u32[]{:S(2)}) copy-start(bf16[256,16]{0,1:T(8,128)(2,1)} %param.9) | copy-start | bytes 24580
  136.4 152.8 %all-gather.4.cloned.1.call-start = ((), (), s32[]{:S(2)}) async-start(), calls=%async_computation.6 | async-start | bytes 2162688 | tf_op jit(solution)/shard_map/all_gather | solution.py:40
  218.5 191.9 %reduce-scatter.6.cloned.1.call-start = ((), (), s32[]{:S(2)}) async-start(), calls=%async_computation.7 | async-start | bytes 4325376 | tf_op jit(solution)/shard_map/reduce_scatter | solution.py:45
  294.2 202.1 %all-reduce.9.cloned.1.call-start = ((), (), s32[]{:S(2)}) async-start(), calls=%async_computation.8 | async-start | bytes 262144 | tf_op jit(solution)/shard_map/psum | solution.py:46
  497.4 6.8 copy-start.10
  499.7 38.7 %all-to-all-start.1 = ((f32[8,32,3136]{2,1,0:T(8,128)}), f32[8,32,3136]{2,1,0:T(8,128)}, u32[]{:S(2)}, u32[]{:S(2)}) async-start(f32[8,32,3136]{2,1,0:T(8,128)} %bitcast.60), calls=%async_computation.2 | async-start | bytes 6553600 | tf_op jit(solution)/shard_map/all_to_all | solution.py:50
  504.2 324.9 %reduce-scatter.8.cloned.1.call-start = ((), (), s32[]{:S(2)}) async-start(), calls=%async_computation.9 | async-start | bytes 9732096 | tf_op jit(solution)/shard_map/reduce_scatter | solution.py:75
  689.3 9.9 %copy-start.7 = (bf16[196,512]{1,0:T(8,128)(2,1)S(1)}, bf16[196,512]{1,0:T(8,128)(2,1)}, u32[]{:S(2)}) copy-start(bf16[196,512]{1,0:T(8,128)(2,1)} %reshape.127) | copy-start | bytes 602116
  700.6 206.2 %reduce-scatter.10.cloned.1.call-start = ((), (), s32[]{:S(2)}) async-start(), calls=%async_computation.11 | async-start | bytes 589824
Sparse Core Ops, SparseCore 0:
  21.2 70.3 all-gather.5
  136.5 80.3 all-reduce.6
  219.4 69.8 all-gather.3
  294.4 116.0 reduce-scatter.5
  413.1 83.2 all-reduce.8
  700.7 128.3 reduce-scatter.7
  833.5 73.2 reduce-scatter.9
where the time goes:
time: 916 us; the launch traced here: 914 us
  waiting for transfers between devices  641 us (70%)
  blocking collectives  158 us (17%)
  matrix products  48.9 us (5%)
  local copies, waits for them, and re-layouts  26.4 us (3%)
  other arithmetic  18.7 us (2%)
  between operations  14.6 us (2%)
    unnamed x1, blocking collectives  129 us
    reduce_scatter x1, waiting for transfers between devices, on_device(): lax.psum_scatter(hidden_terms, 'gy', scatter_dimension=1, tiled=True)  116 us
    reduce_scatter x1, waiting for transfers between devices, on_device(): lax.psum_scatter(kernel_terms, 'gy', scatter_dimension=0, tiled=True)  114 us
    psum x1, waiting for transfers between devices, on_device(): grad_hidden = lax.psum(column_sums, 'gx')  85.9 us
    psum x1, waiting for transfers between devices, on_device(): h6_pre = lax.psum(partial_value, 'gx')  80.4 us
    all_gather x1, waiting for transfers between devices, on_device(): hidden = lax.all_gather(own_block, 'gy', axis=1, tiled=True)  70.5 us
    unnamed x8, waiting for transfers between devices  70.4 us
    all_gather x1, waiting for transfers between devices, on_device(): group_rows = lax.all_gather(feat, 'gy', axis=0, tiled=True)  70.2 us
  transfers between devices with their start and end apart: 8, of which 8 were waited for; matrix products, arithmetic and copies ran while one was open for 2% of the time, Pallas kernels for 0%

commit v1 on v0

v1 whole, which is shorter than its diff:
```python
import jax
import jax.numpy as jnp
from jax import lax
from jax.sharding import Mesh, PartitionSpec as P

BF = jnp.bfloat16
F32 = jnp.float32


def activate(value):
    return value * jax.nn.sigmoid(value)


def slope(value):
    sig = jax.nn.sigmoid(value)
    return sig * (1.0 + value * (1.0 - sig))


def dot(a, b, dims):
    return lax.dot_general(a, b, (dims, ((), ())), preferred_element_type=F32)


def swap(value, axis):
    return lax.all_to_all(value, axis, 0, 0, tiled=True)


def share(value, axis, count):
    return swap(jnp.broadcast_to(value, (count,) + value.shape), axis)


def patches(arr, flip):
    side = arr.shape[1]
    padded = jnp.pad(arr, ((0, 0), (1, 1), (1, 1), (0, 0)))
    out = []
    for row in range(3):
        for col in range(3):
            r, q = (2 - row, 2 - col) if flip else (row, col)
            out.append(padded[:, r : r + side, q : q + side, :].reshape(-1, arr.shape[3]))
    return out


def make(nx, nz, nc):
    ny = nz * nc

    def on_device(images, conv_weight, fc6_weight, fc7_weight, cotangent):
        side, chans = images.shape[1], images.shape[3]
        half = side // 2
        pix = side * side
        feats, units = fc6_weight.shape
        rows7, cols7 = fc7_weight.shape
        group = cotangent.shape[0] // nc
        wide = units * nc

        weight6 = lax.all_gather(fc6_weight, "core", axis=0, tiled=False)
        gathered = lax.all_gather(images[0], "gx", axis=0, tiled=False)
        send7 = fc7_weight.T.reshape(cols7, nz, wide).transpose(1, 0, 2)
        send7 = jnp.broadcast_to(send7[:, None], (nz, nc, cols7, wide)).reshape(ny, cols7, wide)
        weight7 = swap(send7, ("gz", "core")).reshape(ny * cols7, wide)
        cot = cotangent.T.reshape(cols7, nx, nz, nc).transpose(0, 3, 2, 1)
        cot = cot.reshape(cols7, nc * group).astype(F32)

        taps = jnp.concatenate(patches(images, False), axis=1)
        conv_pre = jnp.dot(taps, conv_weight, preferred_element_type=F32)
        pooled = activate(conv_pre).reshape(half, 2, half, 2, chans).sum(axis=(1, 3))
        feat = (0.25 * pooled).astype(BF).reshape(nx, feats)
        inputs = share(swap(feat, "gx"), "gz", nz).reshape(group, feats)

        h6_terms = jnp.concatenate([dot(inputs, weight6[k], ((1,), (0,))) for k in range(nc)], 1)
        h6_pre = share(h6_terms.astype(BF), "gx", nx).astype(F32).sum(axis=0)
        hidden = activate(h6_pre).astype(BF)
        all_hidden = lax.all_gather(hidden, ("gz", "core"), axis=0, tiled=False)

        y7_terms = dot(weight7, hidden, ((1,), (1,))).astype(BF)
        y7_pre = swap(y7_terms.reshape(ny, cols7, group), ("gz", "core"))
        y7_pre = y7_pre.reshape(nz, nc, cols7, group).astype(F32).sum(axis=0)
        y7_pre = y7_pre.transpose(1, 0, 2).reshape(cols7, nc * group)
        g_seven = (cot * slope(y7_pre)).astype(BF)
        send = g_seven.reshape(cols7, nc, group).transpose(1, 0, 2)
        send = jnp.broadcast_to(send[None], (nz, nc, cols7, group)).reshape(ny, cols7, group)
        g7_cols = swap(send, ("gz", "core")).reshape(ny * cols7, group)

        dh6_terms = dot(g7_cols, weight7, ((0,), (0,))).astype(BF)
        grad_hidden = share(dh6_terms, "gx", nx).astype(F32).sum(axis=0)
        g_six = (grad_hidden * slope(h6_pre)).astype(BF)

        feat_terms = sum(
            dot(g_six[:, k * units : (k + 1) * units], weight6[k], ((1,), (1,)))
            for k in range(nc)
        )
        feat_terms = swap(feat_terms.astype(BF).reshape(nz, nx, feats), "gz")
        dfeat = swap(feat_terms.astype(F32).sum(axis=0).astype(BF), "gx")

        spread = jnp.broadcast_to(
            dfeat.reshape(half, 1, half, 1, chans).astype(F32), (half, 2, half, 2, chans)
        ).reshape(pix, chans)
        g_conv = (0.25 * spread * slope(conv_pre)).astype(BF)

        part = chans // nx
        g_cols = swap(g_conv.reshape(pix, nx, part).transpose(1, 0, 2), "gx")
        g_cols = g_cols.reshape(nx * pix, part)
        kernel_terms = jnp.concatenate(
            [dot(p, g_cols, ((0,), (0,))) for p in patches(gathered, False)], axis=0
        )
        block = kernel_terms.shape[0] // ny
        packed = kernel_terms.astype(BF).reshape(ny, 2, block // 2, part)
        packed = jnp.concatenate([packed[:, 0], packed[:, 1]], axis=2)
        summed = swap(packed, ("gz", "core")).astype(F32).sum(axis=0)
        grad_conv = jnp.concatenate([summed[:, :part], summed[:, part:]], axis=0)

        grad6_terms = jnp.stack(
            [dot(inputs, g_six[:, k * units : (k + 1) * units], ((0,), (0,))) for k in range(nc)]
        )
        grad_fc6 = lax.psum_scatter(grad6_terms, "core", scatter_dimension=0, tiled=False)
        all_hidden = all_hidden.reshape(nz, nc, group, wide)
        grad7 = sum(
            dot(g_seven[:, k * group : (k + 1) * group], all_hidden[:, k], ((1,), (1,)))
            for k in range(nc)
        )
        grad_fc7 = grad7.reshape(cols7, rows7).T
        taps = jnp.concatenate(patches(g_conv.reshape(1, side, side, chans), True), axis=1)
        flipped = conv_weight.reshape(9, chans, chans)
        grad_in = sum(
            dot(taps[:, k * chans : (k + 1) * chans], flipped[k], ((1,), (1,))) for k in range(9)
        )
        grad_images = grad_in.reshape(1, side, side, chans)
        return (grad_conv, grad_fc6, grad_fc7, grad_images)

    return on_device


def solution(mesh):
    nx, ny = mesh.shape["gx"], mesh.shape["gy"]
    nc = 2
    nz = ny // nc
    fine = Mesh(mesh.devices.reshape(nx, nz, nc), ("gx", "gz", "core"))
    gy = ("gz", "core")
    both = ("gx", "gz", "core")
    placed = (
        P(both, None, None, None),
        P(),
        P("gx", gy),
        P(None, both),
        P(None, both),
    )
    return jax.shard_map(
        make(nx, nz, nc),
        mesh=fine,
        in_specs=placed,
        out_specs=(
            P(gy, "gx"),
            P("gx", gy),
            P(None, both),
            P(both, None, None, None),
        ),
        check_vma=False,
    )
```

time: 916 us -> 291 us (0.32)
  waiting for transfers between devices: 641 us -> 60.1 us
  blocking collectives: 158 us -> 42.1 us
  local copies, waits for them, and re-layouts: 26.4 us -> 75.1 us
  starting transfers between devices: 5.14 us -> 52 us
  matrix products: 48.9 us -> 36.8 us
  other arithmetic: 18.7 us -> 7.06 us
    reduce_scatter x2 -> x1, waiting for transfers between devices: 230 us -> 0.01 us  [on_device(): lax.psum_scatter(grad6_terms, 'core', scatter_dimension=0, tiled=False)]
    psum x2 -> x0, waiting for transfers between devices: 166 us -> none  [the longest x1 85.9 us: on_device(): grad_hidden = lax.psum(column_sums, 'gx')]
    all_gather x2 -> x3, waiting for transfers between devices: 141 us -> 0.02 us  [the longest x1 0.02 us: on_device(): gathered = lax.all_gather(images[0], 'gx', axis=0, tiled=False)]
    unnamed x1 -> x0, blocking collectives: 129 us -> none
    unnamed x8 -> x4, waiting for transfers between devices: 70.4 us -> 1.41 us
    all_to_all x1 -> x8, starting transfers between devices: 4.45 us -> 51.9 us  [swap(): return lax.all_to_all(value, axis, 0, 0, tiled=True)]
    reshape x20 -> x31, local copies, waits for them, and re-layouts: 4.92 us -> 33.1 us  [the longest x26 29.6 us: patches(): out.append(padded[:, r:r + side, q:q + side, :].reshape(-1, arr.shape[3]))]
    all_to_all x1 -> x8, waiting for transfers between devices: 33.6 us -> 58.7 us  [swap(): return lax.all_to_all(value, axis, 0, 0, tiled=True)]
  transfers between devices with their start and end apart: 8 -> 12, of which waited for: 8 -> 6; matrix products, arithmetic and copies ran while one was open for 2% -> 41% of each run, Pallas kernels for 0% -> 0%
where the time goes in v1:
time: 291 us; the launch traced here: 288 us
  local copies, waits for them, and re-layouts  75.1 us (26%)
  waiting for transfers between devices  60.1 us (21%)
  starting transfers between devices  52 us (18%)
  blocking collectives  42.1 us (14%)
  matrix products  36.8 us (13%)
  between operations  14.5 us (5%)
  other arithmetic  7.06 us (2%)
    all_to_all x8, waiting for transfers between devices, swap(): return lax.all_to_all(value, axis, 0, 0, tiled=True)  58.7 us
    all_to_all x8, starting transfers between devices, swap(): return lax.all_to_all(value, axis, 0, 0, tiled=True)  51.9 us
    all_to_all x3, blocking collectives, swap(): return lax.all_to_all(value, axis, 0, 0, tiled=True)  42.1 us
    dot_general x28, matrix products, dot(): return lax.dot_general(a, b, (dims, ((), ())), preferred_element_type=F32)  32 us
    reshape x26, local copies, waits for them, and re-layouts, patches(): out.append(padded[:, r:r + side, q:q + side, :].reshape(-1, arr.shape[3]))  29.6 us
    slice x3, local copies, waits for them, and re-layouts, patches(): out.append(padded[:, r:r + side, q:q + side, :].reshape(-1, arr.shape[3]))  14.2 us
    unnamed x61, local copies, waits for them, and re-layouts  8.97 us
  transfers between devices with their start and end apart: 12, of which 6 were waited for; matrix products, arithmetic and copies ran while one was open for 41% of the time, Pallas kernels for 0%

profile of v1, /device:TPU:1, one launch (start us, length us, event | category | flops | bytes accessed | tf_op | source)
XLA Modules:
  0.0 287.7 jit_solution(15413464555371305263)
XLA Ops:
  7.9 2.4 pad_slice_fusion.16
  17.4 4.8 %fusion.34 = (f32[196,512]{1,0:T(8,128)S(1)}, f32[196,512]{1,0:T(8,128)}) fusion(bf16[196,4608]{1,0:T(8,128)(2,1)} %constant_dynamic-update-slice_fusion, bf16[4608,512]{1,0:T(8,128)(2,1)} %param.6), kind=kOutput, calls=%fused_computation.78 | convolution fusion | flops 925245440 | bytes 7327744 | tf_op jit(solution)/shard_map/dot_general | solution.py:63
  23.4 0.9 reduce.3
  24.4 13.9 %all_to_all.63 = bf16[8,2,1568]{2,1,0:T(2,128)(2,1)S(1)} all-to-all(bf16[8,2,1568]{2,1,0:T(2,128)(2,1)S(1)} %reshape.288), channel_id=1, replica_groups=mesh['gx'=8,'gz'=16,'core'=2] {'gx'}, dimensions={0} | all-to-all | bytes 100352 | tf_op jit(solution)/shard_map/all_to_all | solution.py:24
  38.5 0.9 broadcast_in_dim.12
  39.5 8.3 %all-to-all-start.1 = ((bf16[16,8,3136]{2,1,0:T(8,128)(2,1)}), bf16[16,8,3136]{2,1,0:T(8,128)(2,1)S(1)}, u32[]{:S(2)}, u32[]{:S(2)}) async-start(bf16[16,8,3136]{2,1,0:T(8,128)(2,1)} %broadcast_in_dim.12), calls=%async_computation.1 | async-start | bytes 1638400 | tf_op jit(solution)/shard_map/all_to_all | solution.py:24
  48.6 17.5 %all-to-all-done.1 = bf16[16,8,3136]{2,1,0:T(8,128)(2,1)S(1)} async-done(((bf16[16,8,3136]{2,1,0:T(8,128)(2,1)}), bf16[16,8,3136]{2,1,0:T(8,128)(2,1)S(1)}, u32[]{:S(2)}, u32[]{:S(2)}) %all-to-all-start.1) | async-done | bytes 802848 | tf_op jit(solution)/shard_map/all_to_all | solution.py:24
  66.1 1.6 convolution_convert_fusion.10
  67.7 1.6 convolution_convert_fusion.11
  70.3 3.7 %all-to-all-start.2 = ((bf16[8,128,256]{2,1,0:T(8,128)(2,1)}), bf16[8,128,256]{2,1,0:T(8,128)(2,1)S(1)}, u32[]{:S(2)}, u32[]{:S(2)}) async-start(bf16[8,128,256]{2,1,0:T(8,128)(2,1)} %broadcast_in_dim.13), calls=%async_computation.2 | async-start | bytes 1048576 | tf_op jit(solution)/shard_map/all_to_all | solution.py:24
  74.1 8.6 %all-to-all-done.2 = bf16[8,128,256]{2,1,0:T(8,128)(2,1)S(1)} async-done(((bf16[8,128,256]{2,1,0:T(8,128)(2,1)}), bf16[8,128,256]{2,1,0:T(8,128)(2,1)S(1)}, u32[]{:S(2)}, u32[]{:S(2)}) %all-to-all-start.2) | async-done | bytes 524320 | tf_op jit(solution)/shard_map/all_to_all | solution.py:24
  83.3 10.2 %all-to-all-start.3 = ((bf16[32,16,256]{2,1,0:T(8,128)(2,1)}), bf16[32,16,256]{2,1,0:T(8,128)(2,1)S(1)}, u32[]{:S(2)}, u32[]{:S(2)}) async-start(bf16[32,16,256]{2,1,0:T(8,128)(2,1)} %bitcast.7), calls=%async_computation.3 | async-start | bytes 524288 | tf_op jit(solution)/shard_map/all_to_all | solution.py:24
  93.6 11.8 %all-to-all-done.3 = bf16[32,16,256]{2,1,0:T(8,128)(2,1)S(1)} async-done(((bf16[32,16,256]{2,1,0:T(8,128)(2,1)}), bf16[32,16,256]{2,1,0:T(8,128)(2,1)S(1)}, u32[]{:S(2)}, u32[]{:S(2)}) %all-to-all-start.3) | async-done | bytes 262176 | tf_op jit(solution)/shard_map/all_to_all | solution.py:24
  106.4 5.0 %all-to-all-start.4 = ((bf16[32,16,128]{2,1,0:T(8,128)(2,1)}), bf16[32,16,128]{2,1,0:T(8,128)(2,1)S(1)}, u32[]{:S(2)}, u32[]{:S(2)}) async-start(bf16[32,16,128]{2,1,0:T(8,128)(2,1)} %bitcast.10), calls=%async_computation.4 | async-start | bytes 262144 | tf_op jit(solution)/shard_map/all_to_all | solution.py:24
  112.5 8.1 %all-to-all-done.4 = bf16[32,16,128]{2,1,0:T(8,128)(2,1)S(1)} async-done(((bf16[32,16,128]{2,1,0:T(8,128)(2,1)}), bf16[32,16,128]{2,1,0:T(8,128)(2,1)S(1)}, u32[]{:S(2)}, u32[]{:S(2)}) %all-to-all-start.4) | async-done | bytes 131104 | tf_op jit(solution)/shard_map/all_to_all | solution.py:24
  120.7 15.0 %all_to_all.64 = bf16[32,16,128]{2,1,0:T(8,128)(2,1)S(1)} all-to-all(bf16[32,16,128]{2,1,0:T(8,128)(2,1)S(1)} %bitcast.181), channel_id=1, replica_groups=mesh['gx'=8,'gz'=16,'core'=2] {'gz','core'}, dimensions={0} | all-to-all | bytes 262144 | tf_op jit(solution)/shard_map/all_to_all | solution.py:24
  136.0 13.1 %all_to_all.65 = bf16[8,128,256]{2,1,0:T(8,128)(2,1)S(1)} all-to-all(bf16[8,128,256]{2,1,0:T(8,128)(2,1)S(1)} %broadcast_in_dim.30), channel_id=1, replica_groups=mesh['gx'=8,'gz'=16,'core'=2] {'gx'}, dimensions={0} | all-to-all | bytes 1048576 | tf_op jit(solution)/shard_map/all_to_all | solution.py:24
  150.0 1.7 copy.102
  151.7 3.8 %all-to-all-start.7 = ((bf16[16,8,3136]{2,1,0:T(8,128)(2,1)}), bf16[16,8,3136]{2,1,0:T(8,128)(2,1)S(1)}, u32[]{:S(2)}, u32[]{:S(2)}) async-start(bf16[16,8,3136]{2,1,0:T(8,128)(2,1)} %bitcast.16), calls=%async_computation.7 | async-start | bytes 1638400 | tf_op jit(solution)/shard_map/all_to_all | solution.py:24
  155.7 10.8 %pad_slice_fusion = (bf16[8,14,14,512]{3,2,1,0:T(8,128)(2,1)}, bf16[8,14,14,512]{3,2,1,0:T(8,128)(2,1)}, bf16[8,14,14,512]{3,2,1,0:T(8,128)(2,1)}, bf16[8,14,14,...) fusion(bf16[8,14,14,512]{3,2,1,0:T(8,128)(2,1)} %all-gather.5.c, ...), kind=kLoop, calls=%fused_computation.5 | loop fusion | bytes 14450688 | tf_op jit(solution)/shard_map/slice | solution.py:38
  166.5 3.7 %reshape.232 = bf16[1568,512]{1,0:T(8,128)(2,1)} reshape(bf16[8,14,14,512]{3,2,1,0:T(8,128)(2,1)} %get-tuple-element.35) | data formatting | bytes 3211264 | tf_op jit(solution)/shard_map/reshape | solution.py:38
  170.1 3.6 %reshape.252 = bf16[1568,512]{1,0:T(8,128)(2,1)} reshape(bf16[8,14,14,512]{3,2,1,0:T(8,128)(2,1)} %get-tuple-element.29) | data formatting | bytes 3211264 | tf_op jit(solution)/shard_map/reshape | solution.py:38
  173.8 3.6 %reshape.253 = bf16[1568,512]{1,0:T(8,128)(2,1)} reshape(bf16[8,14,14,512]{3,2,1,0:T(8,128)(2,1)} %get-tuple-element.30) | data formatting | bytes 3211264 | tf_op jit(solution)/shard_map/reshape | solution.py:38
  177.4 3.6 %reshape.254 = bf16[1568,512]{1,0:T(8,128)(2,1)} reshape(bf16[8,14,14,512]{3,2,1,0:T(8,128)(2,1)} %get-tuple-element.31) | data formatting | bytes 3211264 | tf_op jit(solution)/shard_map/reshape | solution.py:38
  181.1 3.7 %reshape.256 = bf16[1568,512]{1,0:T(8,128)(2,1)} reshape(bf16[8,14,14,512]{3,2,1,0:T(8,128)(2,1)} %get-tuple-element.32) | data formatting | bytes 3211264 | tf_op jit(solution)/shard_map/reshape | solution.py:38
  184.7 3.6 %reshape.257 = bf16[1568,512]{1,0:T(8,128)(2,1)} reshape(bf16[8,14,14,512]{3,2,1,0:T(8,128)(2,1)} %get-tuple-element.33) | data formatting | bytes 3211264 | tf_op jit(solution)/shard_map/reshape | solution.py:38
  188.3 1.4 reshape.258
  189.7 3.8 %reshape.259 = bf16[1568,512]{1,0:T(8,128)(2,1)} reshape(bf16[8,14,14,512]{3,2,1,0:T(8,128)(2,1)} %get-tuple-element.28) | data formatting | bytes 3211264 | tf_op jit(solution)/shard_map/reshape | solution.py:38
  193.6 1.4 reshape.255
  195.4 1.6 convolution_bitcast_fusion.1
  198.5 3.3 %all-to-all-start.8 = ((bf16[8,2,1568]{2,1,0:T(2,128)(2,1)}), bf16[8,2,1568]{2,1,0:T(2,128)(2,1)S(1)}, u32[]{:S(2)}, u32[]{:S(2)}) async-start(bf16[8,2,1568]{2,1,0:T(2,128)(2,1)} %reshape.290), calls=%async_computation.8 | async-start | bytes 106496 | tf_op jit(solution)/shard_map/all_to_all | solution.py:24
  201.9 3.3 %pad_maximum_fusion = f32[2,3136,128]{2,1,0:T(8,128)} fusion(f32[1,3136,128]{2,1,0:T(8,128)S(1)} %convolution_bitcast_fusion, f32[1,3136,128]{2,1,0:T(8,128)} %convolution_bitcast_fusion.1), kind=kLoop, calls=%fused_computation.4 | loop fusion | flops 802816 | bytes 6422528 | tf_op jit(solution)/shard_map/stack | solution.py:110
  205.2 3.2 %all-to-all-done.8 = bf16[8,2,1568]{2,1,0:T(2,128)(2,1)S(1)} async-done(((bf16[8,2,1568]{2,1,0:T(2,128)(2,1)}), bf16[8,2,1568]{2,1,0:T(2,128)(2,1)S(1)}, u32[]{:S(2)}, u32[]{:S(2)}) %all-to-all-start.8) | async-done | bytes 50208 | tf_op jit(solution)/shard_map/all_to_all | solution.py:24
  209.6 0.8 copy.104
  210.5 4.3 %all-to-all-start.9 = ((bf16[8,196,64]{1,2,0:T(8,128)(2,1)}), bf16[8,196,64]{1,2,0:T(8,128)(2,1)}, u32[]{:S(2)}, u32[]{:S(2)}) async-start(bf16[8,196,64]{1,2,0:T(8,128)(2,1)} %bitcast.19), calls=%async_computation.9 | async-start | bytes 524288 | tf_op jit(solution)/shard_map/all_to_all | solution.py:24
  214.8 1.1 pad_slice_fusion.8
  216.1 1.4 fusion.32
  217.5 1.4 convolution_add_fusion.8
  218.9 1.5 convolution_add_fusion.7
  220.4 2.2 convolution_add_fusion.6
  222.6 1.8 copy.105
  224.4 1.3 reshape.251
  225.7 1.0 fusion.11
  226.8 1.1 fusion.10
  227.8 1.1 fusion.9
  228.9 1.0 fusion.8
  229.9 1.0 fusion.13
  231.0 1.1 fusion.7
  232.1 1.1 fusion.6
  233.1 1.1 fusion.5
  234.2 1.0 fusion.4
  235.2 5.2 %convert_element_type.131 = bf16[32,2,72,64]{2,1,0,3:T(2,128)(2,1)S(1)} reshape(bf16[4608,64]{0,1:T(8,128)(2,1)} %fusion.4) | data formatting | bytes 1179648 | tf_op jit(solution)/shard_map/convert_element_type | solution.py:105
  240.4 2.4 fusion.60
  244.3 1.2 copy.108
  245.5 13.3 %all-to-all-start.10 = ((bf16[32,72,128]{2,1,0:T(8,128)(2,1)}), bf16[32,72,128]{2,1,0:T(8,128)(2,1)S(1)}, u32[]{:S(2)}, u32[]{:S(2)}) async-start(bf16[32,72,128]{2,1,0:T(8,128)(2,1)} %copy.108), calls=%async_computation.10 | async-start | bytes 1179648 | tf_op jit(solution)/shard_map/all_to_all | solution.py:24
  258.8 1.4 convolution_add_fusion.5
  260.5 1.4 convolution_add_fusion.4
  261.9 1.4 convolution_add_fusion.3
  263.3 1.4 convolution_add_fusion.2
  264.7 1.4 convolution_add_fusion.1
  266.0 1.2 reshape.286
  267.3 9.3 %all-to-all-done.10 = bf16[32,72,128]{2,1,0:T(8,128)(2,1)S(1)} async-done(((bf16[32,72,128]{2,1,0:T(8,128)(2,1)}), bf16[32,72,128]{2,1,0:T(8,128)(2,1)S(1)}, u32[]{:S(2)}, u32[]{:S(2)}) %all-to-all-start.10) | async-done | bytes 589856 | tf_op jit(solution)/shard_map/all_to_all | solution.py:24
  277.5 1.5 fusion.14
  279.0 1.5 fusion.1
  (135 shorter events, 21.8 us)
Async XLA Ops:
  7.2 3.1 %copy-start.13 = (bf16[1,14,14,512]{3,2,1,0:T(8,128)(2,1)S(1)}, bf16[1,14,14,512]{3,2,1,0:T(8,128)(2,1)}, u32[]{:S(2)}) copy-start(bf16[1,14,14,512]{3,2,1,0:T(8,128)(2,1)} %param.5) | copy-start | bytes 602116
  7.2 58.9 %all-gather.9.cloned.1.call-start = ((), (), s32[]{:S(2)}) async-start(), calls=%async_computation.15 | async-start | bytes 2408448 | tf_op jit(solution)/shard_map/all_gather | solution.py:54
  39.5 26.6 %all-to-all-start.1 = ((bf16[16,8,3136]{2,1,0:T(8,128)(2,1)}), bf16[16,8,3136]{2,1,0:T(8,128)(2,1)S(1)}, u32[]{:S(2)}, u32[]{:S(2)}) async-start(bf16[16,8,3136]{2,1,0:T(8,128)(2,1)} %broadcast_in_dim.12), calls=%async_computation.1 | async-start | bytes 1638400 | tf_op jit(solution)/shard_map/all_to_all | solution.py:24
  47.8 107.8 %all-gather.5.cloned.1.call-start = ((), (), s32[]{:S(2)}) async-start(), calls=%async_computation.12 | async-start | bytes 2064384 | tf_op jit(solution)/shard_map/all_gather | solution.py:55
  67.7 6.3 %copy-start.20 = (bf16[4096,16]{0,1:T(8,128)(2,1)S(1)}, bf16[4096,16]{0,1:T(8,128)(2,1)}, u32[]{:S(2)}) copy-start(bf16[4096,16]{0,1:T(8,128)(2,1)} %param.8) | copy-start | bytes 393220
  70.3 12.4 %all-to-all-start.2 = ((bf16[8,128,256]{2,1,0:T(8,128)(2,1)}), bf16[8,128,256]{2,1,0:T(8,128)(2,1)S(1)}, u32[]{:S(2)}, u32[]{:S(2)}) async-start(bf16[8,128,256]{2,1,0:T(8,128)(2,1)} %broadcast_in_dim.13), calls=%async_computation.2 | async-start | bytes 1048576 | tf_op jit(solution)/shard_map/all_to_all | solution.py:24
  74.0 37.5 %copy-start.21 = (bf16[256,16]{0,1:T(8,128)(2,1)S(1)}, bf16[256,16]{0,1:T(8,128)(2,1)}, u32[]{:S(2)}) copy-start(bf16[256,16]{0,1:T(8,128)(2,1)} %param.9) | copy-start | bytes 24580
  83.3 22.1 %all-to-all-start.3 = ((bf16[32,16,256]{2,1,0:T(8,128)(2,1)}), bf16[32,16,256]{2,1,0:T(8,128)(2,1)S(1)}, u32[]{:S(2)}, u32[]{:S(2)}) async-start(bf16[32,16,256]{2,1,0:T(8,128)(2,1)} %bitcast.7), calls=%async_computation.3 | async-start | bytes 524288 | tf_op jit(solution)/shard_map/all_to_all | solution.py:24
  106.4 14.2 %all-to-all-start.4 = ((bf16[32,16,128]{2,1,0:T(8,128)(2,1)}), bf16[32,16,128]{2,1,0:T(8,128)(2,1)S(1)}, u32[]{:S(2)}, u32[]{:S(2)}) async-start(bf16[32,16,128]{2,1,0:T(8,128)(2,1)} %bitcast.10), calls=%async_computation.4 | async-start | bytes 262144 | tf_op jit(solution)/shard_map/all_to_all | solution.py:24
  111.4 166.0 %all-gather.7.cloned.1.call-start = ((), (), s32[]{:S(2)}) async-start(), calls=%async_computation.14 | async-start | bytes 2162688 | tf_op jit(solution)/shard_map/all_gather | solution.py:71
  120.6 28.6 %copy-start.1 = (bf16[6272,128]{1,0:T(8,128)(2,1)S(1)}, bf16[6272,128]{1,0:T(8,128)(2,1)}, u32[]{:S(2)}) copy-start(bf16[6272,128]{1,0:T(8,128)(2,1)} %all-gather.9.cloned.1.call-done) | copy-start | bytes 4816900
  151.7 45.2 %all-to-all-start.7 = ((bf16[16,8,3136]{2,1,0:T(8,128)(2,1)}), bf16[16,8,3136]{2,1,0:T(8,128)(2,1)S(1)}, u32[]{:S(2)}, u32[]{:S(2)}) async-start(bf16[16,8,3136]{2,1,0:T(8,128)(2,1)} %bitcast.16), calls=%async_computation.7 | async-start | bytes 1638400 | tf_op jit(solution)/shard_map/all_to_all | solution.py:24
  189.7 3.8 %copy-start = (bf16[8,14,14,512]{3,2,1,0:T(8,128)(2,1)S(1)}, bf16[8,14,14,512]{3,2,1,0:T(8,128)(2,1)}, u32[]{:S(2)}) copy-start(bf16[8,14,14,512]{3,2,1,0:T(8,128)(2,1)} %all-gather.5.cloned.1.call-done) | copy-start | bytes 4816900
  198.5 10.0 %all-to-all-start.8 = ((bf16[8,2,1568]{2,1,0:T(2,128)(2,1)}), bf16[8,2,1568]{2,1,0:T(2,128)(2,1)S(1)}, u32[]{:S(2)}, u32[]{:S(2)}) async-start(bf16[8,2,1568]{2,1,0:T(2,128)(2,1)} %reshape.290), calls=%async_computation.8 | async-start | bytes 106496 | tf_op jit(solution)/shard_map/all_to_all | solution.py:24
  201.9 79.3 %reduce-scatter.2.cloned.1.call-start = ((), (), s32[]{:S(2)}) async-start(), calls=%async_computation.13 | async-start | bytes 4816896 | tf_op jit(solution)/shard_map/reduce_scatter | solution.py:113
  205.2 4.2 %copy-start.19 = (f32[196,512]{1,0:T(8,128)S(1)}, f32[196,512]{1,0:T(8,128)}, u32[]{:S(2)}) copy-start(f32[196,512]{1,0:T(8,128)} %get-tuple-element.59) | copy-start | bytes 1204228
  209.6 6.3 %copy-start.11 = (bf16[196,512]{1,0:T(8,128)(2,1)}, bf16[196,512]{1,0:T(8,128)(2,1)S(1)}, u32[]{:S(2)}) copy-start(bf16[196,512]{1,0:T(8,128)(2,1)S(1)} %multiply_convert_fusion) | copy-start | bytes 602116
  210.5 12.1 %all-to-all-start.9 = ((bf16[8,196,64]{1,2,0:T(8,128)(2,1)}), bf16[8,196,64]{1,2,0:T(8,128)(2,1)}, u32[]{:S(2)}, u32[]{:S(2)}) async-start(bf16[8,196,64]{1,2,0:T(8,128)(2,1)} %bitcast.19), calls=%async_computation.9 | async-start | bytes 524288 | tf_op jit(solution)/shard_map/all_to_all | solution.py:24
  218.9 6.8 %copy-start.8 = (bf16[1568,512]{1,0:T(8,128)(2,1)S(1)}, bf16[1568,512]{1,0:T(8,128)(2,1)}, u32[]{:S(2)}) copy-start(bf16[1568,512]{1,0:T(8,128)(2,1)} %reshape.232) | copy-start | bytes 4816900
  220.4 6.4 %copy-start.9 = (bf16[1568,512]{1,0:T(8,128)(2,1)S(1)}, bf16[1568,512]{1,0:T(8,128)(2,1)}, u32[]{:S(2)}) copy-start(bf16[1568,512]{1,0:T(8,128)(2,1)} %reshape.252) | copy-start | bytes 4816900
  225.7 2.1 copy-start.7
  226.8 2.1 copy-start.6
  227.8 2.1 copy-start.10
  228.9 2.1 copy-start.5
  229.9 2.1 copy-start.4
  231.0 2.1 copy-start.2
  232.0 2.1 copy-start.3
  244.3 14.5 %copy-start.12 = (bf16[196,512]{1,0:T(8,128)(2,1)S(1)}, bf16[196,512]{1,0:T(8,128)(2,1)}, u32[]{:S(2)}) copy-start(bf16[196,512]{1,0:T(8,128)(2,1)} %copy-done.11) | copy-start | bytes 602116
  244.3 14.5 %copy-start.14 = (f32[196,512]{1,0:T(8,128)S(1)}, f32[196,512]{1,0:T(8,128)}, u32[]{:S(2)}) copy-start(f32[196,512]{1,0:T(8,128)} %convolution_add_fusion.6) | copy-start | bytes 1204228
  244.3 15.9 %copy-start.18 = (bf16[1,14,14,512]{3,2,1,0:T(8,128)(2,1)S(1)}, bf16[1,14,14,512]{3,2,1,0:T(8,128)(2,1)}, u32[]{:S(2)}) copy-start(bf16[1,14,14,512]{3,2,1,0:T(8,128)(2,1)} %get-tuple-element.42) | copy-start | bytes 602116
  245.5 14.8 %copy-start.17 = (bf16[1,14,14,512]{3,2,1,0:T(8,128)(2,1)S(1)}, bf16[1,14,14,512]{3,2,1,0:T(8,128)(2,1)}, u32[]{:S(2)}) copy-start(bf16[1,14,14,512]{3,2,1,0:T(8,128)(2,1)} %get-tuple-element.43) | copy-start | bytes 602116
  245.5 14.8 %copy-start.16 = (bf16[1,14,14,512]{3,2,1,0:T(8,128)(2,1)S(1)}, bf16[1,14,14,512]{3,2,1,0:T(8,128)(2,1)}, u32[]{:S(2)}) copy-start(bf16[1,14,14,512]{3,2,1,0:T(8,128)(2,1)} %get-tuple-element.44) | copy-start | bytes 602116
  245.5 14.9 %copy-start.15 = (bf16[1,14,14,512]{3,2,1,0:T(8,128)(2,1)S(1)}, bf16[1,14,14,512]{3,2,1,0:T(8,128)(2,1)}, u32[]{:S(2)}) copy-start(bf16[1,14,14,512]{3,2,1,0:T(8,128)(2,1)} %get-tuple-element.38) | copy-start | bytes 602116
  245.5 31.1 %all-to-all-start.10 = ((bf16[32,72,128]{2,1,0:T(8,128)(2,1)}), bf16[32,72,128]{2,1,0:T(8,128)(2,1)S(1)}, u32[]{:S(2)}, u32[]{:S(2)}) async-start(bf16[32,72,128]{2,1,0:T(8,128)(2,1)} %copy.108), calls=%async_computation.10 | async-start | bytes 1179648 | tf_op jit(solution)/shard_map/all_to_all | solution.py:24
Sparse Core Ops, SparseCore 0:
  9.8 19.7 all-gather.8
  51.2 59.9 all-gather.4
  114.1 68.6 all-gather.6
  205.5 21.7 reduce-scatter.1

commit v2 on v1

v2 whole, which is shorter than its diff:
```python
import jax
import jax.numpy as jnp
from jax import lax
from jax.experimental import pallas as pl
from jax.experimental.pallas import tpu as pltpu
from jax.sharding import Mesh, PartitionSpec as P

BF = jnp.bfloat16
F32 = jnp.float32
LANES = 128
LINE = 16


def slope(value):
    sig = jax.nn.sigmoid(value)
    return sig * (1.0 + value * (1.0 - sig))


def activate(value):
    return value * jax.nn.sigmoid(value)


def forward_kernel(image_ref, weight_ref, pre_ref, feat_ref, sums_ref, pool_ref):
    step = pl.program_id(0)
    col = lax.rem(step, 3)
    rows = sums_ref.shape[1]
    start = pl.multiple_of((step // 3) * LINE, LINE)
    part = jnp.dot(
        image_ref[pl.ds(start, rows), :], weight_ref[...], preferred_element_type=F32
    )

    @pl.when(step < 3)
    def _():
        sums_ref[col] = part

    @pl.when(step >= 3)
    def _():
        sums_ref[col] += part

    @pl.when(step == 8)
    def _():
        pix, chans = pre_ref.shape
        pre = sums_ref[0, 0:pix, :] + sums_ref[1, 1 : pix + 1, :] + sums_ref[2, 2 : pix + 2, :]
        pre_ref[...] = pre
        act = activate(pre).reshape(pix // (2 * LINE), 2, LINE, chans)
        lines = (act[:, 0] + act[:, 1]).reshape(pix // 2, chans)
        half = pix // 4
        for k in range(chans // LANES):
            pool_ref[k] = lines[:, k * LANES : (k + 1) * LANES]
            total = pool_ref[k, pl.ds(0, half, 2), :] + pool_ref[k, pl.ds(1, half, 2), :]
            feat_ref[:, k * LANES : (k + 1) * LANES] = 0.25 * total


def conv_forward(lines, weight, side):
    chans = weight.shape[1]
    depth = lines.shape[1]
    pix = side * LINE
    return pl.pallas_call(
        forward_kernel,
        grid=(9,),
        in_specs=[
            pl.BlockSpec(lines.shape, lambda t: (0, 0)),
            pl.BlockSpec((depth, chans), lambda t: (t, 0)),
        ],
        out_specs=[
            pl.BlockSpec((pix, chans), lambda t: (0, 0)),
            pl.BlockSpec((pix // 4, chans), lambda t: (0, 0)),
        ],
        out_shape=[
            jax.ShapeDtypeStruct((pix, chans), F32),
            jax.ShapeDtypeStruct((pix // 4, chans), F32),
        ],
        scratch_shapes=[pltpu.VMEM((3, pix + LINE, chans), F32), pltpu.VMEM((chans // LANES, pix // 2, LANES), F32)],
        compiler_params=pltpu.CompilerParams(vmem_limit_bytes=32 * 2**20),
        cost_estimate=pl.CostEstimate(
            flops=18 * pix * depth * chans, bytes_accessed=weight.size * 2, transcendentals=pix * chans
        ),
    )(lines, weight)


def slope_kernel(pre_ref, dfeat_ref, lines_ref, turned_ref, wide_ref):
    pix, chans = pre_ref.shape
    half = pix // 4
    for k in range(chans // LANES):
        dfeat = dfeat_ref[:, k * LANES : (k + 1) * LANES]
        wide_ref[k, pl.ds(0, half, 2), :] = dfeat
        wide_ref[k, pl.ds(1, half, 2), :] = dfeat
    spread = jnp.concatenate([wide_ref[k] for k in range(chans // LANES)], axis=1)
    spread = spread.reshape(pix // (2 * LINE), 1, LINE, chans)
    spread = jnp.broadcast_to(spread, (pix // (2 * LINE), 2, LINE, chans)).reshape(pix, chans)
    grad = 0.25 * spread * slope(pre_ref[...])
    extra = turned_ref.shape[1] - pix
    grad = jnp.concatenate([grad, jnp.zeros((extra, chans), F32)], axis=0)
    turned_ref[...] = grad.T.astype(BF)
    lines_ref[...] = grad.astype(BF)


def conv_slope(pre, dfeat, rows):
    pix, chans = pre.shape
    return pl.pallas_call(
        slope_kernel,
        out_shape=[
            jax.ShapeDtypeStruct((rows, chans), BF),
            jax.ShapeDtypeStruct((chans, rows), BF),
        ],
        scratch_shapes=[pltpu.VMEM((chans // LANES, pix // 2, LANES), F32)],
        compiler_params=pltpu.CompilerParams(vmem_limit_bytes=32 * 2**20),
        cost_estimate=pl.CostEstimate(
            flops=8 * pix * chans, bytes_accessed=pix * chans * 8, transcendentals=pix * chans
        ),
    )(pre, dfeat)


def kernel_kernel(lines_ref, turned_ref, out_ref, sums_ref, flat_ref):
    step = pl.program_id(0)
    part, rows = turned_ref.shape
    chans = lines_ref.shape[1]
    turned = turned_ref[...].astype(F32)
    moved = [turned] + [pltpu.roll(turned, k, 1) for k in (1, 2)]
    moved = jnp.concatenate(moved, axis=0).astype(BF)

    for row in range(3):
        term = jnp.dot(
            moved, lines_ref[row * LINE : row * LINE + rows, :], preferred_element_type=F32
        )

        @pl.when(step == 0)
        def _():
            sums_ref[row] = term

        @pl.when(step > 0)
        def _():
            sums_ref[row] += term

    @pl.when(step == pl.num_programs(0) - 1)
    def _():
        for row in range(3):
            for col in range(3):
                tap = 3 * row + col
                flat_ref[tap * chans : (tap + 1) * chans, :] = sums_ref[
                    row, col * part : (col + 1) * part, :
                ].T
        count, size, _ = out_ref.shape
        for dest in range(count):
            at = dest * 2 * size
            both = [flat_ref[at : at + size, :], flat_ref[at + size : at + 2 * size, :]]
            out_ref[dest] = jnp.concatenate(both, axis=1).astype(BF)


def conv_kernel_grad(lines, turned, count):
    images, rows, chans = lines.shape
    _, part, cols = turned.shape
    size = 9 * chans // (2 * count)
    return pl.pallas_call(
        kernel_kernel,
        grid=(images,),
        in_specs=[
            pl.BlockSpec((None, rows, chans), lambda n: (n, 0, 0)),
            pl.BlockSpec((None, part, cols), lambda n: (n, 0, 0)),
        ],
        out_specs=pl.BlockSpec((count, size, 2 * part), lambda n: (0, 0, 0)),
        out_shape=jax.ShapeDtypeStruct((count, size, 2 * part), BF),
        scratch_shapes=[
            pltpu.VMEM((3, 3 * part, chans), F32),
            pltpu.VMEM((9 * chans, part), F32),
        ],
        compiler_params=pltpu.CompilerParams(vmem_limit_bytes=32 * 2**20),
        cost_estimate=pl.CostEstimate(
            flops=18 * images * cols * chans * part, bytes_accessed=lines.size * 2, transcendentals=0
        ),
    )(lines, turned)


def backward_kernel(lines_ref, weight_ref, out_ref, sums_ref):
    step = pl.program_id(0)
    col = lax.rem(step, 3)
    rows = sums_ref.shape[1]
    start = pl.multiple_of((2 - step // 3) * LINE, LINE)
    part = lax.dot_general(
        lines_ref[pl.ds(start, rows), :],
        weight_ref[...],
        (((1,), (1,)), ((), ())),
        preferred_element_type=F32,
    )

    @pl.when(step < 3)
    def _():
        sums_ref[col] = part

    @pl.when(step >= 3)
    def _():
        sums_ref[col] += part

    @pl.when(step == 8)
    def _():
        _, side, _, chans = out_ref.shape
        pix = side * LINE
        grad = sums_ref[0, 2 : pix + 2, :] + sums_ref[1, 1 : pix + 1, :] + sums_ref[2, 0:pix, :]
        out_ref[0] = grad.reshape(side, LINE, chans)[:, :side, :]


def conv_backward(lines, weight, side):
    chans = lines.shape[1]
    depth = weight.shape[0] // 9
    pix = side * LINE
    return pl.pallas_call(
        backward_kernel,
        grid=(9,),
        in_specs=[
            pl.BlockSpec(lines.shape, lambda t: (0, 0)),
            pl.BlockSpec((depth, chans), lambda t: (t, 0)),
        ],
        out_specs=pl.BlockSpec((1, side, side, depth), lambda t: (0, 0, 0, 0)),
        out_shape=jax.ShapeDtypeStruct((1, side, side, depth), F32),
        scratch_shapes=[pltpu.VMEM((3, pix + LINE, depth), F32)],
        compiler_params=pltpu.CompilerParams(vmem_limit_bytes=32 * 2**20),
        cost_estimate=pl.CostEstimate(
            flops=18 * pix * depth * chans, bytes_accessed=weight.size * 2, transcendentals=0
        ),
    )(lines, weight)


def dot(a, b, dims):
    return lax.dot_general(a, b, (dims, ((), ())), preferred_element_type=F32)


def swap(value, axis):
    return lax.all_to_all(value, axis, 0, 0, tiled=True)


def share(value, axis, count):
    return swap(jnp.broadcast_to(value, (count,) + value.shape), axis)


def bordered(maps):
    side, _, chans = maps.shape
    padded = jnp.pad(maps, ((1, 3), (1, LINE - side - 1), (0, 0)))
    return padded.reshape((side + 4) * LINE, chans)


def make(nx, nz, nc):
    ny = nz * nc

    def on_device(images, conv_weight, fc6_weight, fc7_weight, cotangent):
        side, chans = images.shape[1], images.shape[3]
        half = side // 2
        feats, units = fc6_weight.shape
        rows7, cols7 = fc7_weight.shape
        group = cotangent.shape[0] // nc
        wide = units * nc

        weight6 = lax.all_gather(fc6_weight, "core", axis=0, tiled=False)
        lines = bordered(images[0])
        gathered = lax.all_gather(lines, "gx", axis=0, tiled=False)
        send7 = fc7_weight.T.reshape(cols7, nz, wide).transpose(1, 0, 2)
        send7 = jnp.broadcast_to(send7[:, None], (nz, nc, cols7, wide)).reshape(ny, cols7, wide)
        weight7 = swap(send7, ("gz", "core")).reshape(ny * cols7, wide)
        cot = cotangent.T.reshape(cols7, nx, nz, nc).transpose(0, 3, 2, 1)
        cot = cot.reshape(cols7, nc * group).astype(F32)

        conv_pre, pooled = conv_forward(lines, conv_weight, side)
        pooled = pooled.reshape(half, half + 1, chans)[:, :half]
        feat = pooled.astype(BF).reshape(nx, feats)
        feat, weight7 = lax.optimization_barrier((feat, weight7))
        inputs = share(swap(feat, "gx"), "gz", nz).reshape(group, feats)

        weight6 = jnp.concatenate([weight6[k] for k in range(nc)], axis=1)
        inputs, weight6 = lax.optimization_barrier((inputs, weight6))
        h6_terms = dot(inputs, weight6, ((1,), (0,)))
        h6_pre = share(h6_terms.astype(BF), "gx", nx).astype(F32).sum(axis=0)
        hidden = activate(h6_pre).astype(BF)
        all_hidden = lax.all_gather(hidden, ("gz", "core"), axis=0, tiled=False)

        y7_terms = dot(weight7, hidden, ((1,), (1,))).astype(BF)
        y7_pre = swap(y7_terms.reshape(ny, cols7, group), ("gz", "core"))
        y7_pre = y7_pre.reshape(nz, nc, cols7, group).astype(F32).sum(axis=0)
        y7_pre = y7_pre.transpose(1, 0, 2).reshape(cols7, nc * group)
        g_seven = (cot * slope(y7_pre)).astype(BF)
        send = g_seven.reshape(cols7, nc, group).transpose(1, 0, 2)
        send = jnp.broadcast_to(send[None], (nz, nc, cols7, group)).reshape(ny, cols7, group)
        g7_cols = swap(send, ("gz", "core")).reshape(ny * cols7, group)

        dh6_terms = dot(g7_cols, weight7, ((0,), (0,))).astype(BF)
        grad_hidden = share(dh6_terms, "gx", nx).astype(F32).sum(axis=0)
        g_six = (grad_hidden * slope(h6_pre)).astype(BF)

        feat_terms = dot(g_six, weight6, ((1,), (1,))).astype(BF)
        feat_terms, g_late = lax.optimization_barrier((feat_terms, g_six))
        feat_terms = swap(feat_terms.reshape(nz, nx, feats), "gz")
        dfeat = swap(feat_terms.astype(F32).sum(axis=0).astype(BF), "gx")
        dfeat = dfeat.reshape(half, half, chans).astype(F32)
        dfeat = jnp.pad(dfeat, ((0, 0), (0, 1), (0, 0))).reshape(half * (half + 1), chans)

        g_lines, g_turned = conv_slope(conv_pre, dfeat, 2 * LANES)
        g_cols = swap(g_turned.reshape(nx, chans // nx, 2 * LANES), "gx")
        packed = swap(conv_kernel_grad(gathered, g_cols, ny), ("gz", "core"))
        packed = packed.astype(F32).sum(axis=0)
        part = chans // nx
        grad_conv = jnp.concatenate([packed[:, :part], packed[:, part:]], axis=0)

        grad6_terms = jnp.stack(
            [dot(inputs, g_late[:, k * units : (k + 1) * units], ((0,), (0,))) for k in range(nc)]
        )
        grad_fc6 = lax.psum_scatter(grad6_terms, "core", scatter_dimension=0, tiled=False)
        all_hidden = all_hidden.reshape(nz, nc, group, wide)
        grad7 = sum(
            dot(g_seven[:, k * group : (k + 1) * group], all_hidden[:, k], ((1,), (1,)))
            for k in range(nc)
        )
        grad_fc7 = grad7.reshape(cols7, rows7).T
        g_maps = g_lines[: side * LINE].reshape(side, LINE, chans)[:, :side]
        grad_images = conv_backward(bordered(g_maps), conv_weight, side)
        return (grad_conv, grad_fc6, grad_fc7, grad_images)

    return on_device


def solution(mesh):
    nx, ny = mesh.shape["gx"], mesh.shape["gy"]
    nc = 2
    nz = ny // nc
    fine = Mesh(mesh.devices.reshape(nx, nz, nc), ("gx", "gz", "core"))
    gy = ("gz", "core")
    both = ("gx", "gz", "core")
    return jax.shard_map(
        make(nx, nz, nc),
        mesh=fine,
        in_specs=(P(both, None, None, None), P(), P("gx", gy), P(None, both), P(None, both)),
        out_specs=(P(gy, "gx"), P("gx", gy), P(None, both), P(both, None, None, None)),
        check_vma=False,
    )
```

time: 291 us -> 244 us (0.84)
  local copies, waits for them, and re-layouts: 75.1 us -> 20.1 us
  blocking collectives: 42.1 us -> 93.9 us
  matrix products: 36.8 us -> 6.81 us
  Pallas kernels: 0 us -> 15.4 us
  waiting for transfers between devices: 60.1 us -> 47.7 us
  starting transfers between devices: 52 us -> 39.7 us
    all_to_all x3 -> x6, blocking collectives: 42.1 us -> 93.9 us  [swap(): return lax.all_to_all(value, axis, 0, 0, tiled=True)]
    reshape x30 -> x1, local copies, waits for them, and re-layouts: 32.3 us -> 0.12 us  [on_device(): feat = pooled.astype(BF).reshape(nx, feats)]
    dot_general x28 -> x8, matrix products: 32 us -> 6.81 us  [dot(): return lax.dot_general(a, b, (dims, ((), ())), preferred_element_type=F32)]
    pallas_call x0 -> x4, Pallas kernels: none -> 15.4 us  [the longest x1 7.65 us: conv_kernel_grad(): pl.pallas_call(kernel_kernel, grid=(images,), in_specs=[pl.BlockSpec((Non...]
    slice x5 -> x3, local copies, waits for them, and re-layouts: 16.7 us -> 1.58 us  [the longest x1 1.49 us: on_device(): weight6 = jnp.concatenate([weight6[k] for k in range(nc)], axis=1)]
    all_to_all x8 -> x5, starting transfers between devices: 51.9 us -> 39.5 us  [swap(): return lax.all_to_all(value, axis, 0, 0, tiled=True)]
    all_to_all x8 -> x5, waiting for transfers between devices: 58.7 us -> 46.9 us  [swap(): return lax.all_to_all(value, axis, 0, 0, tiled=True)]
    convert_element_type x6 -> x1, local copies, waits for them, and re-layouts: 9.17 us -> 0.13 us  [on_device(): dfeat = dfeat.reshape(half, half, chans).astype(F32)]
  transfers between devices with their start and end apart: 12 -> 9, of which waited for: 6 -> 5; matrix products, arithmetic and copies ran while one was open for 41% -> 10% of each run, Pallas kernels for 0% -> 6%
where the time goes in v2:
time: 244 us; the launch traced here: 243 us
  blocking collectives  93.9 us (38%)
  waiting for transfers between devices  47.7 us (20%)
  starting transfers between devices  39.7 us (16%)
  local copies, waits for them, and re-layouts  20.1 us (8%)
  Pallas kernels  15.4 us (6%)
  between operations  14.1 us (6%)
  matrix products  6.81 us (3%)
  other arithmetic  5.48 us (2%)
    all_to_all x6, blocking collectives, swap(): return lax.all_to_all(value, axis, 0, 0, tiled=True)  93.9 us
    all_to_all x5, waiting for transfers between devices, swap(): return lax.all_to_all(value, axis, 0, 0, tiled=True)  46.9 us
    all_to_all x5, starting transfers between devices, swap(): return lax.all_to_all(value, axis, 0, 0, tiled=True)  39.5 us
    unnamed x22, local copies, waits for them, and re-layouts  9.87 us
    pallas_call x1, Pallas kernels, conv_kernel_grad(): pl.pallas_call(kernel_kernel, grid=(images,), in_specs=[pl.BlockSpec((Non...  7.65 us
    dot_general x8, matrix products, dot(): return lax.dot_general(a, b, (dims, ((), ())), preferred_element_type=F32)  6.81 us
  transfers between devices with their start and end apart: 9, of which 5 were waited for; matrix products, arithmetic and copies ran while one was open for 10% of the time, Pallas kernels for 6%

profile of v2, /device:TPU:1, one launch (start us, length us, event | category | flops | bytes accessed | tf_op | source)
XLA Modules:
  0.0 243.0 jit_solution(15817621495649293933)
XLA Ops:
  7.2 0.7 all-gather.9.cloned.1.call-update
  8.0 1.7 pad.12
  9.8 0.7 broadcast_in_dim.10
  10.5 11.1 %all-to-all-start = ((bf16[32,16,256]{2,1,0:T(8,128)(2,1)}), bf16[32,16,256]{2,1,0:T(8,128)(2,1)S(1)}, u32[]{:S(2)}, u32[]{:S(2)}) async-start(bf16[32,16,256]{2,1,0:T(8,128)(2,1)} %bitcast.10), calls=%async_computation | async-start | bytes 524288 | tf_op jit(solution)/shard_map/all_to_all | solution.py:228
  21.6 2.3 copy-done
  23.9 3.3 %shard_map.84 = (f32[224,512]{1,0:T(8,128)S(1)}, f32[56,512]{1,0:T(8,128)S(1)}) custom-call(bf16[288,512]{1,0:T(8,128)(2,1)S(1)} %bitcast.135, bf16[4608,512]{1,0:T(8,128)(2,1)S(1)} %copy-done), custom_call_target="tpu_custom_call" | custom-call | flops 1056964608 | bytes 4718592 | tf_op jit(solution)/shard_map/pallas_call | solution.py:58
  27.2 0.1 reshape.114
  27.4 6.1 %all-to-all-done = bf16[32,16,256]{2,1,0:T(8,128)(2,1)S(1)} async-done(((bf16[32,16,256]{2,1,0:T(8,128)(2,1)}), bf16[32,16,256]{2,1,0:T(8,128)(2,1)S(1)}, u32[]{:S(2)}, u32[]{:S(2)}) %all-to-all-start) | async-done | bytes 262176 | tf_op jit(solution)/shard_map/all_to_all | solution.py:228
  33.5 0.5 broadcast.51
  34.0 0.6 reduce.2
  34.7 0.1 reshape.146
  34.8 12.8 %all_to_all.66 = bf16[8,2,1568]{2,1,0:T(2,128)(2,1)S(1)} all-to-all(bf16[8,2,1568]{2,1,0:T(2,128)(2,1)S(1)} %reshape.146), channel_id=1, replica_groups=mesh['gx'=8,'gz'=16,'core'=2] {'gx'}, dimensions={0} | all-to-all | bytes 100352 | tf_op jit(solution)/shard_map/all_to_all | solution.py:228
  47.6 0.1 reshape.147
  47.8 0.9 broadcast_in_dim.22
  48.7 3.6 %all-to-all-start.2 = ((bf16[16,8,3136]{2,1,0:T(8,128)(2,1)}), bf16[16,8,3136]{2,1,0:T(8,128)(2,1)S(1)}, u32[]{:S(2)}, u32[]{:S(2)}) async-start(bf16[16,8,3136]{2,1,0:T(8,128)(2,1)} %broadcast_in_dim.22), calls=%async_computation.2 | async-start | bytes 1638400 | tf_op jit(solution)/shard_map/all_to_all | solution.py:228
  52.4 1.5 fusion.25
  53.9 0.2 pad_maximum_fusion.1
  54.1 16.1 %all-to-all-done.2 = bf16[16,8,3136]{2,1,0:T(8,128)(2,1)S(1)} async-done(((bf16[16,8,3136]{2,1,0:T(8,128)(2,1)}), bf16[16,8,3136]{2,1,0:T(8,128)(2,1)S(1)}, u32[]{:S(2)}, u32[]{:S(2)}) %all-to-all-start.2) | async-done | bytes 802848 | tf_op jit(solution)/shard_map/all_to_all | solution.py:228
  70.2 0.4 convolution_convert_fusion.3
  70.7 16.5 %all_to_all.67 = bf16[8,128,256]{2,1,0:T(8,128)(2,1)S(1)} all-to-all(bf16[8,128,256]{2,1,0:T(8,128)(2,1)S(1)} %broadcast_in_dim.23), channel_id=1, replica_groups=mesh['gx'=8,'gz'=16,'core'=2] {'gx'}, dimensions={0} | all-to-all | bytes 1048576 | tf_op jit(solution)/shard_map/all_to_all | solution.py:228
  87.2 0.1 convert_reduce_fusion.2
  87.3 0.7 fusion.5
  88.0 0.9 convolution_convert_fusion.1
  88.9 12.0 %all-to-all-start.4 = ((bf16[32,16,128]{2,1,0:T(8,128)(2,1)}), bf16[32,16,128]{2,1,0:T(8,128)(2,1)S(1)}, u32[]{:S(2)}, u32[]{:S(2)}) async-start(bf16[32,16,128]{2,1,0:T(8,128)(2,1)} %bitcast.14), calls=%async_computation.4 | async-start | bytes 262144 | tf_op jit(solution)/shard_map/all_to_all | solution.py:228
  100.9 0.8 copy.53
  101.7 1.0 copy.79
  102.7 0.7 copy.57
  103.3 6.6 %all-to-all-done.4 = bf16[32,16,128]{2,1,0:T(8,128)(2,1)S(1)} async-done(((bf16[32,16,128]{2,1,0:T(8,128)(2,1)}), bf16[32,16,128]{2,1,0:T(8,128)(2,1)S(1)}, u32[]{:S(2)}, u32[]{:S(2)}) %all-to-all-start.4) | async-done | bytes 131104 | tf_op jit(solution)/shard_map/all_to_all | solution.py:228
  109.9 0.7 fusion.23
  110.7 14.3 %all_to_all.68 = bf16[32,16,128]{2,1,0:T(8,128)(2,1)S(1)} all-to-all(bf16[32,16,128]{2,1,0:T(8,128)(2,1)S(1)} %bitcast.150), channel_id=1, replica_groups=mesh['gx'=8,'gz'=16,'core'=2] {'gz','core'}, dimensions={0} | all-to-all | bytes 262144 | tf_op jit(solution)/shard_map/all_to_all | solution.py:228
  125.0 0.2 convolution_convert_fusion.2
  125.3 14.5 %all_to_all.69 = bf16[8,128,256]{2,1,0:T(8,128)(2,1)S(1)} all-to-all(bf16[8,128,256]{2,1,0:T(8,128)(2,1)S(1)} %broadcast_in_dim.25), channel_id=1, replica_groups=mesh['gx'=8,'gz'=16,'core'=2] {'gx'}, dimensions={0} | all-to-all | bytes 1048576 | tf_op jit(solution)/shard_map/all_to_all | solution.py:228
  139.8 0.1 convert_reduce_fusion.1
  139.9 1.5 convolution_convert_fusion
  141.5 0.4 convolution_bitcast_fusion
  141.9 0.4 convolution_bitcast_fusion.1
  142.3 1.9 pad_maximum_fusion
  144.2 1.1 copy-done.4
  145.3 1.1 copy.58
  146.4 24.4 %all_to_all.70 = bf16[16,8,3136]{2,1,0:T(8,128)(2,1)S(1)} all-to-all(bf16[16,8,3136]{2,1,0:T(8,128)(2,1)S(1)} %bitcast.140), channel_id=1, replica_groups=mesh['gx'=8,'gz'=16,'core'=2] {'gz'}, dimensions={0} | all-to-all | bytes 1605632 | tf_op jit(solution)/shard_map/all_to_all | solution.py:228
  170.8 0.1 reduce_sum.53
  170.9 0.6 reduce.3
  171.5 0.1 reshape.148
  171.7 11.3 %all_to_all.71 = bf16[8,2,1568]{2,1,0:T(2,128)(2,1)S(1)} all-to-all(bf16[8,2,1568]{2,1,0:T(2,128)(2,1)S(1)} %reshape.148), channel_id=1, replica_groups=mesh['gx'=8,'gz'=16,'core'=2] {'gx'}, dimensions={0} | all-to-all | bytes 100352 | tf_op jit(solution)/shard_map/all_to_all | solution.py:228
  182.9 0.1 reshape.149
  183.0 0.3 reduce.1
  183.3 0.1 convert_element_type.100
  183.5 0.9 shard_map.85
  184.4 3.4 %all-to-all-start.9 = ((bf16[8,64,256]{2,1,0:T(8,128)(2,1)}), bf16[8,64,256]{2,1,0:T(8,128)(2,1)S(1)}, u32[]{:S(2)}, u32[]{:S(2)}) async-start(bf16[8,64,256]{2,1,0:T(8,128)(2,1)} %bitcast.23), calls=%async_computation.9 | async-start | bytes 524288 | tf_op jit(solution)/shard_map/all_to_all | solution.py:228
  187.9 7.5 %all-to-all-done.9.turned_ref = bf16[8,64,256]{2,1,0:T(8,128)(2,1)S(1)} async-done(((bf16[8,64,256]{2,1,0:T(8,128)(2,1)}), bf16[8,64,256]{2,1,0:T(8,128)(2,1)S(1)}, u32[]{:S(2)}, u32[]{:S(2)}) %all-to-all-start.9) | async-done | bytes 262176 | tf_op jit(solution)/shard_map/all_to_all | solution.py:228
  195.4 1.7 copy-done.3
  197.0 7.6 %shard_map.86 = bf16[32,72,128]{2,1,0:T(8,128)(2,1)} custom-call(bf16[8,288,512]{2,1,0:T(8,128)(2,1)S(1)} %copy-done.3, bf16[8,64,256]{2,1,0:T(8,128)(2,1)S(1)} %all-to-all-done.9.turned_ref), custom_call_target="tpu_custom_call" | custom-call | flops 1207959552 | bytes 2359296 | tf_op jit(solution)/shard_map/pallas_call | solution.py:154
  204.7 9.4 %all-to-all-start.10 = ((bf16[32,72,128]{2,1,0:T(8,128)(2,1)}), bf16[32,72,128]{2,1,0:T(8,128)(2,1)S(1)}, u32[]{:S(2)}, u32[]{:S(2)}) async-start(bf16[32,72,128]{2,1,0:T(8,128)(2,1)} %shard_map.86), calls=%async_computation.10 | async-start | bytes 1179648 | tf_op jit(solution)/shard_map/all_to_all | solution.py:228
  214.3 0.1 pad.14
  214.3 2.3 copy-done.1
  216.7 3.5 %shard_map.87 = f32[1,14,14,512]{3,2,1,0:T(8,128)S(1)} custom-call(bf16[288,512]{1,0:T(8,128)(2,1)S(1)} %bitcast.136, bf16[4608,512]{1,0:T(8,128)(2,1)S(1)} %copy-done.1), custom_call_target="tpu_custom_call" | custom-call | flops 1056964608 | bytes 4718592 | tf_op jit(solution)/shard_map/pallas_call | solution.py:206
  220.2 1.2 copy.67
  221.4 10.6 %all-to-all-done.10 = bf16[32,72,128]{2,1,0:T(8,128)(2,1)S(1)} async-done(((bf16[32,72,128]{2,1,0:T(8,128)(2,1)}), bf16[32,72,128]{2,1,0:T(8,128)(2,1)S(1)}, u32[]{:S(2)}, u32[]{:S(2)}) %all-to-all-start.10) | async-done | bytes 589856 | tf_op jit(solution)/shard_map/all_to_all | solution.py:228
  231.9 0.1 convert_reduce_fusion
  232.0 0.1 fusion.27
  232.1 0.7 copy.66
  232.8 1.5 fusion.1
  234.3 1.5 fusion
  235.8 0.7 copy.72
  (35 shorter events, 0.7 us)
Async XLA Ops:
  7.2 2.5 %copy-start.5 = (bf16[4096,16]{0,1:T(8,128)(2,1)S(1)}, bf16[4096,16]{0,1:T(8,128)(2,1)}, u32[]{:S(2)}) copy-start(bf16[4096,16]{0,1:T(8,128)(2,1)} %param.8) | copy-start | bytes 393220
  7.2 45.2 %all-gather.9.cloned.1.call-start = ((), (), s32[]{:S(2)}) async-start(), calls=%async_computation.15 | async-start | bytes 2408448 | tf_op jit(solution)/shard_map/all_gather | solution.py:252
  7.9 180.0 %all-gather.5.cloned.1.call-start = ((), (), s32[]{:S(2)}) async-start(), calls=%async_computation.12 | async-start | bytes 2654208 | tf_op jit(solution)/shard_map/all_gather | solution.py:254
  9.7 11.9 %copy-start.2 = (bf16[18,16,512]{2,1,0:T(8,128)(2,1)S(1)}, bf16[18,16,512]{2,1,0:T(8,128)(2,1)}, u32[]{:S(2)}) copy-start(bf16[18,16,512]{2,1,0:T(8,128)(2,1)} %pad.12) | copy-start | bytes 884740
  10.5 23.0 %all-to-all-start = ((bf16[32,16,256]{2,1,0:T(8,128)(2,1)}), bf16[32,16,256]{2,1,0:T(8,128)(2,1)S(1)}, u32[]{:S(2)}, u32[]{:S(2)}) async-start(bf16[32,16,256]{2,1,0:T(8,128)(2,1)} %bitcast.10), calls=%async_computation | async-start | bytes 524288 | tf_op jit(solution)/shard_map/all_to_all | solution.py:228
  21.6 2.3 copy-start
  48.7 21.5 %all-to-all-start.2 = ((bf16[16,8,3136]{2,1,0:T(8,128)(2,1)}), bf16[16,8,3136]{2,1,0:T(8,128)(2,1)S(1)}, u32[]{:S(2)}, u32[]{:S(2)}) async-start(bf16[16,8,3136]{2,1,0:T(8,128)(2,1)} %broadcast_in_dim.22), calls=%async_computation.2 | async-start | bytes 1638400 | tf_op jit(solution)/shard_map/all_to_all | solution.py:228
  52.3 180.5 %all-gather.7.cloned.1.call-start = ((), (), s32[]{:S(2)}) async-start(), calls=%async_computation.14 | async-start | bytes 2162688 | tf_op jit(solution)/shard_map/all_gather | solution.py:272
  70.7 30.3 %copy-start.6 = (bf16[256,16]{0,1:T(8,128)(2,1)S(1)}, bf16[256,16]{0,1:T(8,128)(2,1)}, u32[]{:S(2)}) copy-start(bf16[256,16]{0,1:T(8,128)(2,1)} %param.9) | copy-start | bytes 24580
  88.9 21.0 %all-to-all-start.4 = ((bf16[32,16,128]{2,1,0:T(8,128)(2,1)}), bf16[32,16,128]{2,1,0:T(8,128)(2,1)S(1)}, u32[]{:S(2)}, u32[]{:S(2)}) async-start(bf16[32,16,128]{2,1,0:T(8,128)(2,1)} %bitcast.14), calls=%async_computation.4 | async-start | bytes 262144 | tf_op jit(solution)/shard_map/all_to_all | solution.py:228
  100.9 135.6 %reduce-scatter.2.cloned.1.call-start = ((), (), s32[]{:S(2)}) async-start(), calls=%async_computation.13 | async-start | bytes 4816896 | tf_op jit(solution)/shard_map/reduce_scatter | solution.py:304
  144.2 1.1 copy-start.4
  184.4 10.9 %all-to-all-start.9 = ((bf16[8,64,256]{2,1,0:T(8,128)(2,1)}), bf16[8,64,256]{2,1,0:T(8,128)(2,1)S(1)}, u32[]{:S(2)}, u32[]{:S(2)}) async-start(bf16[8,64,256]{2,1,0:T(8,128)(2,1)} %bitcast.23), calls=%async_computation.9 | async-start | bytes 524288 | tf_op jit(solution)/shard_map/all_to_all | solution.py:228
  195.4 1.7 copy-start.3
  204.7 27.2 %all-to-all-start.10 = ((bf16[32,72,128]{2,1,0:T(8,128)(2,1)}), bf16[32,72,128]{2,1,0:T(8,128)(2,1)S(1)}, u32[]{:S(2)}, u32[]{:S(2)}) async-start(bf16[32,72,128]{2,1,0:T(8,128)(2,1)} %shard_map.86), calls=%async_computation.10 | async-start | bytes 1179648 | tf_op jit(solution)/shard_map/all_to_all | solution.py:228
  214.3 2.3 copy-start.1
Sparse Core Ops, SparseCore 0:
  9.8 19.7 all-gather.8
  32.7 68.4 all-gather.4
  103.1 67.1 all-gather.6
  173.2 19.0 reduce-scatter.1

commit v3 on v2

--- a/solution.py
+++ b/solution.py
@@ -238,76 +238,122 @@
     return padded.reshape((side + 4) * LINE, chans)
 
 
+def back_kernel(g_ref, weight_ref, out_ref):
+    out_ref[...] = dot(g_ref[...], weight_ref[...], ((1,), (1,))).astype(BF)
+
+
+def features_back(g_six, weight):
+    count, feats = g_six.shape[0], weight.shape[0]
+    return pl.pallas_call(
+        back_kernel,
+        out_shape=jax.ShapeDtypeStruct((count, feats), BF),
+        compiler_params=pltpu.CompilerParams(vmem_limit_bytes=32 * 2**20),
+        cost_estimate=pl.CostEstimate(
+            flops=2 * count * weight.size, bytes_accessed=weight.size * 2, transcendentals=0
+        ),
+    )(g_six, weight)
+
+
+def outer_kernel(inputs_ref, g_ref, out_ref):
+    out_ref[0] = dot(inputs_ref[...], g_ref[...], ((0,), (0,))).astype(BF)
+
+
+def weight_terms(inputs, g_six, parts):
+    count, feats = inputs.shape
+    units = g_six.shape[1] // parts
+    return pl.pallas_call(
+        outer_kernel,
+        grid=(parts,),
+        in_specs=[
+            pl.BlockSpec((count, feats), lambda k: (0, 0)),
+            pl.BlockSpec((count, units), lambda k: (0, k)),
+        ],
+        out_specs=pl.BlockSpec((1, feats, units), lambda k: (k, 0, 0)),
+        out_shape=jax.ShapeDtypeStruct((parts, feats, units), BF),
+        compiler_params=pltpu.CompilerParams(vmem_limit_bytes=32 * 2**20),
+        cost_estimate=pl.CostEstimate(
+            flops=2 * inputs.size * g_six.shape[1], bytes_accessed=4 * feats * units, transcendentals=0
+        ),
+    )(inputs, g_six)
+
+
 def make(nx, nz, nc):
     ny = nz * nc
+    near = nz // nx
+    gy = ("gz", "core")
 
     def on_device(images, conv_weight, fc6_weight, fc7_weight, cotangent):
         side, chans = images.shape[1], images.shape[3]
         half = side // 2
         feats, units = fc6_weight.shape
         rows7, cols7 = fc7_weight.shape
-        group = cotangent.shape[0] // nc
+        total = cotangent.shape[0]
+        group = total // nc
+        mine = group // nx
         wide = units * nc
 
-        weight6 = lax.all_gather(fc6_weight, "core", axis=0, tiled=False)
+        known = lax.all_gather(
+            jnp.concatenate([fc7_weight.T, cotangent.T], axis=1), "gx", axis=0, tiled=False
+        )
+        gathered = lax.all_gather(images[0], "gx", axis=0, tiled=False)
         lines = bordered(images[0])
-        gathered = lax.all_gather(lines, "gx", axis=0, tiled=False)
-        send7 = fc7_weight.T.reshape(cols7, nz, wide).transpose(1, 0, 2)
-        send7 = jnp.broadcast_to(send7[:, None], (nz, nc, cols7, wide)).reshape(ny, cols7, wide)
-        weight7 = swap(send7, ("gz", "core")).reshape(ny * cols7, wide)
-        cot = cotangent.T.reshape(cols7, nx, nz, nc).transpose(0, 3, 2, 1)
-        cot = cot.reshape(cols7, nc * group).astype(F32)
-
+        weight6 = share(fc6_weight, "core", nc)
         conv_pre, pooled = conv_forward(lines, conv_weight, side)
         pooled = pooled.reshape(half, half + 1, chans)[:, :half]
         feat = pooled.astype(BF).reshape(nx, feats)
-        feat, weight7 = lax.optimization_barrier((feat, weight7))
+        feat, weight6 = lax.optimization_barrier((feat, weight6))
         inputs = share(swap(feat, "gx"), "gz", nz).reshape(group, feats)
-
         weight6 = jnp.concatenate([weight6[k] for k in range(nc)], axis=1)
         inputs, weight6 = lax.optimization_barrier((inputs, weight6))
-        h6_terms = dot(inputs, weight6, ((1,), (0,)))
-        h6_pre = share(h6_terms.astype(BF), "gx", nx).astype(F32).sum(axis=0)
-        hidden = activate(h6_pre).astype(BF)
-        all_hidden = lax.all_gather(hidden, ("gz", "core"), axis=0, tiled=False)
-
-        y7_terms = dot(weight7, hidden, ((1,), (1,))).astype(BF)
-        y7_pre = swap(y7_terms.reshape(ny, cols7, group), ("gz", "core"))
-        y7_pre = y7_pre.reshape(nz, nc, cols7, group).astype(F32).sum(axis=0)
-        y7_pre = y7_pre.transpose(1, 0, 2).reshape(cols7, nc * group)
+
+        h6_terms = dot(inputs, weight6, ((1,), (0,))).astype(BF).reshape(nx, mine, wide)
+        h6_pre = swap(h6_terms, "gx").astype(F32).sum(axis=0)
+        own_hidden = activate(h6_pre).astype(BF)
+        hidden = share(own_hidden, gy, ny).reshape(nz, nc, mine, wide)
+        hidden = hidden.transpose(1, 2, 0, 3).reshape(nc * mine, rows7)
+
+        known = known.reshape(nx * cols7, rows7 + total)
+        weight7 = known[:, :rows7]
+        place = lax.broadcasted_iota(jnp.int32, (total, nc * mine), 1)
+        core, rest = place // mine, place % mine
+        source = (rest % nx) * ny + (lax.axis_index("gx") * near + rest // nx) * nc + core
+        pick = (lax.broadcasted_iota(jnp.int32, (total, nc * mine), 0) == source).astype(BF)
+        cot = dot(known[:, rows7:], pick, ((1,), (0,)))
+        y7_pre = dot(weight7, hidden, ((1,), (1,)))
         g_seven = (cot * slope(y7_pre)).astype(BF)
-        send = g_seven.reshape(cols7, nc, group).transpose(1, 0, 2)
-        send = jnp.broadcast_to(send[None], (nz, nc, cols7, group)).reshape(ny, cols7, group)
-        g7_cols = swap(send, ("gz", "core")).reshape(ny * cols7, group)
-
-        dh6_terms = dot(g7_cols, weight7, ((0,), (0,))).astype(BF)
-        grad_hidden = share(dh6_terms, "gx", nx).astype(F32).sum(axis=0)
-        g_six = (grad_hidden * slope(h6_pre)).astype(BF)
-
-        feat_terms = dot(g_six, weight6, ((1,), (1,))).astype(BF)
-        feat_terms, g_late = lax.optimization_barrier((feat_terms, g_six))
-        feat_terms = swap(feat_terms.reshape(nz, nx, feats), "gz")
-        dfeat = swap(feat_terms.astype(F32).sum(axis=0).astype(BF), "gx")
+        dh6_terms = dot(g_seven, weight7, ((0,), (0,))).astype(BF)
+        dh6_terms = dh6_terms.reshape(nc, mine, nz, wide).transpose(2, 0, 1, 3)
+        grad_hidden = swap(dh6_terms.reshape(ny, mine, wide), gy).astype(F32).sum(axis=0)
+        own_six = (grad_hidden * slope(h6_pre)).astype(BF)
+
+        columns = g_seven.reshape(nx, cols7, nc * mine)
+        columns = jnp.pad(columns, ((0, 0), (0, mine - cols7), (0, LANES - nc * mine)))
+        both = jnp.concatenate([jnp.broadcast_to(own_six, (nx, mine, wide)), columns], axis=2)
+        both = swap(both, "gx")
+        g_six = both[:, :, :wide].reshape(group, wide)
+        columns = both[:, :cols7, wide : wide + nc * mine]
+
+        feat_terms = features_back(g_six, weight6).reshape(nz, nx, feats)
+        dfeat = swap(swap(feat_terms, "gz").astype(F32).sum(axis=0).astype(BF), "gx")
         dfeat = dfeat.reshape(half, half, chans).astype(F32)
         dfeat = jnp.pad(dfeat, ((0, 0), (0, 1), (0, 0))).reshape(half * (half + 1), chans)
 
         g_lines, g_turned = conv_slope(conv_pre, dfeat, 2 * LANES)
-        g_cols = swap(g_turned.reshape(nx, chans // nx, 2 * LANES), "gx")
-        packed = swap(conv_kernel_grad(gathered, g_cols, ny), ("gz", "core"))
-        packed = packed.astype(F32).sum(axis=0)
         part = chans // nx
+        g_cols = swap(g_turned.reshape(nx, part, 2 * LANES), "gx")
+        all_lines = jax.vmap(bordered)(gathered)
+        terms6 = weight_terms(inputs, g_six, nc)
+        g_cols, terms6 = lax.optimization_barrier((g_cols, terms6))
+        terms6 = swap(terms6, "core")
+        packed = conv_kernel_grad(all_lines, g_cols, ny)
+        packed, terms6 = lax.optimization_barrier((packed, terms6))
+        packed = swap(packed, gy).astype(F32).sum(axis=0)
         grad_conv = jnp.concatenate([packed[:, :part], packed[:, part:]], axis=0)
-
-        grad6_terms = jnp.stack(
-            [dot(inputs, g_late[:, k * units : (k + 1) * units], ((0,), (0,))) for k in range(nc)]
-        )
-        grad_fc6 = lax.psum_scatter(grad6_terms, "core", scatter_dimension=0, tiled=False)
-        all_hidden = all_hidden.reshape(nz, nc, group, wide)
-        grad7 = sum(
-            dot(g_seven[:, k * group : (k + 1) * group], all_hidden[:, k], ((1,), (1,)))
-            for k in range(nc)
-        )
-        grad_fc7 = grad7.reshape(cols7, rows7).T
+        grad_fc6 = terms6.astype(F32).sum(axis=0)
+
+        all_hidden = lax.all_gather(hidden, "gx", axis=0, tiled=False).reshape(total, rows7)
+        columns = columns.transpose(1, 0, 2).reshape(cols7, total)
+        grad_fc7 = dot(columns, all_hidden, ((1,), (0,))).T
         g_maps = g_lines[: side * LINE].reshape(side, LINE, chans)[:, :side]
         grad_images = conv_backward(bordered(g_maps), conv_weight, side)
         return (grad_conv, grad_fc6, grad_fc7, grad_images)

time: 244 us -> 230 us (0.943)
  blocking collectives: 93.9 us -> 55.5 us
  starting transfers between devices: 39.7 us -> 52 us
  waiting for transfers between devices: 47.7 us -> 59.4 us
  local copies, waits for them, and re-layouts: 20.1 us -> 16.8 us
    all_to_all x6 -> x4, blocking collectives: 93.9 us -> 55.5 us  [swap(): return lax.all_to_all(value, axis, 0, 0, tiled=True)]
    all_to_all x5 -> x8, starting transfers between devices: 39.5 us -> 51.8 us  [swap(): return lax.all_to_all(value, axis, 0, 0, tiled=True)]
    all_to_all x5 -> x8, waiting for transfers between devices: 46.9 us -> 58.7 us  [swap(): return lax.all_to_all(value, axis, 0, 0, tiled=True)]
    broadcast_in_dim x3, local copies, waits for them, and re-layouts: 1.02 us -> 4.17 us  [share(): return swap(jnp.broadcast_to(value, (count,) + value.shape), axis)]
    reduce_sum x5, other arithmetic: 0.37 us -> 3.28 us  [the longest x1 3.01 us: on_device(): grad_fc6 = terms6.astype(F32).sum(axis=0)]
    unnamed x22 -> x17, local copies, waits for them, and re-layouts: 9.87 us -> 7.19 us
    dot_general x8 -> x5, matrix products: 6.81 us -> 6.29 us  [dot(): return lax.dot_general(a, b, (dims, ((), ())), preferred_element_type=F32)]
  transfers between devices with their start and end apart: 9 -> 11, of which waited for: 5 -> 6; matrix products, arithmetic and copies ran while one was open for 10% -> 9% of each run, Pallas kernels for 6% -> 8%
where the time goes in v3:
time: 230 us; the launch traced here: 229 us
  waiting for transfers between devices  59.4 us (26%)
  blocking collectives  55.5 us (24%)
  starting transfers between devices  52 us (23%)
  Pallas kernels  17.8 us (8%)
  local copies, waits for them, and re-layouts  16.8 us (7%)
  between operations  14.1 us (6%)
  other arithmetic  7.38 us (3%)
  matrix products  6.29 us (3%)
    all_to_all x8, waiting for transfers between devices, swap(): return lax.all_to_all(value, axis, 0, 0, tiled=True)  58.7 us
    all_to_all x4, blocking collectives, swap(): return lax.all_to_all(value, axis, 0, 0, tiled=True)  55.5 us
    all_to_all x8, starting transfers between devices, swap(): return lax.all_to_all(value, axis, 0, 0, tiled=True)  51.8 us
    pallas_call x1, Pallas kernels, conv_kernel_grad(): pl.pallas_call(kernel_kernel, grid=(images,), in_specs=[pl.BlockSpec((Non...  7.64 us
    unnamed x17, local copies, waits for them, and re-layouts  7.19 us
    dot_general x5, matrix products, dot(): return lax.dot_general(a, b, (dims, ((), ())), preferred_element_type=F32)  6.29 us
  transfers between devices with their start and end apart: 11, of which 6 were waited for; matrix products, arithmetic and copies ran while one was open for 9% of the time, Pallas kernels for 8%

profile of v3, /device:TPU:1, one launch (start us, length us, event | category | flops | bytes accessed | tf_op | source)
XLA Modules:
  0.0 229.2 jit_solution(12150070280556343308)
XLA Ops:
  7.2 1.6 pad_maximum_fusion.1
  8.8 2.5 %broadcast_in_dim.12 = bf16[2,3136,128]{2,1,0:T(8,128)(2,1)} broadcast(bf16[3136,128]{1,0:T(8,128)(2,1)} %param.7), dimensions={1,2} | broadcast | bytes 2408448 | tf_op jit(solution)/shard_map/broadcast_in_dim | solution.py:232
  11.3 7.0 %all-to-all-start = ((bf16[2,3136,128]{2,1,0:T(8,128)(2,1)}), bf16[2,3136,128]{2,1,0:T(8,128)(2,1)S(1)}, u32[]{:S(2)}, u32[]{:S(2)}) async-start(bf16[2,3136,128]{2,1,0:T(8,128)(2,1)} %broadcast_in_dim.12), calls=%async_computation | async-start | bytes 3211264 | tf_op jit(solution)/shard_map/all_to_all | solution.py:228
  18.4 0.1 pad.21
  18.5 2.3 %copy-done = bf16[4608,512]{1,0:T(8,128)(2,1)S(1)} copy-done((bf16[4608,512]{1,0:T(8,128)(2,1)S(1)}, bf16[4608,512]{1,0:T(8,128)(2,1)}, u32[]{:S(2)}) %copy-start) | copy-done | bytes 4718616
  20.8 3.3 %shard_map.84 = (f32[224,512]{1,0:T(8,128)S(1)}, f32[56,512]{1,0:T(8,128)S(1)}) custom-call(bf16[288,512]{1,0:T(8,128)(2,1)S(1)} %bitcast.57, bf16[4608,512]{1,0:T(8,128)(2,1)S(1)} %copy-done), custom_call_target="tpu_custom_call" | custom-call | flops 1056964608 | bytes 4718592 | tf_op jit(solution)/shard_map/pallas_call | solution.py:58
  24.1 0.1 reshape.79
  24.2 0.5 broadcast.75
  24.7 0.7 reduce.2
  25.4 0.1 reshape.100
  25.5 11.5 %all_to_all.71 = bf16[8,2,1568]{2,1,0:T(2,128)(2,1)S(1)} all-to-all(bf16[8,2,1568]{2,1,0:T(2,128)(2,1)S(1)} %reshape.100), channel_id=1, replica_groups=mesh['gx'=8,'gz'=16,'core'=2] {'gx'}, dimensions={0} | all-to-all | bytes 100352 | tf_op jit(solution)/shard_map/all_to_all | solution.py:228
  37.0 0.1 reshape.101
  37.1 0.9 broadcast_in_dim.13
  38.1 8.2 %all-to-all-start.2 = ((bf16[16,8,3136]{2,1,0:T(8,128)(2,1)}), bf16[16,8,3136]{2,1,0:T(8,128)(2,1)S(1)}, u32[]{:S(2)}, u32[]{:S(2)}) async-start(bf16[16,8,3136]{2,1,0:T(8,128)(2,1)} %broadcast_in_dim.13), calls=%async_computation.2 | async-start | bytes 1638400 | tf_op jit(solution)/shard_map/all_to_all | solution.py:228
  46.3 0.0 all-gather.5.cloned.1.call-start
  46.4 0.7 all-gather.5.cloned.1.call-update
  47.1 0.1 slice_bitcast_fusion.1
  47.2 0.2 pad_maximum_fusion.weight_ref
  47.4 18.0 %all-to-all-done.2 = bf16[16,8,3136]{2,1,0:T(8,128)(2,1)S(1)} async-done(((bf16[16,8,3136]{2,1,0:T(8,128)(2,1)}), bf16[16,8,3136]{2,1,0:T(8,128)(2,1)S(1)}, u32[]{:S(2)}, u32[]{:S(2)}) %all-to-all-start.2) | async-done | bytes 802848 | tf_op jit(solution)/shard_map/all_to_all | solution.py:228
  65.3 0.4 convolution_convert_fusion.1
  65.7 10.7 %all_to_all.72 = bf16[8,16,256]{2,1,0:T(8,128)(2,1)S(1)} all-to-all(bf16[8,16,256]{2,1,0:T(8,128)(2,1)S(1)} %bitcast.68), channel_id=1, replica_groups=mesh['gx'=8,'gz'=16,'core'=2] {'gx'}, dimensions={0} | all-to-all | bytes 131072 | tf_op jit(solution)/shard_map/all_to_all | solution.py:228
  76.5 0.7 broadcast_in_dim.14
  77.2 8.5 %all-to-all-start.4 = ((bf16[32,16,256]{2,1,0:T(8,128)(2,1)}), bf16[32,16,256]{2,1,0:T(8,128)(2,1)S(1)}, u32[]{:S(2)}, u32[]{:S(2)}) async-start(bf16[32,16,256]{2,1,0:T(8,128)(2,1)} %broadcast_in_dim.14), calls=%async_computation.4 | async-start | bytes 524288 | tf_op jit(solution)/shard_map/all_to_all | solution.py:228
  85.7 11.9 %all-to-all-done.4 = bf16[32,16,256]{2,1,0:T(8,128)(2,1)S(1)} async-done(((bf16[32,16,256]{2,1,0:T(8,128)(2,1)}), bf16[32,16,256]{2,1,0:T(8,128)(2,1)S(1)}, u32[]{:S(2)}, u32[]{:S(2)}) %all-to-all-start.4) | async-done | bytes 262176 | tf_op jit(solution)/shard_map/all_to_all | solution.py:228
  97.6 0.1 copy.26
  97.7 0.1 copy.34
  97.9 1.8 fusion.2
  99.6 1.1 fusion
  100.7 0.3 convolution_convert_fusion
  101.0 0.8 copy.27
  101.8 5.0 %all-to-all-start.5 = ((bf16[32,16,256]{2,1,0:T(8,128)(2,1)}), bf16[32,16,256]{2,1,0:T(8,128)(2,1)S(1)}, u32[]{:S(2)}, u32[]{:S(2)}) async-start(bf16[32,16,256]{2,1,0:T(8,128)(2,1)} %bitcast.64), calls=%async_computation.5 | async-start | bytes 524288 | tf_op jit(solution)/shard_map/all_to_all | solution.py:228
  106.9 0.1 copy.28
  107.0 11.9 %all-to-all-done.5 = bf16[32,16,256]{2,1,0:T(8,128)(2,1)S(1)} async-done(((bf16[32,16,256]{2,1,0:T(8,128)(2,1)}), bf16[32,16,256]{2,1,0:T(8,128)(2,1)S(1)}, u32[]{:S(2)}, u32[]{:S(2)}) %all-to-all-start.5) | async-done | bytes 262176 | tf_op jit(solution)/shard_map/all_to_all | solution.py:228
  119.0 0.7 fusion.16
  119.6 3.4 %all-to-all-start.6 = ((bf16[8,16,384]{2,1,0:T(8,128)(2,1)}), bf16[8,16,384]{2,1,0:T(8,128)(2,1)S(1)}, u32[]{:S(2)}, u32[]{:S(2)}) async-start(bf16[8,16,384]{2,1,0:T(8,128)(2,1)} %fusion.16), calls=%async_computation.6 | async-start | bytes 196608 | tf_op jit(solution)/shard_map/all_to_all | solution.py:228
  123.0 0.8 all_gather_reshape.3
  123.9 5.9 %all-to-all-done.6 = bf16[8,16,384]{2,1,0:T(8,128)(2,1)S(1)} async-done(((bf16[8,16,384]{2,1,0:T(8,128)(2,1)}), bf16[8,16,384]{2,1,0:T(8,128)(2,1)S(1)}, u32[]{:S(2)}, u32[]{:S(2)}) %all-to-all-start.6) | async-done | bytes 98336 | tf_op jit(solution)/shard_map/all_to_all | solution.py:228
  129.8 0.7 shard_map.85
  130.5 22.3 %all_to_all.73 = bf16[16,8,3136]{2,1,0:T(8,128)(2,1)S(1)} all-to-all(bf16[16,8,3136]{2,1,0:T(8,128)(2,1)S(1)} %bitcast.55), channel_id=1, replica_groups=mesh['gx'=8,'gz'=16,'core'=2] {'gz'}, dimensions={0} | all-to-all | bytes 1605632 | tf_op jit(solution)/shard_map/all_to_all | solution.py:228
  152.8 0.1 reduce_sum.50
  152.9 0.7 reduce.3
  153.6 0.1 reshape.102
  153.7 11.0 %all_to_all.74 = bf16[8,2,1568]{2,1,0:T(2,128)(2,1)S(1)} all-to-all(bf16[8,2,1568]{2,1,0:T(2,128)(2,1)S(1)} %reshape.102), channel_id=1, replica_groups=mesh['gx'=8,'gz'=16,'core'=2] {'gx'}, dimensions={0} | all-to-all | bytes 100352 | tf_op jit(solution)/shard_map/all_to_all | solution.py:228
  164.7 0.1 reshape.103
  164.9 0.3 reduce.1
  165.2 0.1 convert_element_type.51
  165.3 0.9 shard_map.86
  166.2 3.4 %all-to-all-start.9 = ((bf16[8,64,256]{2,1,0:T(8,128)(2,1)}), bf16[8,64,256]{2,1,0:T(8,128)(2,1)S(1)}, u32[]{:S(2)}, u32[]{:S(2)}) async-start(bf16[8,64,256]{2,1,0:T(8,128)(2,1)} %bitcast.20), calls=%async_computation.9 | async-start | bytes 524288 | tf_op jit(solution)/shard_map/all_to_all | solution.py:228
  169.7 1.8 shard_map.87
  171.4 2.5 %pad.20 = bf16[8,18,16,512]{3,2,1,0:T(8,128)(2,1)S(1)} pad(bf16[8,14,14,512]{3,2,1,0:T(8,128)(2,1)} %all-gather.5.cloned.1.call-done, bf16[]{:T(256)} %constant.57.clone.1), padding=0_0x1_3x1_1x0_0 | pad | bytes 3964930 | tf_op jit(solution)/shard_map/vmap(jit(_pad))/pad | solution.py:237
  173.9 3.4 %all-to-all-done.9.turned_ref = bf16[8,64,256]{2,1,0:T(8,128)(2,1)S(1)} async-done(((bf16[8,64,256]{2,1,0:T(8,128)(2,1)}), bf16[8,64,256]{2,1,0:T(8,128)(2,1)S(1)}, u32[]{:S(2)}, u32[]{:S(2)}) %all-to-all-start.9) | async-done | bytes 262176 | tf_op jit(solution)/shard_map/all_to_all | solution.py:228
  177.3 11.9 %all-to-all-start.10 = ((bf16[2,3136,128]{2,1,0:T(8,128)(2,1)}), bf16[2,3136,128]{2,1,0:T(8,128)(2,1)}, u32[]{:S(2)}, u32[]{:S(2)}) async-start(bf16[2,3136,128]{2,1,0:T(8,128)(2,1)} %shard_map.87), calls=%async_computation.10 | async-start | bytes 3211264 | tf_op jit(solution)/shard_map/all_to_all | solution.py:228
  189.2 7.6 %shard_map.88 = bf16[32,72,128]{2,1,0:T(8,128)(2,1)} custom-call(bf16[8,288,512]{2,1,0:T(8,128)(2,1)S(1)} %bitcast.56, bf16[8,64,256]{2,1,0:T(8,128)(2,1)S(1)} %all-to-all-done.9.turned_ref), custom_call_target="tpu_custom_call" | custom-call | flops 1207959552 | bytes 2359296 | tf_op jit(solution)/shard_map/pallas_call | solution.py:154
  196.8 4.4 %all-to-all-start.11 = ((bf16[32,72,128]{2,1,0:T(8,128)(2,1)}), bf16[32,72,128]{2,1,0:T(8,128)(2,1)S(1)}, u32[]{:S(2)}, u32[]{:S(2)}) async-start(bf16[32,72,128]{2,1,0:T(8,128)(2,1)} %shard_map.88), calls=%async_computation.11 | async-start | bytes 1179648 | tf_op jit(solution)/shard_map/all_to_all | solution.py:228
  201.2 0.1 pad.24
  201.3 2.3 %copy-done.1 = bf16[4608,512]{1,0:T(8,128)(2,1)S(1)} copy-done((bf16[4608,512]{1,0:T(8,128)(2,1)S(1)}, bf16[4608,512]{1,0:T(8,128)(2,1)}, u32[]{:S(2)}) %copy-start.1) | copy-done | bytes 4718616
  203.7 3.5 %shard_map.89 = f32[1,14,14,512]{3,2,1,0:T(8,128)S(1)} custom-call(bf16[288,512]{1,0:T(8,128)(2,1)S(1)} %bitcast.58, bf16[4608,512]{1,0:T(8,128)(2,1)S(1)} %copy-done.1), custom_call_target="tpu_custom_call" | custom-call | flops 1056964608 | bytes 4718592 | tf_op jit(solution)/shard_map/pallas_call | solution.py:206
  207.2 1.2 copy.32
  208.3 3.0 %convert_reduce_fusion = f32[3136,128]{1,0:T(8,128)} fusion(bf16[2,3136,128]{2,1,0:T(8,128)(2,1)} %all-to-all-done.10), kind=kLoop, calls=%fused_computation.2 | loop fusion | flops 1204224 | bytes 3211264 | tf_op jit(solution)/shard_map/reduce_sum | solution.py:352
  211.4 7.6 %all-to-all-done.11 = bf16[32,72,128]{2,1,0:T(8,128)(2,1)S(1)} async-done(((bf16[32,72,128]{2,1,0:T(8,128)(2,1)}), bf16[32,72,128]{2,1,0:T(8,128)(2,1)S(1)}, u32[]{:S(2)}, u32[]{:S(2)}) %all-to-all-start.11) | async-done | bytes 589856 | tf_op jit(solution)/shard_map/all_to_all | solution.py:228
  219.0 0.1 convert_reduce_fusion.1
  219.1 0.1 fusion.41
  219.2 0.7 copy.31
  219.9 2.8 %convolution_bitcast_fusion = f32[4096,16]{0,1:T(8,128)} fusion(bf16[8,32,4096]{2,1,0:T(8,128)(2,1)} %all-gather.7.cloned.1.call-done, bf16[8,16,384]{2,1,0:T(8,128)(2,1)S(1)} %all-to-all-done.6), kind=kOutput, calls=%fused_computation.1 | convolution fusion | flops 33554432 | bytes 2392064 | tf_op jit(solution)/shard_map/dot_general | solution.py:224
  (30 shorter events, 0.4 us)
Async XLA Ops:
  7.2 90.7 %all-gather.9.cloned.1.call-start = ((), (), s32[]{:S(2)}) async-start(), calls=%async_computation.14 | async-start | bytes 1253376 | tf_op jit(solution)/shard_map/all_gather | solution.py:295
  11.3 7.0 %copy-start.3 = (bf16[1,14,14,512]{3,2,1,0:T(8,128)(2,1)S(1)}, bf16[1,14,14,512]{3,2,1,0:T(8,128)(2,1)}, u32[]{:S(2)}) copy-start(bf16[1,14,14,512]{3,2,1,0:T(8,128)(2,1)} %param.5) | copy-start | bytes 602116
  11.3 12.9 %all-to-all-start = ((bf16[2,3136,128]{2,1,0:T(8,128)(2,1)}), bf16[2,3136,128]{2,1,0:T(8,128)(2,1)S(1)}, u32[]{:S(2)}, u32[]{:S(2)}) async-start(bf16[2,3136,128]{2,1,0:T(8,128)(2,1)} %broadcast_in_dim.12), calls=%async_computation | async-start | bytes 3211264 | tf_op jit(solution)/shard_map/all_to_all | solution.py:228
  18.4 2.3 %copy-start = (bf16[4608,512]{1,0:T(8,128)(2,1)S(1)}, bf16[4608,512]{1,0:T(8,128)(2,1)}, u32[]{:S(2)}) copy-start(bf16[4608,512]{1,0:T(8,128)(2,1)} %weight_ref.3) | copy-start | bytes 14155780
  38.1 27.2 %all-to-all-start.2 = ((bf16[16,8,3136]{2,1,0:T(8,128)(2,1)}), bf16[16,8,3136]{2,1,0:T(8,128)(2,1)S(1)}, u32[]{:S(2)}, u32[]{:S(2)}) async-start(bf16[16,8,3136]{2,1,0:T(8,128)(2,1)} %broadcast_in_dim.13), calls=%async_computation.2 | async-start | bytes 1638400 | tf_op jit(solution)/shard_map/all_to_all | solution.py:228
  46.3 125.1 %all-gather.5.cloned.1.call-start = ((), (), s32[]{:S(2)}) async-start(), calls=%async_computation.12 | async-start | bytes 2064384 | tf_op jit(solution)/shard_map/all_gather | solution.py:298
  77.2 20.4 %all-to-all-start.4 = ((bf16[32,16,256]{2,1,0:T(8,128)(2,1)}), bf16[32,16,256]{2,1,0:T(8,128)(2,1)S(1)}, u32[]{:S(2)}, u32[]{:S(2)}) async-start(bf16[32,16,256]{2,1,0:T(8,128)(2,1)} %broadcast_in_dim.14), calls=%async_computation.4 | async-start | bytes 524288 | tf_op jit(solution)/shard_map/all_to_all | solution.py:228
  97.9 2.8 %copy-start.2 = (bf16[128,4352]{1,0:T(8,128)(2,1)S(1)}, bf16[128,4352]{1,0:T(8,128)(2,1)}, u32[]{:S(2)}) copy-start(bf16[128,4352]{1,0:T(8,128)(2,1)} %all-gather.9.cloned.1.call-done) | copy-start | bytes 3342340
  101.8 17.1 %all-to-all-start.5 = ((bf16[32,16,256]{2,1,0:T(8,128)(2,1)}), bf16[32,16,256]{2,1,0:T(8,128)(2,1)S(1)}, u32[]{:S(2)}, u32[]{:S(2)}) async-start(bf16[32,16,256]{2,1,0:T(8,128)(2,1)} %bitcast.64), calls=%async_computation.5 | async-start | bytes 524288 | tf_op jit(solution)/shard_map/all_to_all | solution.py:228
  119.6 10.2 %all-to-all-start.6 = ((bf16[8,16,384]{2,1,0:T(8,128)(2,1)}), bf16[8,16,384]{2,1,0:T(8,128)(2,1)S(1)}, u32[]{:S(2)}, u32[]{:S(2)}) async-start(bf16[8,16,384]{2,1,0:T(8,128)(2,1)} %fusion.16), calls=%async_computation.6 | async-start | bytes 196608 | tf_op jit(solution)/shard_map/all_to_all | solution.py:228
  123.0 96.9 %all-gather.7.cloned.1.call-start = ((), (), s32[]{:S(2)}) async-start(), calls=%async_computation.13 | async-start | bytes 2359296 | tf_op jit(solution)/shard_map/all_gather | solution.py:354
  166.2 11.0 %all-to-all-start.9 = ((bf16[8,64,256]{2,1,0:T(8,128)(2,1)}), bf16[8,64,256]{2,1,0:T(8,128)(2,1)S(1)}, u32[]{:S(2)}, u32[]{:S(2)}) async-start(bf16[8,64,256]{2,1,0:T(8,128)(2,1)} %bitcast.20), calls=%async_computation.9 | async-start | bytes 524288 | tf_op jit(solution)/shard_map/all_to_all | solution.py:228
  177.3 19.5 %all-to-all-start.10 = ((bf16[2,3136,128]{2,1,0:T(8,128)(2,1)}), bf16[2,3136,128]{2,1,0:T(8,128)(2,1)}, u32[]{:S(2)}, u32[]{:S(2)}) async-start(bf16[2,3136,128]{2,1,0:T(8,128)(2,1)} %shard_map.87), calls=%async_computation.10 | async-start | bytes 3211264 | tf_op jit(solution)/shard_map/all_to_all | solution.py:228
  196.8 22.2 %all-to-all-start.11 = ((bf16[32,72,128]{2,1,0:T(8,128)(2,1)}), bf16[32,72,128]{2,1,0:T(8,128)(2,1)S(1)}, u32[]{:S(2)}, u32[]{:S(2)}) async-start(bf16[32,72,128]{2,1,0:T(8,128)(2,1)} %shard_map.88), calls=%async_computation.11 | async-start | bytes 1179648 | tf_op jit(solution)/shard_map/all_to_all | solution.py:228
  201.3 2.3 %copy-start.1 = (bf16[4608,512]{1,0:T(8,128)(2,1)S(1)}, bf16[4608,512]{1,0:T(8,128)(2,1)}, u32[]{:S(2)}) copy-start(bf16[4608,512]{1,0:T(8,128)(2,1)} %weight_ref.3) | copy-start | bytes 14155780
Sparse Core Ops, SparseCore 0:
  11.2 59.3 all-gather.8
  73.2 58.9 all-gather.4
  134.8 59.8 all-gather.6

commit v4 on v3

v4 whole, which is shorter than its diff:
```python
import jax
import jax.numpy as jnp
from jax import lax
from jax.experimental import pallas as pl
from jax.experimental.pallas import tpu as pltpu
from jax.sharding import Mesh, PartitionSpec as P

BF = jnp.bfloat16
F32 = jnp.float32
LANES = 128
LINE = 16
VMEM = pltpu.CompilerParams(vmem_limit_bytes=20 * 2**20)


def activate(value):
    return value * jax.nn.sigmoid(value)


def slope(value):
    sig = jax.nn.sigmoid(value)
    return sig * (1.0 + value * (1.0 - sig))


def dot(a, b, dims):
    return lax.dot_general(a, b, (dims, ((), ())), preferred_element_type=F32)


def cost(flops, moved, special=0):
    return pl.CostEstimate(flops=flops, bytes_accessed=moved, transcendentals=special)


def forward_kernel(image_ref, weight_ref, pre_ref, feat_ref, held_ref, sums_ref, pool_ref, sems):
    pix, chans = pre_ref.shape
    depth = image_ref.shape[1]
    rows = sums_ref.shape[1]

    def load(tap):
        return pltpu.make_async_copy(
            weight_ref.at[pl.ds(tap * depth, depth), :],
            held_ref.at[tap % 3, pl.ds(tap // 3 * depth, depth), :],
            sems.at[tap],
        )

    order = [3 * row + col for col in range(3) for row in range(3)]
    for tap in order:
        load(tap).start()
    image = jnp.concatenate([image_ref[k * LINE : k * LINE + rows, :] for k in range(3)], axis=1)
    for col in range(3):
        for row in range(3):
            load(3 * row + col).wait()
        sums_ref[col] = dot(image, held_ref[col], ((1,), (0,)))
    pre = sums_ref[0, 0:pix, :] + sums_ref[1, 1 : pix + 1, :] + sums_ref[2, 2 : pix + 2, :]
    pre_ref[...] = pre
    act = activate(pre).reshape(pix // (2 * LINE), 2, LINE, chans)
    lines = (act[:, 0] + act[:, 1]).reshape(pix // 2, chans)
    half = pix // 4
    for k in range(chans // LANES):
        pool_ref[k] = lines[:, k * LANES : (k + 1) * LANES]
        total = pool_ref[k, pl.ds(0, half, 2), :] + pool_ref[k, pl.ds(1, half, 2), :]
        feat_ref[:, k * LANES : (k + 1) * LANES] = (0.25 * total).astype(BF)


def conv_forward(lines, weight, side):
    depth, chans = lines.shape[1], weight.shape[1]
    pix = side * LINE
    return pl.pallas_call(
        forward_kernel,
        in_specs=[
            pl.BlockSpec(memory_space=pltpu.VMEM),
            pl.BlockSpec(memory_space=pl.ANY),
        ],
        out_shape=[
            jax.ShapeDtypeStruct((pix, chans), F32),
            jax.ShapeDtypeStruct((pix // 4, chans), BF),
        ],
        scratch_shapes=[
            pltpu.VMEM((3, 3 * depth, chans), BF),
            pltpu.VMEM((3, pix + LINE, chans), F32),
            pltpu.VMEM((chans // LANES, pix // 2, LANES), F32),
            pltpu.SemaphoreType.DMA((9,)),
        ],
        compiler_params=VMEM,
        cost_estimate=cost(18 * pix * depth * chans, weight.size * 2, pix * chans),
    )(lines, weight)


def turn_kernel(pre_ref, out_ref):
    pix, chans = pre_ref.shape
    grad = 0.25 * slope(pre_ref[...])
    grad = jnp.concatenate([grad, jnp.zeros((out_ref.shape[1] - pix, chans), F32)], axis=0)
    out_ref[...] = grad.T.astype(BF)


def turned_slope(pre, cols):
    pix, chans = pre.shape
    return pl.pallas_call(
        turn_kernel,
        out_shape=jax.ShapeDtypeStruct((chans, cols), BF),
        compiler_params=VMEM,
        cost_estimate=cost(8 * pix * chans, pix * chans * 6, pix * chans),
    )(pre)


def lines_kernel(pre_ref, dfeat_ref, out_ref, wide_ref):
    pix, chans = pre_ref.shape
    half = pix // 4
    for k in range(chans // LANES):
        dfeat = dfeat_ref[:, k * LANES : (k + 1) * LANES]
        wide_ref[k, pl.ds(0, half, 2), :] = dfeat
        wide_ref[k, pl.ds(1, half, 2), :] = dfeat
    spread = jnp.concatenate([wide_ref[k] for k in range(chans // LANES)], axis=1)
    spread = spread.reshape(pix // (2 * LINE), 1, LINE, chans)
    spread = jnp.broadcast_to(spread, (pix // (2 * LINE), 2, LINE, chans)).reshape(pix, chans)
    out_ref[...] = (0.25 * spread * slope(pre_ref[...])).astype(BF)


def conv_slope(pre, dfeat):
    pix, chans = pre.shape
    return pl.pallas_call(
        lines_kernel,
        out_shape=jax.ShapeDtypeStruct((pix, chans), BF),
        scratch_shapes=[pltpu.VMEM((chans // LANES, pix // 2, LANES), F32)],
        compiler_params=VMEM,
        cost_estimate=cost(8 * pix * chans, pix * chans * 6, pix * chans),
    )(pre, dfeat)


def fc7_kernel(known_ref, hidden_ref, pick_ref, seven_ref, terms_ref):
    count, mine, wide = hidden_ref.shape
    rows7 = count // 2 * wide
    y7_pre = jnp.zeros(seven_ref.shape, F32)
    for g in range(count // 2):
        block = hidden_ref[2 * g : 2 * g + 2].reshape(2 * mine, wide)
        y7_pre += dot(known_ref[:, g * wide : (g + 1) * wide], block, ((1,), (1,)))
    cot = dot(known_ref[:, rows7:], pick_ref[...], ((1,), (0,)))
    seven = (cot * slope(y7_pre)).astype(BF)
    seven_ref[...] = seven
    for g in range(count // 2):
        part = dot(seven, known_ref[:, g * wide : (g + 1) * wide], ((0,), (0,)))
        terms_ref[2 * g : 2 * g + 2] = part.astype(BF).reshape(2, mine, wide)


def fc7_step(known, hidden, pick):
    cols = known.shape[0]
    return pl.pallas_call(
        fc7_kernel,
        out_shape=[
            jax.ShapeDtypeStruct((cols, pick.shape[1]), BF),
            jax.ShapeDtypeStruct(hidden.shape, BF),
        ],
        compiler_params=VMEM,
        cost_estimate=cost(4 * known.size * pick.shape[1], known.size * 2),
    )(known, hidden, pick)


def back_kernel(g_ref, weight_ref, out_ref):
    out_ref[...] = dot(g_ref[...], weight_ref[...], ((1,), (1,))).astype(BF)


def features_back(g_six, weight):
    count, feats = g_six.shape[0], weight.shape[0]
    return pl.pallas_call(
        back_kernel,
        out_shape=jax.ShapeDtypeStruct((count, feats), BF),
        compiler_params=VMEM,
        cost_estimate=cost(2 * count * weight.size, weight.size * 2),
    )(g_six, weight)


def outer_kernel(which_ref, inputs_ref, g_ref, out_ref):
    units = out_ref.shape[1]
    g_six = g_ref[:, pl.ds(pl.multiple_of(which_ref[0] * units, units), units)]
    out_ref[...] = dot(inputs_ref[...], g_six, ((0,), (0,))).astype(out_ref.dtype)


def outer_add_kernel(which_ref, inputs_ref, g_ref, more_ref, out_ref):
    units = out_ref.shape[1]
    g_six = g_ref[:, pl.ds(pl.multiple_of(which_ref[0] * units, units), units)]
    out_ref[...] = dot(inputs_ref[...], g_six, ((0,), (0,))) + more_ref[...].astype(F32)


def weight_terms(which, inputs, g_six, units, more=None):
    feats = inputs.shape[1]
    operands = (inputs, g_six) if more is None else (inputs, g_six, more)
    in_vmem = [pl.BlockSpec(memory_space=pltpu.VMEM)] * len(operands)
    return pl.pallas_call(
        outer_kernel if more is None else outer_add_kernel,
        in_specs=[pl.BlockSpec(memory_space=pltpu.SMEM)] + in_vmem,
        out_shape=jax.ShapeDtypeStruct((feats, units), BF if more is None else F32),
        compiler_params=VMEM,
        cost_estimate=cost(2 * inputs.size * units, 4 * feats * units),
    )(which.reshape(1).astype(jnp.int32), *operands)


def pack_kernel(me_ref, terms_ref, out_ref, parts_ref, own_ref):
    nx, rows, _ = out_ref.shape
    feats = terms_ref.shape[2]
    run = LANES // 2
    runs = feats // run
    total = terms_ref[...].astype(F32).sum(axis=0).astype(BF).astype(F32)
    total = jnp.concatenate([total, jnp.zeros((nx, -feats % LANES), F32)], axis=1)
    parts_ref[...] = jnp.zeros(parts_ref.shape, F32)
    own_ref[...] = jnp.zeros(own_ref.shape, F32)
    for t in range(runs):
        tile = total[:, t // 2 * LANES : (t // 2 + 1) * LANES]
        other = pltpu.roll(tile, run, 1)
        low, high = (tile, other) if t % 2 == 0 else (other, tile)
        parts_ref[t % nx, t // nx * nx : (t // nx + 1) * nx, :] = low
        own_ref[pl.ds(t, nx, rows), :] = high
    lane = lax.broadcasted_iota(jnp.int32, (rows, LANES), 1)
    for e in range(nx):
        dest = lax.rem(me_ref[0] + e, nx)
        own = own_ref[pl.ds(pl.multiple_of(dest * rows, rows), rows), :]
        out_ref[dest] = jnp.where(lane < run, parts_ref[e], own).astype(BF)


def pack_dfeat(me, terms):
    _, nx, feats = terms.shape
    rows = nx * nx
    return pl.pallas_call(
        pack_kernel,
        in_specs=[
            pl.BlockSpec(memory_space=pltpu.SMEM),
            pl.BlockSpec(memory_space=pltpu.VMEM),
        ],
        out_shape=jax.ShapeDtypeStruct((nx, rows, LANES), BF),
        scratch_shapes=[
            pltpu.VMEM((nx, rows, LANES), F32),
            pltpu.VMEM((nx * rows, LANES), F32),
        ],
        compiler_params=VMEM,
        cost_estimate=cost(4 * terms.size, terms.size * 2),
    )(me, terms)


def kernel_kernel(lines_ref, slope_ref, dfeat_ref, spread_ref, out_ref, grad_ref, flat_ref, wide_ref):
    images, part, cols = slope_ref.shape
    chans = lines_ref.shape[2]
    wide_ref[...] = dfeat_ref[...].astype(F32).reshape(wide_ref.shape)
    for n in range(images):
        cells = wide_ref[pl.ds(n, wide_ref.shape[0] // images, images), :].astype(BF)
        spread = dot(cells, spread_ref[...], ((0,), (0,)))[:part]
        turned = (spread * slope_ref[n].astype(F32)).astype(BF).astype(F32)
        moved = [turned] + [pltpu.roll(turned, k, 1) for k in (1, 2)]
        grad_ref[:, n * cols : (n + 1) * cols] = jnp.concatenate(moved, axis=0).astype(BF)
    for row in range(3):
        block = lines_ref[:, row * LINE : row * LINE + cols, :].reshape(images * cols, chans)
        term = dot(grad_ref[...], block, ((1,), (0,)))
        for col in range(3):
            tap = 3 * row + col
            flat_ref[tap * chans : (tap + 1) * chans, :] = term[col * part : (col + 1) * part].T
    count, size, _ = out_ref.shape
    for dest in range(count):
        at = dest * 2 * size
        both = [flat_ref[at : at + size, :], flat_ref[at + size : at + 2 * size, :]]
        out_ref[dest] = jnp.concatenate(both, axis=1).astype(BF)


def conv_kernel_grad(lines, slopes, dfeat, spread, count):
    images, rows, chans = lines.shape
    _, part, cols = slopes.shape
    size = 9 * chans // (2 * count)
    return pl.pallas_call(
        kernel_kernel,
        out_shape=jax.ShapeDtypeStruct((count, size, 2 * part), BF),
        scratch_shapes=[
            pltpu.VMEM((3 * part, images * cols), BF),
            pltpu.VMEM((9 * chans, part), F32),
            pltpu.VMEM((dfeat.shape[0] * dfeat.shape[1], LANES), F32),
        ],
        compiler_params=VMEM,
        cost_estimate=cost(18 * images * cols * chans * part, lines.size * 2),
    )(lines, slopes, dfeat, spread)


def backward_kernel(lines_ref, weight_ref, out_ref, sums_ref):
    step = pl.program_id(0)
    col = lax.rem(step, 3)
    rows = sums_ref.shape[1]
    start = pl.multiple_of((2 - step // 3) * LINE, LINE)
    part = dot(lines_ref[pl.ds(start, rows), :], weight_ref[...], ((1,), (1,)))

    @pl.when(step < 3)
    def _():
        sums_ref[col] = part

    @pl.when(step >= 3)
    def _():
        sums_ref[col] += part

    @pl.when(step == 8)
    def _():
        _, side, _, chans = out_ref.shape
        pix = side * LINE
        grad = sums_ref[0, 2 : pix + 2, :] + sums_ref[1, 1 : pix + 1, :] + sums_ref[2, 0:pix, :]
        out_ref[0] = grad.reshape(side, LINE, chans)[:, :side, :]


def conv_backward(lines, weight, side):
    chans = lines.shape[1]
    depth = weight.shape[0] // 9
    pix = side * LINE
    return pl.pallas_call(
        backward_kernel,
        grid=(9,),
        in_specs=[
            pl.BlockSpec(lines.shape, lambda t: (0, 0)),
            pl.BlockSpec((depth, chans), lambda t: (t, 0)),
        ],
        out_specs=pl.BlockSpec((1, side, side, depth), lambda t: (0, 0, 0, 0)),
        out_shape=jax.ShapeDtypeStruct((1, side, side, depth), F32),
        scratch_shapes=[pltpu.VMEM((3, pix + LINE, depth), F32)],
        compiler_params=VMEM,
        cost_estimate=cost(18 * pix * depth * chans, weight.size * 2),
    )(lines, weight)


def spread_matrix(me, nx, half, cols):
    at = lax.broadcasted_iota(jnp.int32, (nx * nx, cols), 0)
    pixel = lax.broadcasted_iota(jnp.int32, (nx * nx, cols), 1)
    source, run = at // nx, at % nx
    line, place = pixel // LINE, pixel % LINE
    per = half * half // nx
    cell = jnp.where((line < 2 * half) & (place < 2 * half), line // 2 * half + place // 2, -1)
    mine = per * source + run + (me < source).astype(jnp.int32)
    return ((cell == mine) & (run <= per)).astype(BF)


def swap(value, axis):
    return lax.all_to_all(value, axis, 0, 0, tiled=True)


def share(value, axis, count):
    return swap(jnp.broadcast_to(value, (count,) + value.shape), axis)


def bordered(maps):
    side, _, chans = maps.shape
    padded = jnp.pad(maps, ((1, 3), (1, LINE - side - 1), (0, 0)))
    return padded.reshape((side + 4) * LINE, chans)


def make(nx, nz, nc):
    ny = nz * nc
    near = nz // nx
    gy = ("gz", "core")
    pair = [(k, nc - 1 - k) for k in range(nc)]

    def on_device(images, conv_weight, fc6_weight, fc7_weight, cotangent):
        side, chans = images.shape[1], images.shape[3]
        half = side // 2
        feats, units = fc6_weight.shape
        rows7, cols7 = fc7_weight.shape
        total = cotangent.shape[0]
        group = total // nc
        mine = group // nx
        wide = units * nc
        part = chans // nx
        cols = 2 * LANES
        me, core = lax.axis_index("gx"), lax.axis_index("core")

        known = lax.all_gather(
            jnp.concatenate([fc7_weight.T, cotangent.T], axis=1), "gx", axis=0, tiled=False
        )
        gathered = lax.all_gather(images[0], "gx", axis=0, tiled=False)
        other6 = lax.ppermute(fc6_weight, "core", pair)
        lines = bordered(images[0])
        conv_pre, pooled = conv_forward(lines, conv_weight, side)
        slopes = turned_slope(conv_pre, cols).reshape(nx, part, cols)
        feat = pooled.reshape(half, half + 1, chans)[:, :half].reshape(nx, feats)
        inputs = share(swap(feat, "gx"), "gz", nz).reshape(group, feats)
        first = jnp.where(core == 0, fc6_weight, other6)
        second = jnp.where(core == 0, other6, fc6_weight)
        weight6 = jnp.concatenate([first, second], axis=1)
        inputs, weight6 = lax.optimization_barrier((inputs, weight6))

        h6_terms = dot(inputs, weight6, ((1,), (0,))).astype(BF).reshape(nx, mine, wide)
        both = swap(jnp.concatenate([h6_terms, slopes], axis=1), "gx")
        h6_pre = both[:, :mine].astype(F32).sum(axis=0)
        slopes = both[:, mine:]
        own_hidden = activate(h6_pre).astype(BF)
        hidden = share(own_hidden, gy, ny)

        place = lax.broadcasted_iota(jnp.int32, (total, nc * mine), 1)
        half_of, rest = place // mine, place % mine
        source = (rest % nx) * ny + (me * near + rest // nx) * nc + half_of
        pick = (lax.broadcasted_iota(jnp.int32, (total, nc * mine), 0) == source).astype(BF)
        g_seven, dh6_terms = fc7_step(known.reshape(nx * cols7, rows7 + total), hidden, pick)
        grad_hidden = swap(dh6_terms, gy).astype(F32).sum(axis=0)
        own_six = (grad_hidden * slope(h6_pre)).astype(BF)

        columns = g_seven.reshape(nx, cols7, nc * mine)
        columns = jnp.pad(columns, ((0, 0), (0, mine - cols7), (0, LANES - nc * mine)))
        both = jnp.concatenate([jnp.broadcast_to(own_six, (nx, mine, wide)), columns], axis=2)
        both = swap(both, "gx")
        g_six = both[:, :, :wide].reshape(group, wide)
        columns = both[:, :cols7, wide : wide + nc * mine]

        feat_terms = features_back(g_six, weight6).reshape(nz, nx, feats)
        feat_terms, g_six = lax.optimization_barrier((feat_terms, g_six))
        feat_terms = swap(feat_terms, "gz")
        sent6 = weight_terms(nc - 1 - core, inputs, g_six, units)
        packs = pack_dfeat(me.reshape(1).astype(jnp.int32), feat_terms)
        packs = swap(packs, "gx")
        gathered, sent6 = lax.optimization_barrier((gathered, sent6))
        all_lines = jax.vmap(bordered)(gathered)
        grad_fc6 = weight_terms(core, inputs, g_six, units, lax.ppermute(sent6, "core", pair))
        spread = spread_matrix(me, nx, half, cols)
        packed = conv_kernel_grad(all_lines, slopes, packs, spread, ny)
        packed = swap(packed, gy)

        runs = feats // part
        dfeat = packs[:, :runs, part : 2 * part].reshape(half, half, chans).astype(F32)
        dfeat = jnp.pad(dfeat, ((0, 0), (0, 1), (0, 0))).reshape(half * (half + 1), chans)
        g_lines = conv_slope(conv_pre, dfeat).reshape(side, LINE, chans)[:, :side]
        grad_images = conv_backward(bordered(g_lines), conv_weight, side)

        hidden = hidden.reshape(nz, nc * mine, wide).transpose(1, 0, 2).reshape(nc * mine, rows7)
        all_hidden = lax.all_gather(hidden, "gx", axis=0, tiled=False).reshape(total, rows7)
        columns = columns.transpose(1, 0, 2).reshape(cols7, total)
        grad_fc7 = dot(columns, all_hidden, ((1,), (0,))).T
        packed, grad_fc7 = lax.optimization_barrier((packed, grad_fc7))
        packed = packed.astype(F32).sum(axis=0)
        grad_conv = jnp.concatenate([packed[:, :part], packed[:, part:]], axis=0)
        return (grad_conv, grad_fc6, grad_fc7, grad_images)

    return on_device


def solution(mesh):
    nx, ny = mesh.shape["gx"], mesh.shape["gy"]
    nc = 2
    nz = ny // nc
    fine = Mesh(mesh.devices.reshape(nx, nz, nc), ("gx", "gz", "core"))
    gy = ("gz", "core")
    both = ("gx", "gz", "core")
    return jax.shard_map(
        make(nx, nz, nc),
        mesh=fine,
        in_specs=(P(both, None, None, None), P(), P("gx", gy), P(None, both), P(None, both)),
        out_specs=(P(gy, "gx"), P("gx", gy), P(None, both), P(both, None, None, None)),
        check_vma=False,
    )
```

time: 230 us -> 207 us (0.900)
  blocking collectives: 55.5 us -> 21.6 us
  waiting for transfers between devices: 59.4 us -> 76.6 us
  matrix products: 6.29 us -> 3.2 us
  local copies, waits for them, and re-layouts: 16.8 us -> 19.8 us
  Pallas kernels: 17.8 us -> 15 us
  other arithmetic: 7.38 us -> 5.05 us
    all_to_all x4 -> x2, blocking collectives: 55.5 us -> 21.6 us  [swap(): return lax.all_to_all(value, axis, 0, 0, tiled=True)]
    all_gather x1, waiting for transfers between devices: 0.01 us -> 11.3 us  [on_device(): lax.all_gather(hidden, 'gx', axis=0, tiled=False).reshape(total, rows7)]
    all_to_all x8 -> x7, starting transfers between devices: 51.8 us -> 41.7 us  [swap(): return lax.all_to_all(value, axis, 0, 0, tiled=True)]
    ppermute x0 -> x2, starting transfers between devices: none -> 8.66 us  [the longest x1 5.33 us: on_device(): lax.ppermute(sent6, 'core', pair)]
    all_to_all x8 -> x7, waiting for transfers between devices: 58.7 us -> 64.6 us  [swap(): return lax.all_to_all(value, axis, 0, 0, tiled=True)]
    pallas_call x4 -> x8, Pallas kernels: 13.6 us -> 9.95 us  [the longest x1 2.83 us: conv_kernel_grad(): pl.pallas_call(kernel_kernel, out_shape=jax.ShapeDtypeStruct((count, size...]
    dot_general x5 -> x2, matrix products: 6.29 us -> 3.2 us  [dot(): return lax.dot_general(a, b, (dims, ((), ())), preferred_element_type=F32)]
    unnamed x17 -> x19, local copies, waits for them, and re-layouts: 7.19 us -> 9.72 us
  transfers between devices with their start and end apart: 11 -> 12, of which waited for: 6 -> 6; matrix products, arithmetic and copies ran while one was open for 9% -> 8% of each run, Pallas kernels for 8% -> 7%
where the time goes in v4:
time: 207 us; the launch traced here: 206 us
  waiting for transfers between devices  76.6 us (37%)
  starting transfers between devices  50.5 us (24%)
  blocking collectives  21.6 us (10%)
  local copies, waits for them, and re-layouts  19.8 us (10%)
  Pallas kernels  15 us (7%)
  between operations  14.1 us (7%)
  other arithmetic  5.05 us (2%)
  matrix products  3.2 us (2%)
    all_to_all x7, waiting for transfers between devices, swap(): return lax.all_to_all(value, axis, 0, 0, tiled=True)  64.6 us
    all_to_all x7, starting transfers between devices, swap(): return lax.all_to_all(value, axis, 0, 0, tiled=True)  41.7 us
    all_to_all x2, blocking collectives, swap(): return lax.all_to_all(value, axis, 0, 0, tiled=True)  21.6 us
    all_gather x1, waiting for transfers between devices, on_device(): lax.all_gather(hidden, 'gx', axis=0, tiled=False).reshape(total, rows7)  11.3 us
    unnamed x19, local copies, waits for them, and re-layouts  9.72 us
    ppermute x1, starting transfers between devices, on_device(): lax.ppermute(sent6, 'core', pair)  5.33 us
    pad x3, local copies, waits for them, and re-layouts, bordered(): padded = jnp.pad(maps, ((1, 3), (1, LINE - side - 1), (0, 0)))  4.74 us
  transfers between devices with their start and end apart: 12, of which 6 were waited for; matrix products, arithmetic and copies ran while one was open for 8% of the time, Pallas kernels for 7%

profile of v4, /device:TPU:1, one launch (start us, length us, event | category | flops | bytes accessed | tf_op | source)
XLA Modules:
  0.0 205.8 jit_solution(4545067456046840257)
XLA Ops:
  7.2 0.0 all-gather.9.cloned.1.call-start
  7.2 1.6 pad_maximum_fusion.2
  8.8 0.0 all-gather.9.cloned.1.call-update
  8.8 3.3 %collective-permute-start = (bf16[3136,128]{1,0:T(8,128)(2,1)}, bf16[3136,128]{1,0:T(8,128)(2,1)S(1)}, u32[]{:S(2)}, u32[]{:S(2)}) collective-permute-start(bf16[3136,128]{1,0:T(8,128)(2,1)} %param.7), channel_id=1, source_target_pairs={{0,1},{1,0},{2,3},{3,2},{4,5},{5,4},{6,7},{7,6},{8,9},{9,8},{10,11... | collective-permute-start | bytes 2408456 | tf_op jit(solution)/shard_map/ppermute | solution.py:366
  12.2 1.0 pad.20
  13.2 2.3 %copy-done = bf16[4608,512]{1,0:T(8,128)(2,1)S(1)} copy-done((bf16[4608,512]{1,0:T(8,128)(2,1)S(1)}, bf16[4608,512]{1,0:T(8,128)(2,1)}, u32[]{:S(2)}) %copy-start) | copy-done | bytes 4718616
  15.5 2.2 %shard_map.84 = (f32[224,512]{1,0:T(8,128)S(1)}, bf16[56,512]{1,0:T(8,128)(2,1)S(1)}) custom-call(bf16[288,512]{1,0:T(8,128)(2,1)S(1)} %bitcast.41, bf16[4608,512]{1,0:T(8,128)(2,1)S(1)} %copy-done), custom_call_target="tpu_custom_call" | custom-call | flops 1056964608 | bytes 4718592 | tf_op jit(solution)/shard_map/pallas_call | solution.py:66
  17.7 0.1 all_to_all.43
  17.8 0.5 broadcast.181
  18.3 0.9 reduce
  19.2 0.1 reshape.93
  19.4 11.4 %all_to_all.53 = bf16[8,2,1568]{2,1,0:T(2,128)(2,1)S(1)} all-to-all(bf16[8,2,1568]{2,1,0:T(2,128)(2,1)S(1)} %reshape.93), channel_id=1, replica_groups=mesh['gx'=8,'gz'=16,'core'=2] {'gx'}, dimensions={0} | all-to-all | bytes 100352 | tf_op jit(solution)/shard_map/all_to_all | solution.py:330
  30.8 0.1 reshape.94
  30.9 0.9 broadcast_in_dim.11
  31.9 8.4 %all-to-all-start.1 = ((bf16[16,8,3136]{2,1,0:T(8,128)(2,1)}), bf16[16,8,3136]{2,1,0:T(8,128)(2,1)S(1)}, u32[]{:S(2)}, u32[]{:S(2)}) async-start(bf16[16,8,3136]{2,1,0:T(8,128)(2,1)} %broadcast_in_dim.11), calls=%async_computation.1 | async-start | bytes 1638400 | tf_op jit(solution)/shard_map/all_to_all | solution.py:330
  40.3 0.0 all-gather.5.cloned.1.call-start
  40.3 0.7 all-gather.5.cloned.1.call-update
  41.1 0.2 shard_map.85
  41.3 0.1 broadcast_select_fusion.1
  41.4 0.2 pad_maximum_fusion.weight_ref
  41.6 17.8 %all-to-all-done.1 = bf16[16,8,3136]{2,1,0:T(8,128)(2,1)S(1)} async-done(((bf16[16,8,3136]{2,1,0:T(8,128)(2,1)}), bf16[16,8,3136]{2,1,0:T(8,128)(2,1)S(1)}, u32[]{:S(2)}, u32[]{:S(2)}) %all-to-all-start.1) | async-done | bytes 802848 | tf_op jit(solution)/shard_map/all_to_all | solution.py:330
  59.4 0.4 convolution_convert_fusion
  59.8 0.7 pad_maximum_fusion.1
  60.6 3.5 %all-to-all-start.2 = ((bf16[8,80,256]{2,1,0:T(8,128)(2,1)}), bf16[8,80,256]{2,1,0:T(8,128)(2,1)S(1)}, u32[]{:S(2)}, u32[]{:S(2)}) async-start(bf16[8,80,256]{2,1,0:T(8,128)(2,1)} %pad_maximum_fusion.1), calls=%async_computation.2 | async-start | bytes 655360 | tf_op jit(solution)/shard_map/all_to_all | solution.py:330
  64.1 7.9 %all-to-all-done.2 = bf16[8,80,256]{2,1,0:T(8,128)(2,1)S(1)} async-done(((bf16[8,80,256]{2,1,0:T(8,128)(2,1)}), bf16[8,80,256]{2,1,0:T(8,128)(2,1)S(1)}, u32[]{:S(2)}, u32[]{:S(2)}) %all-to-all-start.2) | async-done | bytes 327712 | tf_op jit(solution)/shard_map/all_to_all | solution.py:330
  72.0 0.8 broadcast_in_dim.12
  72.8 9.4 %all-to-all-start.3 = ((bf16[32,16,256]{2,1,0:T(8,128)(2,1)}), bf16[32,16,256]{2,1,0:T(8,128)(2,1)S(1)}, u32[]{:S(2)}, u32[]{:S(2)}) async-start(bf16[32,16,256]{2,1,0:T(8,128)(2,1)} %broadcast_in_dim.12), calls=%async_computation.3 | async-start | bytes 524288 | tf_op jit(solution)/shard_map/all_to_all | solution.py:330
  82.3 0.0 all-gather.9.cloned.1.call-done.known_ref
  82.3 11.8 %all-to-all-done.3.hidden_ref = bf16[32,16,256]{2,1,0:T(8,128)(2,1)S(1)} async-done(((bf16[32,16,256]{2,1,0:T(8,128)(2,1)}), bf16[32,16,256]{2,1,0:T(8,128)(2,1)S(1)}, u32[]{:S(2)}, u32[]{:S(2)}) %all-to-all-start.3) | async-done | bytes 262176 | tf_op jit(solution)/shard_map/all_to_all | solution.py:330
  94.1 1.2 copy-done.3
  95.4 1.7 shard_map.86
  97.0 5.0 %all-to-all-start.4 = ((bf16[32,16,256]{2,1,0:T(8,128)(2,1)}), bf16[32,16,256]{2,1,0:T(8,128)(2,1)S(1)}, u32[]{:S(2)}, u32[]{:S(2)}) async-start(bf16[32,16,256]{2,1,0:T(8,128)(2,1)} %get-tuple-element.20), calls=%async_computation.4 | async-start | bytes 524288 | tf_op jit(solution)/shard_map/all_to_all | solution.py:330
  102.1 0.0 all-gather.7.cloned.1.call-start
  102.1 0.9 copy.17
  103.0 1.8 all_gather_reshape.3
  104.8 0.0 all-gather.7.cloned.1.call-update
  104.8 9.3 %all-to-all-done.4 = bf16[32,16,256]{2,1,0:T(8,128)(2,1)S(1)} async-done(((bf16[32,16,256]{2,1,0:T(8,128)(2,1)}), bf16[32,16,256]{2,1,0:T(8,128)(2,1)S(1)}, u32[]{:S(2)}, u32[]{:S(2)}) %all-to-all-start.4) | async-done | bytes 262176 | tf_op jit(solution)/shard_map/all_to_all | solution.py:330
  114.2 10.2 %all_to_all.54 = bf16[8,16,384]{2,1,0:T(8,128)(2,1)S(1)} all-to-all(bf16[8,16,384]{2,1,0:T(8,128)(2,1)S(1)} %fusion.12), channel_id=1, replica_groups=mesh['gx'=8,'gz'=16,'core'=2] {'gx'}, dimensions={0} | all-to-all | bytes 196608 | tf_op jit(solution)/shard_map/all_to_all | solution.py:330
  124.4 1.6 shard_map.87
  126.0 3.8 %all-to-all-start.6 = ((bf16[16,8,3136]{2,1,0:T(8,128)(2,1)}), bf16[16,8,3136]{2,1,0:T(8,128)(2,1)S(1)}, u32[]{:S(2)}, u32[]{:S(2)}) async-start(bf16[16,8,3136]{2,1,0:T(8,128)(2,1)} %bitcast.11), calls=%async_computation.6 | async-start | bytes 1638400 | tf_op jit(solution)/shard_map/all_to_all | solution.py:330
  129.8 17.7 %all-to-all-done.6.terms_ref = bf16[16,8,3136]{2,1,0:T(8,128)(2,1)S(1)} async-done(((bf16[16,8,3136]{2,1,0:T(8,128)(2,1)}), bf16[16,8,3136]{2,1,0:T(8,128)(2,1)S(1)}, u32[]{:S(2)}, u32[]{:S(2)}) %all-to-all-start.6) | async-done | bytes 802848 | tf_op jit(solution)/shard_map/all_to_all | solution.py:330
  147.5 0.9 shard_map.89
  148.4 3.4 %all-to-all-start.7 = ((bf16[8,64,128]{2,1,0:T(8,128)(2,1)}), bf16[8,64,128]{2,1,0:T(8,128)(2,1)S(1)}, u32[]{:S(2)}, u32[]{:S(2)}) async-start(bf16[8,64,128]{2,1,0:T(8,128)(2,1)} %shard_map.89), calls=%async_computation.7 | async-start | bytes 262144 | tf_op jit(solution)/shard_map/all_to_all | solution.py:330
  151.8 0.1 fusion.29.spread_ref
  152.0 0.4 shard_map.88
  152.4 0.0 all-gather.5.cloned.1.call-done
  152.4 5.3 %collective-permute-start.1 = (bf16[3136,128]{1,0:T(8,128)(2,1)S(1)}, bf16[3136,128]{1,0:T(8,128)(2,1)S(1)}, u32[]{:S(2)}, u32[]{:S(2)}) collective-permute-start(bf16[3136,128]{1,0:T(8,128)(2,1)S(1)} %shard_map.88), channel_id=1, source_target_pairs={{0,1},{1,0},{2,3},{3,2},{4,5},{5,4},{6,7},{7,6},{8,9},{9,8},{10,11... | collective-permute-start | bytes 2408456 | tf_op jit(solution)/shard_map/ppermute | solution.py:407
  157.8 3.7 %pad.22 = bf16[8,18,16,512]{3,2,1,0:T(8,128)(2,1)} pad(bf16[8,14,14,512]{3,2,1,0:T(8,128)(2,1)} %all-gather.5.cloned.1.call-done, bf16[]{:T(256)} %constant.119.clone.1), padding=0_0x1_3x1_1x0_0 | pad | bytes 3964930 | tf_op jit(solution)/shard_map/vmap(jit(_pad))/pad | solution.py:339
  161.4 1.7 copy-done.2
  163.1 2.8 %shard_map.90 = bf16[32,72,128]{2,1,0:T(8,128)(2,1)} custom-call(bf16[8,288,512]{2,1,0:T(8,128)(2,1)S(1)} %bitcast.39, bf16[8,64,256]{2,1,0:T(8,128)(2,1)S(1)} %slice.39.slope_ref, bf16[8,64,128]{2,1,0:T(8,128)(2,1)S(1)} %all-to-all-done.7.dfeat_ref, bf16[64,256]{1,0:T(8,128)(2,1)S(1)} %fusion.29.spread_ref), custom_call_target="tpu_custom_call" | custom-call | flops 1207959552 | bytes 2359296 | tf_op jit(solution)/shard_map/pallas_call | solution.py:263
  165.9 8.2 %all-to-all-start.8 = ((bf16[32,72,128]{2,1,0:T(8,128)(2,1)}), bf16[32,72,128]{2,1,0:T(8,128)(2,1)}, u32[]{:S(2)}, u32[]{:S(2)}) async-start(bf16[32,72,128]{2,1,0:T(8,128)(2,1)} %shard_map.90), calls=%async_computation.8 | async-start | bytes 1179648 | tf_op jit(solution)/shard_map/all_to_all | solution.py:330
  174.1 1.6 shard_map.91
  175.7 0.1 slice.43
  175.8 0.1 convert_element_type.49
  175.9 0.2 shard_map.92
  176.1 0.1 pad.24
  176.2 2.3 %copy-done.1 = bf16[4608,512]{1,0:T(8,128)(2,1)S(1)} copy-done((bf16[4608,512]{1,0:T(8,128)(2,1)S(1)}, bf16[4608,512]{1,0:T(8,128)(2,1)}, u32[]{:S(2)}) %copy-start.1) | copy-done | bytes 4718616
  178.5 3.5 %shard_map.93 = f32[1,14,14,512]{3,2,1,0:T(8,128)S(1)} custom-call(bf16[288,512]{1,0:T(8,128)(2,1)S(1)} %bitcast.42, bf16[4608,512]{1,0:T(8,128)(2,1)S(1)} %copy-done.1), custom_call_target="tpu_custom_call" | custom-call | flops 1056964608 | bytes 4718592 | tf_op jit(solution)/shard_map/pallas_call | solution.py:303
  182.1 1.2 copy.19
  183.2 11.3 %all-gather.7.cloned.1.call-done = bf16[8,32,4096]{2,1,0:T(8,128)(2,1)} async-done(((bf16[1,32,4096]{2,1,0:T(8,128)(2,1)}), bf16[8,32,4096]{2,1,0:T(8,128)(2,1)}) %all-gather.7.cloned.1.call-update) | async-done | bytes 2097168 | tf_op jit(solution)/shard_map/all_gather | solution.py:419
  194.5 2.8 %convolution_bitcast_fusion = f32[4096,16]{0,1:T(8,128)} fusion(bf16[8,32,4096]{2,1,0:T(8,128)(2,1)} %all-gather.7.cloned.1.call-done, bf16[8,16,384]{2,1,0:T(8,128)(2,1)S(1)} %all_to_all.54), kind=kOutput, calls=%fused_computation | convolution fusion | flops 33554432 | bytes 2392064 | tf_op jit(solution)/shard_map/dot_general | solution.py:25
  197.3 1.2 convert_reduce_fusion
  198.5 0.1 fusion.33
  198.6 0.7 copy.18
  (35 shorter events, 0.3 us)
Async XLA Ops:
  7.2 75.1 %all-gather.9.cloned.1.call-start = ((), (), s32[]{:S(2)}) async-start(), calls=%async_computation.11 | async-start | bytes 1253376 | tf_op jit(solution)/shard_map/all_gather | solution.py:362
  8.8 32.5 %collective-permute-start = (bf16[3136,128]{1,0:T(8,128)(2,1)}, bf16[3136,128]{1,0:T(8,128)(2,1)S(1)}, u32[]{:S(2)}, u32[]{:S(2)}) collective-permute-start(bf16[3136,128]{1,0:T(8,128)(2,1)} %param.7), channel_id=1, source_target_pairs={{0,1},{1,0},{2,3},{3,2},{4,5},{5,4},{6,7},{7,6},{8,9},{9,8},{10,11... | collective-permute-start | bytes 2408456 | tf_op jit(solution)/shard_map/ppermute | solution.py:366
  13.2 2.3 %copy-start = (bf16[4608,512]{1,0:T(8,128)(2,1)S(1)}, bf16[4608,512]{1,0:T(8,128)(2,1)}, u32[]{:S(2)}) copy-start(bf16[4608,512]{1,0:T(8,128)(2,1)} %weight_ref.3) | copy-start | bytes 14155780
  30.9 10.4 %copy-start.6 = (bf16[3136,128]{1,0:T(8,128)(2,1)S(1)}, bf16[3136,128]{1,0:T(8,128)(2,1)}, u32[]{:S(2)}) copy-start(bf16[3136,128]{1,0:T(8,128)(2,1)} %param.7) | copy-start | bytes 2408452
  31.9 27.6 %all-to-all-start.1 = ((bf16[16,8,3136]{2,1,0:T(8,128)(2,1)}), bf16[16,8,3136]{2,1,0:T(8,128)(2,1)S(1)}, u32[]{:S(2)}, u32[]{:S(2)}) async-start(bf16[16,8,3136]{2,1,0:T(8,128)(2,1)} %broadcast_in_dim.11), calls=%async_computation.1 | async-start | bytes 1638400 | tf_op jit(solution)/shard_map/all_to_all | solution.py:330
  40.3 112.1 %all-gather.5.cloned.1.call-start = ((), (), s32[]{:S(2)}) async-start(), calls=%async_computation.9 | async-start | bytes 2064384 | tf_op jit(solution)/shard_map/all_gather | solution.py:365
  60.6 11.4 %all-to-all-start.2 = ((bf16[8,80,256]{2,1,0:T(8,128)(2,1)}), bf16[8,80,256]{2,1,0:T(8,128)(2,1)S(1)}, u32[]{:S(2)}, u32[]{:S(2)}) async-start(bf16[8,80,256]{2,1,0:T(8,128)(2,1)} %pad_maximum_fusion.1), calls=%async_computation.2 | async-start | bytes 655360 | tf_op jit(solution)/shard_map/all_to_all | solution.py:330
  72.0 0.8 copy-start.4
  72.8 21.3 %all-to-all-start.3 = ((bf16[32,16,256]{2,1,0:T(8,128)(2,1)}), bf16[32,16,256]{2,1,0:T(8,128)(2,1)S(1)}, u32[]{:S(2)}, u32[]{:S(2)}) async-start(bf16[32,16,256]{2,1,0:T(8,128)(2,1)} %broadcast_in_dim.12), calls=%async_computation.3 | async-start | bytes 524288 | tf_op jit(solution)/shard_map/all_to_all | solution.py:330
  94.1 1.2 copy-start.3
  97.0 17.1 %all-to-all-start.4 = ((bf16[32,16,256]{2,1,0:T(8,128)(2,1)}), bf16[32,16,256]{2,1,0:T(8,128)(2,1)S(1)}, u32[]{:S(2)}, u32[]{:S(2)}) async-start(bf16[32,16,256]{2,1,0:T(8,128)(2,1)} %get-tuple-element.20), calls=%async_computation.4 | async-start | bytes 524288 | tf_op jit(solution)/shard_map/all_to_all | solution.py:330
  102.1 92.4 %all-gather.7.cloned.1.call-start = ((), (), s32[]{:S(2)}) async-start(), calls=%async_computation.10 | async-start | bytes 2359296 | tf_op jit(solution)/shard_map/all_gather | solution.py:419
  126.0 26.0 %copy-start.5 = (bf16[8,80,256]{2,1,0:T(8,128)(2,1)S(1)}, bf16[8,80,256]{2,1,0:T(8,128)(2,1)}, u32[]{:S(2)}) copy-start(bf16[8,80,256]{2,1,0:T(8,128)(2,1)} %copy-done.4) | copy-start | bytes 983044
  126.0 21.6 %all-to-all-start.6 = ((bf16[16,8,3136]{2,1,0:T(8,128)(2,1)}), bf16[16,8,3136]{2,1,0:T(8,128)(2,1)S(1)}, u32[]{:S(2)}, u32[]{:S(2)}) async-start(bf16[16,8,3136]{2,1,0:T(8,128)(2,1)} %bitcast.11), calls=%async_computation.6 | async-start | bytes 1638400 | tf_op jit(solution)/shard_map/all_to_all | solution.py:330
  148.4 13.0 %all-to-all-start.7 = ((bf16[8,64,128]{2,1,0:T(8,128)(2,1)}), bf16[8,64,128]{2,1,0:T(8,128)(2,1)S(1)}, u32[]{:S(2)}, u32[]{:S(2)}) async-start(bf16[8,64,128]{2,1,0:T(8,128)(2,1)} %shard_map.89), calls=%async_computation.7 | async-start | bytes 262144 | tf_op jit(solution)/shard_map/all_to_all | solution.py:330
  152.4 21.7 %collective-permute-start.1 = (bf16[3136,128]{1,0:T(8,128)(2,1)S(1)}, bf16[3136,128]{1,0:T(8,128)(2,1)S(1)}, u32[]{:S(2)}, u32[]{:S(2)}) collective-permute-start(bf16[3136,128]{1,0:T(8,128)(2,1)S(1)} %shard_map.88), channel_id=1, source_target_pairs={{0,1},{1,0},{2,3},{3,2},{4,5},{5,4},{6,7},{7,6},{8,9},{9,8},{10,11... | collective-permute-start | bytes 2408456 | tf_op jit(solution)/shard_map/ppermute | solution.py:407
  161.4 1.7 copy-start.2
  165.9 31.4 %all-to-all-start.8 = ((bf16[32,72,128]{2,1,0:T(8,128)(2,1)}), bf16[32,72,128]{2,1,0:T(8,128)(2,1)}, u32[]{:S(2)}, u32[]{:S(2)}) async-start(bf16[32,72,128]{2,1,0:T(8,128)(2,1)} %shard_map.90), calls=%async_computation.8 | async-start | bytes 1179648 | tf_op jit(solution)/shard_map/all_to_all | solution.py:330
  176.2 2.3 %copy-start.1 = (bf16[4608,512]{1,0:T(8,128)(2,1)S(1)}, bf16[4608,512]{1,0:T(8,128)(2,1)}, u32[]{:S(2)}) copy-start(bf16[4608,512]{1,0:T(8,128)(2,1)} %weight_ref.3) | copy-start | bytes 14155780
Sparse Core Ops, SparseCore 0:
  10.6 57.2 all-gather.8
  70.5 58.5 all-gather.4
  131.7 62.7 all-gather.6

commit v5 on v4

--- a/solution.py
+++ b/solution.py
@@ -125,32 +125,34 @@
     )(pre, dfeat)
 
 
-def fc7_kernel(known_ref, hidden_ref, pick_ref, seven_ref, terms_ref):
+def fc7_kernel(own_ref, other_ref, hidden_ref, pick_ref, seven_ref, terms_ref):
     count, mine, wide = hidden_ref.shape
-    rows7 = count // 2 * wide
-    y7_pre = jnp.zeros(seven_ref.shape, F32)
-    for g in range(count // 2):
-        block = hidden_ref[2 * g : 2 * g + 2].reshape(2 * mine, wide)
-        y7_pre += dot(known_ref[:, g * wide : (g + 1) * wide], block, ((1,), (1,)))
-    cot = dot(known_ref[:, rows7:], pick_ref[...], ((1,), (0,)))
-    seven = (cot * slope(y7_pre)).astype(BF)
-    seven_ref[...] = seven
-    for g in range(count // 2):
-        part = dot(seven, known_ref[:, g * wide : (g + 1) * wide], ((0,), (0,)))
-        terms_ref[2 * g : 2 * g + 2] = part.astype(BF).reshape(2, mine, wide)
-
-
-def fc7_step(known, hidden, pick):
-    cols = known.shape[0]
+    rows7 = count * wide
+    weights = (own_ref, other_ref)
+    sevens = []
+    for k, ref in enumerate(weights):
+        y7_pre = jnp.zeros((ref.shape[0], mine), F32)
+        for g in range(count):
+            y7_pre += dot(ref[:, g * wide : (g + 1) * wide], hidden_ref[g], ((1,), (1,)))
+        cot = dot(ref[:, rows7:], pick_ref[...], ((1,), (0,)))
+        sevens.append((cot * slope(y7_pre)).astype(BF))
+        seven_ref[:, k * mine : (k + 1) * mine] = sevens[k]
+    for g in range(count):
+        parts = [dot(v, ref[:, g * wide : (g + 1) * wide], ((0,), (0,))) for v, ref in zip(sevens, weights)]
+        terms_ref[g] = (parts[0] + parts[1]).astype(BF)
+
+
+def fc7_step(own, other, hidden, pick):
+    cols = own.shape[0]
     return pl.pallas_call(
         fc7_kernel,
         out_shape=[
-            jax.ShapeDtypeStruct((cols, pick.shape[1]), BF),
+            jax.ShapeDtypeStruct((cols, 2 * pick.shape[1]), BF),
             jax.ShapeDtypeStruct(hidden.shape, BF),
         ],
         compiler_params=VMEM,
-        cost_estimate=cost(4 * known.size * pick.shape[1], known.size * 2),
-    )(known, hidden, pick)
+        cost_estimate=cost(8 * own.size * pick.shape[1], own.size * 4),
+    )(own, other, hidden, pick)
 
 
 def back_kernel(g_ref, weight_ref, out_ref):
@@ -233,19 +235,22 @@
     )(me, terms)
 
 
-def kernel_kernel(lines_ref, slope_ref, dfeat_ref, spread_ref, out_ref, grad_ref, flat_ref, wide_ref):
+def kernel_kernel(me_ref, slope_ref, dfeat_ref, spread_ref, *refs):
     images, part, cols = slope_ref.shape
-    chans = lines_ref.shape[2]
+    lines_refs = refs[:images]
+    out_ref, grad_ref, flat_ref, wide_ref = refs[images:]
+    chans = lines_refs[0].shape[1]
     wide_ref[...] = dfeat_ref[...].astype(F32).reshape(wide_ref.shape)
-    for n in range(images):
+    for k in range(images):
+        n = lax.rem(me_ref[0] + images - k, images)
         cells = wide_ref[pl.ds(n, wide_ref.shape[0] // images, images), :].astype(BF)
         spread = dot(cells, spread_ref[...], ((0,), (0,)))[:part]
         turned = (spread * slope_ref[n].astype(F32)).astype(BF).astype(F32)
-        moved = [turned] + [pltpu.roll(turned, k, 1) for k in (1, 2)]
-        grad_ref[:, n * cols : (n + 1) * cols] = jnp.concatenate(moved, axis=0).astype(BF)
+        moved = [turned] + [pltpu.roll(turned, j, 1) for j in (1, 2)]
+        grad_ref[:, k * cols : (k + 1) * cols] = jnp.concatenate(moved, axis=0).astype(BF)
     for row in range(3):
-        block = lines_ref[:, row * LINE : row * LINE + cols, :].reshape(images * cols, chans)
-        term = dot(grad_ref[...], block, ((1,), (0,)))
+        block = [ref[row * LINE : row * LINE + cols, :] for ref in lines_refs]
+        term = dot(grad_ref[...], jnp.concatenate(block, axis=0), ((1,), (0,)))
         for col in range(3):
             tap = 3 * row + col
             flat_ref[tap * chans : (tap + 1) * chans, :] = term[col * part : (col + 1) * part].T
@@ -256,12 +261,14 @@
         out_ref[dest] = jnp.concatenate(both, axis=1).astype(BF)
 
 
-def conv_kernel_grad(lines, slopes, dfeat, spread, count):
-    images, rows, chans = lines.shape
-    _, part, cols = slopes.shape
+def conv_kernel_grad(me, lines, slopes, dfeat, spread, count):
+    chans = lines[0].shape[1]
+    images, part, cols = slopes.shape
     size = 9 * chans // (2 * count)
+    in_vmem = [pl.BlockSpec(memory_space=pltpu.VMEM)] * (3 + images)
     return pl.pallas_call(
         kernel_kernel,
+        in_specs=[pl.BlockSpec(memory_space=pltpu.SMEM)] + in_vmem,
         out_shape=jax.ShapeDtypeStruct((count, size, 2 * part), BF),
         scratch_shapes=[
             pltpu.VMEM((3 * part, images * cols), BF),
@@ -269,8 +276,8 @@
             pltpu.VMEM((dfeat.shape[0] * dfeat.shape[1], LANES), F32),
         ],
         compiler_params=VMEM,
-        cost_estimate=cost(18 * images * cols * chans * part, lines.size * 2),
-    )(lines, slopes, dfeat, spread)
+        cost_estimate=cost(18 * images * cols * chans * part, images * lines[0].size * 2),
+    )(me, slopes, dfeat, spread, *lines)
 
 
 def backward_kernel(lines_ref, weight_ref, out_ref, sums_ref):
@@ -358,13 +365,16 @@
         part = chans // nx
         cols = 2 * LANES
         me, core = lax.axis_index("gx"), lax.axis_index("core")
+        me_word = me.reshape(1).astype(jnp.int32)
 
         known = lax.all_gather(
             jnp.concatenate([fc7_weight.T, cotangent.T], axis=1), "gx", axis=0, tiled=False
         )
-        gathered = lax.all_gather(images[0], "gx", axis=0, tiled=False)
         other6 = lax.ppermute(fc6_weight, "core", pair)
         lines = bordered(images[0])
+        all_lines = [lines]
+        for _ in range(1, nx):
+            all_lines.append(lax.ppermute(all_lines[-1], "gx", [(k, (k + 1) % nx) for k in range(nx)]))
         conv_pre, pooled = conv_forward(lines, conv_weight, side)
         slopes = turned_slope(conv_pre, cols).reshape(nx, part, cols)
         feat = pooled.reshape(half, half + 1, chans)[:, :half].reshape(nx, feats)
@@ -376,17 +386,20 @@
 
         h6_terms = dot(inputs, weight6, ((1,), (0,))).astype(BF).reshape(nx, mine, wide)
         both = swap(jnp.concatenate([h6_terms, slopes], axis=1), "gx")
+        both, known = lax.optimization_barrier((both, known.reshape(nx * cols7, rows7 + total)))
+        known_other = lax.ppermute(known, "core", pair)
         h6_pre = both[:, :mine].astype(F32).sum(axis=0)
         slopes = both[:, mine:]
         own_hidden = activate(h6_pre).astype(BF)
-        hidden = share(own_hidden, gy, ny)
-
-        place = lax.broadcasted_iota(jnp.int32, (total, nc * mine), 1)
-        half_of, rest = place // mine, place % mine
-        source = (rest % nx) * ny + (me * near + rest // nx) * nc + half_of
-        pick = (lax.broadcasted_iota(jnp.int32, (total, nc * mine), 0) == source).astype(BF)
-        g_seven, dh6_terms = fc7_step(known.reshape(nx * cols7, rows7 + total), hidden, pick)
-        grad_hidden = swap(dh6_terms, gy).astype(F32).sum(axis=0)
+        hidden = share(own_hidden, "gz", nz)
+
+        place = lax.broadcasted_iota(jnp.int32, (total, mine), 1)
+        source = (place % nx) * ny + (me * near + place // nx) * nc + core
+        pick = (lax.broadcasted_iota(jnp.int32, (total, mine), 0) == source).astype(BF)
+        g_seven, dh6_terms = fc7_step(known, known_other, hidden, pick)
+        hidden = hidden.transpose(1, 0, 2).reshape(mine, rows7)
+        all_hidden = lax.all_gather(hidden, "gx", axis=0, tiled=False).reshape(group, rows7)
+        grad_hidden = swap(dh6_terms, "gz").astype(F32).sum(axis=0)
         own_six = (grad_hidden * slope(h6_pre)).astype(BF)
 
         columns = g_seven.reshape(nx, cols7, nc * mine)
@@ -399,14 +412,13 @@
         feat_terms = features_back(g_six, weight6).reshape(nz, nx, feats)
         feat_terms, g_six = lax.optimization_barrier((feat_terms, g_six))
         feat_terms = swap(feat_terms, "gz")
+        feat_terms, all_hidden = lax.optimization_barrier((feat_terms, all_hidden))
         sent6 = weight_terms(nc - 1 - core, inputs, g_six, units)
-        packs = pack_dfeat(me.reshape(1).astype(jnp.int32), feat_terms)
+        packs = pack_dfeat(me_word, feat_terms)
         packs = swap(packs, "gx")
-        gathered, sent6 = lax.optimization_barrier((gathered, sent6))
-        all_lines = jax.vmap(bordered)(gathered)
         grad_fc6 = weight_terms(core, inputs, g_six, units, lax.ppermute(sent6, "core", pair))
         spread = spread_matrix(me, nx, half, cols)
-        packed = conv_kernel_grad(all_lines, slopes, packs, spread, ny)
+        packed = conv_kernel_grad(me_word, all_lines, slopes, packs, spread, ny)
         packed = swap(packed, gy)
 
         runs = feats // part
@@ -415,10 +427,9 @@
         g_lines = conv_slope(conv_pre, dfeat).reshape(side, LINE, chans)[:, :side]
         grad_images = conv_backward(bordered(g_lines), conv_weight, side)
 
-        hidden = hidden.reshape(nz, nc * mine, wide).transpose(1, 0, 2).reshape(nc * mine, rows7)
-        all_hidden = lax.all_gather(hidden, "gx", axis=0, tiled=False).reshape(total, rows7)
-        columns = columns.transpose(1, 0, 2).reshape(cols7, total)
-        grad_fc7 = dot(columns, all_hidden, ((1,), (0,))).T
+        columns = columns.reshape(nx, cols7, nc, mine).transpose(2, 1, 0, 3).reshape(nc * cols7, group)
+        terms7 = dot(columns, all_hidden, ((1,), (0,)))
+        grad_fc7 = (terms7[:cols7] + lax.ppermute(terms7[cols7:], "core", pair)).T
         packed, grad_fc7 = lax.optimization_barrier((packed, grad_fc7))
         packed = packed.astype(F32).sum(axis=0)
         grad_conv = jnp.concatenate([packed[:, :part], packed[:, part:]], axis=0)

time: 207 us -> 256 us (1.24)
  waiting for transfers between devices: 76.6 us -> 108 us
  blocking collectives: 21.6 us -> 36.1 us
  Pallas kernels: 15 us -> 19.7 us
  local copies, waits for them, and re-layouts: 19.8 us -> 16 us
  starting transfers between devices: 50.5 us -> 54.3 us
    ppermute x0 -> x9, waiting for transfers between devices: none -> 48.5 us  [the longest x7 48.5 us: on_device(): lax.ppermute(all_lines[-1], 'gx', [(k, (k + 1) % nx) for k in range(nx)])]
    all_to_all x7 -> x6, waiting for transfers between devices: 64.6 us -> 36.5 us  [swap(): return lax.all_to_all(value, axis, 0, 0, tiled=True)]
    all_gather x1, waiting for transfers between devices: 0.02 us -> 22.7 us  [on_device(): lax.all_gather(jnp.concatenate([fc7_weight.T, cotangent.T], axis=1), 'gx'...]
    all_to_all x2 -> x3, blocking collectives: 21.6 us -> 36.1 us  [swap(): return lax.all_to_all(value, axis, 0, 0, tiled=True)]
    all_gather x2 -> x1, waiting for transfers between devices: 11.3 us -> 0.02 us  [on_device(): lax.all_gather(hidden, 'gx', axis=0, tiled=False).reshape(group, rows7)]
    ppermute x0 -> x9, starting transfers between devices: none -> 7.79 us  [the longest x1 3.96 us: on_device(): grad_fc7 = (terms7[:cols7] + lax.ppermute(terms7[cols7:], 'core', pair)).T]
    pad x3 -> x2, local copies, waits for them, and re-layouts: 4.74 us -> 1.07 us  [bordered(): padded = jnp.pad(maps, ((1, 3), (1, LINE - side - 1), (0, 0)))]
    ppermute x1, starting transfers between devices: 5.33 us -> 2.48 us  [on_device(): lax.ppermute(sent6, 'core', pair)]
  transfers between devices with their start and end apart: 12 -> 19, of which waited for: 6 -> 10; matrix products, arithmetic and copies ran while one was open for 8% -> 6% of each run, Pallas kernels for 7% -> 8%
where the time goes in v5:
time: 256 us; the launch traced here: 255 us
  waiting for transfers between devices  108 us (42%)
  starting transfers between devices  54.3 us (21%)
  blocking collectives  36.1 us (14%)
  Pallas kernels  19.7 us (8%)
  local copies, waits for them, and re-layouts  16 us (6%)
  between operations  14.4 us (6%)
  other arithmetic  4.82 us (2%)
    ppermute x7, waiting for transfers between devices, on_device(): lax.ppermute(all_lines[-1], 'gx', [(k, (k + 1) % nx) for k in range(nx)])  48.5 us
    all_to_all x6, starting transfers between devices, swap(): return lax.all_to_all(value, axis, 0, 0, tiled=True)  40.6 us
    all_to_all x6, waiting for transfers between devices, swap(): return lax.all_to_all(value, axis, 0, 0, tiled=True)  36.5 us
    all_to_all x3, blocking collectives, swap(): return lax.all_to_all(value, axis, 0, 0, tiled=True)  36.1 us
    all_gather x1, waiting for transfers between devices, on_device(): lax.all_gather(jnp.concatenate([fc7_weight.T, cotangent.T], axis=1), 'gx'...  22.7 us
    unnamed x25, local copies, waits for them, and re-layouts  8.08 us
  transfers between devices with their start and end apart: 19, of which 10 were waited for; matrix products, arithmetic and copies ran while one was open for 6% of the time, Pallas kernels for 8%

profile of v5, /device:TPU:1, one launch (start us, length us, event | category | flops | bytes accessed | tf_op | source)
XLA Modules:
  0.0 255.1 jit_solution(975121582503206682)
XLA Ops:
  7.2 3.3 %collective-permute-start = (bf16[3136,128]{1,0:T(8,128)(2,1)}, bf16[3136,128]{1,0:T(8,128)(2,1)S(1)}, u32[]{:S(2)}, u32[]{:S(2)}) collective-permute-start(bf16[3136,128]{1,0:T(8,128)(2,1)} %param.7), channel_id=1, source_target_pairs={{0,1},{1,0},{2,3},{3,2},{4,5},{5,4},{6,7},{7,6},{8,9},{9,8},{10,11... | collective-permute-start | bytes 2408456 | tf_op jit(solution)/shard_map/ppermute | solution.py:373
  10.5 1.0 pad.16
  11.5 2.3 copy-done
  13.8 2.2 shard_map.84
  16.0 0.1 all_to_all.43
  16.2 0.5 broadcast.163
  16.7 0.9 reduce
  17.6 0.1 reshape.94
  17.7 11.4 %all_to_all.53 = bf16[8,2,1568]{2,1,0:T(2,128)(2,1)S(1)} all-to-all(bf16[8,2,1568]{2,1,0:T(2,128)(2,1)S(1)} %reshape.94), channel_id=1, replica_groups=mesh['gx'=8,'gz'=16,'core'=2] {'gx'}, dimensions={0} | all-to-all | bytes 100352 | tf_op jit(solution)/shard_map/all_to_all | solution.py:337
  29.1 0.1 reshape.95
  29.3 0.9 broadcast_in_dim.11
  30.2 8.5 %all-to-all-start.1 = ((bf16[16,8,3136]{2,1,0:T(8,128)(2,1)}), bf16[16,8,3136]{2,1,0:T(8,128)(2,1)S(1)}, u32[]{:S(2)}, u32[]{:S(2)}) async-start(bf16[16,8,3136]{2,1,0:T(8,128)(2,1)} %broadcast_in_dim.11), calls=%async_computation.1 | async-start | bytes 1638400 | tf_op jit(solution)/shard_map/all_to_all | solution.py:337
  38.7 0.7 pad_maximum_fusion.2
  39.4 0.2 shard_map.85
  39.7 0.1 broadcast_select_fusion.1
  39.8 0.2 pad_maximum_fusion.weight_ref
  40.0 17.6 %all-to-all-done.1 = bf16[16,8,3136]{2,1,0:T(8,128)(2,1)S(1)} async-done(((bf16[16,8,3136]{2,1,0:T(8,128)(2,1)}), bf16[16,8,3136]{2,1,0:T(8,128)(2,1)S(1)}, u32[]{:S(2)}, u32[]{:S(2)}) %all-to-all-start.1) | async-done | bytes 802848 | tf_op jit(solution)/shard_map/all_to_all | solution.py:337
  57.6 0.4 convolution_convert_fusion
  58.1 12.0 %all_to_all.54 = bf16[8,80,256]{2,1,0:T(8,128)(2,1)} all-to-all(bf16[8,80,256]{2,1,0:T(8,128)(2,1)S(1)} %pad_maximum_fusion.1), channel_id=1, replica_groups=mesh['gx'=8,'gz'=16,'core'=2] {'gx'}, dimensions={0} | all-to-all | bytes 655360 | tf_op jit(solution)/shard_map/all_to_all | solution.py:337
  70.1 22.7 %all-gather.6.cloned.1.call-done.own_ref = bf16[128,4352]{1,0:T(8,128)(2,1)} async-done(((bf16[16,4352]{1,0:T(8,128)(2,1)}), bf16[128,4352]{1,0:T(8,128)(2,1)}) %all-gather.6.cloned.1.call-update) | async-done | bytes 1114128 | tf_op jit(solution)/shard_map/all_gather | solution.py:370
  92.8 2.4 collective-permute-start.1
  95.2 0.9 collective-permute-start.2
  96.1 0.9 convert_reduce_fusion.2
  97.0 0.7 broadcast_in_dim.12
  97.7 6.8 %all-to-all-start.3 = ((bf16[16,16,256]{2,1,0:T(8,128)(2,1)}), bf16[16,16,256]{2,1,0:T(8,128)(2,1)S(1)}, u32[]{:S(2)}, u32[]{:S(2)}) async-start(bf16[16,16,256]{2,1,0:T(8,128)(2,1)} %broadcast_in_dim.12), calls=%async_computation.3 | async-start | bytes 262144 | tf_op jit(solution)/shard_map/all_to_all | solution.py:337
  104.6 7.4 %all-to-all-done.3.hidden_ref = bf16[16,16,256]{2,1,0:T(8,128)(2,1)S(1)} async-done(((bf16[16,16,256]{2,1,0:T(8,128)(2,1)}), bf16[16,16,256]{2,1,0:T(8,128)(2,1)S(1)}, u32[]{:S(2)}, u32[]{:S(2)}) %all-to-all-start.3) | async-done | bytes 131104 | tf_op jit(solution)/shard_map/all_to_all | solution.py:337
  112.0 1.2 copy-done.2
  113.2 3.0 %shard_map.86 = (bf16[128,32]{1,0:T(8,128)(2,1)S(1)}, bf16[16,16,256]{2,1,0:T(8,128)(2,1)}) custom-call(bf16[128,4352]{1,0:T(8,128)(2,1)S(1)} %copy-done.2, bf16[128,4352]{1,0:T(8,128)(2,1)} %collective-permute-done.1.other_ref, bf16[16,16,256]{2,1,0:T(8,128)(2,1)S(1)} %all-to-all-done.3.hidden_ref, bf16[256,16]{1,0:T(8,128)(2,1)S(1)} %fusion.2.pick_ref), custom_call_target="tpu_custom_call" | custom-call | flops 71303168 | bytes 2228224 | tf_op jit(solution)/shard_map/pallas_call | solution.py:147
  116.2 4.0 %all-to-all-start.4 = ((bf16[16,16,256]{2,1,0:T(8,128)(2,1)}), bf16[16,16,256]{2,1,0:T(8,128)(2,1)S(1)}, u32[]{:S(2)}, u32[]{:S(2)}) async-start(bf16[16,16,256]{2,1,0:T(8,128)(2,1)} %get-tuple-element.24), calls=%async_computation.4 | async-start | bytes 262144 | tf_op jit(solution)/shard_map/all_to_all | solution.py:337
  120.3 0.1 collective-permute-start.3
  120.5 0.7 copy.26
  121.2 1.6 all_gather_reshape.3
  122.8 5.0 %all-to-all-done.4 = bf16[16,16,256]{2,1,0:T(8,128)(2,1)S(1)} async-done(((bf16[16,16,256]{2,1,0:T(8,128)(2,1)}), bf16[16,16,256]{2,1,0:T(8,128)(2,1)S(1)}, u32[]{:S(2)}, u32[]{:S(2)}) %all-to-all-start.4) | async-done | bytes 131104 | tf_op jit(solution)/shard_map/all_to_all | solution.py:337
  127.9 12.7 %all_to_all.55 = bf16[8,16,384]{2,1,0:T(8,128)(2,1)S(1)} all-to-all(bf16[8,16,384]{2,1,0:T(8,128)(2,1)S(1)} %fusion.3), channel_id=1, replica_groups=mesh['gx'=8,'gz'=16,'core'=2] {'gx'}, dimensions={0} | all-to-all | bytes 196608 | tf_op jit(solution)/shard_map/all_to_all | solution.py:337
  140.6 1.6 shard_map.87
  142.1 3.6 %all-to-all-start.6 = ((bf16[16,8,3136]{2,1,0:T(8,128)(2,1)}), bf16[16,8,3136]{2,1,0:T(8,128)(2,1)S(1)}, u32[]{:S(2)}, u32[]{:S(2)}) async-start(bf16[16,8,3136]{2,1,0:T(8,128)(2,1)} %bitcast.11), calls=%async_computation.6 | async-start | bytes 1638400 | tf_op jit(solution)/shard_map/all_to_all | solution.py:337
  145.8 0.4 collective-permute-start.4
  146.1 14.6 %collective-permute-done.4.refs_3_ = bf16[288,512]{1,0:T(8,128)(2,1)S(1)} collective-permute-done((bf16[288,512]{1,0:T(8,128)(2,1)}, bf16[288,512]{1,0:T(8,128)(2,1)S(1)}, u32[]{:S(2)}, u32[]{:S(2)}) %collective-permute-start.4) | collective-permute-done | bytes 294944 | tf_op jit(solution)/shard_map/ppermute | solution.py:377
  160.8 17.4 %collective-permute-done.5.refs_4_ = bf16[288,512]{1,0:T(8,128)(2,1)S(1)} collective-permute-done((bf16[288,512]{1,0:T(8,128)(2,1)S(1)}, bf16[288,512]{1,0:T(8,128)(2,1)S(1)}, u32[]{:S(2)}, u32[]{:S(2)}) %collective-permute-start.5) | collective-permute-done | bytes 294944 | tf_op jit(solution)/shard_map/ppermute | solution.py:377
  178.3 10.5 %collective-permute-done.6.refs_5_ = bf16[288,512]{1,0:T(8,128)(2,1)S(1)} collective-permute-done((bf16[288,512]{1,0:T(8,128)(2,1)S(1)}, bf16[288,512]{1,0:T(8,128)(2,1)S(1)}, u32[]{:S(2)}, u32[]{:S(2)}) %collective-permute-start.6) | collective-permute-done | bytes 294944 | tf_op jit(solution)/shard_map/ppermute | solution.py:377
  188.8 1.3 shard_map.90
  190.1 2.5 collective-permute-start.10
  192.6 5.9 %collective-permute-done.7.refs_6_ = bf16[288,512]{1,0:T(8,128)(2,1)} collective-permute-done((bf16[288,512]{1,0:T(8,128)(2,1)S(1)}, bf16[288,512]{1,0:T(8,128)(2,1)}, u32[]{:S(2)}, u32[]{:S(2)}) %collective-permute-start.7) | collective-permute-done | bytes 294944 | tf_op jit(solution)/shard_map/ppermute | solution.py:377
  198.5 0.1 fusion.20.spread_ref
  198.7 1.0 slice.34.slope_ref
  199.8 0.1 reshape.83
  199.9 0.9 shard_map.88
  200.8 6.5 %all-to-all-start.7 = ((bf16[8,64,128]{2,1,0:T(8,128)(2,1)}), bf16[8,64,128]{2,1,0:T(8,128)(2,1)S(1)}, u32[]{:S(2)}, u32[]{:S(2)}) async-start(bf16[8,64,128]{2,1,0:T(8,128)(2,1)} %shard_map.88), calls=%async_computation.7 | async-start | bytes 262144 | tf_op jit(solution)/shard_map/all_to_all | solution.py:337
  207.3 1.5 fusion.25
  208.8 0.8 slice.48
  209.6 4.0 %collective-permute-start.9 = (f32[16,4096]{1,0:T(8,128)}, f32[16,4096]{1,0:T(8,128)}, u32[]{:S(2)}, u32[]{:S(2)}) collective-permute-start(f32[16,4096]{1,0:T(8,128)} %slice.48), channel_id=1, source_target_pairs={{0,1},{1,0},{2,3},{3,2},{4,5},{5,4},{6,7},{7,6},{8,9},{9,8},{10,11... | collective-permute-start | bytes 786440 | tf_op jit(solution)/shard_map/ppermute | solution.py:432
  213.6 0.7 all-to-all-done.7.dfeat_ref
  214.3 4.1 %shard_map.89 = bf16[32,72,128]{2,1,0:T(8,128)(2,1)} custom-call(s32[1]{0:T(128)} %bitcast.me_ref, bf16[8,64,256]{2,1,0:T(8,128)(2,1)S(1)} %slice.34.slope_ref, bf16[8,64,128]{2,1,0:T(8,128)(2,1)S(1)} %all-to-all-done.7.dfeat_ref, bf16[64,256]{1,0:T(8,128)(2,1)S(1)} %fusion.20.spread_ref, bf16[288,512]{1,0:T(8,128)(2,1)S(1)} %bitcast.40, ...), custom_call_target="tpu_custom_call" | custom-call | flops 1207959552 | bytes 2359296 | tf_op jit(solution)/shard_map/pallas_call | solution.py:269
  218.3 11.2 %all-to-all-start.8 = ((bf16[32,72,128]{2,1,0:T(8,128)(2,1)}), bf16[32,72,128]{2,1,0:T(8,128)(2,1)S(1)}, u32[]{:S(2)}, u32[]{:S(2)}) async-start(bf16[32,72,128]{2,1,0:T(8,128)(2,1)} %shard_map.89), calls=%async_computation.8 | async-start | bytes 1179648 | tf_op jit(solution)/shard_map/all_to_all | solution.py:337
  229.6 2.7 %shard_map.91 = f32[3136,128]{1,0:T(8,128)} custom-call(s32[1]{0:T(128)} %bitcast.16.which_ref, bf16[128,3136]{1,0:T(8,128)(2,1)S(1)} %bitcast.37, bf16[128,256]{1,0:T(8,128)(2,1)S(1)} %bitcast.45, bf16[3136,128]{1,0:T(8,128)(2,1)} %collective-permute-done.10.more_ref), custom_call_target="tpu_custom_call" | custom-call | flops 102760448 | bytes 1605632 | tf_op jit(solution)/shard_map/pallas_call | solution.py:188
  232.3 0.1 slice.51
  232.4 0.1 convert_element_type.47
  232.5 0.2 shard_map.92
  232.8 2.3 copy-done.1
  235.1 3.5 %shard_map.93 = f32[1,14,14,512]{3,2,1,0:T(8,128)S(1)} custom-call(bf16[288,512]{1,0:T(8,128)(2,1)S(1)} %bitcast.42, bf16[4608,512]{1,0:T(8,128)(2,1)S(1)} %copy-done.1), custom_call_target="tpu_custom_call" | custom-call | flops 1056964608 | bytes 4718592 | tf_op jit(solution)/shard_map/pallas_call | solution.py:310
  238.7 1.2 copy.29
  239.8 1.7 fusion
  241.5 5.8 %all-to-all-done.8 = bf16[32,72,128]{2,1,0:T(8,128)(2,1)S(1)} async-done(((bf16[32,72,128]{2,1,0:T(8,128)(2,1)}), bf16[32,72,128]{2,1,0:T(8,128)(2,1)S(1)}, u32[]{:S(2)}, u32[]{:S(2)}) %all-to-all-start.8) | async-done | bytes 589856 | tf_op jit(solution)/shard_map/all_to_all | solution.py:337
  247.5 0.7 copy.28
  (60 shorter events, 0.8 us)
Async XLA Ops:
  7.2 32.5 %collective-permute-start = (bf16[3136,128]{1,0:T(8,128)(2,1)}, bf16[3136,128]{1,0:T(8,128)(2,1)S(1)}, u32[]{:S(2)}, u32[]{:S(2)}) collective-permute-start(bf16[3136,128]{1,0:T(8,128)(2,1)} %param.7), channel_id=1, source_target_pairs={{0,1},{1,0},{2,3},{3,2},{4,5},{5,4},{6,7},{7,6},{8,9},{9,8},{10,11... | collective-permute-start | bytes 2408456 | tf_op jit(solution)/shard_map/ppermute | solution.py:373
  11.5 2.3 copy-start
  16.1 22.6 %copy-start.8 = (bf16[4096,16]{0,1:T(8,128)(2,1)S(1)}, bf16[4096,16]{0,1:T(8,128)(2,1)}, u32[]{:S(2)}) copy-start(bf16[4096,16]{0,1:T(8,128)(2,1)} %param.8) | copy-start | bytes 393220
  16.2 22.6 %copy-start.9 = (bf16[256,16]{0,1:T(8,128)(2,1)S(1)}, bf16[256,16]{0,1:T(8,128)(2,1)}, u32[]{:S(2)}) copy-start(bf16[256,16]{0,1:T(8,128)(2,1)} %param.9) | copy-start | bytes 24580
  30.2 9.5 %copy-start.7 = (bf16[3136,128]{1,0:T(8,128)(2,1)S(1)}, bf16[3136,128]{1,0:T(8,128)(2,1)}, u32[]{:S(2)}) copy-start(bf16[3136,128]{1,0:T(8,128)(2,1)} %param.7) | copy-start | bytes 2408452
  30.2 27.4 %all-to-all-start.1 = ((bf16[16,8,3136]{2,1,0:T(8,128)(2,1)}), bf16[16,8,3136]{2,1,0:T(8,128)(2,1)S(1)}, u32[]{:S(2)}, u32[]{:S(2)}) async-start(bf16[16,8,3136]{2,1,0:T(8,128)(2,1)} %broadcast_in_dim.11), calls=%async_computation.1 | async-start | bytes 1638400 | tf_op jit(solution)/shard_map/all_to_all | solution.py:337
  38.7 54.1 %all-gather.6.cloned.1.call-start = ((), (), s32[]{:S(2)}) async-start(), calls=%async_computation.10 | async-start | bytes 1253376 | tf_op jit(solution)/shard_map/all_gather | solution.py:370
  92.8 19.1 %collective-permute-start.1 = (bf16[128,4352]{1,0:T(8,128)(2,1)}, bf16[128,4352]{1,0:T(8,128)(2,1)}, u32[]{:S(2)}, u32[]{:S(2)}) collective-permute-start(bf16[128,4352]{1,0:T(8,128)(2,1)} %all-gather.6.cloned.1.call-done.own_ref), channel_id=1, source_target_pairs={{0,1},{1,0},{2,3},{3,2},{4,5},{5,4},{6,7},{7,6},{8,9},{9,8},{10,11... | collective-permute-start | bytes 3342344 | tf_op jit(solution)/shard_map/ppermute | solution.py:390
  95.2 25.1 %collective-permute-start.2 = (bf16[288,512]{1,0:T(8,128)(2,1)S(1)}, bf16[288,512]{1,0:T(8,128)(2,1)}, u32[]{:S(2)}, u32[]{:S(2)}) collective-permute-start(bf16[288,512]{1,0:T(8,128)(2,1)S(1)} %bitcast.39), channel_id=1, source_target_pairs={{0,32},{32,64},{64,96},{96,128},{128,160},{160,192},{192,224},{224... | collective-permute-start | bytes 884744 | tf_op jit(solution)/shard_map/ppermute | solution.py:377
  97.7 14.3 %all-to-all-start.3 = ((bf16[16,16,256]{2,1,0:T(8,128)(2,1)}), bf16[16,16,256]{2,1,0:T(8,128)(2,1)S(1)}, u32[]{:S(2)}, u32[]{:S(2)}) async-start(bf16[16,16,256]{2,1,0:T(8,128)(2,1)} %broadcast_in_dim.12), calls=%async_computation.3 | async-start | bytes 262144 | tf_op jit(solution)/shard_map/all_to_all | solution.py:337
  112.0 1.2 copy-start.2
  116.2 11.5 %all-to-all-start.4 = ((bf16[16,16,256]{2,1,0:T(8,128)(2,1)}), bf16[16,16,256]{2,1,0:T(8,128)(2,1)S(1)}, u32[]{:S(2)}, u32[]{:S(2)}) async-start(bf16[16,16,256]{2,1,0:T(8,128)(2,1)} %get-tuple-element.24), calls=%async_computation.4 | async-start | bytes 262144 | tf_op jit(solution)/shard_map/all_to_all | solution.py:337
  120.3 79.7 %all-gather.4.cloned.1.call-start = ((), (), s32[]{:S(2)}) async-start(), calls=%async_computation.9 | async-start | bytes 1179648 | tf_op jit(solution)/shard_map/all_gather | solution.py:401
  120.3 25.4 %collective-permute-start.3 = (bf16[288,512]{1,0:T(8,128)(2,1)}, bf16[288,512]{1,0:T(8,128)(2,1)}, u32[]{:S(2)}, u32[]{:S(2)}) collective-permute-start(bf16[288,512]{1,0:T(8,128)(2,1)} %collective-permute-done.2.refs_1_), channel_id=1, source_target_pairs={{0,32},{32,64},{64,96},{96,128},{128,160},{160,192},{192,224},{224... | collective-permute-start | bytes 884744 | tf_op jit(solution)/shard_map/ppermute | solution.py:377
  142.1 57.8 %all-to-all-start.6 = ((bf16[16,8,3136]{2,1,0:T(8,128)(2,1)}), bf16[16,8,3136]{2,1,0:T(8,128)(2,1)S(1)}, u32[]{:S(2)}, u32[]{:S(2)}) async-start(bf16[16,8,3136]{2,1,0:T(8,128)(2,1)} %bitcast.11), calls=%async_computation.6 | async-start | bytes 1638400 | tf_op jit(solution)/shard_map/all_to_all | solution.py:337
  145.8 15.0 %collective-permute-start.4 = (bf16[288,512]{1,0:T(8,128)(2,1)}, bf16[288,512]{1,0:T(8,128)(2,1)S(1)}, u32[]{:S(2)}, u32[]{:S(2)}) collective-permute-start(bf16[288,512]{1,0:T(8,128)(2,1)} %collective-permute-done.3.refs_2_), channel_id=1, source_target_pairs={{0,32},{32,64},{64,96},{96,128},{128,160},{160,192},{192,224},{224... | collective-permute-start | bytes 884744 | tf_op jit(solution)/shard_map/ppermute | solution.py:377
  160.8 17.4 %collective-permute-start.5 = (bf16[288,512]{1,0:T(8,128)(2,1)S(1)}, bf16[288,512]{1,0:T(8,128)(2,1)S(1)}, u32[]{:S(2)}, u32[]{:S(2)}) collective-permute-start(bf16[288,512]{1,0:T(8,128)(2,1)S(1)} %collective-permute-done.4.refs_3_), channel_id=1, source_target_pairs={{0,32},{32,64},{64,96},{96,128},{128,160},{160,192},{192,224},{224... | collective-permute-start | bytes 884744 | tf_op jit(solution)/shard_map/ppermute | solution.py:377
  178.2 10.6 %collective-permute-start.6 = (bf16[288,512]{1,0:T(8,128)(2,1)S(1)}, bf16[288,512]{1,0:T(8,128)(2,1)S(1)}, u32[]{:S(2)}, u32[]{:S(2)}) collective-permute-start(bf16[288,512]{1,0:T(8,128)(2,1)S(1)} %collective-permute-done.5.refs_4_), channel_id=1, source_target_pairs={{0,32},{32,64},{64,96},{96,128},{128,160},{160,192},{192,224},{224... | collective-permute-start | bytes 884744 | tf_op jit(solution)/shard_map/ppermute | solution.py:377
  188.8 9.7 %copy-start.3 = (bf16[288,512]{1,0:T(8,128)(2,1)}, bf16[288,512]{1,0:T(8,128)(2,1)S(1)}, u32[]{:S(2)}) copy-start(bf16[288,512]{1,0:T(8,128)(2,1)S(1)} %collective-permute-done.6.refs_5_) | copy-start | bytes 884740
  188.8 9.7 %collective-permute-start.7 = (bf16[288,512]{1,0:T(8,128)(2,1)S(1)}, bf16[288,512]{1,0:T(8,128)(2,1)}, u32[]{:S(2)}, u32[]{:S(2)}) collective-permute-start(bf16[288,512]{1,0:T(8,128)(2,1)S(1)} %collective-permute-done.6.refs_5_), channel_id=1, source_target_pairs={{0,32},{32,64},{64,96},{96,128},{128,160},{160,192},{192,224},{224... | collective-permute-start | bytes 884744 | tf_op jit(solution)/shard_map/ppermute | solution.py:377
  190.1 39.5 %collective-permute-start.10 = (bf16[3136,128]{1,0:T(8,128)(2,1)}, bf16[3136,128]{1,0:T(8,128)(2,1)}, u32[]{:S(2)}, u32[]{:S(2)}) collective-permute-start(bf16[3136,128]{1,0:T(8,128)(2,1)} %shard_map.90), channel_id=1, source_target_pairs={{0,1},{1,0},{2,3},{3,2},{4,5},{5,4},{6,7},{7,6},{8,9},{9,8},{10,11... | collective-permute-start | bytes 2408456 | tf_op jit(solution)/shard_map/ppermute | solution.py:419
  198.5 15.1 %collective-permute-start.8 = (bf16[288,512]{1,0:T(8,128)(2,1)}, bf16[288,512]{1,0:T(8,128)(2,1)}, u32[]{:S(2)}, u32[]{:S(2)}) collective-permute-start(bf16[288,512]{1,0:T(8,128)(2,1)} %collective-permute-done.7.refs_6_), channel_id=1, source_target_pairs={{0,32},{32,64},{64,96},{96,128},{128,160},{160,192},{192,224},{224... | collective-permute-start | bytes 884744 | tf_op jit(solution)/shard_map/ppermute | solution.py:377
  200.8 13.4 %copy-start.4 = (bf16[288,512]{1,0:T(8,128)(2,1)S(1)}, bf16[288,512]{1,0:T(8,128)(2,1)}, u32[]{:S(2)}) copy-start(bf16[288,512]{1,0:T(8,128)(2,1)} %copy-done.3) | copy-start | bytes 884740
  200.8 13.4 %all-to-all-start.7 = ((bf16[8,64,128]{2,1,0:T(8,128)(2,1)}), bf16[8,64,128]{2,1,0:T(8,128)(2,1)S(1)}, u32[]{:S(2)}, u32[]{:S(2)}) async-start(bf16[8,64,128]{2,1,0:T(8,128)(2,1)} %shard_map.88), calls=%async_computation.7 | async-start | bytes 262144 | tf_op jit(solution)/shard_map/all_to_all | solution.py:337
  208.8 4.8 %copy-start.5 = (f32[32,4096]{1,0:T(8,128)}, f32[32,4096]{1,0:T(8,128)S(1)}, u32[]{:S(2)}) copy-start(f32[32,4096]{1,0:T(8,128)S(1)} %fusion.25) | copy-start | bytes 1572868
  209.6 30.2 %collective-permute-start.9 = (f32[16,4096]{1,0:T(8,128)}, f32[16,4096]{1,0:T(8,128)}, u32[]{:S(2)}, u32[]{:S(2)}) collective-permute-start(f32[16,4096]{1,0:T(8,128)} %slice.48), channel_id=1, source_target_pairs={{0,1},{1,0},{2,3},{3,2},{4,5},{5,4},{6,7},{7,6},{8,9},{9,8},{10,11... | collective-permute-start | bytes 786440 | tf_op jit(solution)/shard_map/ppermute | solution.py:432
  218.3 29.0 %all-to-all-start.8 = ((bf16[32,72,128]{2,1,0:T(8,128)(2,1)}), bf16[32,72,128]{2,1,0:T(8,128)(2,1)S(1)}, u32[]{:S(2)}, u32[]{:S(2)}) async-start(bf16[32,72,128]{2,1,0:T(8,128)(2,1)} %shard_map.89), calls=%async_computation.8 | async-start | bytes 1179648 | tf_op jit(solution)/shard_map/all_to_all | solution.py:337
  232.8 2.3 copy-start.1
  235.1 4.7 %copy-start.6 = (f32[32,4096]{1,0:T(8,128)S(1)}, f32[32,4096]{1,0:T(8,128)}, u32[]{:S(2)}) copy-start(f32[32,4096]{1,0:T(8,128)} %copy-done.5) | copy-start | bytes 1572868
Sparse Core Ops, SparseCore 0:
  42.7 50.0 all-gather.5
  123.8 57.2 all-gather.3

commit v6 on v4

--- a/solution.py
+++ b/solution.py
@@ -127,25 +127,32 @@
 
 def fc7_kernel(known_ref, hidden_ref, pick_ref, seven_ref, terms_ref):
     count, mine, wide = hidden_ref.shape
-    rows7 = count // 2 * wide
-    y7_pre = jnp.zeros(seven_ref.shape, F32)
-    for g in range(count // 2):
-        block = hidden_ref[2 * g : 2 * g + 2].reshape(2 * mine, wide)
-        y7_pre += dot(known_ref[:, g * wide : (g + 1) * wide], block, ((1,), (1,)))
-    cot = dot(known_ref[:, rows7:], pick_ref[...], ((1,), (0,)))
-    seven = (cot * slope(y7_pre)).astype(BF)
-    seven_ref[...] = seven
-    for g in range(count // 2):
-        part = dot(seven, known_ref[:, g * wide : (g + 1) * wide], ((0,), (0,)))
-        terms_ref[2 * g : 2 * g + 2] = part.astype(BF).reshape(2, mine, wide)
+    lines, both, _ = known_ref.shape
+    rows7, cols7 = count * wide, both // 2
+
+    def weight(k, start, size):
+        block = known_ref[:, k * cols7 : (k + 1) * cols7, start : start + size]
+        return block.reshape(lines * cols7, size)
+
+    sevens = []
+    for k in range(2):
+        y7_pre = jnp.zeros((lines * cols7, mine), F32)
+        for g in range(count):
+            y7_pre += dot(weight(k, g * wide, wide), hidden_ref[g], ((1,), (1,)))
+        cot = dot(weight(k, rows7, pick_ref.shape[0]), pick_ref[...], ((1,), (0,)))
+        sevens.append((cot * slope(y7_pre)).astype(BF))
+        seven_ref[:, k * mine : (k + 1) * mine] = sevens[k]
+    for g in range(count):
+        parts = [dot(sevens[k], weight(k, g * wide, wide), ((0,), (0,))) for k in range(2)]
+        terms_ref[g] = (parts[0] + parts[1]).astype(BF)
 
 
 def fc7_step(known, hidden, pick):
-    cols = known.shape[0]
+    lines, both, _ = known.shape
     return pl.pallas_call(
         fc7_kernel,
         out_shape=[
-            jax.ShapeDtypeStruct((cols, pick.shape[1]), BF),
+            jax.ShapeDtypeStruct((lines * both // 2, 2 * pick.shape[1]), BF),
             jax.ShapeDtypeStruct(hidden.shape, BF),
         ],
         compiler_params=VMEM,
@@ -344,6 +351,8 @@
     ny = nz * nc
     near = nz // nx
     gy = ("gz", "core")
+    rise = [(k, (k + 1) % nx) for k in range(nx)]
+    fall = [(k, (k - 1) % nx) for k in range(nx)]
     pair = [(k, nc - 1 - k) for k in range(nc)]
 
     def on_device(images, conv_weight, fc6_weight, fc7_weight, cotangent):
@@ -358,10 +367,11 @@
         part = chans // nx
         cols = 2 * LANES
         me, core = lax.axis_index("gx"), lax.axis_index("core")
-
-        known = lax.all_gather(
-            jnp.concatenate([fc7_weight.T, cotangent.T], axis=1), "gx", axis=0, tiled=False
-        )
+        me_word = me.reshape(1).astype(jnp.int32)
+
+        known = jnp.concatenate([fc7_weight.T, cotangent.T], axis=1)
+        known = jnp.concatenate([known, lax.ppermute(known, "core", pair)], axis=0)
+        known = lax.all_gather(known, "gx", axis=0, tiled=False)
         gathered = lax.all_gather(images[0], "gx", axis=0, tiled=False)
         other6 = lax.ppermute(fc6_weight, "core", pair)
         lines = bordered(images[0])
@@ -379,28 +389,39 @@
         h6_pre = both[:, :mine].astype(F32).sum(axis=0)
         slopes = both[:, mine:]
         own_hidden = activate(h6_pre).astype(BF)
-        hidden = share(own_hidden, gy, ny)
-
-        place = lax.broadcasted_iota(jnp.int32, (total, nc * mine), 1)
-        half_of, rest = place // mine, place % mine
-        source = (rest % nx) * ny + (me * near + rest // nx) * nc + half_of
-        pick = (lax.broadcasted_iota(jnp.int32, (total, nc * mine), 0) == source).astype(BF)
-        g_seven, dh6_terms = fc7_step(known.reshape(nx * cols7, rows7 + total), hidden, pick)
-        grad_hidden = swap(dh6_terms, gy).astype(F32).sum(axis=0)
+        hidden = share(own_hidden, "gz", nz)
+
+        place = lax.broadcasted_iota(jnp.int32, (total, mine), 1)
+        source = (place % nx) * ny + (me * near + place // nx) * nc + core
+        pick = (lax.broadcasted_iota(jnp.int32, (total, mine), 0) == source).astype(BF)
+        g_seven, dh6_terms = fc7_step(known, hidden, pick)
+        hidden = hidden.transpose(1, 0, 2).reshape(mine, rows7)
+        up = [hidden, lax.ppermute(hidden, "gx", rise)]
+        down = [hidden, lax.ppermute(hidden, "gx", fall)]
+        dh6_terms = swap(dh6_terms, "gz")
+        dh6_terms, up[1], down[1] = lax.optimization_barrier((dh6_terms, up[1], down[1]))
+        grad_hidden = dh6_terms.astype(F32).sum(axis=0)
         own_six = (grad_hidden * slope(h6_pre)).astype(BF)
 
         columns = g_seven.reshape(nx, cols7, nc * mine)
         columns = jnp.pad(columns, ((0, 0), (0, mine - cols7), (0, LANES - nc * mine)))
         both = jnp.concatenate([jnp.broadcast_to(own_six, (nx, mine, wide)), columns], axis=2)
         both = swap(both, "gx")
+        up.append(lax.ppermute(up[1], "gx", rise))
+        down.append(lax.ppermute(down[1], "gx", fall))
+        both, up[2], down[2] = lax.optimization_barrier((both, up[2], down[2]))
         g_six = both[:, :, :wide].reshape(group, wide)
         columns = both[:, :cols7, wide : wide + nc * mine]
 
         feat_terms = features_back(g_six, weight6).reshape(nz, nx, feats)
         feat_terms, g_six = lax.optimization_barrier((feat_terms, g_six))
         feat_terms = swap(feat_terms, "gz")
+        up.append(lax.ppermute(up[2], "gx", rise))
+        down.append(lax.ppermute(down[2], "gx", fall))
+        up.append(lax.ppermute(up[3], "gx", rise))
+        feat_terms, up[3], down[3] = lax.optimization_barrier((feat_terms, up[3], down[3]))
         sent6 = weight_terms(nc - 1 - core, inputs, g_six, units)
-        packs = pack_dfeat(me.reshape(1).astype(jnp.int32), feat_terms)
+        packs = pack_dfeat(me_word, feat_terms)
         packs = swap(packs, "gx")
         gathered, sent6 = lax.optimization_barrier((gathered, sent6))
         all_lines = jax.vmap(bordered)(gathered)
@@ -415,10 +436,11 @@
         g_lines = conv_slope(conv_pre, dfeat).reshape(side, LINE, chans)[:, :side]
         grad_images = conv_backward(bordered(g_lines), conv_weight, side)
 
-        hidden = hidden.reshape(nz, nc * mine, wide).transpose(1, 0, 2).reshape(nc * mine, rows7)
-        all_hidden = lax.all_gather(hidden, "gx", axis=0, tiled=False).reshape(total, rows7)
-        columns = columns.transpose(1, 0, 2).reshape(cols7, total)
-        grad_fc7 = dot(columns, all_hidden, ((1,), (0,))).T
+        all_hidden = jnp.concatenate([down[k] for k in range(nx // 2)] + up[nx // 2 : 0 : -1], axis=0)
+        columns = lax.dynamic_slice_in_dim(jnp.concatenate([columns, columns]), me, nx)
+        columns = columns.reshape(nx, cols7, nc, mine).transpose(2, 1, 0, 3).reshape(nc * cols7, group)
+        terms7 = dot(columns, all_hidden, ((1,), (0,)))
+        grad_fc7 = (terms7[:cols7] + lax.ppermute(terms7[cols7:], "core", pair)).T
         packed, grad_fc7 = lax.optimization_barrier((packed, grad_fc7))
         packed = packed.astype(F32).sum(axis=0)
         grad_conv = jnp.concatenate([packed[:, :part], packed[:, part:]], axis=0)

time: 207 us -> 218 us (1.053)
  starting transfers between devices: 50.5 us -> 75.5 us
  blocking collectives: 21.6 us -> 0 us
  local copies, waits for them, and re-layouts: 19.8 us -> 28.2 us
  waiting for transfers between devices: 76.6 us -> 72.4 us
  other arithmetic: 5.05 us -> 7.8 us
    all_to_all x2 -> x0, blocking collectives: 21.6 us -> none  [swap(): return lax.all_to_all(value, axis, 0, 0, tiled=True)]
    ppermute x0 -> x9, starting transfers between devices: none -> 20.3 us  [the longest x1 5.07 us: on_device(): down.append(lax.ppermute(down[1], 'gx', fall))]
    all_gather x2 -> x1, waiting for transfers between devices: 11.3 us -> 0.01 us  [on_device(): known = lax.all_gather(known, 'gx', axis=0, tiled=False)]
    ppermute x0 -> x9, waiting for transfers between devices: none -> 11.2 us  [the longest x1 7.28 us: on_device(): up.append(lax.ppermute(up[3], 'gx', rise))]
    all_to_all x7 -> x9, starting transfers between devices: 41.7 us -> 52.1 us  [swap(): return lax.all_to_all(value, axis, 0, 0, tiled=True)]
    all_to_all x7 -> x9, waiting for transfers between devices: 64.6 us -> 55.1 us  [swap(): return lax.all_to_all(value, axis, 0, 0, tiled=True)]
    unnamed x19 -> x28, local copies, waits for them, and re-layouts: 9.72 us -> 19 us
    all_gather x1, waiting for transfers between devices: 0.02 us -> 5.37 us  [on_device(): gathered = lax.all_gather(images[0], 'gx', axis=0, tiled=False)]
  transfers between devices with their start and end apart: 12 -> 22, of which waited for: 6 -> 12; matrix products, arithmetic and copies ran while one was open for 8% -> 12% of each run, Pallas kernels for 7% -> 8%
where the time goes in v6:
time: 218 us; the launch traced here: 217 us
  starting transfers between devices  75.5 us (35%)
  waiting for transfers between devices  72.4 us (33%)
  local copies, waits for them, and re-layouts  28.2 us (13%)
  Pallas kernels  16.3 us (7%)
  between operations  14.5 us (7%)
  other arithmetic  7.8 us (4%)
    all_to_all x9, waiting for transfers between devices, swap(): return lax.all_to_all(value, axis, 0, 0, tiled=True)  55.1 us
    all_to_all x9, starting transfers between devices, swap(): return lax.all_to_all(value, axis, 0, 0, tiled=True)  52.1 us
    unnamed x28, local copies, waits for them, and re-layouts  19 us
    ppermute x1, waiting for transfers between devices, on_device(): up.append(lax.ppermute(up[3], 'gx', rise))  7.28 us
    all_gather x1, waiting for transfers between devices, on_device(): gathered = lax.all_gather(images[0], 'gx', axis=0, tiled=False)  5.37 us
    ppermute x1, starting transfers between devices, on_device(): down.append(lax.ppermute(down[1], 'gx', fall))  5.07 us
    ppermute x1, starting transfers between devices, on_device(): down.append(lax.ppermute(down[2], 'gx', fall))  4.9 us
    pad x3, local copies, waits for them, and re-layouts, bordered(): padded = jnp.pad(maps, ((1, 3), (1, LINE - side - 1), (0, 0)))  4.76 us
  transfers between devices with their start and end apart: 22, of which 12 were waited for; matrix products, arithmetic and copies ran while one was open for 12% of the time, Pallas kernels for 8%

profile of v6, /device:TPU:1, one launch (start us, length us, event | category | flops | bytes accessed | tf_op | source)
XLA Modules:
  0.0 216.5 jit_solution(15386667463664020054)
XLA Ops:
  7.2 0.9 pad_maximum_fusion.3
  8.1 3.3 %collective-permute-start.1 = (bf16[16,4352]{1,0:T(8,128)(2,1)S(1)}, bf16[16,4352]{1,0:T(8,128)(2,1)S(1)}, u32[]{:S(2)}, u32[]{:S(2)}) collective-permute-start(bf16[16,4352]{1,0:T(8,128)(2,1)S(1)} %pad_maximum_fusion.3), channel_id=1, source_target_pairs={{0,1},{1,0},{2,3},{3,2},{4,5},{5,4},{6,7},{7,6},{8,9},{9,8},{10,11... | collective-permute-start | bytes 417800 | tf_op jit(solution)/shard_map/ppermute | solution.py:373
  11.5 1.0 collective-permute-done.1
  12.5 1.7 pad_maximum_fusion.2
  14.6 1.0 pad.20
  15.6 2.3 %copy-done = bf16[4608,512]{1,0:T(8,128)(2,1)S(1)} copy-done((bf16[4608,512]{1,0:T(8,128)(2,1)S(1)}, bf16[4608,512]{1,0:T(8,128)(2,1)}, u32[]{:S(2)}) %copy-start) | copy-done | bytes 4718616
  18.0 2.2 %shard_map.84 = (f32[224,512]{1,0:T(8,128)S(1)}, bf16[56,512]{1,0:T(8,128)(2,1)S(1)}) custom-call(bf16[288,512]{1,0:T(8,128)(2,1)S(1)} %bitcast.43, bf16[4608,512]{1,0:T(8,128)(2,1)S(1)} %copy-done), custom_call_target="tpu_custom_call" | custom-call | flops 1056964608 | bytes 4718592 | tf_op jit(solution)/shard_map/pallas_call | solution.py:66
  20.3 0.5 broadcast.165
  20.8 0.9 reduce
  21.7 0.7 reshape.93
  22.5 4.9 %all-to-all-start = ((bf16[8,2,1568]{2,1,0:T(2,128)(2,1)}), bf16[8,2,1568]{2,1,0:T(2,128)(2,1)S(1)}, u32[]{:S(2)}, u32[]{:S(2)}) async-start(bf16[8,2,1568]{2,1,0:T(2,128)(2,1)} %reshape.93), calls=%async_computation | async-start | bytes 106496 | tf_op jit(solution)/shard_map/all_to_all | solution.py:337
  27.4 0.7 all-gather.4.cloned.1.call-update
  28.1 5.9 %all-to-all-done = bf16[8,2,1568]{2,1,0:T(2,128)(2,1)S(1)} async-done(((bf16[8,2,1568]{2,1,0:T(2,128)(2,1)}), bf16[8,2,1568]{2,1,0:T(2,128)(2,1)S(1)}, u32[]{:S(2)}, u32[]{:S(2)}) %all-to-all-start) | async-done | bytes 50208 | tf_op jit(solution)/shard_map/all_to_all | solution.py:337
  34.2 0.9 broadcast_in_dim.11
  35.1 8.3 %all-to-all-start.1 = ((bf16[16,8,3136]{2,1,0:T(8,128)(2,1)}), bf16[16,8,3136]{2,1,0:T(8,128)(2,1)S(1)}, u32[]{:S(2)}, u32[]{:S(2)}) async-start(bf16[16,8,3136]{2,1,0:T(8,128)(2,1)} %broadcast_in_dim.11), calls=%async_computation.1 | async-start | bytes 1638400 | tf_op jit(solution)/shard_map/all_to_all | solution.py:337
  44.0 18.3 %all-to-all-done.1 = bf16[16,8,3136]{2,1,0:T(8,128)(2,1)S(1)} async-done(((bf16[16,8,3136]{2,1,0:T(8,128)(2,1)}), bf16[16,8,3136]{2,1,0:T(8,128)(2,1)S(1)}, u32[]{:S(2)}, u32[]{:S(2)}) %all-to-all-start.1) | async-done | bytes 802848 | tf_op jit(solution)/shard_map/all_to_all | solution.py:337
  62.7 0.7 pad_maximum_fusion.1
  63.4 3.8 %all-to-all-start.2 = ((bf16[8,80,256]{2,1,0:T(8,128)(2,1)}), bf16[8,80,256]{2,1,0:T(8,128)(2,1)S(1)}, u32[]{:S(2)}, u32[]{:S(2)}) async-start(bf16[8,80,256]{2,1,0:T(8,128)(2,1)} %pad_maximum_fusion.1), calls=%async_computation.2 | async-start | bytes 655360 | tf_op jit(solution)/shard_map/all_to_all | solution.py:337
  67.2 7.8 %all-to-all-done.2 = bf16[8,80,256]{2,1,0:T(8,128)(2,1)S(1)} async-done(((bf16[8,80,256]{2,1,0:T(8,128)(2,1)}), bf16[8,80,256]{2,1,0:T(8,128)(2,1)S(1)}, u32[]{:S(2)}, u32[]{:S(2)}) %all-to-all-start.2) | async-done | bytes 327712 | tf_op jit(solution)/shard_map/all_to_all | solution.py:337
  75.1 0.7 broadcast_in_dim.12
  75.8 6.2 %all-to-all-start.3 = ((bf16[16,16,256]{2,1,0:T(8,128)(2,1)}), bf16[16,16,256]{2,1,0:T(8,128)(2,1)S(1)}, u32[]{:S(2)}, u32[]{:S(2)}) async-start(bf16[16,16,256]{2,1,0:T(8,128)(2,1)} %broadcast_in_dim.12), calls=%async_computation.3 | async-start | bytes 262144 | tf_op jit(solution)/shard_map/all_to_all | solution.py:337
  82.0 7.4 %all-to-all-done.3.hidden_ref = bf16[16,16,256]{2,1,0:T(8,128)(2,1)S(1)} async-done(((bf16[16,16,256]{2,1,0:T(8,128)(2,1)}), bf16[16,16,256]{2,1,0:T(8,128)(2,1)S(1)}, u32[]{:S(2)}, u32[]{:S(2)}) %all-to-all-start.3) | async-done | bytes 131104 | tf_op jit(solution)/shard_map/all_to_all | solution.py:337
  89.4 1.6 copy-done.3
  91.0 1.8 shard_map.86
  92.8 4.2 %all-to-all-start.4 = ((bf16[16,16,256]{2,1,0:T(8,128)(2,1)}), bf16[16,16,256]{2,1,0:T(8,128)(2,1)}, u32[]{:S(2)}, u32[]{:S(2)}) async-start(bf16[16,16,256]{2,1,0:T(8,128)(2,1)} %get-tuple-element.29), calls=%async_computation.4 | async-start | bytes 262144 | tf_op jit(solution)/shard_map/all_to_all | solution.py:337
  97.5 4.7 %collective-permute-start.3 = (bf16[16,4096]{1,0:T(8,128)(2,1)S(1)}, bf16[16,4096]{1,0:T(8,128)(2,1)}, u32[]{:S(2)}, u32[]{:S(2)}) collective-permute-start(bf16[16,4096]{1,0:T(8,128)(2,1)S(1)} %bitcast.57), channel_id=1, source_target_pairs={{0,224},{32,0},{64,32},{96,64},{128,96},{160,128},{192,160},{224,1... | collective-permute-start | bytes 393224 | tf_op jit(solution)/shard_map/ppermute | solution.py:400
  102.7 2.4 %collective-permute-done.2 = bf16[16,4096]{1,0:T(8,128)(2,1)} collective-permute-done((bf16[16,4096]{1,0:T(8,128)(2,1)S(1)}, bf16[16,4096]{1,0:T(8,128)(2,1)}, u32[]{:S(2)}, u32[]{:S(2)}) %collective-permute-start.2) | collective-permute-done | bytes 131104 | tf_op jit(solution)/shard_map/ppermute | solution.py:399
  105.0 5.1 %collective-permute-start.5 = (bf16[16,4096]{1,0:T(8,128)(2,1)}, bf16[16,4096]{1,0:T(8,128)(2,1)}, u32[]{:S(2)}, u32[]{:S(2)}) collective-permute-start(bf16[16,4096]{1,0:T(8,128)(2,1)} %collective-permute-done.3), channel_id=1, source_target_pairs={{0,224},{32,0},{64,32},{96,64},{128,96},{160,128},{192,160},{224,1... | collective-permute-start | bytes 393224 | tf_op jit(solution)/shard_map/ppermute | solution.py:411
  110.1 0.9 convert_reduce_fusion.1
  111.1 0.7 fusion.3
  111.7 4.1 %all-to-all-start.5 = ((bf16[8,16,384]{2,1,0:T(8,128)(2,1)}), bf16[8,16,384]{2,1,0:T(8,128)(2,1)S(1)}, u32[]{:S(2)}, u32[]{:S(2)}) async-start(bf16[8,16,384]{2,1,0:T(8,128)(2,1)} %fusion.3), calls=%async_computation.5 | async-start | bytes 196608 | tf_op jit(solution)/shard_map/all_to_all | solution.py:337
  115.8 6.8 %all-to-all-done.5 = bf16[8,16,384]{2,1,0:T(8,128)(2,1)S(1)} async-done(((bf16[8,16,384]{2,1,0:T(8,128)(2,1)}), bf16[8,16,384]{2,1,0:T(8,128)(2,1)S(1)}, u32[]{:S(2)}, u32[]{:S(2)}) %all-to-all-start.5) | async-done | bytes 98336 | tf_op jit(solution)/shard_map/all_to_all | solution.py:337
  122.7 1.6 shard_map.87
  124.3 7.0 %all-to-all-start.6 = ((bf16[16,8,3136]{2,1,0:T(8,128)(2,1)}), bf16[16,8,3136]{2,1,0:T(8,128)(2,1)S(1)}, u32[]{:S(2)}, u32[]{:S(2)}) async-start(bf16[16,8,3136]{2,1,0:T(8,128)(2,1)} %bitcast.13), calls=%async_computation.6 | async-start | bytes 1638400 | tf_op jit(solution)/shard_map/all_to_all | solution.py:337
  131.4 0.7 constant_dynamic-update-slice_fusion.7
  132.1 1.6 constant_dynamic-update-slice_fusion.6
  134.1 0.9 copy-done.4
  135.0 5.4 %all-gather.4.cloned.1.call-done = bf16[8,14,14,512]{3,2,1,0:T(8,128)(2,1)} async-done(((bf16[1,14,14,512]{3,2,1,0:T(8,128)(2,1)}), bf16[8,14,14,512]{3,2,1,0:T(8,128)(2,1)}) %all-gather.4.cloned.1.call-update) | async-done | bytes 1605648 | tf_op jit(solution)/shard_map/all_gather | solution.py:375
  140.3 2.6 %collective-permute-start.10 = (bf16[3136,128]{1,0:T(8,128)(2,1)}, bf16[3136,128]{1,0:T(8,128)(2,1)}, u32[]{:S(2)}, u32[]{:S(2)}) collective-permute-start(bf16[3136,128]{1,0:T(8,128)(2,1)} %copy-done.4), channel_id=1, source_target_pairs={{0,1},{1,0},{2,3},{3,2},{4,5},{5,4},{6,7},{7,6},{8,9},{9,8},{10,11... | collective-permute-start | bytes 2408456 | tf_op jit(solution)/shard_map/ppermute | solution.py:428
  143.1 4.9 %collective-permute-start.7 = (bf16[16,4096]{1,0:T(8,128)(2,1)}, bf16[16,4096]{1,0:T(8,128)(2,1)S(1)}, u32[]{:S(2)}, u32[]{:S(2)}) collective-permute-start(bf16[16,4096]{1,0:T(8,128)(2,1)} %collective-permute-done.5), channel_id=1, source_target_pairs={{0,224},{32,0},{64,32},{96,64},{128,96},{160,128},{192,160},{224,1... | collective-permute-start | bytes 393224 | tf_op jit(solution)/shard_map/ppermute | solution.py:420
  148.0 1.6 constant_dynamic-update-slice_fusion.5
  149.9 3.7 %pad.22 = bf16[8,18,16,512]{3,2,1,0:T(8,128)(2,1)} pad(bf16[8,14,14,512]{3,2,1,0:T(8,128)(2,1)} %all-gather.4.cloned.1.call-done, bf16[]{:T(256)} %constant.107.clone.1), padding=0_0x1_3x1_1x0_0 | pad | bytes 3964930 | tf_op jit(solution)/shard_map/vmap(jit(_pad))/pad | solution.py:346
  153.6 0.6 collective-permute-done.6
  154.3 0.7 constant_dynamic-update-slice_fusion.4
  154.9 7.3 %collective-permute-done.8 = bf16[16,4096]{1,0:T(8,128)(2,1)S(1)} collective-permute-done((bf16[16,4096]{1,0:T(8,128)(2,1)S(1)}, bf16[16,4096]{1,0:T(8,128)(2,1)S(1)}, u32[]{:S(2)}, u32[]{:S(2)}) %collective-permute-start.8) | collective-permute-done | bytes 131104 | tf_op jit(solution)/shard_map/ppermute | solution.py:421
  162.2 0.7 constant_dynamic-update-slice_fusion.3
  162.9 0.7 constant_dynamic-update-slice_fusion.2
  163.5 1.6 constant_dynamic-update-slice_fusion.1
  165.1 0.9 shard_map.89
  166.0 3.4 %all-to-all-start.7 = ((bf16[8,64,128]{2,1,0:T(8,128)(2,1)}), bf16[8,64,128]{2,1,0:T(8,128)(2,1)S(1)}, u32[]{:S(2)}, u32[]{:S(2)}) async-start(bf16[8,64,128]{2,1,0:T(8,128)(2,1)} %shard_map.89), calls=%async_computation.7 | async-start | bytes 262144 | tf_op jit(solution)/shard_map/all_to_all | solution.py:337
  169.4 1.6 constant_dynamic-update-slice_fusion
  171.0 1.5 fusion.26
  172.5 1.6 collective-permute-start.9
  174.1 2.1 all-to-all-done.7.dfeat_ref
  176.3 1.7 copy-done.2
  177.9 2.8 %shard_map.90 = bf16[32,72,128]{2,1,0:T(8,128)(2,1)} custom-call(bf16[8,288,512]{2,1,0:T(8,128)(2,1)S(1)} %bitcast.41, bf16[8,64,256]{2,1,0:T(8,128)(2,1)S(1)} %slice.46.slope_ref, bf16[8,64,128]{2,1,0:T(8,128)(2,1)S(1)} %all-to-all-done.7.dfeat_ref, bf16[64,256]{1,0:T(8,128)(2,1)S(1)} %fusion.20.spread_ref), custom_call_target="tpu_custom_call" | custom-call | flops 1207959552 | bytes 2359296 | tf_op jit(solution)/shard_map/pallas_call | solution.py:270
  180.7 10.3 %all-to-all-start.8 = ((bf16[32,72,128]{2,1,0:T(8,128)(2,1)}), bf16[32,72,128]{2,1,0:T(8,128)(2,1)S(1)}, u32[]{:S(2)}, u32[]{:S(2)}) async-start(bf16[32,72,128]{2,1,0:T(8,128)(2,1)} %shard_map.90), calls=%async_computation.8 | async-start | bytes 1179648 | tf_op jit(solution)/shard_map/all_to_all | solution.py:337
  191.0 2.7 %shard_map.91 = f32[3136,128]{1,0:T(8,128)} custom-call(s32[1]{0:T(128)} %bitcast.18.which_ref, bf16[128,3136]{1,0:T(8,128)(2,1)S(1)} %bitcast.40, bf16[128,256]{1,0:T(8,128)(2,1)S(1)} %bitcast.48, bf16[3136,128]{1,0:T(8,128)(2,1)} %collective-permute-done.10.more_ref), custom_call_target="tpu_custom_call" | custom-call | flops 102760448 | bytes 1605632 | tf_op jit(solution)/shard_map/pallas_call | solution.py:193
  194.3 2.3 %copy-done.1 = bf16[4608,512]{1,0:T(8,128)(2,1)S(1)} copy-done((bf16[4608,512]{1,0:T(8,128)(2,1)S(1)}, bf16[4608,512]{1,0:T(8,128)(2,1)}, u32[]{:S(2)}) %copy-start.1) | copy-done | bytes 4718616
  196.6 3.5 %shard_map.93 = f32[1,14,14,512]{3,2,1,0:T(8,128)S(1)} custom-call(bf16[288,512]{1,0:T(8,128)(2,1)S(1)} %bitcast.45, bf16[4608,512]{1,0:T(8,128)(2,1)S(1)} %copy-done.1), custom_call_target="tpu_custom_call" | custom-call | flops 1056964608 | bytes 4718592 | tf_op jit(solution)/shard_map/pallas_call | solution.py:310
  200.1 1.2 copy.29
  201.3 0.7 fusion
  202.0 6.8 %all-to-all-done.8 = bf16[32,72,128]{2,1,0:T(8,128)(2,1)S(1)} async-done(((bf16[32,72,128]{2,1,0:T(8,128)(2,1)}), bf16[32,72,128]{2,1,0:T(8,128)(2,1)S(1)}, u32[]{:S(2)}, u32[]{:S(2)}) %all-to-all-start.8) | async-done | bytes 589856 | tf_op jit(solution)/shard_map/all_to_all | solution.py:337
  209.0 0.7 copy.28
  (69 shorter events, 4.6 us)
Async XLA Ops:
  7.2 82.2 %all-gather.6.cloned.1.call-start = ((), (), s32[]{:S(2)}) async-start(), calls=%async_computation.10 | async-start | bytes 2506752 | tf_op jit(solution)/shard_map/all_gather | solution.py:374
  8.1 4.3 %collective-permute-start.1 = (bf16[16,4352]{1,0:T(8,128)(2,1)S(1)}, bf16[16,4352]{1,0:T(8,128)(2,1)S(1)}, u32[]{:S(2)}, u32[]{:S(2)}) collective-permute-start(bf16[16,4352]{1,0:T(8,128)(2,1)S(1)} %pad_maximum_fusion.3), channel_id=1, source_target_pairs={{0,1},{1,0},{2,3},{3,2},{4,5},{5,4},{6,7},{7,6},{8,9},{9,8},{10,11... | collective-permute-start | bytes 417800 | tf_op jit(solution)/shard_map/ppermute | solution.py:373
  14.2 29.6 %collective-permute-start = (bf16[3136,128]{1,0:T(8,128)(2,1)}, bf16[3136,128]{1,0:T(8,128)(2,1)S(1)}, u32[]{:S(2)}, u32[]{:S(2)}) collective-permute-start(bf16[3136,128]{1,0:T(8,128)(2,1)} %param.7), channel_id=1, source_target_pairs={{0,1},{1,0},{2,3},{3,2},{4,5},{5,4},{6,7},{7,6},{8,9},{9,8},{10,11... | collective-permute-start | bytes 2408456 | tf_op jit(solution)/shard_map/ppermute | solution.py:376
  15.6 2.3 %copy-start = (bf16[4608,512]{1,0:T(8,128)(2,1)S(1)}, bf16[4608,512]{1,0:T(8,128)(2,1)}, u32[]{:S(2)}) copy-start(bf16[4608,512]{1,0:T(8,128)(2,1)} %weight_ref.3) | copy-start | bytes 14155780
  22.5 11.6 %all-to-all-start = ((bf16[8,2,1568]{2,1,0:T(2,128)(2,1)}), bf16[8,2,1568]{2,1,0:T(2,128)(2,1)S(1)}, u32[]{:S(2)}, u32[]{:S(2)}) async-start(bf16[8,2,1568]{2,1,0:T(2,128)(2,1)} %reshape.93), calls=%async_computation | async-start | bytes 106496 | tf_op jit(solution)/shard_map/all_to_all | solution.py:337
  27.4 113.0 %all-gather.4.cloned.1.call-start = ((), (), s32[]{:S(2)}) async-start(), calls=%async_computation.9 | async-start | bytes 2064384 | tf_op jit(solution)/shard_map/all_gather | solution.py:375
  34.2 9.5 %copy-start.5 = (bf16[3136,128]{1,0:T(8,128)(2,1)S(1)}, bf16[3136,128]{1,0:T(8,128)(2,1)}, u32[]{:S(2)}) copy-start(bf16[3136,128]{1,0:T(8,128)(2,1)} %param.7) | copy-start | bytes 2408452
  35.1 27.2 %all-to-all-start.1 = ((bf16[16,8,3136]{2,1,0:T(8,128)(2,1)}), bf16[16,8,3136]{2,1,0:T(8,128)(2,1)S(1)}, u32[]{:S(2)}, u32[]{:S(2)}) async-start(bf16[16,8,3136]{2,1,0:T(8,128)(2,1)} %broadcast_in_dim.11), calls=%async_computation.1 | async-start | bytes 1638400 | tf_op jit(solution)/shard_map/all_to_all | solution.py:337
  63.4 11.6 %all-to-all-start.2 = ((bf16[8,80,256]{2,1,0:T(8,128)(2,1)}), bf16[8,80,256]{2,1,0:T(8,128)(2,1)S(1)}, u32[]{:S(2)}, u32[]{:S(2)}) async-start(bf16[8,80,256]{2,1,0:T(8,128)(2,1)} %pad_maximum_fusion.1), calls=%async_computation.2 | async-start | bytes 655360 | tf_op jit(solution)/shard_map/all_to_all | solution.py:337
  75.8 13.6 %all-to-all-start.3 = ((bf16[16,16,256]{2,1,0:T(8,128)(2,1)}), bf16[16,16,256]{2,1,0:T(8,128)(2,1)S(1)}, u32[]{:S(2)}, u32[]{:S(2)}) async-start(bf16[16,16,256]{2,1,0:T(8,128)(2,1)} %broadcast_in_dim.12), calls=%async_computation.3 | async-start | bytes 262144 | tf_op jit(solution)/shard_map/all_to_all | solution.py:337
  89.4 1.6 copy-start.3
  92.8 12.2 %all-to-all-start.4 = ((bf16[16,16,256]{2,1,0:T(8,128)(2,1)}), bf16[16,16,256]{2,1,0:T(8,128)(2,1)}, u32[]{:S(2)}, u32[]{:S(2)}) async-start(bf16[16,16,256]{2,1,0:T(8,128)(2,1)} %get-tuple-element.29), calls=%async_computation.4 | async-start | bytes 262144 | tf_op jit(solution)/shard_map/all_to_all | solution.py:337
  97.0 8.0 %collective-permute-start.2 = (bf16[16,4096]{1,0:T(8,128)(2,1)S(1)}, bf16[16,4096]{1,0:T(8,128)(2,1)}, u32[]{:S(2)}, u32[]{:S(2)}) collective-permute-start(bf16[16,4096]{1,0:T(8,128)(2,1)S(1)} %bitcast.56), channel_id=1, source_target_pairs={{0,32},{32,64},{64,96},{96,128},{128,160},{160,192},{192,224},{224... | collective-permute-start | bytes 393224 | tf_op jit(solution)/shard_map/ppermute | solution.py:399
  97.5 7.5 %collective-permute-start.3 = (bf16[16,4096]{1,0:T(8,128)(2,1)S(1)}, bf16[16,4096]{1,0:T(8,128)(2,1)}, u32[]{:S(2)}, u32[]{:S(2)}) collective-permute-start(bf16[16,4096]{1,0:T(8,128)(2,1)S(1)} %bitcast.57), channel_id=1, source_target_pairs={{0,224},{32,0},{64,32},{96,64},{128,96},{160,128},{192,160},{224,1... | collective-permute-start | bytes 393224 | tf_op jit(solution)/shard_map/ppermute | solution.py:400
  105.0 17.6 %collective-permute-start.4 = (bf16[16,4096]{1,0:T(8,128)(2,1)}, bf16[16,4096]{1,0:T(8,128)(2,1)}, u32[]{:S(2)}, u32[]{:S(2)}) collective-permute-start(bf16[16,4096]{1,0:T(8,128)(2,1)} %collective-permute-done.2), channel_id=1, source_target_pairs={{0,32},{32,64},{64,96},{96,128},{128,160},{160,192},{192,224},{224... | collective-permute-start | bytes 393224 | tf_op jit(solution)/shard_map/ppermute | solution.py:410
  105.0 17.6 %collective-permute-start.5 = (bf16[16,4096]{1,0:T(8,128)(2,1)}, bf16[16,4096]{1,0:T(8,128)(2,1)}, u32[]{:S(2)}, u32[]{:S(2)}) collective-permute-start(bf16[16,4096]{1,0:T(8,128)(2,1)} %collective-permute-done.3), channel_id=1, source_target_pairs={{0,224},{32,0},{64,32},{96,64},{128,96},{160,128},{192,160},{224,1... | collective-permute-start | bytes 393224 | tf_op jit(solution)/shard_map/ppermute | solution.py:411
  111.7 10.9 %all-to-all-start.5 = ((bf16[8,16,384]{2,1,0:T(8,128)(2,1)}), bf16[8,16,384]{2,1,0:T(8,128)(2,1)S(1)}, u32[]{:S(2)}, u32[]{:S(2)}) async-start(bf16[8,16,384]{2,1,0:T(8,128)(2,1)} %fusion.3), calls=%async_computation.5 | async-start | bytes 196608 | tf_op jit(solution)/shard_map/all_to_all | solution.py:337
  122.6 8.6 %copy-start.6 = (s32[64]{0:T(128)S(1)}, s32[64]{0:T(128)}, u32[]{:S(2)}) copy-start(s32[64]{0:T(128)} %get-tuple-element.86) | copy-start | bytes 772
  122.7 8.6 %copy-start.7 = (s32[64]{0:T(128)S(1)}, s32[64]{0:T(128)}, u32[]{:S(2)}) copy-start(s32[64]{0:T(128)} %get-tuple-element.87) | copy-start | bytes 772
  124.3 30.0 %all-to-all-start.6 = ((bf16[16,8,3136]{2,1,0:T(8,128)(2,1)}), bf16[16,8,3136]{2,1,0:T(8,128)(2,1)S(1)}, u32[]{:S(2)}, u32[]{:S(2)}) async-start(bf16[16,8,3136]{2,1,0:T(8,128)(2,1)} %bitcast.13), calls=%async_computation.6 | async-start | bytes 1638400 | tf_op jit(solution)/shard_map/all_to_all | solution.py:337
  134.1 0.9 copy-start.4
  140.3 50.7 %collective-permute-start.10 = (bf16[3136,128]{1,0:T(8,128)(2,1)}, bf16[3136,128]{1,0:T(8,128)(2,1)}, u32[]{:S(2)}, u32[]{:S(2)}) collective-permute-start(bf16[3136,128]{1,0:T(8,128)(2,1)} %copy-done.4), channel_id=1, source_target_pairs={{0,1},{1,0},{2,3},{3,2},{4,5},{5,4},{6,7},{7,6},{8,9},{9,8},{10,11... | collective-permute-start | bytes 2408456 | tf_op jit(solution)/shard_map/ppermute | solution.py:428
  142.9 11.3 %collective-permute-start.6 = (bf16[16,4096]{1,0:T(8,128)(2,1)}, bf16[16,4096]{1,0:T(8,128)(2,1)S(1)}, u32[]{:S(2)}, u32[]{:S(2)}) collective-permute-start(bf16[16,4096]{1,0:T(8,128)(2,1)} %collective-permute-done.4), channel_id=1, source_target_pairs={{0,32},{32,64},{64,96},{96,128},{128,160},{160,192},{192,224},{224... | collective-permute-start | bytes 393224 | tf_op jit(solution)/shard_map/ppermute | solution.py:419
  143.1 11.1 %collective-permute-start.7 = (bf16[16,4096]{1,0:T(8,128)(2,1)}, bf16[16,4096]{1,0:T(8,128)(2,1)S(1)}, u32[]{:S(2)}, u32[]{:S(2)}) collective-permute-start(bf16[16,4096]{1,0:T(8,128)(2,1)} %collective-permute-done.5), channel_id=1, source_target_pairs={{0,224},{32,0},{64,32},{96,64},{128,96},{160,128},{192,160},{224,1... | collective-permute-start | bytes 393224 | tf_op jit(solution)/shard_map/ppermute | solution.py:420
  154.2 8.0 %collective-permute-start.8 = (bf16[16,4096]{1,0:T(8,128)(2,1)S(1)}, bf16[16,4096]{1,0:T(8,128)(2,1)S(1)}, u32[]{:S(2)}, u32[]{:S(2)}) collective-permute-start(bf16[16,4096]{1,0:T(8,128)(2,1)S(1)} %collective-permute-done.6), channel_id=1, source_target_pairs={{0,32},{32,64},{64,96},{96,128},{128,160},{160,192},{192,224},{224... | collective-permute-start | bytes 393224 | tf_op jit(solution)/shard_map/ppermute | solution.py:421
  166.0 10.3 %all-to-all-start.7 = ((bf16[8,64,128]{2,1,0:T(8,128)(2,1)}), bf16[8,64,128]{2,1,0:T(8,128)(2,1)S(1)}, u32[]{:S(2)}, u32[]{:S(2)}) async-start(bf16[8,64,128]{2,1,0:T(8,128)(2,1)} %shard_map.89), calls=%async_computation.7 | async-start | bytes 262144 | tf_op jit(solution)/shard_map/all_to_all | solution.py:337
  172.5 28.8 %collective-permute-start.9 = (f32[16,4096]{1,0:T(8,128)S(1)}, f32[16,4096]{1,0:T(8,128)S(1)}, u32[]{:S(2)}, u32[]{:S(2)}) collective-permute-start(f32[16,4096]{1,0:T(8,128)S(1)} %slice.48), channel_id=1, source_target_pairs={{0,1},{1,0},{2,3},{3,2},{4,5},{5,4},{6,7},{7,6},{8,9},{9,8},{10,11... | collective-permute-start | bytes 786440 | tf_op jit(solution)/shard_map/ppermute | solution.py:443
  176.3 1.7 copy-start.2
  180.7 28.1 %all-to-all-start.8 = ((bf16[32,72,128]{2,1,0:T(8,128)(2,1)}), bf16[32,72,128]{2,1,0:T(8,128)(2,1)S(1)}, u32[]{:S(2)}, u32[]{:S(2)}) async-start(bf16[32,72,128]{2,1,0:T(8,128)(2,1)} %shard_map.90), calls=%async_computation.8 | async-start | bytes 1179648 | tf_op jit(solution)/shard_map/all_to_all | solution.py:337
  194.2 2.3 %copy-start.1 = (bf16[4608,512]{1,0:T(8,128)(2,1)S(1)}, bf16[4608,512]{1,0:T(8,128)(2,1)}, u32[]{:S(2)}) copy-start(bf16[4608,512]{1,0:T(8,128)(2,1)} %weight_ref.3) | copy-start | bytes 14155780
Sparse Core Ops, SparseCore 0:
  14.3 66.1 all-gather.5
  83.1 57.1 all-gather.3

commit v7 on v6

--- a/solution.py
+++ b/solution.py
@@ -199,7 +199,7 @@
     )(which.reshape(1).astype(jnp.int32), *operands)
 
 
-def pack_kernel(me_ref, terms_ref, out_ref, parts_ref, own_ref):
+def pack_kernel(me_ref, terms_ref, slope_ref, out_ref, parts_ref, own_ref):
     nx, rows, _ = out_ref.shape
     feats = terms_ref.shape[2]
     run = LANES // 2
@@ -218,10 +218,11 @@
     for e in range(nx):
         dest = lax.rem(me_ref[0] + e, nx)
         own = own_ref[pl.ds(pl.multiple_of(dest * rows, rows), rows), :]
-        out_ref[dest] = jnp.where(lane < run, parts_ref[e], own).astype(BF)
-
-
-def pack_dfeat(me, terms):
+        out_ref[dest, :, :LANES] = jnp.where(lane < run, parts_ref[e], own).astype(BF)
+    out_ref[:, :, LANES:] = slope_ref[...]
+
+
+def pack_dfeat(me, terms, slopes):
     _, nx, feats = terms.shape
     rows = nx * nx
     return pl.pallas_call(
@@ -229,27 +230,30 @@
         in_specs=[
             pl.BlockSpec(memory_space=pltpu.SMEM),
             pl.BlockSpec(memory_space=pltpu.VMEM),
-        ],
-        out_shape=jax.ShapeDtypeStruct((nx, rows, LANES), BF),
+            pl.BlockSpec(memory_space=pltpu.VMEM),
+        ],
+        out_shape=jax.ShapeDtypeStruct((nx, rows, LANES + slopes.shape[2]), BF),
         scratch_shapes=[
             pltpu.VMEM((nx, rows, LANES), F32),
             pltpu.VMEM((nx * rows, LANES), F32),
         ],
         compiler_params=VMEM,
         cost_estimate=cost(4 * terms.size, terms.size * 2),
-    )(me, terms)
-
-
-def kernel_kernel(lines_ref, slope_ref, dfeat_ref, spread_ref, out_ref, grad_ref, flat_ref, wide_ref):
-    images, part, cols = slope_ref.shape
+    )(me, terms, slopes)
+
+
+def kernel_kernel(high_ref, lines_ref, packs_ref, spread_ref, out_ref, grad_ref, flat_ref, wide_ref):
+    images, part, _ = packs_ref.shape
+    cols = spread_ref.shape[1]
     chans = lines_ref.shape[2]
-    wide_ref[...] = dfeat_ref[...].astype(F32).reshape(wide_ref.shape)
-    for n in range(images):
+    wide_ref[...] = packs_ref[:, :, :LANES].astype(F32).reshape(wide_ref.shape)
+    for k in range(images):
+        n = lax.rem(high_ref[0] + k % 2, 2) * (images // 2) + k // 2
         cells = wide_ref[pl.ds(n, wide_ref.shape[0] // images, images), :].astype(BF)
         spread = dot(cells, spread_ref[...], ((0,), (0,)))[:part]
-        turned = (spread * slope_ref[n].astype(F32)).astype(BF).astype(F32)
-        moved = [turned] + [pltpu.roll(turned, k, 1) for k in (1, 2)]
-        grad_ref[:, n * cols : (n + 1) * cols] = jnp.concatenate(moved, axis=0).astype(BF)
+        turned = (spread * packs_ref[n, :, LANES:].astype(F32)).astype(BF).astype(F32)
+        moved = [turned] + [pltpu.roll(turned, j, 1) for j in (1, 2)]
+        grad_ref[:, k * cols : (k + 1) * cols] = jnp.concatenate(moved, axis=0).astype(BF)
     for row in range(3):
         block = lines_ref[:, row * LINE : row * LINE + cols, :].reshape(images * cols, chans)
         term = dot(grad_ref[...], block, ((1,), (0,)))
@@ -263,21 +267,23 @@
         out_ref[dest] = jnp.concatenate(both, axis=1).astype(BF)
 
 
-def conv_kernel_grad(lines, slopes, dfeat, spread, count):
-    images, rows, chans = lines.shape
-    _, part, cols = slopes.shape
+def conv_kernel_grad(high, lines, packs, spread, count):
+    images, _, chans = lines.shape
+    _, part, _ = packs.shape
+    cols = spread.shape[1]
     size = 9 * chans // (2 * count)
     return pl.pallas_call(
         kernel_kernel,
+        in_specs=[pl.BlockSpec(memory_space=pltpu.SMEM)] + [pl.BlockSpec(memory_space=pltpu.VMEM)] * 3,
         out_shape=jax.ShapeDtypeStruct((count, size, 2 * part), BF),
         scratch_shapes=[
             pltpu.VMEM((3 * part, images * cols), BF),
             pltpu.VMEM((9 * chans, part), F32),
-            pltpu.VMEM((dfeat.shape[0] * dfeat.shape[1], LANES), F32),
+            pltpu.VMEM((images * part, LANES), F32),
         ],
         compiler_params=VMEM,
         cost_estimate=cost(18 * images * cols * chans * part, lines.size * 2),
-    )(lines, slopes, dfeat, spread)
+    )(high, lines, packs, spread)
 
 
 def backward_kernel(lines_ref, weight_ref, out_ref, sums_ref):
@@ -347,12 +353,15 @@
     return padded.reshape((side + 4) * LINE, chans)
 
 
-def make(nx, nz, nc):
-    ny = nz * nc
+def make(nh, nv, nz, nc):
+    nx, ny = nh * nv, nz * nc
+    gx = ("xh", "y")
     near = nz // nx
     gy = ("gz", "core")
-    rise = [(k, (k + 1) % nx) for k in range(nx)]
-    fall = [(k, (k - 1) % nx) for k in range(nx)]
+    across = [(k, nh - 1 - k) for k in range(nh)]
+
+    def paired(value, axis, way):
+        return jnp.concatenate([value, lax.ppermute(value, axis, way)], axis=0)
     pair = [(k, nc - 1 - k) for k in range(nc)]
 
     def on_device(images, conv_weight, fc6_weight, fc7_weight, cotangent):
@@ -366,28 +375,27 @@
         wide = units * nc
         part = chans // nx
         cols = 2 * LANES
-        me, core = lax.axis_index("gx"), lax.axis_index("core")
+        high, core = lax.axis_index("xh"), lax.axis_index("core")
+        me = high * nv + lax.axis_index("y")
         me_word = me.reshape(1).astype(jnp.int32)
 
         known = jnp.concatenate([fc7_weight.T, cotangent.T], axis=1)
-        known = jnp.concatenate([known, lax.ppermute(known, "core", pair)], axis=0)
-        known = lax.all_gather(known, "gx", axis=0, tiled=False)
-        gathered = lax.all_gather(images[0], "gx", axis=0, tiled=False)
+        known = lax.all_gather(known, gx + ("core",), axis=0, tiled=False)
+        known = known.reshape(nx, nc * cols7, rows7 + total)
+        gathered = lax.all_gather(paired(images, "xh", across), "y", axis=0, tiled=True)
         other6 = lax.ppermute(fc6_weight, "core", pair)
         lines = bordered(images[0])
         conv_pre, pooled = conv_forward(lines, conv_weight, side)
         slopes = turned_slope(conv_pre, cols).reshape(nx, part, cols)
         feat = pooled.reshape(half, half + 1, chans)[:, :half].reshape(nx, feats)
-        inputs = share(swap(feat, "gx"), "gz", nz).reshape(group, feats)
+        inputs = share(swap(feat, gx), "gz", nz).reshape(group, feats)
         first = jnp.where(core == 0, fc6_weight, other6)
         second = jnp.where(core == 0, other6, fc6_weight)
         weight6 = jnp.concatenate([first, second], axis=1)
         inputs, weight6 = lax.optimization_barrier((inputs, weight6))
 
         h6_terms = dot(inputs, weight6, ((1,), (0,))).astype(BF).reshape(nx, mine, wide)
-        both = swap(jnp.concatenate([h6_terms, slopes], axis=1), "gx")
-        h6_pre = both[:, :mine].astype(F32).sum(axis=0)
-        slopes = both[:, mine:]
+        h6_pre = swap(h6_terms, gx).astype(F32).sum(axis=0)
         own_hidden = activate(h6_pre).astype(BF)
         hidden = share(own_hidden, "gz", nz)
 
@@ -396,38 +404,29 @@
         pick = (lax.broadcasted_iota(jnp.int32, (total, mine), 0) == source).astype(BF)
         g_seven, dh6_terms = fc7_step(known, hidden, pick)
         hidden = hidden.transpose(1, 0, 2).reshape(mine, rows7)
-        up = [hidden, lax.ppermute(hidden, "gx", rise)]
-        down = [hidden, lax.ppermute(hidden, "gx", fall)]
-        dh6_terms = swap(dh6_terms, "gz")
-        dh6_terms, up[1], down[1] = lax.optimization_barrier((dh6_terms, up[1], down[1]))
+        hidden = paired(hidden, "xh", across)
+        dh6_terms, hidden = lax.optimization_barrier((swap(dh6_terms, "gz"), hidden))
+        all_hidden = lax.all_gather(hidden, "y", axis=0, tiled=False).reshape(group, rows7)
         grad_hidden = dh6_terms.astype(F32).sum(axis=0)
         own_six = (grad_hidden * slope(h6_pre)).astype(BF)
 
         columns = g_seven.reshape(nx, cols7, nc * mine)
         columns = jnp.pad(columns, ((0, 0), (0, mine - cols7), (0, LANES - nc * mine)))
         both = jnp.concatenate([jnp.broadcast_to(own_six, (nx, mine, wide)), columns], axis=2)
-        both = swap(both, "gx")
-        up.append(lax.ppermute(up[1], "gx", rise))
-        down.append(lax.ppermute(down[1], "gx", fall))
-        both, up[2], down[2] = lax.optimization_barrier((both, up[2], down[2]))
+        both = swap(both, gx)
         g_six = both[:, :, :wide].reshape(group, wide)
         columns = both[:, :cols7, wide : wide + nc * mine]
 
         feat_terms = features_back(g_six, weight6).reshape(nz, nx, feats)
         feat_terms, g_six = lax.optimization_barrier((feat_terms, g_six))
-        feat_terms = swap(feat_terms, "gz")
-        up.append(lax.ppermute(up[2], "gx", rise))
-        down.append(lax.ppermute(down[2], "gx", fall))
-        up.append(lax.ppermute(up[3], "gx", rise))
-        feat_terms, up[3], down[3] = lax.optimization_barrier((feat_terms, up[3], down[3]))
+        feat_terms, gathered = lax.optimization_barrier((swap(feat_terms, "gz"), gathered))
         sent6 = weight_terms(nc - 1 - core, inputs, g_six, units)
-        packs = pack_dfeat(me_word, feat_terms)
-        packs = swap(packs, "gx")
+        packs = swap(pack_dfeat(me_word, feat_terms, slopes), gx)
         gathered, sent6 = lax.optimization_barrier((gathered, sent6))
         all_lines = jax.vmap(bordered)(gathered)
         grad_fc6 = weight_terms(core, inputs, g_six, units, lax.ppermute(sent6, "core", pair))
         spread = spread_matrix(me, nx, half, cols)
-        packed = conv_kernel_grad(all_lines, slopes, packs, spread, ny)
+        packed = conv_kernel_grad(high.reshape(1).astype(jnp.int32), all_lines, packs, spread, ny)
         packed = swap(packed, gy)
 
         runs = feats // part
@@ -436,11 +435,14 @@
         g_lines = conv_slope(conv_pre, dfeat).reshape(side, LINE, chans)[:, :side]
         grad_images = conv_backward(bordered(g_lines), conv_weight, side)
 
-        all_hidden = jnp.concatenate([down[k] for k in range(nx // 2)] + up[nx // 2 : 0 : -1], axis=0)
-        columns = lax.dynamic_slice_in_dim(jnp.concatenate([columns, columns]), me, nx)
-        columns = columns.reshape(nx, cols7, nc, mine).transpose(2, 1, 0, 3).reshape(nc * cols7, group)
+        columns = columns.reshape(nh, nv, cols7, nc * mine)
+        columns = jnp.where(high == 0, columns, columns[::-1])
+        columns = columns.reshape(nh, nv, cols7, nc, mine).transpose(3, 2, 1, 0, 4)
+        columns = columns.reshape(nc * cols7, group)
         terms7 = dot(columns, all_hidden, ((1,), (0,)))
-        grad_fc7 = (terms7[:cols7] + lax.ppermute(terms7[cols7:], "core", pair)).T
+        own7 = jnp.where(core == 0, terms7[:cols7], terms7[cols7:])
+        sent7 = jnp.where(core == 0, terms7[cols7:], terms7[:cols7])
+        grad_fc7 = (own7 + lax.ppermute(sent7, "core", pair)).T
         packed, grad_fc7 = lax.optimization_barrier((packed, grad_fc7))
         packed = packed.astype(F32).sum(axis=0)
         grad_conv = jnp.concatenate([packed[:, :part], packed[:, part:]], axis=0)
@@ -451,15 +453,15 @@
 
 def solution(mesh):
     nx, ny = mesh.shape["gx"], mesh.shape["gy"]
-    nc = 2
-    nz = ny // nc
-    fine = Mesh(mesh.devices.reshape(nx, nz, nc), ("gx", "gz", "core"))
-    gy = ("gz", "core")
-    both = ("gx", "gz", "core")
+    nh = nc = 2
+    nv, nz = nx // nh, ny // nc
+    fine = Mesh(mesh.devices.reshape(nh, nv, nz, nc), ("xh", "y", "gz", "core"))
+    gx, gy = ("xh", "y"), ("gz", "core")
+    both = gx + gy
     return jax.shard_map(
-        make(nx, nz, nc),
+        make(nh, nv, nz, nc),
         mesh=fine,
-        in_specs=(P(both, None, None, None), P(), P("gx", gy), P(None, both), P(None, both)),
-        out_specs=(P(gy, "gx"), P("gx", gy), P(None, both), P(both, None, None, None)),
+        in_specs=(P(both, None, None, None), P(), P(gx, gy), P(None, both), P(None, both)),
+        out_specs=(P(gy, gx), P(gx, gy), P(None, both), P(both, None, None, None)),
         check_vma=False,
     )

time: 218 us -> 216 us (level)
  blocking collectives: 0 us -> 32.3 us
  starting transfers between devices: 75.5 us -> 45 us
  local copies, waits for them, and re-layouts: 28.2 us -> 16.4 us
  waiting for transfers between devices: 72.4 us -> 80.7 us
    all_to_all x0 -> x3, blocking collectives: none -> 32.3 us  [swap(): return lax.all_to_all(value, axis, 0, 0, tiled=True)]
    all_gather x2 -> x3, waiting for transfers between devices: 5.37 us -> 34.6 us  [the longest x1 33.3 us: on_device(): lax.all_gather(paired(images, 'xh', across), 'y', axis=0, tiled=True)]
    ppermute x9 -> x3, starting transfers between devices: 20.3 us -> 4.51 us  [the longest x2 3.55 us: paired(): return jnp.concatenate([value, lax.ppermute(value, axis, way)], axis=0)]
    all_to_all x9 -> x6, starting transfers between devices: 52.1 us -> 36.6 us  [swap(): return lax.all_to_all(value, axis, 0, 0, tiled=True)]
    all_to_all x9 -> x6, waiting for transfers between devices: 55.1 us -> 41.7 us  [swap(): return lax.all_to_all(value, axis, 0, 0, tiled=True)]
    unnamed x28 -> x21, local copies, waits for them, and re-layouts: 19 us -> 10.1 us
    ppermute x9 -> x3, waiting for transfers between devices: 11.2 us -> 4.36 us  [the longest x2 4.36 us: paired(): return jnp.concatenate([value, lax.ppermute(value, axis, way)], axis=0)]
    ppermute x1, starting transfers between devices: 0.45 us -> 3.33 us  [on_device(): other6 = lax.ppermute(fc6_weight, 'core', pair)]
  transfers between devices with their start and end apart: 22 -> 14, of which waited for: 12 -> 8; matrix products, arithmetic and copies ran while one was open for 12% -> 7% of each run, Pallas kernels for 8% -> 7%
where the time goes in v7:
time: 216 us; the launch traced here: 215 us
  waiting for transfers between devices  80.7 us (37%)
  starting transfers between devices  45 us (21%)
  blocking collectives  32.3 us (15%)
  local copies, waits for them, and re-layouts  16.4 us (8%)
  Pallas kernels  15.4 us (7%)
  between operations  14.2 us (7%)
  other arithmetic  9.31 us (4%)
    all_to_all x6, waiting for transfers between devices, swap(): return lax.all_to_all(value, axis, 0, 0, tiled=True)  41.7 us
    all_to_all x6, starting transfers between devices, swap(): return lax.all_to_all(value, axis, 0, 0, tiled=True)  36.6 us
    all_gather x1, waiting for transfers between devices, on_device(): lax.all_gather(paired(images, 'xh', across), 'y', axis=0, tiled=True)  33.3 us
    all_to_all x3, blocking collectives, swap(): return lax.all_to_all(value, axis, 0, 0, tiled=True)  32.3 us
    unnamed x21, local copies, waits for them, and re-layouts  10.1 us
    ppermute x2, waiting for transfers between devices, paired(): return jnp.concatenate([value, lax.ppermute(value, axis, way)], axis=0)  4.36 us
  transfers between devices with their start and end apart: 14, of which 8 were waited for; matrix products, arithmetic and copies ran while one was open for 7% of the time, Pallas kernels for 7%

profile of v7, /device:TPU:1, one launch (start us, length us, event | category | flops | bytes accessed | tf_op | source)
XLA Modules:
  0.0 215.1 jit_solution(3425502582926282669)
XLA Ops:
  7.2 1.6 pad_maximum_fusion.3
  8.8 3.3 %collective-permute-start = (bf16[3136,128]{1,0:T(8,128)(2,1)}, bf16[3136,128]{1,0:T(8,128)(2,1)S(1)}, u32[]{:S(2)}, u32[]{:S(2)}) collective-permute-start(bf16[3136,128]{1,0:T(8,128)(2,1)} %param.7), channel_id=1, source_target_pairs={{0,1},{1,0},{2,3},{3,2},{4,5},{5,4},{6,7},{7,6},{8,9},{9,8},{10,11... | collective-permute-start | bytes 2408456 | tf_op jit(solution)/shard_map/ppermute | solution.py:386
  12.2 1.0 pad.20
  13.2 2.3 %copy-done = bf16[4608,512]{1,0:T(8,128)(2,1)S(1)} copy-done((bf16[4608,512]{1,0:T(8,128)(2,1)S(1)}, bf16[4608,512]{1,0:T(8,128)(2,1)}, u32[]{:S(2)}) %copy-start) | copy-done | bytes 4718616
  15.5 2.2 %shard_map.84 = (f32[224,512]{1,0:T(8,128)S(1)}, bf16[56,512]{1,0:T(8,128)(2,1)S(1)}) custom-call(bf16[288,512]{1,0:T(8,128)(2,1)S(1)} %bitcast.45, bf16[4608,512]{1,0:T(8,128)(2,1)S(1)} %copy-done), custom_call_target="tpu_custom_call" | custom-call | flops 1056964608 | bytes 4718592 | tf_op jit(solution)/shard_map/pallas_call | solution.py:66
  17.7 0.1 all_to_all.43
  17.8 0.5 broadcast.165
  18.3 0.9 reduce
  19.3 0.1 reshape.112
  19.4 11.4 %all_to_all.53 = bf16[8,2,1568]{2,1,0:T(2,128)(2,1)S(1)} all-to-all(bf16[8,2,1568]{2,1,0:T(2,128)(2,1)S(1)} %reshape.112), channel_id=1, replica_groups=mesh['xh'=2,'y'=4,'gz'=16,'core'=2] {'xh','y'}, dimensions={0} | all-to-all | bytes 100352 | tf_op jit(solution)/shard_map/all_to_all | solution.py:343
  30.8 0.1 reshape.113
  30.9 0.9 broadcast_in_dim.11
  31.9 8.4 %all-to-all-start.1 = ((bf16[16,8,3136]{2,1,0:T(8,128)(2,1)}), bf16[16,8,3136]{2,1,0:T(8,128)(2,1)S(1)}, u32[]{:S(2)}, u32[]{:S(2)}) async-start(bf16[16,8,3136]{2,1,0:T(8,128)(2,1)} %broadcast_in_dim.11), calls=%async_computation.1 | async-start | bytes 1638400 | tf_op jit(solution)/shard_map/all_to_all | solution.py:343
  40.3 0.1 broadcast_select_fusion.1
  40.4 0.2 pad_maximum_fusion.weight_ref
  40.6 18.6 %all-to-all-done.1 = bf16[16,8,3136]{2,1,0:T(8,128)(2,1)S(1)} async-done(((bf16[16,8,3136]{2,1,0:T(8,128)(2,1)}), bf16[16,8,3136]{2,1,0:T(8,128)(2,1)S(1)}, u32[]{:S(2)}, u32[]{:S(2)}) %all-to-all-start.1) | async-done | bytes 802848 | tf_op jit(solution)/shard_map/all_to_all | solution.py:343
  59.2 0.4 convolution_convert_fusion
  59.6 10.3 %all_to_all.54 = bf16[8,16,256]{2,1,0:T(8,128)(2,1)S(1)} all-to-all(bf16[8,16,256]{2,1,0:T(8,128)(2,1)S(1)} %bitcast.58), channel_id=1, replica_groups=mesh['xh'=2,'y'=4,'gz'=16,'core'=2] {'xh','y'}, dimensions={0} | all-to-all | bytes 131072 | tf_op jit(solution)/shard_map/all_to_all | solution.py:343
  69.9 0.7 broadcast_in_dim.12
  70.6 6.0 %all-to-all-start.3 = ((bf16[16,16,256]{2,1,0:T(8,128)(2,1)}), bf16[16,16,256]{2,1,0:T(8,128)(2,1)S(1)}, u32[]{:S(2)}, u32[]{:S(2)}) async-start(bf16[16,16,256]{2,1,0:T(8,128)(2,1)} %broadcast_in_dim.12), calls=%async_computation.3 | async-start | bytes 262144 | tf_op jit(solution)/shard_map/all_to_all | solution.py:343
  76.6 7.4 %all-to-all-done.3.hidden_ref = bf16[16,16,256]{2,1,0:T(8,128)(2,1)S(1)} async-done(((bf16[16,16,256]{2,1,0:T(8,128)(2,1)}), bf16[16,16,256]{2,1,0:T(8,128)(2,1)S(1)}, u32[]{:S(2)}, u32[]{:S(2)}) %all-to-all-start.3) | async-done | bytes 131104 | tf_op jit(solution)/shard_map/all_to_all | solution.py:343
  84.0 1.2 collective-permute-start.1
  85.3 1.6 copy-done.3
  86.9 1.8 shard_map.85
  88.7 3.5 %all-to-all-start.4 = ((bf16[16,16,256]{2,1,0:T(8,128)(2,1)}), bf16[16,16,256]{2,1,0:T(8,128)(2,1)S(1)}, u32[]{:S(2)}, u32[]{:S(2)}) async-start(bf16[16,16,256]{2,1,0:T(8,128)(2,1)} %get-tuple-element.23), calls=%async_computation.4 | async-start | bytes 262144 | tf_op jit(solution)/shard_map/all_to_all | solution.py:343
  92.2 1.6 pad_maximum_fusion.2
  93.9 5.7 %all-to-all-done.4 = bf16[16,16,256]{2,1,0:T(8,128)(2,1)S(1)} async-done(((bf16[16,16,256]{2,1,0:T(8,128)(2,1)}), bf16[16,16,256]{2,1,0:T(8,128)(2,1)S(1)}, u32[]{:S(2)}, u32[]{:S(2)}) %all-to-all-start.4) | async-done | bytes 131104 | tf_op jit(solution)/shard_map/all_to_all | solution.py:343
  99.6 2.4 %collective-permute-start.2 = (bf16[1,14,14,512]{3,2,1,0:T(8,128)(2,1)S(1)}, bf16[1,14,14,512]{3,2,1,0:T(8,128)(2,1)S(1)}, u32[]{:S(2)}, u32[]{:S(2)}) collective-permute-start(bf16[1,14,14,512]{3,2,1,0:T(8,128)(2,1)S(1)} %copy-done.6), channel_id=1, source_target_pairs={{0,128},{128,0},{1,129},{129,1},{2,130},{130,2},{3,131},{131,3},{4... | collective-permute-start | bytes 602120 | tf_op jit(solution)/shard_map/ppermute | solution.py:364
  102.0 4.4 %collective-permute-done.2 = bf16[1,14,14,512]{3,2,1,0:T(8,128)(2,1)S(1)} collective-permute-done((bf16[1,14,14,512]{3,2,1,0:T(8,128)(2,1)S(1)}, bf16[1,14,14,512]{3,2,1,0:T(8,128)(2,1)S(1)}, u32[]{:S(2)}, u32[]{:S(2)}) %collective-permute-start.2) | collective-permute-done | bytes 200736 | tf_op jit(solution)/shard_map/ppermute | solution.py:364
  106.4 0.8 pad_maximum_fusion.1
  107.3 10.7 %all_to_all.55 = bf16[8,16,384]{2,1,0:T(8,128)(2,1)S(1)} all-to-all(bf16[8,16,384]{2,1,0:T(8,128)(2,1)S(1)} %fusion.2), channel_id=1, replica_groups=mesh['xh'=2,'y'=4,'gz'=16,'core'=2] {'xh','y'}, dimensions={0} | all-to-all | bytes 196608 | tf_op jit(solution)/shard_map/all_to_all | solution.py:343
  118.0 1.6 shard_map.86
  119.6 3.6 %all-to-all-start.6 = ((bf16[16,8,3136]{2,1,0:T(8,128)(2,1)}), bf16[16,8,3136]{2,1,0:T(8,128)(2,1)S(1)}, u32[]{:S(2)}, u32[]{:S(2)}) async-start(bf16[16,8,3136]{2,1,0:T(8,128)(2,1)} %bitcast.12), calls=%async_computation.6 | async-start | bytes 1638400 | tf_op jit(solution)/shard_map/all_to_all | solution.py:343
  123.2 0.2 shard_map.88
  123.6 0.1 reshape.98
  123.7 0.1 copy.27
  123.7 0.1 reshape.99
  123.8 1.3 all-gather.10.cloned.1.call-done
  125.1 1.5 fusion.24
  126.6 33.3 %all-gather.6.cloned.1.call-done = bf16[8,14,14,512]{3,2,1,0:T(8,128)(2,1)} async-done(((bf16[2,14,14,512]{3,2,1,0:T(8,128)(2,1)}), bf16[8,14,14,512]{3,2,1,0:T(8,128)(2,1)}) %all-gather.6.cloned.1.call-update) | async-done | bytes 1605648 | tf_op jit(solution)/shard_map/all_gather | solution.py:385
  159.9 1.0 shard_map.89
  161.0 5.1 %all-to-all-start.7 = ((bf16[8,64,384]{2,1,0:T(8,128)(2,1)}), bf16[8,64,384]{2,1,0:T(8,128)(2,1)S(1)}, u32[]{:S(2)}, u32[]{:S(2)}) async-start(bf16[8,64,384]{2,1,0:T(8,128)(2,1)} %shard_map.89), calls=%async_computation.7 | async-start | bytes 786432 | tf_op jit(solution)/shard_map/all_to_all | solution.py:343
  166.1 0.7 slice_select_fusion
  166.8 1.0 collective-permute-start.3
  167.8 0.1 fusion.19.spread_ref
  167.9 0.4 shard_map.87
  168.3 2.4 %pad.22 = bf16[8,18,16,512]{3,2,1,0:T(8,128)(2,1)} pad(bf16[8,14,14,512]{3,2,1,0:T(8,128)(2,1)S(1)} %copy-done.5, bf16[]{:T(256)} %constant.111.clone.1), padding=0_0x1_3x1_1x0_0 | pad | bytes 3964930 | tf_op jit(solution)/shard_map/vmap(jit(_pad))/pad | solution.py:352
  170.7 3.5 %all-to-all-done.7.packs_ref = bf16[8,64,384]{2,1,0:T(8,128)(2,1)S(1)} async-done(((bf16[8,64,384]{2,1,0:T(8,128)(2,1)}), bf16[8,64,384]{2,1,0:T(8,128)(2,1)S(1)}, u32[]{:S(2)}, u32[]{:S(2)}) %all-to-all-start.7) | async-done | bytes 393248 | tf_op jit(solution)/shard_map/all_to_all | solution.py:343
  174.2 1.7 copy-done.2
  175.8 2.9 %shard_map.90 = bf16[32,72,128]{2,1,0:T(8,128)(2,1)} custom-call(s32[1]{0:T(128)} %bitcast.high_ref, bf16[8,288,512]{2,1,0:T(8,128)(2,1)S(1)} %bitcast.43, bf16[8,64,384]{2,1,0:T(8,128)(2,1)S(1)} %all-to-all-done.7.packs_ref, bf16[64,256]{1,0:T(8,128)(2,1)S(1)} %fusion.19.spread_ref), custom_call_target="tpu_custom_call" | custom-call | flops 1207959552 | bytes 2359296 | tf_op jit(solution)/shard_map/pallas_call | solution.py:275
  178.8 10.0 %all-to-all-start.8 = ((bf16[32,72,128]{2,1,0:T(8,128)(2,1)}), bf16[32,72,128]{2,1,0:T(8,128)(2,1)}, u32[]{:S(2)}, u32[]{:S(2)}) async-start(bf16[32,72,128]{2,1,0:T(8,128)(2,1)} %shard_map.90), calls=%async_computation.8 | async-start | bytes 1179648 | tf_op jit(solution)/shard_map/all_to_all | solution.py:343
  188.8 0.4 collective-permute-start.4
  189.2 1.8 add_bitcast_fusion
  191.0 0.1 slice.45
  191.1 0.1 convert_element_type.49
  191.3 0.2 shard_map.92
  191.6 2.3 %copy-done.1 = bf16[4608,512]{1,0:T(8,128)(2,1)S(1)} copy-done((bf16[4608,512]{1,0:T(8,128)(2,1)S(1)}, bf16[4608,512]{1,0:T(8,128)(2,1)}, u32[]{:S(2)}) %copy-start.1) | copy-done | bytes 4718616
  193.9 3.5 %shard_map.93 = f32[1,14,14,512]{3,2,1,0:T(8,128)S(1)} custom-call(bf16[288,512]{1,0:T(8,128)(2,1)S(1)} %bitcast.47, bf16[4608,512]{1,0:T(8,128)(2,1)S(1)} %copy-done.1), custom_call_target="tpu_custom_call" | custom-call | flops 1056964608 | bytes 4718592 | tf_op jit(solution)/shard_map/pallas_call | solution.py:316
  197.4 1.2 copy.29
  198.6 1.6 shard_map.91
  200.2 6.5 %all-to-all-done.8 = bf16[32,72,128]{2,1,0:T(8,128)(2,1)} async-done(((bf16[32,72,128]{2,1,0:T(8,128)(2,1)}), bf16[32,72,128]{2,1,0:T(8,128)(2,1)}, u32[]{:S(2)}, u32[]{:S(2)}) %all-to-all-start.8) | async-done | bytes 589856 | tf_op jit(solution)/shard_map/all_to_all | solution.py:343
  206.6 1.2 convert_reduce_fusion
  207.8 0.1 fusion.23
  207.9 0.7 copy.28
  (48 shorter events, 0.5 us)
Async XLA Ops:
  7.2 78.1 %all-gather.8.cloned.1.call-start = ((), (), s32[]{:S(2)}) async-start(), calls=%async_computation.10 | async-start | bytes 2367488 | tf_op jit(solution)/shard_map/all_gather | solution.py:383
  8.8 31.5 %collective-permute-start = (bf16[3136,128]{1,0:T(8,128)(2,1)}, bf16[3136,128]{1,0:T(8,128)(2,1)S(1)}, u32[]{:S(2)}, u32[]{:S(2)}) collective-permute-start(bf16[3136,128]{1,0:T(8,128)(2,1)} %param.7), channel_id=1, source_target_pairs={{0,1},{1,0},{2,3},{3,2},{4,5},{5,4},{6,7},{7,6},{8,9},{9,8},{10,11... | collective-permute-start | bytes 2408456 | tf_op jit(solution)/shard_map/ppermute | solution.py:386
  13.2 2.3 %copy-start = (bf16[4608,512]{1,0:T(8,128)(2,1)S(1)}, bf16[4608,512]{1,0:T(8,128)(2,1)}, u32[]{:S(2)}) copy-start(bf16[4608,512]{1,0:T(8,128)(2,1)} %weight_ref.3) | copy-start | bytes 14155780
  17.8 22.5 %copy-start.7 = (bf16[3136,128]{1,0:T(8,128)(2,1)S(1)}, bf16[3136,128]{1,0:T(8,128)(2,1)}, u32[]{:S(2)}) copy-start(bf16[3136,128]{1,0:T(8,128)(2,1)} %param.7) | copy-start | bytes 2408452
  31.9 27.4 %all-to-all-start.1 = ((bf16[16,8,3136]{2,1,0:T(8,128)(2,1)}), bf16[16,8,3136]{2,1,0:T(8,128)(2,1)S(1)}, u32[]{:S(2)}, u32[]{:S(2)}) async-start(bf16[16,8,3136]{2,1,0:T(8,128)(2,1)} %broadcast_in_dim.11), calls=%async_computation.1 | async-start | bytes 1638400 | tf_op jit(solution)/shard_map/all_to_all | solution.py:343
  70.6 13.4 %all-to-all-start.3 = ((bf16[16,16,256]{2,1,0:T(8,128)(2,1)}), bf16[16,16,256]{2,1,0:T(8,128)(2,1)S(1)}, u32[]{:S(2)}, u32[]{:S(2)}) async-start(bf16[16,16,256]{2,1,0:T(8,128)(2,1)} %broadcast_in_dim.12), calls=%async_computation.3 | async-start | bytes 262144 | tf_op jit(solution)/shard_map/all_to_all | solution.py:343
  84.0 8.2 %collective-permute-start.1 = (bf16[16,4096]{1,0:T(8,128)(2,1)S(1)}, bf16[16,4096]{1,0:T(8,128)(2,1)}, u32[]{:S(2)}, u32[]{:S(2)}) collective-permute-start(bf16[16,4096]{1,0:T(8,128)(2,1)S(1)} %bitcast.56), channel_id=1, source_target_pairs={{0,128},{128,0},{1,129},{129,1},{2,130},{130,2},{3,131},{131,3},{4... | collective-permute-start | bytes 393224 | tf_op jit(solution)/shard_map/ppermute | solution.py:364
  85.2 1.6 copy-start.3
  86.9 12.8 %copy-start.6 = (bf16[1,14,14,512]{3,2,1,0:T(8,128)(2,1)S(1)}, bf16[1,14,14,512]{3,2,1,0:T(8,128)(2,1)}, u32[]{:S(2)}) copy-start(bf16[1,14,14,512]{3,2,1,0:T(8,128)(2,1)} %param.5) | copy-start | bytes 602116
  88.7 10.9 %all-to-all-start.4 = ((bf16[16,16,256]{2,1,0:T(8,128)(2,1)}), bf16[16,16,256]{2,1,0:T(8,128)(2,1)S(1)}, u32[]{:S(2)}, u32[]{:S(2)}) async-start(bf16[16,16,256]{2,1,0:T(8,128)(2,1)} %get-tuple-element.23), calls=%async_computation.4 | async-start | bytes 262144 | tf_op jit(solution)/shard_map/all_to_all | solution.py:343
  92.2 32.9 %all-gather.10.cloned.1.call-start = ((), (), s32[]{:S(2)}) async-start(), calls=%async_computation.11 | async-start | bytes 1310720 | tf_op jit(solution)/shard_map/all_gather | solution.py:409
  99.6 60.4 %all-gather.6.cloned.1.call-start = ((), (), s32[]{:S(2)}) async-start(), calls=%async_computation.9 | async-start | bytes 2293760 | tf_op jit(solution)/shard_map/all_gather | solution.py:385
  99.6 6.7 %collective-permute-start.2 = (bf16[1,14,14,512]{3,2,1,0:T(8,128)(2,1)S(1)}, bf16[1,14,14,512]{3,2,1,0:T(8,128)(2,1)S(1)}, u32[]{:S(2)}, u32[]{:S(2)}) collective-permute-start(bf16[1,14,14,512]{3,2,1,0:T(8,128)(2,1)S(1)} %copy-done.6), channel_id=1, source_target_pairs={{0,128},{128,0},{1,129},{129,1},{2,130},{130,2},{3,131},{131,3},{4... | collective-permute-start | bytes 602120 | tf_op jit(solution)/shard_map/ppermute | solution.py:364
  119.6 40.3 %all-to-all-start.6 = ((bf16[16,8,3136]{2,1,0:T(8,128)(2,1)}), bf16[16,8,3136]{2,1,0:T(8,128)(2,1)S(1)}, u32[]{:S(2)}, u32[]{:S(2)}) async-start(bf16[16,8,3136]{2,1,0:T(8,128)(2,1)} %bitcast.12), calls=%async_computation.6 | async-start | bytes 1638400 | tf_op jit(solution)/shard_map/all_to_all | solution.py:343
  126.6 52.2 %copy-start.4 = (f32[32,4096]{1,0:T(8,128)}, f32[32,4096]{1,0:T(8,128)S(1)}, u32[]{:S(2)}) copy-start(f32[32,4096]{1,0:T(8,128)S(1)} %fusion.24) | copy-start | bytes 1572868
  161.0 13.2 %all-to-all-start.7 = ((bf16[8,64,384]{2,1,0:T(8,128)(2,1)}), bf16[8,64,384]{2,1,0:T(8,128)(2,1)S(1)}, u32[]{:S(2)}, u32[]{:S(2)}) async-start(bf16[8,64,384]{2,1,0:T(8,128)(2,1)} %shard_map.89), calls=%async_computation.7 | async-start | bytes 786432 | tf_op jit(solution)/shard_map/all_to_all | solution.py:343
  166.1 2.2 %copy-start.5 = (bf16[8,14,14,512]{3,2,1,0:T(8,128)(2,1)S(1)}, bf16[8,14,14,512]{3,2,1,0:T(8,128)(2,1)}, u32[]{:S(2)}) copy-start(bf16[8,14,14,512]{3,2,1,0:T(8,128)(2,1)} %all-gather.6.cloned.1.call-done) | copy-start | bytes 4816900
  166.8 22.4 %collective-permute-start.3 = (f32[16,4096]{1,0:T(8,128)}, f32[16,4096]{1,0:T(8,128)}, u32[]{:S(2)}, u32[]{:S(2)}) collective-permute-start(f32[16,4096]{1,0:T(8,128)} %slice_select_fusion), channel_id=1, source_target_pairs={{0,1},{1,0},{2,3},{3,2},{4,5},{5,4},{6,7},{7,6},{8,9},{9,8},{10,11... | collective-permute-start | bytes 786440 | tf_op jit(solution)/shard_map/ppermute | solution.py:445
  174.2 1.7 copy-start.2
  178.8 27.9 %all-to-all-start.8 = ((bf16[32,72,128]{2,1,0:T(8,128)(2,1)}), bf16[32,72,128]{2,1,0:T(8,128)(2,1)}, u32[]{:S(2)}, u32[]{:S(2)}) async-start(bf16[32,72,128]{2,1,0:T(8,128)(2,1)} %shard_map.90), calls=%async_computation.8 | async-start | bytes 1179648 | tf_op jit(solution)/shard_map/all_to_all | solution.py:343
  188.8 9.8 %collective-permute-start.4 = (bf16[3136,128]{1,0:T(8,128)(2,1)S(1)}, bf16[3136,128]{1,0:T(8,128)(2,1)S(1)}, u32[]{:S(2)}, u32[]{:S(2)}) collective-permute-start(bf16[3136,128]{1,0:T(8,128)(2,1)S(1)} %shard_map.87), channel_id=1, source_target_pairs={{0,1},{1,0},{2,3},{3,2},{4,5},{5,4},{6,7},{7,6},{8,9},{9,8},{10,11... | collective-permute-start | bytes 2408456 | tf_op jit(solution)/shard_map/ppermute | solution.py:427
  191.6 2.3 %copy-start.1 = (bf16[4608,512]{1,0:T(8,128)(2,1)S(1)}, bf16[4608,512]{1,0:T(8,128)(2,1)}, u32[]{:S(2)}) copy-start(bf16[4608,512]{1,0:T(8,128)(2,1)} %weight_ref.3) | copy-start | bytes 14155780
Sparse Core Ops, SparseCore 0:
  11.3 59.9 all-gather.7
  99.7 25.3 all-gather.9
  126.9 32.9 all-gather.5

commit v8 on v7

--- a/solution.py
+++ b/solution.py
@@ -242,18 +242,17 @@
     )(me, terms, slopes)
 
 
-def kernel_kernel(high_ref, lines_ref, packs_ref, spread_ref, out_ref, grad_ref, flat_ref, wide_ref):
+def kernel_kernel(lines_ref, packs_ref, spread_ref, out_ref, grad_ref, flat_ref, wide_ref):
     images, part, _ = packs_ref.shape
     cols = spread_ref.shape[1]
     chans = lines_ref.shape[2]
     wide_ref[...] = packs_ref[:, :, :LANES].astype(F32).reshape(wide_ref.shape)
-    for k in range(images):
-        n = lax.rem(high_ref[0] + k % 2, 2) * (images // 2) + k // 2
+    for n in range(images):
         cells = wide_ref[pl.ds(n, wide_ref.shape[0] // images, images), :].astype(BF)
         spread = dot(cells, spread_ref[...], ((0,), (0,)))[:part]
         turned = (spread * packs_ref[n, :, LANES:].astype(F32)).astype(BF).astype(F32)
         moved = [turned] + [pltpu.roll(turned, j, 1) for j in (1, 2)]
-        grad_ref[:, k * cols : (k + 1) * cols] = jnp.concatenate(moved, axis=0).astype(BF)
+        grad_ref[:, n * cols : (n + 1) * cols] = jnp.concatenate(moved, axis=0).astype(BF)
     for row in range(3):
         block = lines_ref[:, row * LINE : row * LINE + cols, :].reshape(images * cols, chans)
         term = dot(grad_ref[...], block, ((1,), (0,)))
@@ -267,14 +266,13 @@
         out_ref[dest] = jnp.concatenate(both, axis=1).astype(BF)
 
 
-def conv_kernel_grad(high, lines, packs, spread, count):
+def conv_kernel_grad(lines, packs, spread, count):
     images, _, chans = lines.shape
     _, part, _ = packs.shape
     cols = spread.shape[1]
     size = 9 * chans // (2 * count)
     return pl.pallas_call(
         kernel_kernel,
-        in_specs=[pl.BlockSpec(memory_space=pltpu.SMEM)] + [pl.BlockSpec(memory_space=pltpu.VMEM)] * 3,
         out_shape=jax.ShapeDtypeStruct((count, size, 2 * part), BF),
         scratch_shapes=[
             pltpu.VMEM((3 * part, images * cols), BF),
@@ -283,7 +281,7 @@
         ],
         compiler_params=VMEM,
         cost_estimate=cost(18 * images * cols * chans * part, lines.size * 2),
-    )(high, lines, packs, spread)
+    )(lines, packs, spread)
 
 
 def backward_kernel(lines_ref, weight_ref, out_ref, sums_ref):
@@ -382,7 +380,7 @@
         known = jnp.concatenate([fc7_weight.T, cotangent.T], axis=1)
         known = lax.all_gather(known, gx + ("core",), axis=0, tiled=False)
         known = known.reshape(nx, nc * cols7, rows7 + total)
-        gathered = lax.all_gather(paired(images, "xh", across), "y", axis=0, tiled=True)
+        gathered = lax.all_gather(images[0], gx, axis=0, tiled=False)
         other6 = lax.ppermute(fc6_weight, "core", pair)
         lines = bordered(images[0])
         conv_pre, pooled = conv_forward(lines, conv_weight, side)
@@ -406,14 +404,14 @@
         hidden = hidden.transpose(1, 0, 2).reshape(mine, rows7)
         hidden = paired(hidden, "xh", across)
         dh6_terms, hidden = lax.optimization_barrier((swap(dh6_terms, "gz"), hidden))
-        all_hidden = lax.all_gather(hidden, "y", axis=0, tiled=False).reshape(group, rows7)
         grad_hidden = dh6_terms.astype(F32).sum(axis=0)
         own_six = (grad_hidden * slope(h6_pre)).astype(BF)
 
         columns = g_seven.reshape(nx, cols7, nc * mine)
         columns = jnp.pad(columns, ((0, 0), (0, mine - cols7), (0, LANES - nc * mine)))
         both = jnp.concatenate([jnp.broadcast_to(own_six, (nx, mine, wide)), columns], axis=2)
-        both = swap(both, gx)
+        both, hidden = lax.optimization_barrier((swap(both, gx), hidden))
+        all_hidden = lax.all_gather(hidden, "y", axis=0, tiled=False).reshape(group, rows7)
         g_six = both[:, :, :wide].reshape(group, wide)
         columns = both[:, :cols7, wide : wide + nc * mine]
 
@@ -426,7 +424,7 @@
         all_lines = jax.vmap(bordered)(gathered)
         grad_fc6 = weight_terms(core, inputs, g_six, units, lax.ppermute(sent6, "core", pair))
         spread = spread_matrix(me, nx, half, cols)
-        packed = conv_kernel_grad(high.reshape(1).astype(jnp.int32), all_lines, packs, spread, ny)
+        packed = conv_kernel_grad(all_lines, packs, spread, ny)
         packed = swap(packed, gy)
 
         runs = feats // part

time: 216 us -> 208 us (0.963)
  starting transfers between devices: 45 us -> 39.1 us
    all_gather x1, waiting for transfers between devices: 1.29 us -> 23.1 us  [on_device(): lax.all_gather(hidden, 'y', axis=0, tiled=False).reshape(group, rows7)]
    all_gather x1, waiting for transfers between devices: 33.3 us -> 17.6 us  [on_device(): gathered = lax.all_gather(images[0], gx, axis=0, tiled=False)]
    ppermute x2 -> x1, waiting for transfers between devices: 4.36 us -> 0.01 us  [paired(): return jnp.concatenate([value, lax.ppermute(value, axis, way)], axis=0)]
    all_to_all x6, starting transfers between devices: 36.6 us -> 32.5 us  [swap(): return lax.all_to_all(value, axis, 0, 0, tiled=True)]
    all_to_all x6, waiting for transfers between devices: 41.7 us -> 38.4 us  [swap(): return lax.all_to_all(value, axis, 0, 0, tiled=True)]
    ppermute x2 -> x1, starting transfers between devices: 3.55 us -> 1.18 us  [paired(): return jnp.concatenate([value, lax.ppermute(value, axis, way)], axis=0)]
    unnamed x21 -> x19, local copies, waits for them, and re-layouts: 10.1 us -> 10.1 us
  transfers between devices with their start and end apart: 14 -> 13, of which waited for: 8 -> 6; matrix products, arithmetic and copies ran while one was open for 7% -> 7% of each run, Pallas kernels for 7% -> 7%
where the time goes in v8:
time: 208 us; the launch traced here: 207 us
  waiting for transfers between devices  79.8 us (38%)
  starting transfers between devices  39.1 us (19%)
  blocking collectives  32.6 us (16%)
  local copies, waits for them, and re-layouts  16.4 us (8%)
  Pallas kernels  15.3 us (7%)
  between operations  14.2 us (7%)
  other arithmetic  7.57 us (4%)
    all_to_all x6, waiting for transfers between devices, swap(): return lax.all_to_all(value, axis, 0, 0, tiled=True)  38.4 us
    all_to_all x3, blocking collectives, swap(): return lax.all_to_all(value, axis, 0, 0, tiled=True)  32.6 us
    all_to_all x6, starting transfers between devices, swap(): return lax.all_to_all(value, axis, 0, 0, tiled=True)  32.5 us
    all_gather x1, waiting for transfers between devices, on_device(): lax.all_gather(hidden, 'y', axis=0, tiled=False).reshape(group, rows7)  23.1 us
    all_gather x1, waiting for transfers between devices, on_device(): gathered = lax.all_gather(images[0], gx, axis=0, tiled=False)  17.6 us
    unnamed x19, local copies, waits for them, and re-layouts  10.1 us
  transfers between devices with their start and end apart: 13, of which 6 were waited for; matrix products, arithmetic and copies ran while one was open for 7% of the time, Pallas kernels for 7%

profile of v8, /device:TPU:1, one launch (start us, length us, event | category | flops | bytes accessed | tf_op | source)
XLA Modules:
  0.0 206.7 jit_solution(2956850301993279584)
XLA Ops:
  7.2 1.6 pad_maximum_fusion.2
  8.8 3.3 %collective-permute-start = (bf16[3136,128]{1,0:T(8,128)(2,1)}, bf16[3136,128]{1,0:T(8,128)(2,1)S(1)}, u32[]{:S(2)}, u32[]{:S(2)}) collective-permute-start(bf16[3136,128]{1,0:T(8,128)(2,1)} %param.7), channel_id=1, source_target_pairs={{0,1},{1,0},{2,3},{3,2},{4,5},{5,4},{6,7},{7,6},{8,9},{9,8},{10,11... | collective-permute-start | bytes 2408456 | tf_op jit(solution)/shard_map/ppermute | solution.py:384
  12.2 1.0 pad.20
  13.2 2.3 %copy-done = bf16[4608,512]{1,0:T(8,128)(2,1)S(1)} copy-done((bf16[4608,512]{1,0:T(8,128)(2,1)S(1)}, bf16[4608,512]{1,0:T(8,128)(2,1)}, u32[]{:S(2)}) %copy-start) | copy-done | bytes 4718616
  15.5 2.2 %shard_map.84 = (f32[224,512]{1,0:T(8,128)S(1)}, bf16[56,512]{1,0:T(8,128)(2,1)S(1)}) custom-call(bf16[288,512]{1,0:T(8,128)(2,1)S(1)} %bitcast.44, bf16[4608,512]{1,0:T(8,128)(2,1)S(1)} %copy-done), custom_call_target="tpu_custom_call" | custom-call | flops 1056964608 | bytes 4718592 | tf_op jit(solution)/shard_map/pallas_call | solution.py:66
  17.7 0.1 all_to_all.43
  17.8 0.5 broadcast.165
  18.3 0.9 reduce
  19.3 0.1 reshape.108
  19.4 11.5 %all_to_all.53 = bf16[8,2,1568]{2,1,0:T(2,128)(2,1)S(1)} all-to-all(bf16[8,2,1568]{2,1,0:T(2,128)(2,1)S(1)} %reshape.108), channel_id=1, replica_groups=mesh['xh'=2,'y'=4,'gz'=16,'core'=2] {'xh','y'}, dimensions={0} | all-to-all | bytes 100352 | tf_op jit(solution)/shard_map/all_to_all | solution.py:341
  30.9 0.1 reshape.109
  31.0 0.9 broadcast_in_dim.11
  32.0 8.4 %all-to-all-start.1 = ((bf16[16,8,3136]{2,1,0:T(8,128)(2,1)}), bf16[16,8,3136]{2,1,0:T(8,128)(2,1)S(1)}, u32[]{:S(2)}, u32[]{:S(2)}) async-start(bf16[16,8,3136]{2,1,0:T(8,128)(2,1)} %broadcast_in_dim.11), calls=%async_computation.1 | async-start | bytes 1638400 | tf_op jit(solution)/shard_map/all_to_all | solution.py:341
  40.4 0.0 all-gather.6.cloned.1.call-start
  40.4 0.7 all-gather.6.cloned.1.call-update
  41.2 0.1 broadcast_select_fusion.1
  41.3 0.2 pad_maximum_fusion.weight_ref
  41.5 17.9 %all-to-all-done.1 = bf16[16,8,3136]{2,1,0:T(8,128)(2,1)S(1)} async-done(((bf16[16,8,3136]{2,1,0:T(8,128)(2,1)}), bf16[16,8,3136]{2,1,0:T(8,128)(2,1)S(1)}, u32[]{:S(2)}, u32[]{:S(2)}) %all-to-all-start.1) | async-done | bytes 802848 | tf_op jit(solution)/shard_map/all_to_all | solution.py:341
  59.4 0.4 convolution_convert_fusion
  59.8 10.3 %all_to_all.54 = bf16[8,16,256]{2,1,0:T(8,128)(2,1)S(1)} all-to-all(bf16[8,16,256]{2,1,0:T(8,128)(2,1)S(1)} %bitcast.57), channel_id=1, replica_groups=mesh['xh'=2,'y'=4,'gz'=16,'core'=2] {'xh','y'}, dimensions={0} | all-to-all | bytes 131072 | tf_op jit(solution)/shard_map/all_to_all | solution.py:341
  70.1 0.7 broadcast_in_dim.12
  70.7 6.0 %all-to-all-start.3 = ((bf16[16,16,256]{2,1,0:T(8,128)(2,1)}), bf16[16,16,256]{2,1,0:T(8,128)(2,1)S(1)}, u32[]{:S(2)}, u32[]{:S(2)}) async-start(bf16[16,16,256]{2,1,0:T(8,128)(2,1)} %broadcast_in_dim.12), calls=%async_computation.3 | async-start | bytes 262144 | tf_op jit(solution)/shard_map/all_to_all | solution.py:341
  76.7 7.4 %all-to-all-done.3.hidden_ref = bf16[16,16,256]{2,1,0:T(8,128)(2,1)S(1)} async-done(((bf16[16,16,256]{2,1,0:T(8,128)(2,1)}), bf16[16,16,256]{2,1,0:T(8,128)(2,1)S(1)}, u32[]{:S(2)}, u32[]{:S(2)}) %all-to-all-start.3) | async-done | bytes 131104 | tf_op jit(solution)/shard_map/all_to_all | solution.py:341
  84.1 1.2 collective-permute-start.1
  85.4 1.6 copy-done.3
  87.0 1.8 shard_map.85
  88.8 3.5 %all-to-all-start.4 = ((bf16[16,16,256]{2,1,0:T(8,128)(2,1)}), bf16[16,16,256]{2,1,0:T(8,128)(2,1)S(1)}, u32[]{:S(2)}, u32[]{:S(2)}) async-start(bf16[16,16,256]{2,1,0:T(8,128)(2,1)} %get-tuple-element.25), calls=%async_computation.4 | async-start | bytes 262144 | tf_op jit(solution)/shard_map/all_to_all | solution.py:341
  92.3 0.0 all-gather.10.cloned.1.call-start
  92.4 0.7 pad_maximum_fusion.1
  93.1 6.6 %all-to-all-done.4 = bf16[16,16,256]{2,1,0:T(8,128)(2,1)S(1)} async-done(((bf16[16,16,256]{2,1,0:T(8,128)(2,1)}), bf16[16,16,256]{2,1,0:T(8,128)(2,1)S(1)}, u32[]{:S(2)}, u32[]{:S(2)}) %all-to-all-start.4) | async-done | bytes 131104 | tf_op jit(solution)/shard_map/all_to_all | solution.py:341
  99.8 10.8 %all_to_all.55 = bf16[8,16,384]{2,1,0:T(8,128)(2,1)S(1)} all-to-all(bf16[8,16,384]{2,1,0:T(8,128)(2,1)S(1)} %fusion.2), channel_id=1, replica_groups=mesh['xh'=2,'y'=4,'gz'=16,'core'=2] {'xh','y'}, dimensions={0} | all-to-all | bytes 196608 | tf_op jit(solution)/shard_map/all_to_all | solution.py:341
  110.6 1.6 shard_map.86
  112.2 3.6 %all-to-all-start.6 = ((bf16[16,8,3136]{2,1,0:T(8,128)(2,1)}), bf16[16,8,3136]{2,1,0:T(8,128)(2,1)S(1)}, u32[]{:S(2)}, u32[]{:S(2)}) async-start(bf16[16,8,3136]{2,1,0:T(8,128)(2,1)} %bitcast.11), calls=%async_computation.6 | async-start | bytes 1638400 | tf_op jit(solution)/shard_map/all_to_all | solution.py:341
  115.8 0.2 shard_map.88
  116.1 0.1 reshape.94
  116.2 0.1 copy.27
  116.3 0.1 reshape.95
  116.4 17.6 %all-gather.6.cloned.1.call-done = bf16[8,14,14,512]{3,2,1,0:T(8,128)(2,1)} async-done(((bf16[1,14,14,512]{3,2,1,0:T(8,128)(2,1)}), bf16[8,14,14,512]{3,2,1,0:T(8,128)(2,1)}) %all-gather.6.cloned.1.call-update) | async-done | bytes 1605648 | tf_op jit(solution)/shard_map/all_gather | solution.py:383
  134.0 1.0 shard_map.89
  135.1 3.5 %all-to-all-start.7 = ((bf16[8,64,384]{2,1,0:T(8,128)(2,1)}), bf16[8,64,384]{2,1,0:T(8,128)(2,1)S(1)}, u32[]{:S(2)}, u32[]{:S(2)}) async-start(bf16[8,64,384]{2,1,0:T(8,128)(2,1)} %shard_map.89), calls=%async_computation.7 | async-start | bytes 786432 | tf_op jit(solution)/shard_map/all_to_all | solution.py:341
  138.5 23.1 %all-gather.10.cloned.1.call-done = bf16[128,4096]{1,0:T(8,128)(2,1)} async-done(((bf16[32,4096]{1,0:T(8,128)(2,1)}), bf16[128,4096]{1,0:T(8,128)(2,1)}) %all-gather.10.cloned.1.call-update) | async-done | bytes 1048592 | tf_op jit(solution)/shard_map/all_gather | solution.py:414
  161.6 1.5 fusion.24
  163.1 0.7 slice_select_fusion
  163.9 1.5 collective-permute-start.2
  165.4 0.1 fusion.19.spread_ref
  165.6 0.4 shard_map.87
  166.0 2.4 %pad.22 = bf16[8,18,16,512]{3,2,1,0:T(8,128)(2,1)} pad(bf16[8,14,14,512]{3,2,1,0:T(8,128)(2,1)S(1)} %copy-done.5, bf16[]{:T(256)} %constant.109.clone.1), padding=0_0x1_3x1_1x0_0 | pad | bytes 3964930 | tf_op jit(solution)/shard_map/vmap(jit(_pad))/pad | solution.py:350
  168.4 1.7 copy-done.2
  170.0 2.8 %shard_map.90 = bf16[32,72,128]{2,1,0:T(8,128)(2,1)} custom-call(bf16[8,288,512]{2,1,0:T(8,128)(2,1)S(1)} %bitcast.42, bf16[8,64,384]{2,1,0:T(8,128)(2,1)S(1)} %all-to-all-done.7.packs_ref, bf16[64,256]{1,0:T(8,128)(2,1)S(1)} %fusion.19.spread_ref), custom_call_target="tpu_custom_call" | custom-call | flops 1207959552 | bytes 2359296 | tf_op jit(solution)/shard_map/pallas_call | solution.py:274
  172.9 7.6 %all-to-all-start.8 = ((bf16[32,72,128]{2,1,0:T(8,128)(2,1)}), bf16[32,72,128]{2,1,0:T(8,128)(2,1)}, u32[]{:S(2)}, u32[]{:S(2)}) async-start(bf16[32,72,128]{2,1,0:T(8,128)(2,1)} %shard_map.90), calls=%async_computation.8 | async-start | bytes 1179648 | tf_op jit(solution)/shard_map/all_to_all | solution.py:341
  180.4 0.4 collective-permute-start.3
  180.8 1.8 add_bitcast_fusion
  182.7 0.1 slice.43
  182.8 0.1 convert_element_type.49
  182.9 0.2 shard_map.92
  183.1 0.1 pad.24
  183.2 2.3 %copy-done.1 = bf16[4608,512]{1,0:T(8,128)(2,1)S(1)} copy-done((bf16[4608,512]{1,0:T(8,128)(2,1)S(1)}, bf16[4608,512]{1,0:T(8,128)(2,1)}, u32[]{:S(2)}) %copy-start.1) | copy-done | bytes 4718616
  185.5 3.5 %shard_map.93 = f32[1,14,14,512]{3,2,1,0:T(8,128)S(1)} custom-call(bf16[288,512]{1,0:T(8,128)(2,1)S(1)} %bitcast.46, bf16[4608,512]{1,0:T(8,128)(2,1)S(1)} %copy-done.1), custom_call_target="tpu_custom_call" | custom-call | flops 1056964608 | bytes 4718592 | tf_op jit(solution)/shard_map/pallas_call | solution.py:314
  189.0 1.2 copy.29
  190.2 1.6 shard_map.91
  191.8 6.5 %all-to-all-done.8 = bf16[32,72,128]{2,1,0:T(8,128)(2,1)} async-done(((bf16[32,72,128]{2,1,0:T(8,128)(2,1)}), bf16[32,72,128]{2,1,0:T(8,128)(2,1)}, u32[]{:S(2)}, u32[]{:S(2)}) %all-to-all-start.8) | async-done | bytes 589856 | tf_op jit(solution)/shard_map/all_to_all | solution.py:341
  198.3 1.2 convert_reduce_fusion
  199.4 0.1 fusion.23
  199.5 0.7 copy.28
  (43 shorter events, 0.4 us)
Async XLA Ops:
  7.2 78.2 %all-gather.8.cloned.1.call-start = ((), (), s32[]{:S(2)}) async-start(), calls=%async_computation.10 | async-start | bytes 2367488 | tf_op jit(solution)/shard_map/all_gather | solution.py:381
  8.8 32.3 %collective-permute-start = (bf16[3136,128]{1,0:T(8,128)(2,1)}, bf16[3136,128]{1,0:T(8,128)(2,1)S(1)}, u32[]{:S(2)}, u32[]{:S(2)}) collective-permute-start(bf16[3136,128]{1,0:T(8,128)(2,1)} %param.7), channel_id=1, source_target_pairs={{0,1},{1,0},{2,3},{3,2},{4,5},{5,4},{6,7},{7,6},{8,9},{9,8},{10,11... | collective-permute-start | bytes 2408456 | tf_op jit(solution)/shard_map/ppermute | solution.py:384
  13.2 2.3 %copy-start = (bf16[4608,512]{1,0:T(8,128)(2,1)S(1)}, bf16[4608,512]{1,0:T(8,128)(2,1)}, u32[]{:S(2)}) copy-start(bf16[4608,512]{1,0:T(8,128)(2,1)} %weight_ref.3) | copy-start | bytes 14155780
  19.4 21.8 %copy-start.6 = (bf16[3136,128]{1,0:T(8,128)(2,1)S(1)}, bf16[3136,128]{1,0:T(8,128)(2,1)}, u32[]{:S(2)}) copy-start(bf16[3136,128]{1,0:T(8,128)(2,1)} %param.7) | copy-start | bytes 2408452
  32.0 27.4 %all-to-all-start.1 = ((bf16[16,8,3136]{2,1,0:T(8,128)(2,1)}), bf16[16,8,3136]{2,1,0:T(8,128)(2,1)S(1)}, u32[]{:S(2)}, u32[]{:S(2)}) async-start(bf16[16,8,3136]{2,1,0:T(8,128)(2,1)} %broadcast_in_dim.11), calls=%async_computation.1 | async-start | bytes 1638400 | tf_op jit(solution)/shard_map/all_to_all | solution.py:341
  40.4 93.6 %all-gather.6.cloned.1.call-start = ((), (), s32[]{:S(2)}) async-start(), calls=%async_computation.9 | async-start | bytes 2064384 | tf_op jit(solution)/shard_map/all_gather | solution.py:383
  70.7 13.4 %all-to-all-start.3 = ((bf16[16,16,256]{2,1,0:T(8,128)(2,1)}), bf16[16,16,256]{2,1,0:T(8,128)(2,1)S(1)}, u32[]{:S(2)}, u32[]{:S(2)}) async-start(bf16[16,16,256]{2,1,0:T(8,128)(2,1)} %broadcast_in_dim.12), calls=%async_computation.3 | async-start | bytes 262144 | tf_op jit(solution)/shard_map/all_to_all | solution.py:341
  84.1 8.2 %collective-permute-start.1 = (bf16[16,4096]{1,0:T(8,128)(2,1)S(1)}, bf16[16,4096]{1,0:T(8,128)(2,1)S(1)}, u32[]{:S(2)}, u32[]{:S(2)}) collective-permute-start(bf16[16,4096]{1,0:T(8,128)(2,1)S(1)} %bitcast.55), channel_id=1, source_target_pairs={{0,128},{128,0},{1,129},{129,1},{2,130},{130,2},{3,131},{131,3},{4... | collective-permute-start | bytes 393224 | tf_op jit(solution)/shard_map/ppermute | solution.py:362
  85.4 1.6 copy-start.3
  88.8 10.9 %all-to-all-start.4 = ((bf16[16,16,256]{2,1,0:T(8,128)(2,1)}), bf16[16,16,256]{2,1,0:T(8,128)(2,1)S(1)}, u32[]{:S(2)}, u32[]{:S(2)}) async-start(bf16[16,16,256]{2,1,0:T(8,128)(2,1)} %get-tuple-element.25), calls=%async_computation.4 | async-start | bytes 262144 | tf_op jit(solution)/shard_map/all_to_all | solution.py:341
  92.3 69.3 %all-gather.10.cloned.1.call-start = ((), (), s32[]{:S(2)}) async-start(), calls=%async_computation.11 | async-start | bytes 1310720 | tf_op jit(solution)/shard_map/all_gather | solution.py:414
  112.2 21.8 %all-to-all-start.6 = ((bf16[16,8,3136]{2,1,0:T(8,128)(2,1)}), bf16[16,8,3136]{2,1,0:T(8,128)(2,1)S(1)}, u32[]{:S(2)}, u32[]{:S(2)}) async-start(bf16[16,8,3136]{2,1,0:T(8,128)(2,1)} %bitcast.11), calls=%async_computation.6 | async-start | bytes 1638400 | tf_op jit(solution)/shard_map/all_to_all | solution.py:341
  135.1 33.3 %all-to-all-start.7 = ((bf16[8,64,384]{2,1,0:T(8,128)(2,1)}), bf16[8,64,384]{2,1,0:T(8,128)(2,1)S(1)}, u32[]{:S(2)}, u32[]{:S(2)}) async-start(bf16[8,64,384]{2,1,0:T(8,128)(2,1)} %shard_map.89), calls=%async_computation.7 | async-start | bytes 786432 | tf_op jit(solution)/shard_map/all_to_all | solution.py:341
  163.1 2.4 %copy-start.4 = (f32[32,4096]{1,0:T(8,128)}, f32[32,4096]{1,0:T(8,128)S(1)}, u32[]{:S(2)}) copy-start(f32[32,4096]{1,0:T(8,128)S(1)} %fusion.24) | copy-start | bytes 1572868
  163.1 2.8 %copy-start.5 = (bf16[8,14,14,512]{3,2,1,0:T(8,128)(2,1)S(1)}, bf16[8,14,14,512]{3,2,1,0:T(8,128)(2,1)}, u32[]{:S(2)}) copy-start(bf16[8,14,14,512]{3,2,1,0:T(8,128)(2,1)} %all-gather.6.cloned.1.call-done) | copy-start | bytes 4816900
  163.9 16.9 %collective-permute-start.2 = (f32[16,4096]{1,0:T(8,128)}, f32[16,4096]{1,0:T(8,128)}, u32[]{:S(2)}, u32[]{:S(2)}) collective-permute-start(f32[16,4096]{1,0:T(8,128)} %slice_select_fusion), channel_id=1, source_target_pairs={{0,1},{1,0},{2,3},{3,2},{4,5},{5,4},{6,7},{7,6},{8,9},{9,8},{10,11... | collective-permute-start | bytes 786440 | tf_op jit(solution)/shard_map/ppermute | solution.py:443
  168.4 1.7 copy-start.2
  172.9 25.4 %all-to-all-start.8 = ((bf16[32,72,128]{2,1,0:T(8,128)(2,1)}), bf16[32,72,128]{2,1,0:T(8,128)(2,1)}, u32[]{:S(2)}, u32[]{:S(2)}) async-start(bf16[32,72,128]{2,1,0:T(8,128)(2,1)} %shard_map.90), calls=%async_computation.8 | async-start | bytes 1179648 | tf_op jit(solution)/shard_map/all_to_all | solution.py:341
  180.4 9.8 %collective-permute-start.3 = (bf16[3136,128]{1,0:T(8,128)(2,1)S(1)}, bf16[3136,128]{1,0:T(8,128)(2,1)S(1)}, u32[]{:S(2)}, u32[]{:S(2)}) collective-permute-start(bf16[3136,128]{1,0:T(8,128)(2,1)S(1)} %shard_map.87), channel_id=1, source_target_pairs={{0,1},{1,0},{2,3},{3,2},{4,5},{5,4},{6,7},{7,6},{8,9},{9,8},{10,11... | collective-permute-start | bytes 2408456 | tf_op jit(solution)/shard_map/ppermute | solution.py:425
  183.2 2.3 %copy-start.1 = (bf16[4608,512]{1,0:T(8,128)(2,1)S(1)}, bf16[4608,512]{1,0:T(8,128)(2,1)}, u32[]{:S(2)}) copy-start(bf16[4608,512]{1,0:T(8,128)(2,1)} %weight_ref.3) | copy-start | bytes 14155780
Sparse Core Ops, SparseCore 0:
  11.3 59.9 all-gather.7
  73.9 60.0 all-gather.5
  136.4 25.1 all-gather.9

commit v9 on v7

--- a/solution.py
+++ b/solution.py
@@ -25,11 +25,14 @@
     return lax.dot_general(a, b, (dims, ((), ())), preferred_element_type=F32)
 
 
+LITTLE = pl.CostEstimate(flops=1000, bytes_accessed=1000, transcendentals=0)
+
+
 def cost(flops, moved, special=0):
     return pl.CostEstimate(flops=flops, bytes_accessed=moved, transcendentals=special)
 
 
-def forward_kernel(image_ref, weight_ref, pre_ref, feat_ref, held_ref, sums_ref, pool_ref, sems):
+def forward_kernel(image_ref, weight_ref, pre_ref, feat_ref, held_ref, sums_ref, pool_ref, runs_ref, sems):
     pix, chans = pre_ref.shape
     depth = image_ref.shape[1]
     rows = sums_ref.shape[1]
@@ -54,15 +57,27 @@
     act = activate(pre).reshape(pix // (2 * LINE), 2, LINE, chans)
     lines = (act[:, 0] + act[:, 1]).reshape(pix // 2, chans)
     half = pix // 4
+    side = pix // LINE // 2
+    run = LANES // 2
+    runs = feat_ref.shape[1] // run
     for k in range(chans // LANES):
         pool_ref[k] = lines[:, k * LANES : (k + 1) * LANES]
-        total = pool_ref[k, pl.ds(0, half, 2), :] + pool_ref[k, pl.ds(1, half, 2), :]
-        feat_ref[:, k * LANES : (k + 1) * LANES] = (0.25 * total).astype(BF)
-
-
-def conv_forward(lines, weight, side):
+        total = 0.25 * (pool_ref[k, pl.ds(0, half, 2), :] + pool_ref[k, pl.ds(1, half, 2), :])
+        other = pltpu.roll(total, run, 1)
+        for cell in range(side * side):
+            row = cell // side * (LINE // 2) + cell % side
+            for part in range(2):
+                dest, t = divmod(cell * (chans // run) + 2 * k + part, runs)
+                at = t % 2 * run
+                piece = total if t % 2 == part else other
+                runs_ref[dest : dest + 1, t * run : (t + 1) * run] = piece[row : row + 1, at : at + run]
+    feat_ref[...] = runs_ref[...].astype(BF)
+
+
+def conv_forward(lines, weight, side, nx):
     depth, chans = lines.shape[1], weight.shape[1]
     pix = side * LINE
+    feats = side * side // 4 * chans // nx
     return pl.pallas_call(
         forward_kernel,
         in_specs=[
@@ -71,12 +86,13 @@
         ],
         out_shape=[
             jax.ShapeDtypeStruct((pix, chans), F32),
-            jax.ShapeDtypeStruct((pix // 4, chans), BF),
+            jax.ShapeDtypeStruct((nx, feats), BF),
         ],
         scratch_shapes=[
             pltpu.VMEM((3, 3 * depth, chans), BF),
             pltpu.VMEM((3, pix + LINE, chans), F32),
             pltpu.VMEM((chans // LANES, pix // 2, LANES), F32),
+            pltpu.VMEM((nx, feats), F32),
             pltpu.SemaphoreType.DMA((9,)),
         ],
         compiler_params=VMEM,
@@ -121,7 +137,7 @@
         out_shape=jax.ShapeDtypeStruct((pix, chans), BF),
         scratch_shapes=[pltpu.VMEM((chans // LANES, pix // 2, LANES), F32)],
         compiler_params=VMEM,
-        cost_estimate=cost(8 * pix * chans, pix * chans * 6, pix * chans),
+        cost_estimate=LITTLE,
     )(pre, dfeat)
 
 
@@ -195,7 +211,7 @@
         in_specs=[pl.BlockSpec(memory_space=pltpu.SMEM)] + in_vmem,
         out_shape=jax.ShapeDtypeStruct((feats, units), BF if more is None else F32),
         compiler_params=VMEM,
-        cost_estimate=cost(2 * inputs.size * units, 4 * feats * units),
+        cost_estimate=LITTLE,
     )(which.reshape(1).astype(jnp.int32), *operands)
 
 
@@ -242,13 +258,13 @@
     )(me, terms, slopes)
 
 
-def kernel_kernel(high_ref, lines_ref, packs_ref, spread_ref, out_ref, grad_ref, flat_ref, wide_ref):
+def kernel_kernel(place_ref, lines_ref, packs_ref, spread_ref, own_ref, sent_ref, grad_ref, flat_ref, wide_ref):
     images, part, _ = packs_ref.shape
     cols = spread_ref.shape[1]
     chans = lines_ref.shape[2]
     wide_ref[...] = packs_ref[:, :, :LANES].astype(F32).reshape(wide_ref.shape)
     for k in range(images):
-        n = lax.rem(high_ref[0] + k % 2, 2) * (images // 2) + k // 2
+        n = lax.rem(place_ref[0] + k % 2, 2) * (images // 2) + k // 2
         cells = wide_ref[pl.ds(n, wide_ref.shape[0] // images, images), :].astype(BF)
         spread = dot(cells, spread_ref[...], ((0,), (0,)))[:part]
         turned = (spread * packs_ref[n, :, LANES:].astype(F32)).astype(BF).astype(F32)
@@ -260,22 +276,23 @@
         for col in range(3):
             tap = 3 * row + col
             flat_ref[tap * chans : (tap + 1) * chans, :] = term[col * part : (col + 1) * part].T
-    count, size, _ = out_ref.shape
-    for dest in range(count):
-        at = dest * 2 * size
-        both = [flat_ref[at : at + size, :], flat_ref[at + size : at + 2 * size, :]]
-        out_ref[dest] = jnp.concatenate(both, axis=1).astype(BF)
-
-
-def conv_kernel_grad(high, lines, packs, spread, count):
+    count, size, _ = own_ref.shape
+    for core, out_ref in ((place_ref[1], own_ref), (1 - place_ref[1], sent_ref)):
+        for dest in range(count):
+            at = pl.multiple_of((2 * dest + core) * (2 * size), 2 * size)
+            both = [flat_ref[pl.ds(at + k * size, size), :] for k in range(2)]
+            out_ref[dest] = jnp.concatenate(both, axis=1).astype(out_ref.dtype)
+
+
+def conv_kernel_grad(place, lines, packs, spread, count):
     images, _, chans = lines.shape
     _, part, _ = packs.shape
     cols = spread.shape[1]
-    size = 9 * chans // (2 * count)
+    size = 9 * chans // (4 * count)
     return pl.pallas_call(
         kernel_kernel,
         in_specs=[pl.BlockSpec(memory_space=pltpu.SMEM)] + [pl.BlockSpec(memory_space=pltpu.VMEM)] * 3,
-        out_shape=jax.ShapeDtypeStruct((count, size, 2 * part), BF),
+        out_shape=[jax.ShapeDtypeStruct((count, size, 2 * part), kind) for kind in (F32, BF)],
         scratch_shapes=[
             pltpu.VMEM((3 * part, images * cols), BF),
             pltpu.VMEM((9 * chans, part), F32),
@@ -283,7 +300,7 @@
         ],
         compiler_params=VMEM,
         cost_estimate=cost(18 * images * cols * chans * part, lines.size * 2),
-    )(high, lines, packs, spread)
+    )(place, lines, packs, spread)
 
 
 def backward_kernel(lines_ref, weight_ref, out_ref, sums_ref):
@@ -324,7 +341,7 @@
         out_shape=jax.ShapeDtypeStruct((1, side, side, depth), F32),
         scratch_shapes=[pltpu.VMEM((3, pix + LINE, depth), F32)],
         compiler_params=VMEM,
-        cost_estimate=cost(18 * pix * depth * chans, weight.size * 2),
+        cost_estimate=LITTLE,
     )(lines, weight)
 
 
@@ -382,12 +399,12 @@
         known = jnp.concatenate([fc7_weight.T, cotangent.T], axis=1)
         known = lax.all_gather(known, gx + ("core",), axis=0, tiled=False)
         known = known.reshape(nx, nc * cols7, rows7 + total)
-        gathered = lax.all_gather(paired(images, "xh", across), "y", axis=0, tiled=True)
         other6 = lax.ppermute(fc6_weight, "core", pair)
         lines = bordered(images[0])
-        conv_pre, pooled = conv_forward(lines, conv_weight, side)
+        conv_pre, feat = conv_forward(lines, conv_weight, side, nx)
         slopes = turned_slope(conv_pre, cols).reshape(nx, part, cols)
-        feat = pooled.reshape(half, half + 1, chans)[:, :half].reshape(nx, feats)
+        feat, image = lax.optimization_barrier((feat, images))
+        gathered = lax.all_gather(paired(image, "xh", across), "y", axis=0, tiled=True)
         inputs = share(swap(feat, gx), "gz", nz).reshape(group, feats)
         first = jnp.where(core == 0, fc6_weight, other6)
         second = jnp.where(core == 0, other6, fc6_weight)
@@ -403,6 +420,7 @@
         source = (place % nx) * ny + (me * near + place // nx) * nc + core
         pick = (lax.broadcasted_iota(jnp.int32, (total, mine), 0) == source).astype(BF)
         g_seven, dh6_terms = fc7_step(known, hidden, pick)
+        dh6_terms, hidden = lax.optimization_barrier((dh6_terms, hidden))
         hidden = hidden.transpose(1, 0, 2).reshape(mine, rows7)
         hidden = paired(hidden, "xh", across)
         dh6_terms, hidden = lax.optimization_barrier((swap(dh6_terms, "gz"), hidden))
@@ -413,28 +431,22 @@
         columns = g_seven.reshape(nx, cols7, nc * mine)
         columns = jnp.pad(columns, ((0, 0), (0, mine - cols7), (0, LANES - nc * mine)))
         both = jnp.concatenate([jnp.broadcast_to(own_six, (nx, mine, wide)), columns], axis=2)
-        both = swap(both, gx)
+        both, gathered = lax.optimization_barrier((swap(both, gx), gathered))
         g_six = both[:, :, :wide].reshape(group, wide)
         columns = both[:, :cols7, wide : wide + nc * mine]
 
         feat_terms = features_back(g_six, weight6).reshape(nz, nx, feats)
         feat_terms, g_six = lax.optimization_barrier((feat_terms, g_six))
-        feat_terms, gathered = lax.optimization_barrier((swap(feat_terms, "gz"), gathered))
+        feat_terms = swap(feat_terms, "gz")
         sent6 = weight_terms(nc - 1 - core, inputs, g_six, units)
         packs = swap(pack_dfeat(me_word, feat_terms, slopes), gx)
         gathered, sent6 = lax.optimization_barrier((gathered, sent6))
         all_lines = jax.vmap(bordered)(gathered)
         grad_fc6 = weight_terms(core, inputs, g_six, units, lax.ppermute(sent6, "core", pair))
         spread = spread_matrix(me, nx, half, cols)
-        packed = conv_kernel_grad(high.reshape(1).astype(jnp.int32), all_lines, packs, spread, ny)
-        packed = swap(packed, gy)
-
-        runs = feats // part
-        dfeat = packs[:, :runs, part : 2 * part].reshape(half, half, chans).astype(F32)
-        dfeat = jnp.pad(dfeat, ((0, 0), (0, 1), (0, 0))).reshape(half * (half + 1), chans)
-        g_lines = conv_slope(conv_pre, dfeat).reshape(side, LINE, chans)[:, :side]
-        grad_images = conv_backward(bordered(g_lines), conv_weight, side)
-
+        place = jnp.stack([high, core]).astype(jnp.int32)
+        packed, sent = conv_kernel_grad(place, all_lines, packs, spread, nz)
+        packed = (packed + lax.ppermute(sent, "core", pair).astype(F32)).astype(BF)
         columns = columns.reshape(nh, nv, cols7, nc * mine)
         columns = jnp.where(high == 0, columns, columns[::-1])
         columns = columns.reshape(nh, nv, cols7, nc, mine).transpose(3, 2, 1, 0, 4)
@@ -442,6 +454,14 @@
         terms7 = dot(columns, all_hidden, ((1,), (0,)))
         own7 = jnp.where(core == 0, terms7[:cols7], terms7[cols7:])
         sent7 = jnp.where(core == 0, terms7[cols7:], terms7[:cols7])
+        packed = swap(packed, "gz")
+
+        runs = feats // part
+        dfeat = packs[:, :runs, part : 2 * part].reshape(half, half, chans).astype(F32)
+        dfeat = jnp.pad(dfeat, ((0, 0), (0, 1), (0, 0))).reshape(half * (half + 1), chans)
+        g_lines = conv_slope(conv_pre, dfeat).reshape(side, LINE, chans)[:, :side]
+        grad_images = conv_backward(bordered(g_lines), conv_weight, side)
+
         grad_fc7 = (own7 + lax.ppermute(sent7, "core", pair)).T
         packed, grad_fc7 = lax.optimization_barrier((packed, grad_fc7))
         packed = packed.astype(F32).sum(axis=0)

time: 216 us -> 190 us (0.88)
  blocking collectives: 32.3 us -> 0 us
  starting transfers between devices: 45 us -> 60.8 us
  waiting for transfers between devices: 80.7 us -> 68.9 us
  other arithmetic: 9.31 us -> 6.74 us
    all_gather x1, waiting for transfers between devices: 33.3 us -> 0.01 us  [on_device(): lax.all_gather(paired(image, 'xh', across), 'y', axis=0, tiled=True)]
    all_to_all x3 -> x0, blocking collectives: 32.3 us -> none  [swap(): return lax.all_to_all(value, axis, 0, 0, tiled=True)]
    all_to_all x6 -> x9, waiting for transfers between devices: 41.7 us -> 56.3 us  [swap(): return lax.all_to_all(value, axis, 0, 0, tiled=True)]
    all_gather x1, waiting for transfers between devices: 1.29 us -> 10.4 us  [on_device(): lax.all_gather(hidden, 'y', axis=0, tiled=False).reshape(group, rows7)]
    all_to_all x6 -> x9, starting transfers between devices: 36.6 us -> 45.7 us  [swap(): return lax.all_to_all(value, axis, 0, 0, tiled=True)]
    ppermute x1, starting transfers between devices: 0.39 us -> 7.46 us  [on_device(): lax.ppermute(sent6, 'core', pair)]
    ppermute x2, waiting for transfers between devices: 4.36 us -> 0.62 us  [paired(): return jnp.concatenate([value, lax.ppermute(value, axis, way)], axis=0)]
    unnamed x21 -> x19, local copies, waits for them, and re-layouts: 10.1 us -> 10.7 us
  transfers between devices with their start and end apart: 14 -> 18, of which waited for: 8 -> 11; matrix products, arithmetic and copies ran while one was open for 7% -> 9% of each run, Pallas kernels for 7% -> 7%
where the time goes in v9:
time: 190 us; the launch traced here: 189 us
  waiting for transfers between devices  68.9 us (36%)
  starting transfers between devices  60.8 us (32%)
  local copies, waits for them, and re-layouts  18.3 us (10%)
  Pallas kernels  17.3 us (9%)
  between operations  14.1 us (7%)
  other arithmetic  6.74 us (4%)
  matrix products  2.52 us (1%)
    all_to_all x9, waiting for transfers between devices, swap(): return lax.all_to_all(value, axis, 0, 0, tiled=True)  56.3 us
    all_to_all x9, starting transfers between devices, swap(): return lax.all_to_all(value, axis, 0, 0, tiled=True)  45.7 us
    unnamed x19, local copies, waits for them, and re-layouts  10.7 us
    all_gather x1, waiting for transfers between devices, on_device(): lax.all_gather(hidden, 'y', axis=0, tiled=False).reshape(group, rows7)  10.4 us
    ppermute x1, starting transfers between devices, on_device(): lax.ppermute(sent6, 'core', pair)  7.46 us
    pad x3, local copies, waits for them, and re-layouts, bordered(): padded = jnp.pad(maps, ((1, 3), (1, LINE - side - 1), (0, 0)))  4.83 us
    pallas_call x2, Pallas kernels, weight_terms(): pl.pallas_call(outer_kernel if more is None else outer_add_kernel, in_spe...  4.01 us
  transfers between devices with their start and end apart: 18, of which 11 were waited for; matrix products, arithmetic and copies ran while one was open for 9% of the time, Pallas kernels for 7%

profile of v9, /device:TPU:1, one launch (start us, length us, event | category | flops | bytes accessed | tf_op | source)
XLA Modules:
  0.0 188.6 jit_solution(1783658685497030068)
XLA Ops:
  7.2 1.6 pad_maximum_fusion.3
  8.8 3.3 %collective-permute-start = (bf16[3136,128]{1,0:T(8,128)(2,1)}, bf16[3136,128]{1,0:T(8,128)(2,1)S(1)}, u32[]{:S(2)}, u32[]{:S(2)}) collective-permute-start(bf16[3136,128]{1,0:T(8,128)(2,1)} %param.7), channel_id=1, source_target_pairs={{0,1},{1,0},{2,3},{3,2},{4,5},{5,4},{6,7},{7,6},{8,9},{9,8},{10,11... | collective-permute-start | bytes 2408456 | tf_op jit(solution)/shard_map/ppermute | solution.py:402
  12.2 1.0 pad.20
  13.2 2.3 %copy-done = bf16[4608,512]{1,0:T(8,128)(2,1)S(1)} copy-done((bf16[4608,512]{1,0:T(8,128)(2,1)S(1)}, bf16[4608,512]{1,0:T(8,128)(2,1)}, u32[]{:S(2)}) %copy-start) | copy-done | bytes 4718616
  15.5 2.3 %shard_map.84 = (f32[224,512]{1,0:T(8,128)S(1)}, bf16[8,3136]{1,0:T(8,128)(2,1)S(1)}) custom-call(bf16[288,512]{1,0:T(8,128)(2,1)S(1)} %bitcast.44, bf16[4608,512]{1,0:T(8,128)(2,1)S(1)} %copy-done), custom_call_target="tpu_custom_call" | custom-call | flops 1056964608 | bytes 4718592 | tf_op jit(solution)/shard_map/pallas_call | solution.py:81
  17.8 1.1 collective-permute-start.2
  18.9 0.5 broadcast.165
  19.4 0.7 reduce
  20.1 0.7 reshape.99
  20.8 4.2 %all-to-all-start = ((bf16[8,2,1568]{2,1,0:T(2,128)(2,1)}), bf16[8,2,1568]{2,1,0:T(2,128)(2,1)S(1)}, u32[]{:S(2)}, u32[]{:S(2)}) async-start(bf16[8,2,1568]{2,1,0:T(2,128)(2,1)} %reshape.99), calls=%async_computation | async-start | bytes 106496 | tf_op jit(solution)/shard_map/all_to_all | solution.py:360
  25.0 6.7 %all-to-all-done = bf16[8,2,1568]{2,1,0:T(2,128)(2,1)S(1)} async-done(((bf16[8,2,1568]{2,1,0:T(2,128)(2,1)}), bf16[8,2,1568]{2,1,0:T(2,128)(2,1)S(1)}, u32[]{:S(2)}, u32[]{:S(2)}) %all-to-all-start) | async-done | bytes 50208 | tf_op jit(solution)/shard_map/all_to_all | solution.py:360
  31.7 0.1 reshape.100
  31.8 0.9 broadcast_in_dim.11
  32.8 9.3 %all-to-all-start.1 = ((bf16[16,8,3136]{2,1,0:T(8,128)(2,1)}), bf16[16,8,3136]{2,1,0:T(8,128)(2,1)S(1)}, u32[]{:S(2)}, u32[]{:S(2)}) async-start(bf16[16,8,3136]{2,1,0:T(8,128)(2,1)} %broadcast_in_dim.11), calls=%async_computation.1 | async-start | bytes 1638400 | tf_op jit(solution)/shard_map/all_to_all | solution.py:360
  42.1 0.8 pad_maximum_fusion.1
  43.0 0.1 broadcast_select_fusion.1
  43.1 0.2 pad_maximum_fusion.weight_ref
  43.3 17.6 %all-to-all-done.1 = bf16[16,8,3136]{2,1,0:T(8,128)(2,1)S(1)} async-done(((bf16[16,8,3136]{2,1,0:T(8,128)(2,1)}), bf16[16,8,3136]{2,1,0:T(8,128)(2,1)S(1)}, u32[]{:S(2)}, u32[]{:S(2)}) %all-to-all-start.1) | async-done | bytes 802848 | tf_op jit(solution)/shard_map/all_to_all | solution.py:360
  60.9 1.0 convolution_convert_fusion
  62.0 3.5 %all-to-all-start.2 = ((bf16[8,16,256]{2,1,0:T(8,128)(2,1)}), bf16[8,16,256]{2,1,0:T(8,128)(2,1)S(1)}, u32[]{:S(2)}, u32[]{:S(2)}) async-start(bf16[8,16,256]{2,1,0:T(8,128)(2,1)} %bitcast.9), calls=%async_computation.2 | async-start | bytes 131072 | tf_op jit(solution)/shard_map/all_to_all | solution.py:360
  65.4 6.7 %all-to-all-done.2 = bf16[8,16,256]{2,1,0:T(8,128)(2,1)S(1)} async-done(((bf16[8,16,256]{2,1,0:T(8,128)(2,1)}), bf16[8,16,256]{2,1,0:T(8,128)(2,1)S(1)}, u32[]{:S(2)}, u32[]{:S(2)}) %all-to-all-start.2) | async-done | bytes 65568 | tf_op jit(solution)/shard_map/all_to_all | solution.py:360
  72.1 0.7 broadcast_in_dim.12
  72.8 6.2 %all-to-all-start.3 = ((bf16[16,16,256]{2,1,0:T(8,128)(2,1)}), bf16[16,16,256]{2,1,0:T(8,128)(2,1)S(1)}, u32[]{:S(2)}, u32[]{:S(2)}) async-start(bf16[16,16,256]{2,1,0:T(8,128)(2,1)} %broadcast_in_dim.12), calls=%async_computation.3 | async-start | bytes 262144 | tf_op jit(solution)/shard_map/all_to_all | solution.py:360
  79.0 7.4 %all-to-all-done.3.hidden_ref = bf16[16,16,256]{2,1,0:T(8,128)(2,1)S(1)} async-done(((bf16[16,16,256]{2,1,0:T(8,128)(2,1)}), bf16[16,16,256]{2,1,0:T(8,128)(2,1)S(1)}, u32[]{:S(2)}, u32[]{:S(2)}) %all-to-all-start.3) | async-done | bytes 131104 | tf_op jit(solution)/shard_map/all_to_all | solution.py:360
  86.4 1.6 copy-done.3
  88.1 1.8 shard_map.85
  89.8 1.3 collective-permute-start.1
  91.2 3.5 %all-to-all-start.4 = ((bf16[16,16,256]{2,1,0:T(8,128)(2,1)}), bf16[16,16,256]{2,1,0:T(8,128)(2,1)S(1)}, u32[]{:S(2)}, u32[]{:S(2)}) async-start(bf16[16,16,256]{2,1,0:T(8,128)(2,1)} %get-tuple-element.31), calls=%async_computation.4 | async-start | bytes 262144 | tf_op jit(solution)/shard_map/all_to_all | solution.py:360
  94.7 0.6 collective-permute-done.1
  95.3 0.7 pad_maximum_fusion.2
  96.0 6.0 %all-to-all-done.4 = bf16[16,16,256]{2,1,0:T(8,128)(2,1)S(1)} async-done(((bf16[16,16,256]{2,1,0:T(8,128)(2,1)}), bf16[16,16,256]{2,1,0:T(8,128)(2,1)S(1)}, u32[]{:S(2)}, u32[]{:S(2)}) %all-to-all-start.4) | async-done | bytes 131104 | tf_op jit(solution)/shard_map/all_to_all | solution.py:360
  102.1 0.7 fusion.2
  102.8 4.1 %all-to-all-start.5 = ((bf16[8,16,384]{2,1,0:T(8,128)(2,1)}), bf16[8,16,384]{2,1,0:T(8,128)(2,1)S(1)}, u32[]{:S(2)}, u32[]{:S(2)}) async-start(bf16[8,16,384]{2,1,0:T(8,128)(2,1)} %fusion.2), calls=%async_computation.5 | async-start | bytes 196608 | tf_op jit(solution)/shard_map/all_to_all | solution.py:360
  106.9 6.8 %all-to-all-done.5 = bf16[8,16,384]{2,1,0:T(8,128)(2,1)S(1)} async-done(((bf16[8,16,384]{2,1,0:T(8,128)(2,1)}), bf16[8,16,384]{2,1,0:T(8,128)(2,1)S(1)}, u32[]{:S(2)}, u32[]{:S(2)}) %all-to-all-start.5) | async-done | bytes 98336 | tf_op jit(solution)/shard_map/all_to_all | solution.py:360
  113.7 1.6 shard_map.86
  115.3 3.6 %all-to-all-start.6 = ((bf16[16,8,3136]{2,1,0:T(8,128)(2,1)}), bf16[16,8,3136]{2,1,0:T(8,128)(2,1)S(1)}, u32[]{:S(2)}, u32[]{:S(2)}) async-start(bf16[16,8,3136]{2,1,0:T(8,128)(2,1)} %bitcast.14), calls=%async_computation.6 | async-start | bytes 1638400 | tf_op jit(solution)/shard_map/all_to_all | solution.py:360
  118.9 0.7 all-gather.10.cloned.1.call-update
  119.7 1.3 shard_map.87
  121.0 7.5 %collective-permute-start.5 = (bf16[3136,128]{1,0:T(8,128)(2,1)}, bf16[3136,128]{1,0:T(8,128)(2,1)}, u32[]{:S(2)}, u32[]{:S(2)}) collective-permute-start(bf16[3136,128]{1,0:T(8,128)(2,1)} %shard_map.87), channel_id=1, source_target_pairs={{0,1},{1,0},{2,3},{3,2},{4,5},{5,4},{6,7},{7,6},{8,9},{9,8},{10,11... | collective-permute-start | bytes 2408456 | tf_op jit(solution)/shard_map/ppermute | solution.py:445
  128.5 0.2 shard_map.88
  128.8 0.1 fusion.19.spread_ref
  128.9 3.6 %all-to-all-done.6.terms_ref = bf16[16,8,3136]{2,1,0:T(8,128)(2,1)S(1)} async-done(((bf16[16,8,3136]{2,1,0:T(8,128)(2,1)}), bf16[16,8,3136]{2,1,0:T(8,128)(2,1)S(1)}, u32[]{:S(2)}, u32[]{:S(2)}) %all-to-all-start.6) | async-done | bytes 802848 | tf_op jit(solution)/shard_map/all_to_all | solution.py:360
  132.5 1.0 shard_map.89
  133.6 3.6 %all-to-all-start.7 = ((bf16[8,64,384]{2,1,0:T(8,128)(2,1)}), bf16[8,64,384]{2,1,0:T(8,128)(2,1)S(1)}, u32[]{:S(2)}, u32[]{:S(2)}) async-start(bf16[8,64,384]{2,1,0:T(8,128)(2,1)} %shard_map.89), calls=%async_computation.7 | async-start | bytes 786432 | tf_op jit(solution)/shard_map/all_to_all | solution.py:360
  137.4 0.1 reshape.87
  137.5 3.8 %pad.22 = bf16[8,18,16,512]{3,2,1,0:T(8,128)(2,1)} pad(bf16[8,14,14,512]{3,2,1,0:T(8,128)(2,1)} %all-gather.6.cloned.1.call-done, bf16[]{:T(256)} %constant.111.clone.1), padding=0_0x1_3x1_1x0_0 | pad | bytes 3964930 | tf_op jit(solution)/shard_map/vmap(jit(_pad))/pad | solution.py:369
  141.3 2.7 %shard_map.91 = f32[3136,128]{1,0:T(8,128)} custom-call(s32[1]{0:T(128)} %bitcast.1.which_ref, bf16[128,3136]{1,0:T(8,128)(2,1)S(1)} %bitcast.41, bf16[128,256]{1,0:T(8,128)(2,1)S(1)} %bitcast.49, bf16[3136,128]{1,0:T(8,128)(2,1)} %collective-permute-done.5.more_ref), custom_call_target="tpu_custom_call" | custom-call | flops 1000 | bytes 1000 | tf_op jit(solution)/shard_map/pallas_call | solution.py:209
  144.0 10.4 %all-gather.10.cloned.1.call-done = bf16[128,4096]{1,0:T(8,128)(2,1)} async-done(((bf16[32,4096]{1,0:T(8,128)(2,1)}), bf16[128,4096]{1,0:T(8,128)(2,1)}) %all-gather.10.cloned.1.call-update) | async-done | bytes 1048592 | tf_op jit(solution)/shard_map/all_gather | solution.py:427
  154.4 1.5 fusion.24
  155.9 1.7 copy-done.2
  157.5 2.7 %shard_map.90 = (f32[16,72,128]{2,1,0:T(8,128)S(1)}, bf16[16,72,128]{2,1,0:T(8,128)(2,1)S(1)}) custom-call(s32[2]{0:T(128)S(1)} %pad_add_fusion.place_ref, bf16[8,288,512]{2,1,0:T(8,128)(2,1)S(1)} %bitcast.42, bf16[8,64,384]{2,1,0:T(8,128)(2,1)S(1)} %all-to-all-done.7.packs_ref, bf16[64,256]{1,0:T(8,128)(2,1)S(1)} %fusion.19.spread_ref), custom_call_target="tpu_custom_call" | custom-call | flops 1207959552 | bytes 2359296 | tf_op jit(solution)/shard_map/pallas_call | solution.py:292
  160.3 1.8 collective-permute-start.3
  162.1 0.1 collective-permute-start.4
  162.3 0.1 convert_element_type.57
  162.4 0.8 collective-permute-done.3
  163.2 0.8 add_convert_fusion
  164.0 7.7 %all-to-all-start.8 = ((bf16[16,72,128]{2,1,0:T(8,128)(2,1)}), bf16[16,72,128]{2,1,0:T(8,128)(2,1)S(1)}, u32[]{:S(2)}, u32[]{:S(2)}) async-start(bf16[16,72,128]{2,1,0:T(8,128)(2,1)} %add_convert_fusion), calls=%async_computation.8 | async-start | bytes 589824 | tf_op jit(solution)/shard_map/all_to_all | solution.py:360
  171.7 0.8 add_bitcast_fusion
  172.5 0.2 shard_map.92
  172.8 2.3 %copy-done.1 = bf16[4608,512]{1,0:T(8,128)(2,1)S(1)} copy-done((bf16[4608,512]{1,0:T(8,128)(2,1)S(1)}, bf16[4608,512]{1,0:T(8,128)(2,1)}, u32[]{:S(2)}) %copy-start.1) | copy-done | bytes 4718616
  175.1 3.5 %shard_map.93 = f32[1,14,14,512]{3,2,1,0:T(8,128)S(1)} custom-call(bf16[288,512]{1,0:T(8,128)(2,1)S(1)} %bitcast.46, bf16[4608,512]{1,0:T(8,128)(2,1)S(1)} %copy-done.1), custom_call_target="tpu_custom_call" | custom-call | flops 1000 | bytes 1000 | tf_op jit(solution)/shard_map/pallas_call | solution.py:333
  178.6 1.2 copy.30
  179.8 1.5 all-to-all-done.8
  181.4 0.7 copy.29
  (53 shorter events, 1.0 us)
Async XLA Ops:
  7.2 79.3 %all-gather.8.cloned.1.call-start = ((), (), s32[]{:S(2)}) async-start(), calls=%async_computation.10 | async-start | bytes 2367488 | tf_op jit(solution)/shard_map/all_gather | solution.py:400
  8.8 34.2 %collective-permute-start = (bf16[3136,128]{1,0:T(8,128)(2,1)}, bf16[3136,128]{1,0:T(8,128)(2,1)S(1)}, u32[]{:S(2)}, u32[]{:S(2)}) collective-permute-start(bf16[3136,128]{1,0:T(8,128)(2,1)} %param.7), channel_id=1, source_target_pairs={{0,1},{1,0},{2,3},{3,2},{4,5},{5,4},{6,7},{7,6},{8,9},{9,8},{10,11... | collective-permute-start | bytes 2408456 | tf_op jit(solution)/shard_map/ppermute | solution.py:402
  13.2 2.3 %copy-start = (bf16[4608,512]{1,0:T(8,128)(2,1)S(1)}, bf16[4608,512]{1,0:T(8,128)(2,1)}, u32[]{:S(2)}) copy-start(bf16[4608,512]{1,0:T(8,128)(2,1)} %weight_ref.3) | copy-start | bytes 14155780
  15.5 2.3 %copy-start.4 = (bf16[1,14,14,512]{3,2,1,0:T(8,128)(2,1)S(1)}, bf16[1,14,14,512]{3,2,1,0:T(8,128)(2,1)}, u32[]{:S(2)}) copy-start(bf16[1,14,14,512]{3,2,1,0:T(8,128)(2,1)} %param.5) | copy-start | bytes 602116
  17.8 24.3 %collective-permute-start.2 = (bf16[1,14,14,512]{3,2,1,0:T(8,128)(2,1)S(1)}, bf16[1,14,14,512]{3,2,1,0:T(8,128)(2,1)S(1)}, u32[]{:S(2)}, u32[]{:S(2)}) collective-permute-start(bf16[1,14,14,512]{3,2,1,0:T(8,128)(2,1)S(1)} %copy-done.4), channel_id=1, source_target_pairs={{0,128},{128,0},{1,129},{129,1},{2,130},{130,2},{3,131},{131,3},{4... | collective-permute-start | bytes 602120 | tf_op jit(solution)/shard_map/ppermute | solution.py:381
  20.8 10.9 %all-to-all-start = ((bf16[8,2,1568]{2,1,0:T(2,128)(2,1)}), bf16[8,2,1568]{2,1,0:T(2,128)(2,1)S(1)}, u32[]{:S(2)}, u32[]{:S(2)}) async-start(bf16[8,2,1568]{2,1,0:T(2,128)(2,1)} %reshape.99), calls=%async_computation | async-start | bytes 106496 | tf_op jit(solution)/shard_map/all_to_all | solution.py:360
  32.8 10.2 %copy-start.5 = (bf16[3136,128]{1,0:T(8,128)(2,1)S(1)}, bf16[3136,128]{1,0:T(8,128)(2,1)}, u32[]{:S(2)}) copy-start(bf16[3136,128]{1,0:T(8,128)(2,1)} %param.7) | copy-start | bytes 2408452
  32.8 28.1 %all-to-all-start.1 = ((bf16[16,8,3136]{2,1,0:T(8,128)(2,1)}), bf16[16,8,3136]{2,1,0:T(8,128)(2,1)S(1)}, u32[]{:S(2)}, u32[]{:S(2)}) async-start(bf16[16,8,3136]{2,1,0:T(8,128)(2,1)} %broadcast_in_dim.11), calls=%async_computation.1 | async-start | bytes 1638400 | tf_op jit(solution)/shard_map/all_to_all | solution.py:360
  42.1 64.8 %all-gather.6.cloned.1.call-start = ((), (), s32[]{:S(2)}) async-start(), calls=%async_computation.9 | async-start | bytes 2293760 | tf_op jit(solution)/shard_map/all_gather | solution.py:407
  62.0 10.2 %all-to-all-start.2 = ((bf16[8,16,256]{2,1,0:T(8,128)(2,1)}), bf16[8,16,256]{2,1,0:T(8,128)(2,1)S(1)}, u32[]{:S(2)}, u32[]{:S(2)}) async-start(bf16[8,16,256]{2,1,0:T(8,128)(2,1)} %bitcast.9), calls=%async_computation.2 | async-start | bytes 131072 | tf_op jit(solution)/shard_map/all_to_all | solution.py:360
  72.8 13.6 %all-to-all-start.3 = ((bf16[16,16,256]{2,1,0:T(8,128)(2,1)}), bf16[16,16,256]{2,1,0:T(8,128)(2,1)S(1)}, u32[]{:S(2)}, u32[]{:S(2)}) async-start(bf16[16,16,256]{2,1,0:T(8,128)(2,1)} %broadcast_in_dim.12), calls=%async_computation.3 | async-start | bytes 262144 | tf_op jit(solution)/shard_map/all_to_all | solution.py:360
  86.4 1.6 copy-start.3
  89.8 5.5 %collective-permute-start.1 = (bf16[16,4096]{1,0:T(8,128)(2,1)S(1)}, bf16[16,4096]{1,0:T(8,128)(2,1)S(1)}, u32[]{:S(2)}, u32[]{:S(2)}) collective-permute-start(bf16[16,4096]{1,0:T(8,128)(2,1)S(1)} %bitcast.55), channel_id=1, source_target_pairs={{0,128},{128,0},{1,129},{129,1},{2,130},{130,2},{3,131},{131,3},{4... | collective-permute-start | bytes 393224 | tf_op jit(solution)/shard_map/ppermute | solution.py:381
  91.2 10.9 %all-to-all-start.4 = ((bf16[16,16,256]{2,1,0:T(8,128)(2,1)}), bf16[16,16,256]{2,1,0:T(8,128)(2,1)S(1)}, u32[]{:S(2)}, u32[]{:S(2)}) async-start(bf16[16,16,256]{2,1,0:T(8,128)(2,1)} %get-tuple-element.31), calls=%async_computation.4 | async-start | bytes 262144 | tf_op jit(solution)/shard_map/all_to_all | solution.py:360
  102.8 10.9 %all-to-all-start.5 = ((bf16[8,16,384]{2,1,0:T(8,128)(2,1)}), bf16[8,16,384]{2,1,0:T(8,128)(2,1)S(1)}, u32[]{:S(2)}, u32[]{:S(2)}) async-start(bf16[8,16,384]{2,1,0:T(8,128)(2,1)} %fusion.2), calls=%async_computation.5 | async-start | bytes 196608 | tf_op jit(solution)/shard_map/all_to_all | solution.py:360
  113.7 15.2 %copy-start.6 = (bf16[8,16,384]{2,1,0:T(8,128)(2,1)}, bf16[8,16,384]{2,1,0:T(8,128)(2,1)S(1)}, u32[]{:S(2)}) copy-start(bf16[8,16,384]{2,1,0:T(8,128)(2,1)S(1)} %all-to-all-done.5) | copy-start | bytes 294916
  115.3 17.3 %all-to-all-start.6 = ((bf16[16,8,3136]{2,1,0:T(8,128)(2,1)}), bf16[16,8,3136]{2,1,0:T(8,128)(2,1)S(1)}, u32[]{:S(2)}, u32[]{:S(2)}) async-start(bf16[16,8,3136]{2,1,0:T(8,128)(2,1)} %bitcast.14), calls=%async_computation.6 | async-start | bytes 1638400 | tf_op jit(solution)/shard_map/all_to_all | solution.py:360
  118.9 35.5 %all-gather.10.cloned.1.call-start = ((), (), s32[]{:S(2)}) async-start(), calls=%async_computation.11 | async-start | bytes 1310720 | tf_op jit(solution)/shard_map/all_gather | solution.py:427
  121.0 20.3 %collective-permute-start.5 = (bf16[3136,128]{1,0:T(8,128)(2,1)}, bf16[3136,128]{1,0:T(8,128)(2,1)}, u32[]{:S(2)}, u32[]{:S(2)}) collective-permute-start(bf16[3136,128]{1,0:T(8,128)(2,1)} %shard_map.87), channel_id=1, source_target_pairs={{0,1},{1,0},{2,3},{3,2},{4,5},{5,4},{6,7},{7,6},{8,9},{9,8},{10,11... | collective-permute-start | bytes 2408456 | tf_op jit(solution)/shard_map/ppermute | solution.py:445
  128.9 8.3 %slice-start = ((bf16[8,16,384]{2,1,0:T(8,128)(2,1)}), bf16[8,16,32]{2,1,0:T(8,128)(2,1)S(1)}, s32[]{:S(2)}) async-start(bf16[8,16,384]{2,1,0:T(8,128)(2,1)} %copy-done.6), calls=%async_computation.12 | async-start | bytes 65536 | tf_op jit(solution)/shard_map/slice | solution.py:436
  133.6 22.3 %all-to-all-start.7 = ((bf16[8,64,384]{2,1,0:T(8,128)(2,1)}), bf16[8,64,384]{2,1,0:T(8,128)(2,1)S(1)}, u32[]{:S(2)}, u32[]{:S(2)}) async-start(bf16[8,64,384]{2,1,0:T(8,128)(2,1)} %shard_map.89), calls=%async_computation.7 | async-start | bytes 786432 | tf_op jit(solution)/shard_map/all_to_all | solution.py:360
  155.9 1.7 copy-start.2
  160.3 3.0 %collective-permute-start.3 = (bf16[16,72,128]{2,1,0:T(8,128)(2,1)S(1)}, bf16[16,72,128]{2,1,0:T(8,128)(2,1)S(1)}, u32[]{:S(2)}, u32[]{:S(2)}) collective-permute-start(bf16[16,72,128]{2,1,0:T(8,128)(2,1)S(1)} %get-tuple-element.43), channel_id=1, source_target_pairs={{0,1},{1,0},{2,3},{3,2},{4,5},{5,4},{6,7},{7,6},{8,9},{9,8},{10,11... | collective-permute-start | bytes 884744 | tf_op jit(solution)/shard_map/ppermute | solution.py:449
  162.1 9.7 %collective-permute-start.4 = (f32[16,4096]{1,0:T(8,128)S(1)}, f32[16,4096]{1,0:T(8,128)S(1)}, u32[]{:S(2)}, u32[]{:S(2)}) collective-permute-start(f32[16,4096]{1,0:T(8,128)S(1)} %slice_select_fusion), channel_id=1, source_target_pairs={{0,1},{1,0},{2,3},{3,2},{4,5},{5,4},{6,7},{7,6},{8,9},{9,8},{10,11... | collective-permute-start | bytes 786440 | tf_op jit(solution)/shard_map/ppermute | solution.py:465
  164.0 17.2 %all-to-all-start.8 = ((bf16[16,72,128]{2,1,0:T(8,128)(2,1)}), bf16[16,72,128]{2,1,0:T(8,128)(2,1)S(1)}, u32[]{:S(2)}, u32[]{:S(2)}) async-start(bf16[16,72,128]{2,1,0:T(8,128)(2,1)} %add_convert_fusion), calls=%async_computation.8 | async-start | bytes 589824 | tf_op jit(solution)/shard_map/all_to_all | solution.py:360
  172.7 2.3 %copy-start.1 = (bf16[4608,512]{1,0:T(8,128)(2,1)S(1)}, bf16[4608,512]{1,0:T(8,128)(2,1)}, u32[]{:S(2)}) copy-start(bf16[4608,512]{1,0:T(8,128)(2,1)} %weight_ref.3) | copy-start | bytes 14155780
Sparse Core Ops, SparseCore 0:
  11.3 59.9 all-gather.7
  73.1 30.1 all-gather.5
  122.1 32.2 all-gather.9

commit v10 on v9

--- a/solution.py
+++ b/solution.py
@@ -59,25 +59,29 @@
     half = pix // 4
     side = pix // LINE // 2
     run = LANES // 2
-    runs = feat_ref.shape[1] // run
+    dests, rows, width = feat_ref.shape
+    runs = side * side * chans // (dests * run)
+    runs_ref[...] = jnp.zeros(runs_ref.shape, F32)
     for k in range(chans // LANES):
         pool_ref[k] = lines[:, k * LANES : (k + 1) * LANES]
         total = 0.25 * (pool_ref[k, pl.ds(0, half, 2), :] + pool_ref[k, pl.ds(1, half, 2), :])
         other = pltpu.roll(total, run, 1)
         for cell in range(side * side):
-            row = cell // side * (LINE // 2) + cell % side
+            line = cell // side * (LINE // 2) + cell % side
             for part in range(2):
                 dest, t = divmod(cell * (chans // run) + 2 * k + part, runs)
                 at = t % 2 * run
                 piece = total if t % 2 == part else other
-                runs_ref[dest : dest + 1, t * run : (t + 1) * run] = piece[row : row + 1, at : at + run]
-    feat_ref[...] = runs_ref[...].astype(BF)
+                row, lane = divmod(t * run, width)
+                row = dest * rows + row
+                runs_ref[row : row + 1, lane : lane + run] = piece[line : line + 1, at : at + run]
+    feat_ref[...] = runs_ref[...].astype(BF).reshape(dests, rows, width)
 
 
 def conv_forward(lines, weight, side, nx):
     depth, chans = lines.shape[1], weight.shape[1]
     pix = side * LINE
-    feats = side * side // 4 * chans // nx
+    rows, width = LINE, 2 * LANES
     return pl.pallas_call(
         forward_kernel,
         in_specs=[
@@ -86,18 +90,36 @@
         ],
         out_shape=[
             jax.ShapeDtypeStruct((pix, chans), F32),
-            jax.ShapeDtypeStruct((nx, feats), BF),
+            jax.ShapeDtypeStruct((nx, rows, width), BF),
         ],
         scratch_shapes=[
             pltpu.VMEM((3, 3 * depth, chans), BF),
             pltpu.VMEM((3, pix + LINE, chans), F32),
             pltpu.VMEM((chans // LANES, pix // 2, LANES), F32),
-            pltpu.VMEM((nx, feats), F32),
+            pltpu.VMEM((nx * rows, width), F32),
             pltpu.SemaphoreType.DMA((9,)),
         ],
         compiler_params=VMEM,
         cost_estimate=cost(18 * pix * depth * chans, weight.size * 2, pix * chans),
     )(lines, weight)
+
+
+def copies_kernel(feat_ref, out_ref):
+    feats = out_ref.shape[2]
+    _, rows, width = feat_ref.shape
+    value = feat_ref[...].astype(F32)
+    flat = jnp.concatenate([value[:, k, :] for k in range(rows)], axis=1)[:, :feats].astype(BF)
+    for k in range(out_ref.shape[0]):
+        out_ref[k] = flat
+
+
+def feature_copies(feat, count, feats):
+    return pl.pallas_call(
+        copies_kernel,
+        out_shape=jax.ShapeDtypeStruct((count, feat.shape[0], feats), BF),
+        compiler_params=VMEM,
+        cost_estimate=cost(feat.size, feat.size * 2 * count),
+    )(feat)
 
 
 def turn_kernel(pre_ref, out_ref):
@@ -403,9 +425,9 @@
         lines = bordered(images[0])
         conv_pre, feat = conv_forward(lines, conv_weight, side, nx)
         slopes = turned_slope(conv_pre, cols).reshape(nx, part, cols)
-        feat, image = lax.optimization_barrier((feat, images))
+        other6, image = lax.optimization_barrier((other6, images))
         gathered = lax.all_gather(paired(image, "xh", across), "y", axis=0, tiled=True)
-        inputs = share(swap(feat, gx), "gz", nz).reshape(group, feats)
+        inputs = swap(feature_copies(swap(feat, gx), nz, feats), "gz").reshape(group, feats)
         first = jnp.where(core == 0, fc6_weight, other6)
         second = jnp.where(core == 0, other6, fc6_weight)
         weight6 = jnp.concatenate([first, second], axis=1)
@@ -437,7 +459,7 @@
 
         feat_terms = features_back(g_six, weight6).reshape(nz, nx, feats)
         feat_terms, g_six = lax.optimization_barrier((feat_terms, g_six))
-        feat_terms = swap(feat_terms, "gz")
+        feat_terms, all_hidden = lax.optimization_barrier((swap(feat_terms, "gz"), all_hidden))
         sent6 = weight_terms(nc - 1 - core, inputs, g_six, units)
         packs = swap(pack_dfeat(me_word, feat_terms, slopes), gx)
         gathered, sent6 = lax.optimization_barrier((gathered, sent6))

time: 190 us -> 187 us (0.984)
  waiting for transfers between devices: 68.9 us -> 62.2 us
  other arithmetic: 6.74 us -> 9.36 us
  starting transfers between devices: 60.8 us -> 63.2 us
  local copies, waits for them, and re-layouts: 18.3 us -> 15.9 us
    all_to_all x9, waiting for transfers between devices: 56.3 us -> 39.3 us  [swap(): return lax.all_to_all(value, axis, 0, 0, tiled=True)]
    ppermute x2, waiting for transfers between devices: 0.62 us -> 10.8 us  [paired(): return jnp.concatenate([value, lax.ppermute(value, axis, way)], axis=0)]
    unnamed x19 -> x18, local copies, waits for them, and re-layouts: 10.7 us -> 9.85 us
  transfers between devices with their start and end apart: 18 -> 18, of which waited for: 11 -> 12; matrix products, arithmetic and copies ran while one was open for 9% -> 9% of each run, Pallas kernels for 7% -> 9%
where the time goes in v10:
time: 187 us; the launch traced here: 185 us
  starting transfers between devices  63.2 us (34%)
  waiting for transfers between devices  62.2 us (33%)
  Pallas kernels  19 us (10%)
  local copies, waits for them, and re-layouts  15.9 us (9%)
  between operations  14.1 us (8%)
  other arithmetic  9.36 us (5%)
    all_to_all x9, starting transfers between devices, swap(): return lax.all_to_all(value, axis, 0, 0, tiled=True)  46.7 us
    all_to_all x9, waiting for transfers between devices, swap(): return lax.all_to_all(value, axis, 0, 0, tiled=True)  39.3 us
    all_gather x1, waiting for transfers between devices, on_device(): lax.all_gather(hidden, 'y', axis=0, tiled=False).reshape(group, rows7)  11.2 us
    ppermute x2, waiting for transfers between devices, paired(): return jnp.concatenate([value, lax.ppermute(value, axis, way)], axis=0)  10.8 us
    unnamed x18, local copies, waits for them, and re-layouts  9.85 us
    ppermute x1, starting transfers between devices, on_device(): lax.ppermute(sent6, 'core', pair)  7.27 us
    pad x3, local copies, waits for them, and re-layouts, bordered(): padded = jnp.pad(maps, ((1, 3), (1, LINE - side - 1), (0, 0)))  4.76 us
    pallas_call x2, Pallas kernels, weight_terms(): pl.pallas_call(outer_kernel if more is None else outer_add_kernel, in_spe...  4.09 us
  transfers between devices with their start and end apart: 18, of which 12 were waited for; matrix products, arithmetic and copies ran while one was open for 9% of the time, Pallas kernels for 9%

profile of v10, /device:TPU:1, one launch (start us, length us, event | category | flops | bytes accessed | tf_op | source)
XLA Modules:
  0.0 185.0 jit_solution(14629566285198419196)
XLA Ops:
  7.2 1.6 pad_maximum_fusion.3
  8.8 3.3 %collective-permute-start = (bf16[3136,128]{1,0:T(8,128)(2,1)}, bf16[3136,128]{1,0:T(8,128)(2,1)S(1)}, u32[]{:S(2)}, u32[]{:S(2)}) collective-permute-start(bf16[3136,128]{1,0:T(8,128)(2,1)} %param.7), channel_id=1, source_target_pairs={{0,1},{1,0},{2,3},{3,2},{4,5},{5,4},{6,7},{7,6},{8,9},{9,8},{10,11... | collective-permute-start | bytes 2408456 | tf_op jit(solution)/shard_map/ppermute | solution.py:424
  12.2 1.0 pad.20
  13.2 2.3 %copy-done = bf16[4608,512]{1,0:T(8,128)(2,1)S(1)} copy-done((bf16[4608,512]{1,0:T(8,128)(2,1)S(1)}, bf16[4608,512]{1,0:T(8,128)(2,1)}, u32[]{:S(2)}) %copy-start) | copy-done | bytes 4718616
  15.5 2.9 %shard_map.84 = (f32[224,512]{1,0:T(8,128)S(1)}, bf16[8,16,256]{2,1,0:T(8,128)(2,1)}) custom-call(bf16[288,512]{1,0:T(8,128)(2,1)S(1)} %bitcast.40, bf16[4608,512]{1,0:T(8,128)(2,1)S(1)} %copy-done), custom_call_target="tpu_custom_call" | custom-call | flops 1056964608 | bytes 4718592 | tf_op jit(solution)/shard_map/pallas_call | solution.py:85
  18.4 5.1 %all-to-all-start = ((bf16[8,16,256]{2,1,0:T(8,128)(2,1)}), bf16[8,16,256]{2,1,0:T(8,128)(2,1)S(1)}, u32[]{:S(2)}, u32[]{:S(2)}) async-start(bf16[8,16,256]{2,1,0:T(8,128)(2,1)} %get-tuple-element.28), calls=%async_computation | async-start | bytes 131072 | tf_op jit(solution)/shard_map/all_to_all | solution.py:382
  23.5 6.7 %all-to-all-done.feat_ref = bf16[8,16,256]{2,1,0:T(8,128)(2,1)S(1)} async-done(((bf16[8,16,256]{2,1,0:T(8,128)(2,1)}), bf16[8,16,256]{2,1,0:T(8,128)(2,1)S(1)}, u32[]{:S(2)}, u32[]{:S(2)}) %all-to-all-start) | async-done | bytes 65568 | tf_op jit(solution)/shard_map/all_to_all | solution.py:382
  30.2 1.0 shard_map.85
  31.2 8.3 %all-to-all-start.1 = ((bf16[16,8,3136]{2,1,0:T(8,128)(2,1)}), bf16[16,8,3136]{2,1,0:T(8,128)(2,1)S(1)}, u32[]{:S(2)}, u32[]{:S(2)}) async-start(bf16[16,8,3136]{2,1,0:T(8,128)(2,1)} %shard_map.85), calls=%async_computation.1 | async-start | bytes 1638400 | tf_op jit(solution)/shard_map/all_to_all | solution.py:382
  39.5 1.2 collective-permute-start.2
  40.7 1.3 broadcast_select_fusion.1
  42.1 10.3 %collective-permute-done.2 = bf16[1,14,14,512]{3,2,1,0:T(8,128)(2,1)S(1)} collective-permute-done((bf16[1,14,14,512]{3,2,1,0:T(8,128)(2,1)S(1)}, bf16[1,14,14,512]{3,2,1,0:T(8,128)(2,1)S(1)}, u32[]{:S(2)}, u32[]{:S(2)}) %collective-permute-start.2) | collective-permute-done | bytes 200736 | tf_op jit(solution)/shard_map/ppermute | solution.py:403
  52.3 0.8 pad_maximum_fusion.1
  53.2 1.6 pad_maximum_fusion.weight_ref
  54.7 3.7 %all-to-all-done.1 = bf16[16,8,3136]{2,1,0:T(8,128)(2,1)S(1)} async-done(((bf16[16,8,3136]{2,1,0:T(8,128)(2,1)}), bf16[16,8,3136]{2,1,0:T(8,128)(2,1)S(1)}, u32[]{:S(2)}, u32[]{:S(2)}) %all-to-all-start.1) | async-done | bytes 802848 | tf_op jit(solution)/shard_map/all_to_all | solution.py:382
  58.4 1.0 convolution_convert_fusion
  59.4 3.9 %all-to-all-start.2 = ((bf16[8,16,256]{2,1,0:T(8,128)(2,1)}), bf16[8,16,256]{2,1,0:T(8,128)(2,1)S(1)}, u32[]{:S(2)}, u32[]{:S(2)}) async-start(bf16[8,16,256]{2,1,0:T(8,128)(2,1)} %bitcast.8), calls=%async_computation.2 | async-start | bytes 131072 | tf_op jit(solution)/shard_map/all_to_all | solution.py:382
  63.4 6.7 %all-to-all-done.2 = bf16[8,16,256]{2,1,0:T(8,128)(2,1)S(1)} async-done(((bf16[8,16,256]{2,1,0:T(8,128)(2,1)}), bf16[8,16,256]{2,1,0:T(8,128)(2,1)S(1)}, u32[]{:S(2)}, u32[]{:S(2)}) %all-to-all-start.2) | async-done | bytes 65568 | tf_op jit(solution)/shard_map/all_to_all | solution.py:382
  70.1 0.7 broadcast_in_dim.8
  70.8 6.0 %all-to-all-start.3 = ((bf16[16,16,256]{2,1,0:T(8,128)(2,1)}), bf16[16,16,256]{2,1,0:T(8,128)(2,1)S(1)}, u32[]{:S(2)}, u32[]{:S(2)}) async-start(bf16[16,16,256]{2,1,0:T(8,128)(2,1)} %broadcast_in_dim.8), calls=%async_computation.3 | async-start | bytes 262144 | tf_op jit(solution)/shard_map/all_to_all | solution.py:382
  76.8 7.4 %all-to-all-done.3.hidden_ref = bf16[16,16,256]{2,1,0:T(8,128)(2,1)S(1)} async-done(((bf16[16,16,256]{2,1,0:T(8,128)(2,1)}), bf16[16,16,256]{2,1,0:T(8,128)(2,1)S(1)}, u32[]{:S(2)}, u32[]{:S(2)}) %all-to-all-start.3) | async-done | bytes 131104 | tf_op jit(solution)/shard_map/all_to_all | solution.py:382
  84.2 1.6 copy-done.3
  85.8 1.8 shard_map.86
  87.6 1.4 collective-permute-start.1
  88.9 3.5 %all-to-all-start.4 = ((bf16[16,16,256]{2,1,0:T(8,128)(2,1)}), bf16[16,16,256]{2,1,0:T(8,128)(2,1)S(1)}, u32[]{:S(2)}, u32[]{:S(2)}) async-start(bf16[16,16,256]{2,1,0:T(8,128)(2,1)} %get-tuple-element.33), calls=%async_computation.4 | async-start | bytes 262144 | tf_op jit(solution)/shard_map/all_to_all | solution.py:382
  92.5 0.5 collective-permute-done.1
  93.0 0.7 pad_maximum_fusion.2
  93.7 6.1 %all-to-all-done.4 = bf16[16,16,256]{2,1,0:T(8,128)(2,1)S(1)} async-done(((bf16[16,16,256]{2,1,0:T(8,128)(2,1)}), bf16[16,16,256]{2,1,0:T(8,128)(2,1)S(1)}, u32[]{:S(2)}, u32[]{:S(2)}) %all-to-all-start.4) | async-done | bytes 131104 | tf_op jit(solution)/shard_map/all_to_all | solution.py:382
  99.9 0.7 fusion.2
  100.6 4.0 %all-to-all-start.5 = ((bf16[8,16,384]{2,1,0:T(8,128)(2,1)}), bf16[8,16,384]{2,1,0:T(8,128)(2,1)S(1)}, u32[]{:S(2)}, u32[]{:S(2)}) async-start(bf16[8,16,384]{2,1,0:T(8,128)(2,1)} %fusion.2), calls=%async_computation.5 | async-start | bytes 196608 | tf_op jit(solution)/shard_map/all_to_all | solution.py:382
  104.6 0.7 all-gather.10.cloned.1.call-update
  105.3 6.0 %all-to-all-done.5 = bf16[8,16,384]{2,1,0:T(8,128)(2,1)S(1)} async-done(((bf16[8,16,384]{2,1,0:T(8,128)(2,1)}), bf16[8,16,384]{2,1,0:T(8,128)(2,1)S(1)}, u32[]{:S(2)}, u32[]{:S(2)}) %all-to-all-start.5) | async-done | bytes 98336 | tf_op jit(solution)/shard_map/all_to_all | solution.py:382
  111.4 1.6 shard_map.87
  112.9 3.6 %all-to-all-start.6 = ((bf16[16,8,3136]{2,1,0:T(8,128)(2,1)}), bf16[16,8,3136]{2,1,0:T(8,128)(2,1)S(1)}, u32[]{:S(2)}, u32[]{:S(2)}) async-start(bf16[16,8,3136]{2,1,0:T(8,128)(2,1)} %bitcast.13), calls=%async_computation.6 | async-start | bytes 1638400 | tf_op jit(solution)/shard_map/all_to_all | solution.py:382
  116.6 1.3 shard_map.88
  117.9 7.3 %collective-permute-start.5 = (bf16[3136,128]{1,0:T(8,128)(2,1)}, bf16[3136,128]{1,0:T(8,128)(2,1)}, u32[]{:S(2)}, u32[]{:S(2)}) collective-permute-start(bf16[3136,128]{1,0:T(8,128)(2,1)} %shard_map.88), channel_id=1, source_target_pairs={{0,1},{1,0},{2,3},{3,2},{4,5},{5,4},{6,7},{7,6},{8,9},{9,8},{10,11... | collective-permute-start | bytes 2408456 | tf_op jit(solution)/shard_map/ppermute | solution.py:467
  125.2 0.2 shard_map.89
  125.5 0.1 fusion.19.spread_ref
  125.7 11.2 %all-gather.10.cloned.1.call-done = bf16[128,4096]{1,0:T(8,128)(2,1)} async-done(((bf16[32,4096]{1,0:T(8,128)(2,1)}), bf16[128,4096]{1,0:T(8,128)(2,1)}) %all-gather.10.cloned.1.call-update) | async-done | bytes 1048592 | tf_op jit(solution)/shard_map/all_gather | solution.py:449
  136.8 1.0 shard_map.90
  137.8 5.5 %all-to-all-start.7 = ((bf16[8,64,384]{2,1,0:T(8,128)(2,1)}), bf16[8,64,384]{2,1,0:T(8,128)(2,1)S(1)}, u32[]{:S(2)}, u32[]{:S(2)}) async-start(bf16[8,64,384]{2,1,0:T(8,128)(2,1)} %shard_map.90), calls=%async_computation.7 | async-start | bytes 786432 | tf_op jit(solution)/shard_map/all_to_all | solution.py:382
  143.4 0.1 reshape.85
  143.6 0.1 reshape.86
  143.7 3.7 %pad.22 = bf16[8,18,16,512]{3,2,1,0:T(8,128)(2,1)} pad(bf16[8,14,14,512]{3,2,1,0:T(8,128)(2,1)} %all-gather.6.cloned.1.call-done, bf16[]{:T(256)} %constant.111.clone.1), padding=0_0x1_3x1_1x0_0 | pad | bytes 3964930 | tf_op jit(solution)/shard_map/vmap(jit(_pad))/pad | solution.py:391
  147.4 2.8 %shard_map.92 = f32[3136,128]{1,0:T(8,128)} custom-call(s32[1]{0:T(128)} %bitcast.1.which_ref, bf16[128,3136]{1,0:T(8,128)(2,1)S(1)} %bitcast.37, bf16[128,256]{1,0:T(8,128)(2,1)S(1)} %bitcast.45, bf16[3136,128]{1,0:T(8,128)(2,1)} %collective-permute-done.5.more_ref), custom_call_target="tpu_custom_call" | custom-call | flops 1000 | bytes 1000 | tf_op jit(solution)/shard_map/pallas_call | solution.py:231
  150.2 0.3 fusion.24
  150.4 1.2 all-to-all-done.7.packs_ref
  151.6 1.7 copy-done.2
  153.3 2.7 %shard_map.91 = (f32[16,72,128]{2,1,0:T(8,128)S(1)}, bf16[16,72,128]{2,1,0:T(8,128)(2,1)S(1)}) custom-call(s32[2]{0:T(128)S(1)} %pad_add_fusion.place_ref, bf16[8,288,512]{2,1,0:T(8,128)(2,1)S(1)} %bitcast.38, bf16[8,64,384]{2,1,0:T(8,128)(2,1)S(1)} %all-to-all-done.7.packs_ref, bf16[64,256]{1,0:T(8,128)(2,1)S(1)} %fusion.19.spread_ref), custom_call_target="tpu_custom_call" | custom-call | flops 1207959552 | bytes 2359296 | tf_op jit(solution)/shard_map/pallas_call | solution.py:314
  156.0 3.2 %collective-permute-start.3 = (bf16[16,72,128]{2,1,0:T(8,128)(2,1)S(1)}, bf16[16,72,128]{2,1,0:T(8,128)(2,1)S(1)}, u32[]{:S(2)}, u32[]{:S(2)}) collective-permute-start(bf16[16,72,128]{2,1,0:T(8,128)(2,1)S(1)} %get-tuple-element.47), channel_id=1, source_target_pairs={{0,1},{1,0},{2,3},{3,2},{4,5},{5,4},{6,7},{7,6},{8,9},{9,8},{10,11... | collective-permute-start | bytes 884744 | tf_op jit(solution)/shard_map/ppermute | solution.py:471
  159.3 0.7 slice_select_fusion
  160.0 0.1 slice.38
  160.1 0.1 convert_element_type.57
  160.3 0.2 collective-permute-done.3
  160.5 0.8 add_convert_fusion
  161.3 6.8 %all-to-all-start.8 = ((bf16[16,72,128]{2,1,0:T(8,128)(2,1)}), bf16[16,72,128]{2,1,0:T(8,128)(2,1)S(1)}, u32[]{:S(2)}, u32[]{:S(2)}) async-start(bf16[16,72,128]{2,1,0:T(8,128)(2,1)} %add_convert_fusion), calls=%async_computation.8 | async-start | bytes 589824 | tf_op jit(solution)/shard_map/all_to_all | solution.py:382
  168.1 0.8 add_bitcast_fusion
  168.8 0.2 shard_map.93
  169.1 2.3 %copy-done.1 = bf16[4608,512]{1,0:T(8,128)(2,1)S(1)} copy-done((bf16[4608,512]{1,0:T(8,128)(2,1)S(1)}, bf16[4608,512]{1,0:T(8,128)(2,1)}, u32[]{:S(2)}) %copy-start.1) | copy-done | bytes 4718616
  171.4 3.5 %shard_map.94 = f32[1,14,14,512]{3,2,1,0:T(8,128)S(1)} custom-call(bf16[288,512]{1,0:T(8,128)(2,1)S(1)} %bitcast.42, bf16[4608,512]{1,0:T(8,128)(2,1)S(1)} %copy-done.1), custom_call_target="tpu_custom_call" | custom-call | flops 1000 | bytes 1000 | tf_op jit(solution)/shard_map/pallas_call | solution.py:355
  175.0 1.2 copy.23
  176.1 1.5 all-to-all-done.8
  177.7 0.1 fusion.23
  177.8 0.7 copy.22
  (50 shorter events, 0.7 us)
Async XLA Ops:
  7.2 77.0 %all-gather.8.cloned.1.call-start = ((), (), s32[]{:S(2)}) async-start(), calls=%async_computation.10 | async-start | bytes 2367488 | tf_op jit(solution)/shard_map/all_gather | solution.py:422
  8.8 30.7 %collective-permute-start = (bf16[3136,128]{1,0:T(8,128)(2,1)}, bf16[3136,128]{1,0:T(8,128)(2,1)S(1)}, u32[]{:S(2)}, u32[]{:S(2)}) collective-permute-start(bf16[3136,128]{1,0:T(8,128)(2,1)} %param.7), channel_id=1, source_target_pairs={{0,1},{1,0},{2,3},{3,2},{4,5},{5,4},{6,7},{7,6},{8,9},{9,8},{10,11... | collective-permute-start | bytes 2408456 | tf_op jit(solution)/shard_map/ppermute | solution.py:424
  13.2 2.3 %copy-start = (bf16[4608,512]{1,0:T(8,128)(2,1)S(1)}, bf16[4608,512]{1,0:T(8,128)(2,1)}, u32[]{:S(2)}) copy-start(bf16[4608,512]{1,0:T(8,128)(2,1)} %weight_ref.3) | copy-start | bytes 14155780
  18.4 21.1 %copy-start.5 = (bf16[1,14,14,512]{3,2,1,0:T(8,128)(2,1)S(1)}, bf16[1,14,14,512]{3,2,1,0:T(8,128)(2,1)}, u32[]{:S(2)}) copy-start(bf16[1,14,14,512]{3,2,1,0:T(8,128)(2,1)} %param.5) | copy-start | bytes 602116
  18.4 22.3 %copy-start.6 = (bf16[3136,128]{1,0:T(8,128)(2,1)S(1)}, bf16[3136,128]{1,0:T(8,128)(2,1)}, u32[]{:S(2)}) copy-start(bf16[3136,128]{1,0:T(8,128)(2,1)} %param.7) | copy-start | bytes 2408452
  18.4 11.8 %all-to-all-start = ((bf16[8,16,256]{2,1,0:T(8,128)(2,1)}), bf16[8,16,256]{2,1,0:T(8,128)(2,1)S(1)}, u32[]{:S(2)}, u32[]{:S(2)}) async-start(bf16[8,16,256]{2,1,0:T(8,128)(2,1)} %get-tuple-element.28), calls=%async_computation | async-start | bytes 131072 | tf_op jit(solution)/shard_map/all_to_all | solution.py:382
  31.2 27.3 %all-to-all-start.1 = ((bf16[16,8,3136]{2,1,0:T(8,128)(2,1)}), bf16[16,8,3136]{2,1,0:T(8,128)(2,1)S(1)}, u32[]{:S(2)}, u32[]{:S(2)}) async-start(bf16[16,8,3136]{2,1,0:T(8,128)(2,1)} %shard_map.85), calls=%async_computation.1 | async-start | bytes 1638400 | tf_op jit(solution)/shard_map/all_to_all | solution.py:382
  39.5 65.8 %all-gather.6.cloned.1.call-start = ((), (), s32[]{:S(2)}) async-start(), calls=%async_computation.9 | async-start | bytes 2293760 | tf_op jit(solution)/shard_map/all_gather | solution.py:429
  39.5 12.8 %collective-permute-start.2 = (bf16[1,14,14,512]{3,2,1,0:T(8,128)(2,1)S(1)}, bf16[1,14,14,512]{3,2,1,0:T(8,128)(2,1)S(1)}, u32[]{:S(2)}, u32[]{:S(2)}) collective-permute-start(bf16[1,14,14,512]{3,2,1,0:T(8,128)(2,1)S(1)} %copy-done.5), channel_id=1, source_target_pairs={{0,128},{128,0},{1,129},{129,1},{2,130},{130,2},{3,131},{131,3},{4... | collective-permute-start | bytes 602120 | tf_op jit(solution)/shard_map/ppermute | solution.py:403
  59.4 10.6 %all-to-all-start.2 = ((bf16[8,16,256]{2,1,0:T(8,128)(2,1)}), bf16[8,16,256]{2,1,0:T(8,128)(2,1)S(1)}, u32[]{:S(2)}, u32[]{:S(2)}) async-start(bf16[8,16,256]{2,1,0:T(8,128)(2,1)} %bitcast.8), calls=%async_computation.2 | async-start | bytes 131072 | tf_op jit(solution)/shard_map/all_to_all | solution.py:382
  70.8 13.4 %all-to-all-start.3 = ((bf16[16,16,256]{2,1,0:T(8,128)(2,1)}), bf16[16,16,256]{2,1,0:T(8,128)(2,1)S(1)}, u32[]{:S(2)}, u32[]{:S(2)}) async-start(bf16[16,16,256]{2,1,0:T(8,128)(2,1)} %broadcast_in_dim.8), calls=%async_computation.3 | async-start | bytes 262144 | tf_op jit(solution)/shard_map/all_to_all | solution.py:382
  84.2 1.6 copy-start.3
  87.6 5.4 %collective-permute-start.1 = (bf16[16,4096]{1,0:T(8,128)(2,1)S(1)}, bf16[16,4096]{1,0:T(8,128)(2,1)S(1)}, u32[]{:S(2)}, u32[]{:S(2)}) collective-permute-start(bf16[16,4096]{1,0:T(8,128)(2,1)S(1)} %bitcast.50), channel_id=1, source_target_pairs={{0,128},{128,0},{1,129},{129,1},{2,130},{130,2},{3,131},{131,3},{4... | collective-permute-start | bytes 393224 | tf_op jit(solution)/shard_map/ppermute | solution.py:403
  88.9 10.9 %all-to-all-start.4 = ((bf16[16,16,256]{2,1,0:T(8,128)(2,1)}), bf16[16,16,256]{2,1,0:T(8,128)(2,1)S(1)}, u32[]{:S(2)}, u32[]{:S(2)}) async-start(bf16[16,16,256]{2,1,0:T(8,128)(2,1)} %get-tuple-element.33), calls=%async_computation.4 | async-start | bytes 262144 | tf_op jit(solution)/shard_map/all_to_all | solution.py:382
  100.6 10.8 %all-to-all-start.5 = ((bf16[8,16,384]{2,1,0:T(8,128)(2,1)}), bf16[8,16,384]{2,1,0:T(8,128)(2,1)S(1)}, u32[]{:S(2)}, u32[]{:S(2)}) async-start(bf16[8,16,384]{2,1,0:T(8,128)(2,1)} %fusion.2), calls=%async_computation.5 | async-start | bytes 196608 | tf_op jit(solution)/shard_map/all_to_all | solution.py:382
  104.6 32.2 %all-gather.10.cloned.1.call-start = ((), (), s32[]{:S(2)}) async-start(), calls=%async_computation.11 | async-start | bytes 1310720 | tf_op jit(solution)/shard_map/all_gather | solution.py:449
  111.4 14.3 %copy-start.7 = (bf16[8,16,384]{2,1,0:T(8,128)(2,1)}, bf16[8,16,384]{2,1,0:T(8,128)(2,1)S(1)}, u32[]{:S(2)}) copy-start(bf16[8,16,384]{2,1,0:T(8,128)(2,1)S(1)} %all-to-all-done.5) | copy-start | bytes 294916
  112.9 23.9 %all-to-all-start.6 = ((bf16[16,8,3136]{2,1,0:T(8,128)(2,1)}), bf16[16,8,3136]{2,1,0:T(8,128)(2,1)S(1)}, u32[]{:S(2)}, u32[]{:S(2)}) async-start(bf16[16,8,3136]{2,1,0:T(8,128)(2,1)} %bitcast.13), calls=%async_computation.6 | async-start | bytes 1638400 | tf_op jit(solution)/shard_map/all_to_all | solution.py:382
  117.9 29.5 %collective-permute-start.5 = (bf16[3136,128]{1,0:T(8,128)(2,1)}, bf16[3136,128]{1,0:T(8,128)(2,1)}, u32[]{:S(2)}, u32[]{:S(2)}) collective-permute-start(bf16[3136,128]{1,0:T(8,128)(2,1)} %shard_map.88), channel_id=1, source_target_pairs={{0,1},{1,0},{2,3},{3,2},{4,5},{5,4},{6,7},{7,6},{8,9},{9,8},{10,11... | collective-permute-start | bytes 2408456 | tf_op jit(solution)/shard_map/ppermute | solution.py:467
  125.6 17.7 %slice-start = ((bf16[8,16,384]{2,1,0:T(8,128)(2,1)}), bf16[8,16,32]{2,1,0:T(8,128)(2,1)S(1)}, s32[]{:S(2)}) async-start(bf16[8,16,384]{2,1,0:T(8,128)(2,1)} %copy-done.7), calls=%async_computation.12 | async-start | bytes 65536 | tf_op jit(solution)/shard_map/slice | solution.py:458
  137.8 13.8 %all-to-all-start.7 = ((bf16[8,64,384]{2,1,0:T(8,128)(2,1)}), bf16[8,64,384]{2,1,0:T(8,128)(2,1)S(1)}, u32[]{:S(2)}, u32[]{:S(2)}) async-start(bf16[8,64,384]{2,1,0:T(8,128)(2,1)} %shard_map.90), calls=%async_computation.7 | async-start | bytes 786432 | tf_op jit(solution)/shard_map/all_to_all | solution.py:382
  147.4 2.8 %copy-start.4 = (bf16[128,4096]{1,0:T(8,128)(2,1)S(1)}, bf16[128,4096]{1,0:T(8,128)(2,1)}, u32[]{:S(2)}) copy-start(bf16[128,4096]{1,0:T(8,128)(2,1)} %all-gather.10.cloned.1.call-done) | copy-start | bytes 3145732
  151.6 1.7 copy-start.2
  156.0 4.5 %collective-permute-start.3 = (bf16[16,72,128]{2,1,0:T(8,128)(2,1)S(1)}, bf16[16,72,128]{2,1,0:T(8,128)(2,1)S(1)}, u32[]{:S(2)}, u32[]{:S(2)}) collective-permute-start(bf16[16,72,128]{2,1,0:T(8,128)(2,1)S(1)} %get-tuple-element.47), channel_id=1, source_target_pairs={{0,1},{1,0},{2,3},{3,2},{4,5},{5,4},{6,7},{7,6},{8,9},{9,8},{10,11... | collective-permute-start | bytes 884744 | tf_op jit(solution)/shard_map/ppermute | solution.py:471
  160.0 8.1 %collective-permute-start.4 = (f32[16,4096]{1,0:T(8,128)}, f32[16,4096]{1,0:T(8,128)S(1)}, u32[]{:S(2)}, u32[]{:S(2)}) collective-permute-start(f32[16,4096]{1,0:T(8,128)} %slice_select_fusion), channel_id=1, source_target_pairs={{0,1},{1,0},{2,3},{3,2},{4,5},{5,4},{6,7},{7,6},{8,9},{9,8},{10,11... | collective-permute-start | bytes 786440 | tf_op jit(solution)/shard_map/ppermute | solution.py:487
  161.3 16.4 %all-to-all-start.8 = ((bf16[16,72,128]{2,1,0:T(8,128)(2,1)}), bf16[16,72,128]{2,1,0:T(8,128)(2,1)S(1)}, u32[]{:S(2)}, u32[]{:S(2)}) async-start(bf16[16,72,128]{2,1,0:T(8,128)(2,1)} %add_convert_fusion), calls=%async_computation.8 | async-start | bytes 589824 | tf_op jit(solution)/shard_map/all_to_all | solution.py:382
  169.1 2.3 %copy-start.1 = (bf16[4608,512]{1,0:T(8,128)(2,1)S(1)}, bf16[4608,512]{1,0:T(8,128)(2,1)}, u32[]{:S(2)}) copy-start(bf16[4608,512]{1,0:T(8,128)(2,1)} %weight_ref.3) | copy-start | bytes 14155780
Sparse Core Ops, SparseCore 0:
  11.3 59.5 all-gather.7
  72.7 29.0 all-gather.5
  107.8 28.9 all-gather.9

commit v11 on v10

--- a/solution.py
+++ b/solution.py
@@ -32,9 +32,11 @@
     return pl.CostEstimate(flops=flops, bytes_accessed=moved, transcendentals=special)
 
 
-def forward_kernel(image_ref, weight_ref, pre_ref, feat_ref, held_ref, sums_ref, pool_ref, runs_ref, sems):
+def forward_kernel(
+    maps_ref, weight_ref, pre_ref, feat_ref, held_ref, lines_ref, sums_ref, pool_ref, runs_ref, sems
+):
     pix, chans = pre_ref.shape
-    depth = image_ref.shape[1]
+    _, height, width, depth = maps_ref.shape
     rows = sums_ref.shape[1]
 
     def load(tap):
@@ -47,7 +49,12 @@
     order = [3 * row + col for col in range(3) for row in range(3)]
     for tap in order:
         load(tap).start()
-    image = jnp.concatenate([image_ref[k * LINE : k * LINE + rows, :] for k in range(3)], axis=1)
+    lines_ref[...] = jnp.zeros(lines_ref.shape, F32)
+    for k in range(height):
+        at = (k + 1) * LINE + 1
+        lines_ref[at : at + width, :] = maps_ref[0, k].astype(F32)
+    image = [lines_ref[k * LINE : k * LINE + rows, :].astype(BF) for k in range(3)]
+    image = jnp.concatenate(image, axis=1)
     for col in range(3):
         for row in range(3):
             load(3 * row + col).wait()
@@ -59,7 +66,7 @@
     half = pix // 4
     side = pix // LINE // 2
     run = LANES // 2
-    dests, rows, width = feat_ref.shape
+    dests, rows, across = feat_ref.shape
     runs = side * side * chans // (dests * run)
     runs_ref[...] = jnp.zeros(runs_ref.shape, F32)
     for k in range(chans // LANES):
@@ -72,14 +79,15 @@
                 dest, t = divmod(cell * (chans // run) + 2 * k + part, runs)
                 at = t % 2 * run
                 piece = total if t % 2 == part else other
-                row, lane = divmod(t * run, width)
+                row, lane = divmod(t * run, across)
                 row = dest * rows + row
                 runs_ref[row : row + 1, lane : lane + run] = piece[line : line + 1, at : at + run]
-    feat_ref[...] = runs_ref[...].astype(BF).reshape(dests, rows, width)
-
-
-def conv_forward(lines, weight, side, nx):
-    depth, chans = lines.shape[1], weight.shape[1]
+    feat_ref[...] = runs_ref[...].astype(BF).reshape(dests, rows, across)
+
+
+def conv_forward(maps, weight, nx):
+    _, side, _, depth = maps.shape
+    chans = weight.shape[1]
     pix = side * LINE
     rows, width = LINE, 2 * LANES
     return pl.pallas_call(
@@ -94,6 +102,7 @@
         ],
         scratch_shapes=[
             pltpu.VMEM((3, 3 * depth, chans), BF),
+            pltpu.VMEM((pix + 3 * LINE, depth), F32),
             pltpu.VMEM((3, pix + LINE, chans), F32),
             pltpu.VMEM((chans // LANES, pix // 2, LANES), F32),
             pltpu.VMEM((nx * rows, width), F32),
@@ -101,7 +110,22 @@
         ],
         compiler_params=VMEM,
         cost_estimate=cost(18 * pix * depth * chans, weight.size * 2, pix * chans),
-    )(lines, weight)
+    )(maps, weight)
+
+
+def join_kernel(left_ref, right_ref, out_ref):
+    cut = left_ref.shape[1]
+    out_ref[:, :cut] = left_ref[...]
+    out_ref[:, cut:] = right_ref[...]
+
+
+def join(left, right):
+    rows, cut = left.shape
+    return pl.pallas_call(
+        join_kernel,
+        out_shape=jax.ShapeDtypeStruct((rows, cut + right.shape[1]), left.dtype),
+        cost_estimate=cost(0, left.size * 4),
+    )(left, right)
 
 
 def copies_kernel(feat_ref, out_ref):
@@ -418,16 +442,16 @@
         me = high * nv + lax.axis_index("y")
         me_word = me.reshape(1).astype(jnp.int32)
 
-        known = jnp.concatenate([fc7_weight.T, cotangent.T], axis=1)
+        known = join(fc7_weight.T, cotangent.T)
         known = lax.all_gather(known, gx + ("core",), axis=0, tiled=False)
         known = known.reshape(nx, nc * cols7, rows7 + total)
         other6 = lax.ppermute(fc6_weight, "core", pair)
-        lines = bordered(images[0])
-        conv_pre, feat = conv_forward(lines, conv_weight, side, nx)
+        conv_pre, feat = conv_forward(images, conv_weight, nx)
         slopes = turned_slope(conv_pre, cols).reshape(nx, part, cols)
+        feat, other6 = lax.optimization_barrier((swap(feat, gx), other6))
         other6, image = lax.optimization_barrier((other6, images))
         gathered = lax.all_gather(paired(image, "xh", across), "y", axis=0, tiled=True)
-        inputs = swap(feature_copies(swap(feat, gx), nz, feats), "gz").reshape(group, feats)
+        inputs = swap(feature_copies(feat, nz, feats), "gz").reshape(group, feats)
         first = jnp.where(core == 0, fc6_weight, other6)
         second = jnp.where(core == 0, other6, fc6_weight)
         weight6 = jnp.concatenate([first, second], axis=1)

time: 187 us -> 187 us (level)
    pad x3 -> x2, local copies, waits for them, and re-layouts: 4.76 us -> 3.75 us  [bordered(): padded = jnp.pad(maps, ((1, 3), (1, LINE - side - 1), (0, 0)))]
    unnamed x18 -> x20, local copies, waits for them, and re-layouts: 9.85 us -> 10.8 us
  transfers between devices with their start and end apart: 18 -> 18, of which waited for: 12 -> 12; matrix products, arithmetic and copies ran while one was open for 9% -> 8% of each run, Pallas kernels for 9% -> 9%
where the time goes in v11:
time: 187 us; the launch traced here: 185 us
  starting transfers between devices  63 us (34%)
  waiting for transfers between devices  62.2 us (33%)
  Pallas kernels  20.6 us (11%)
  local copies, waits for them, and re-layouts  15.8 us (8%)
  between operations  14.1 us (8%)
  other arithmetic  7.77 us (4%)
    all_to_all x9, starting transfers between devices, swap(): return lax.all_to_all(value, axis, 0, 0, tiled=True)  46.7 us
    all_to_all x9, waiting for transfers between devices, swap(): return lax.all_to_all(value, axis, 0, 0, tiled=True)  39.3 us
    all_gather x1, waiting for transfers between devices, on_device(): lax.all_gather(hidden, 'y', axis=0, tiled=False).reshape(group, rows7)  11.2 us
    ppermute x2, waiting for transfers between devices, paired(): return jnp.concatenate([value, lax.ppermute(value, axis, way)], axis=0)  10.8 us
    unnamed x20, local copies, waits for them, and re-layouts  10.8 us
    ppermute x1, starting transfers between devices, on_device(): lax.ppermute(sent6, 'core', pair)  7.26 us
    pallas_call x2, Pallas kernels, weight_terms(): pl.pallas_call(outer_kernel if more is None else outer_add_kernel, in_spe...  4.1 us
    pad x2, local copies, waits for them, and re-layouts, bordered(): padded = jnp.pad(maps, ((1, 3), (1, LINE - side - 1), (0, 0)))  3.75 us
  transfers between devices with their start and end apart: 18, of which 12 were waited for; matrix products, arithmetic and copies ran while one was open for 8% of the time, Pallas kernels for 9%

profile of v11, /device:TPU:1, one launch (start us, length us, event | category | flops | bytes accessed | tf_op | source)
XLA Modules:
  0.0 184.8 jit_solution(12106045366614305344)
XLA Ops:
  7.2 1.6 shard_map.84
  8.8 3.3 %collective-permute-start = (bf16[3136,128]{1,0:T(8,128)(2,1)}, bf16[3136,128]{1,0:T(8,128)(2,1)S(1)}, u32[]{:S(2)}, u32[]{:S(2)}) collective-permute-start(bf16[3136,128]{1,0:T(8,128)(2,1)} %param.7), channel_id=1, source_target_pairs={{0,1},{1,0},{2,3},{3,2},{4,5},{5,4},{6,7},{7,6},{8,9},{9,8},{10,11... | collective-permute-start | bytes 2408456 | tf_op jit(solution)/shard_map/ppermute | solution.py:448
  12.1 2.3 %copy-done = bf16[4608,512]{1,0:T(8,128)(2,1)S(1)} copy-done((bf16[4608,512]{1,0:T(8,128)(2,1)S(1)}, bf16[4608,512]{1,0:T(8,128)(2,1)}, u32[]{:S(2)}) %copy-start) | copy-done | bytes 4718616
  14.5 0.9 copy-done.4
  15.4 3.0 %shard_map.85 = (f32[224,512]{1,0:T(8,128)S(1)}, bf16[8,16,256]{2,1,0:T(8,128)(2,1)}) custom-call(bf16[1,14,14,512]{3,2,1,0:T(8,128)(2,1)S(1)} %copy-done.4, bf16[4608,512]{1,0:T(8,128)(2,1)S(1)} %copy-done), custom_call_target="tpu_custom_call" | custom-call | flops 1056964608 | bytes 4718592 | tf_op jit(solution)/shard_map/pallas_call | solution.py:93
  18.4 5.1 %all-to-all-start = ((bf16[8,16,256]{2,1,0:T(8,128)(2,1)}), bf16[8,16,256]{2,1,0:T(8,128)(2,1)S(1)}, u32[]{:S(2)}, u32[]{:S(2)}) async-start(bf16[8,16,256]{2,1,0:T(8,128)(2,1)} %get-tuple-element.30), calls=%async_computation | async-start | bytes 131072 | tf_op jit(solution)/shard_map/all_to_all | solution.py:406
  23.5 6.7 %all-to-all-done.feat_ref = bf16[8,16,256]{2,1,0:T(8,128)(2,1)S(1)} async-done(((bf16[8,16,256]{2,1,0:T(8,128)(2,1)}), bf16[8,16,256]{2,1,0:T(8,128)(2,1)S(1)}, u32[]{:S(2)}, u32[]{:S(2)}) %all-to-all-start) | async-done | bytes 65568 | tf_op jit(solution)/shard_map/all_to_all | solution.py:406
  30.2 1.0 shard_map.86
  31.1 8.3 %all-to-all-start.1 = ((bf16[16,8,3136]{2,1,0:T(8,128)(2,1)}), bf16[16,8,3136]{2,1,0:T(8,128)(2,1)S(1)}, u32[]{:S(2)}, u32[]{:S(2)}) async-start(bf16[16,8,3136]{2,1,0:T(8,128)(2,1)} %shard_map.86), calls=%async_computation.1 | async-start | bytes 1638400 | tf_op jit(solution)/shard_map/all_to_all | solution.py:406
  39.5 1.2 collective-permute-start.2
  40.7 1.3 broadcast_select_fusion.1
  42.0 10.3 %collective-permute-done.2 = bf16[1,14,14,512]{3,2,1,0:T(8,128)(2,1)S(1)} collective-permute-done((bf16[1,14,14,512]{3,2,1,0:T(8,128)(2,1)S(1)}, bf16[1,14,14,512]{3,2,1,0:T(8,128)(2,1)S(1)}, u32[]{:S(2)}, u32[]{:S(2)}) %collective-permute-start.2) | collective-permute-done | bytes 200736 | tf_op jit(solution)/shard_map/ppermute | solution.py:427
  52.3 0.8 pad_maximum_fusion.1
  53.2 1.6 pad_maximum_fusion.weight_ref
  54.7 3.6 %all-to-all-done.1 = bf16[16,8,3136]{2,1,0:T(8,128)(2,1)S(1)} async-done(((bf16[16,8,3136]{2,1,0:T(8,128)(2,1)}), bf16[16,8,3136]{2,1,0:T(8,128)(2,1)S(1)}, u32[]{:S(2)}, u32[]{:S(2)}) %all-to-all-start.1) | async-done | bytes 802848 | tf_op jit(solution)/shard_map/all_to_all | solution.py:406
  58.4 1.0 convolution_convert_fusion
  59.4 3.9 %all-to-all-start.2 = ((bf16[8,16,256]{2,1,0:T(8,128)(2,1)}), bf16[8,16,256]{2,1,0:T(8,128)(2,1)S(1)}, u32[]{:S(2)}, u32[]{:S(2)}) async-start(bf16[8,16,256]{2,1,0:T(8,128)(2,1)} %bitcast.6), calls=%async_computation.2 | async-start | bytes 131072 | tf_op jit(solution)/shard_map/all_to_all | solution.py:406
  63.3 6.7 %all-to-all-done.2 = bf16[8,16,256]{2,1,0:T(8,128)(2,1)S(1)} async-done(((bf16[8,16,256]{2,1,0:T(8,128)(2,1)}), bf16[8,16,256]{2,1,0:T(8,128)(2,1)S(1)}, u32[]{:S(2)}, u32[]{:S(2)}) %all-to-all-start.2) | async-done | bytes 65568 | tf_op jit(solution)/shard_map/all_to_all | solution.py:406
  70.1 0.7 broadcast_in_dim.8
  70.7 6.0 %all-to-all-start.3 = ((bf16[16,16,256]{2,1,0:T(8,128)(2,1)}), bf16[16,16,256]{2,1,0:T(8,128)(2,1)S(1)}, u32[]{:S(2)}, u32[]{:S(2)}) async-start(bf16[16,16,256]{2,1,0:T(8,128)(2,1)} %broadcast_in_dim.8), calls=%async_computation.3 | async-start | bytes 262144 | tf_op jit(solution)/shard_map/all_to_all | solution.py:406
  76.8 7.4 %all-to-all-done.3.hidden_ref = bf16[16,16,256]{2,1,0:T(8,128)(2,1)S(1)} async-done(((bf16[16,16,256]{2,1,0:T(8,128)(2,1)}), bf16[16,16,256]{2,1,0:T(8,128)(2,1)S(1)}, u32[]{:S(2)}, u32[]{:S(2)}) %all-to-all-start.3) | async-done | bytes 131104 | tf_op jit(solution)/shard_map/all_to_all | solution.py:406
  84.1 1.6 copy-done.3
  85.8 1.8 shard_map.87
  87.6 1.4 collective-permute-start.1
  88.9 3.5 %all-to-all-start.4 = ((bf16[16,16,256]{2,1,0:T(8,128)(2,1)}), bf16[16,16,256]{2,1,0:T(8,128)(2,1)S(1)}, u32[]{:S(2)}, u32[]{:S(2)}) async-start(bf16[16,16,256]{2,1,0:T(8,128)(2,1)} %get-tuple-element.37), calls=%async_computation.4 | async-start | bytes 262144 | tf_op jit(solution)/shard_map/all_to_all | solution.py:406
  92.4 0.5 collective-permute-done.1
  93.0 0.7 pad_maximum_fusion.2
  93.7 6.1 %all-to-all-done.4 = bf16[16,16,256]{2,1,0:T(8,128)(2,1)S(1)} async-done(((bf16[16,16,256]{2,1,0:T(8,128)(2,1)}), bf16[16,16,256]{2,1,0:T(8,128)(2,1)S(1)}, u32[]{:S(2)}, u32[]{:S(2)}) %all-to-all-start.4) | async-done | bytes 131104 | tf_op jit(solution)/shard_map/all_to_all | solution.py:406
  99.9 0.7 fusion.2
  100.5 4.0 %all-to-all-start.5 = ((bf16[8,16,384]{2,1,0:T(8,128)(2,1)}), bf16[8,16,384]{2,1,0:T(8,128)(2,1)S(1)}, u32[]{:S(2)}, u32[]{:S(2)}) async-start(bf16[8,16,384]{2,1,0:T(8,128)(2,1)} %fusion.2), calls=%async_computation.5 | async-start | bytes 196608 | tf_op jit(solution)/shard_map/all_to_all | solution.py:406
  104.6 0.7 all-gather.10.cloned.1.call-update
  105.3 6.0 %all-to-all-done.5 = bf16[8,16,384]{2,1,0:T(8,128)(2,1)S(1)} async-done(((bf16[8,16,384]{2,1,0:T(8,128)(2,1)}), bf16[8,16,384]{2,1,0:T(8,128)(2,1)S(1)}, u32[]{:S(2)}, u32[]{:S(2)}) %all-to-all-start.5) | async-done | bytes 98336 | tf_op jit(solution)/shard_map/all_to_all | solution.py:406
  111.4 1.6 shard_map.88
  112.9 3.6 %all-to-all-start.6 = ((bf16[16,8,3136]{2,1,0:T(8,128)(2,1)}), bf16[16,8,3136]{2,1,0:T(8,128)(2,1)S(1)}, u32[]{:S(2)}, u32[]{:S(2)}) async-start(bf16[16,8,3136]{2,1,0:T(8,128)(2,1)} %bitcast.11), calls=%async_computation.6 | async-start | bytes 1638400 | tf_op jit(solution)/shard_map/all_to_all | solution.py:406
  116.6 1.3 shard_map.89
  117.9 7.3 %collective-permute-start.5 = (bf16[3136,128]{1,0:T(8,128)(2,1)}, bf16[3136,128]{1,0:T(8,128)(2,1)}, u32[]{:S(2)}, u32[]{:S(2)}) collective-permute-start(bf16[3136,128]{1,0:T(8,128)(2,1)} %shard_map.89), channel_id=1, source_target_pairs={{0,1},{1,0},{2,3},{3,2},{4,5},{5,4},{6,7},{7,6},{8,9},{9,8},{10,11... | collective-permute-start | bytes 2408456 | tf_op jit(solution)/shard_map/ppermute | solution.py:491
  125.2 0.2 shard_map.90
  125.5 0.1 fusion.19.spread_ref
  125.6 11.2 %all-gather.10.cloned.1.call-done = bf16[128,4096]{1,0:T(8,128)(2,1)} async-done(((bf16[32,4096]{1,0:T(8,128)(2,1)}), bf16[128,4096]{1,0:T(8,128)(2,1)}) %all-gather.10.cloned.1.call-update) | async-done | bytes 1048592 | tf_op jit(solution)/shard_map/all_gather | solution.py:473
  136.8 1.0 shard_map.91
  137.8 5.5 %all-to-all-start.7 = ((bf16[8,64,384]{2,1,0:T(8,128)(2,1)}), bf16[8,64,384]{2,1,0:T(8,128)(2,1)S(1)}, u32[]{:S(2)}, u32[]{:S(2)}) async-start(bf16[8,64,384]{2,1,0:T(8,128)(2,1)} %shard_map.91), calls=%async_computation.7 | async-start | bytes 786432 | tf_op jit(solution)/shard_map/all_to_all | solution.py:406
  143.4 0.1 reshape.81
  143.5 0.1 reshape.82
  143.6 3.7 %pad.18 = bf16[8,18,16,512]{3,2,1,0:T(8,128)(2,1)} pad(bf16[8,14,14,512]{3,2,1,0:T(8,128)(2,1)} %all-gather.6.cloned.1.call-done, bf16[]{:T(256)} %constant.124.clone.1), padding=0_0x1_3x1_1x0_0 | pad | bytes 3964930 | tf_op jit(solution)/shard_map/vmap(jit(_pad))/pad | solution.py:415
  147.3 2.8 %shard_map.93 = f32[3136,128]{1,0:T(8,128)} custom-call(s32[1]{0:T(128)} %bitcast.1.which_ref, bf16[128,3136]{1,0:T(8,128)(2,1)S(1)} %bitcast.35, bf16[128,256]{1,0:T(8,128)(2,1)S(1)} %bitcast.42, bf16[3136,128]{1,0:T(8,128)(2,1)} %collective-permute-done.5.more_ref), custom_call_target="tpu_custom_call" | custom-call | flops 1000 | bytes 1000 | tf_op jit(solution)/shard_map/pallas_call | solution.py:255
  150.1 0.3 fusion.24
  150.4 1.2 all-to-all-done.7.packs_ref
  151.6 1.7 copy-done.2
  153.3 2.7 %shard_map.92 = (f32[16,72,128]{2,1,0:T(8,128)S(1)}, bf16[16,72,128]{2,1,0:T(8,128)(2,1)S(1)}) custom-call(s32[2]{0:T(128)S(1)} %pad_add_fusion.place_ref, bf16[8,288,512]{2,1,0:T(8,128)(2,1)S(1)} %bitcast.36, bf16[8,64,384]{2,1,0:T(8,128)(2,1)S(1)} %all-to-all-done.7.packs_ref, bf16[64,256]{1,0:T(8,128)(2,1)S(1)} %fusion.19.spread_ref), custom_call_target="tpu_custom_call" | custom-call | flops 1207959552 | bytes 2359296 | tf_op jit(solution)/shard_map/pallas_call | solution.py:338
  156.0 3.1 %collective-permute-start.3 = (bf16[16,72,128]{2,1,0:T(8,128)(2,1)S(1)}, bf16[16,72,128]{2,1,0:T(8,128)(2,1)S(1)}, u32[]{:S(2)}, u32[]{:S(2)}) collective-permute-start(bf16[16,72,128]{2,1,0:T(8,128)(2,1)S(1)} %get-tuple-element.51), channel_id=1, source_target_pairs={{0,1},{1,0},{2,3},{3,2},{4,5},{5,4},{6,7},{7,6},{8,9},{9,8},{10,11... | collective-permute-start | bytes 884744 | tf_op jit(solution)/shard_map/ppermute | solution.py:495
  159.1 0.7 slice_select_fusion
  159.8 0.1 slice.38
  159.9 0.1 convert_element_type.56
  160.1 0.2 collective-permute-done.3
  160.3 0.8 add_convert_fusion
  161.1 6.8 %all-to-all-start.8 = ((bf16[16,72,128]{2,1,0:T(8,128)(2,1)}), bf16[16,72,128]{2,1,0:T(8,128)(2,1)S(1)}, u32[]{:S(2)}, u32[]{:S(2)}) async-start(bf16[16,72,128]{2,1,0:T(8,128)(2,1)} %add_convert_fusion), calls=%async_computation.8 | async-start | bytes 589824 | tf_op jit(solution)/shard_map/all_to_all | solution.py:406
  167.9 0.8 add_bitcast_fusion
  168.6 0.2 shard_map.94
  168.9 2.3 %copy-done.1 = bf16[4608,512]{1,0:T(8,128)(2,1)S(1)} copy-done((bf16[4608,512]{1,0:T(8,128)(2,1)S(1)}, bf16[4608,512]{1,0:T(8,128)(2,1)}, u32[]{:S(2)}) %copy-start.1) | copy-done | bytes 4718616
  171.2 3.5 %shard_map.95 = f32[1,14,14,512]{3,2,1,0:T(8,128)S(1)} custom-call(bf16[288,512]{1,0:T(8,128)(2,1)S(1)} %bitcast.39, bf16[4608,512]{1,0:T(8,128)(2,1)S(1)} %copy-done.1), custom_call_target="tpu_custom_call" | custom-call | flops 1000 | bytes 1000 | tf_op jit(solution)/shard_map/pallas_call | solution.py:379
  174.8 1.2 copy.23
  175.9 1.5 all-to-all-done.8
  177.5 0.1 fusion.23
  177.6 0.7 copy.22
  (51 shorter events, 0.7 us)
Async XLA Ops:
  7.2 77.0 %all-gather.8.cloned.1.call-start = ((), (), s32[]{:S(2)}) async-start(), calls=%async_computation.10 | async-start | bytes 2367488 | tf_op jit(solution)/shard_map/all_gather | solution.py:446
  8.8 21.4 %collective-permute-start = (bf16[3136,128]{1,0:T(8,128)(2,1)}, bf16[3136,128]{1,0:T(8,128)(2,1)S(1)}, u32[]{:S(2)}, u32[]{:S(2)}) collective-permute-start(bf16[3136,128]{1,0:T(8,128)(2,1)} %param.7), channel_id=1, source_target_pairs={{0,1},{1,0},{2,3},{3,2},{4,5},{5,4},{6,7},{7,6},{8,9},{9,8},{10,11... | collective-permute-start | bytes 2408456 | tf_op jit(solution)/shard_map/ppermute | solution.py:448
  12.1 2.3 %copy-start = (bf16[4608,512]{1,0:T(8,128)(2,1)S(1)}, bf16[4608,512]{1,0:T(8,128)(2,1)}, u32[]{:S(2)}) copy-start(bf16[4608,512]{1,0:T(8,128)(2,1)} %weight_ref.3) | copy-start | bytes 14155780
  14.5 0.9 copy-start.4
  18.4 21.1 %copy-start.5 = (bf16[1,14,14,512]{3,2,1,0:T(8,128)(2,1)S(1)}, bf16[1,14,14,512]{3,2,1,0:T(8,128)(2,1)}, u32[]{:S(2)}) copy-start(bf16[1,14,14,512]{3,2,1,0:T(8,128)(2,1)} %maps_ref.1) | copy-start | bytes 602116
  18.4 22.3 %copy-start.7 = (bf16[3136,128]{1,0:T(8,128)(2,1)S(1)}, bf16[3136,128]{1,0:T(8,128)(2,1)}, u32[]{:S(2)}) copy-start(bf16[3136,128]{1,0:T(8,128)(2,1)} %param.7) | copy-start | bytes 2408452
  18.4 11.8 %all-to-all-start = ((bf16[8,16,256]{2,1,0:T(8,128)(2,1)}), bf16[8,16,256]{2,1,0:T(8,128)(2,1)S(1)}, u32[]{:S(2)}, u32[]{:S(2)}) async-start(bf16[8,16,256]{2,1,0:T(8,128)(2,1)} %get-tuple-element.30), calls=%async_computation | async-start | bytes 131072 | tf_op jit(solution)/shard_map/all_to_all | solution.py:406
  31.1 27.3 %all-to-all-start.1 = ((bf16[16,8,3136]{2,1,0:T(8,128)(2,1)}), bf16[16,8,3136]{2,1,0:T(8,128)(2,1)S(1)}, u32[]{:S(2)}, u32[]{:S(2)}) async-start(bf16[16,8,3136]{2,1,0:T(8,128)(2,1)} %shard_map.86), calls=%async_computation.1 | async-start | bytes 1638400 | tf_op jit(solution)/shard_map/all_to_all | solution.py:406
  39.5 65.9 %all-gather.6.cloned.1.call-start = ((), (), s32[]{:S(2)}) async-start(), calls=%async_computation.9 | async-start | bytes 2293760 | tf_op jit(solution)/shard_map/all_gather | solution.py:453
  39.5 12.8 %collective-permute-start.2 = (bf16[1,14,14,512]{3,2,1,0:T(8,128)(2,1)S(1)}, bf16[1,14,14,512]{3,2,1,0:T(8,128)(2,1)S(1)}, u32[]{:S(2)}, u32[]{:S(2)}) collective-permute-start(bf16[1,14,14,512]{3,2,1,0:T(8,128)(2,1)S(1)} %copy-done.5), channel_id=1, source_target_pairs={{0,128},{128,0},{1,129},{129,1},{2,130},{130,2},{3,131},{131,3},{4... | collective-permute-start | bytes 602120 | tf_op jit(solution)/shard_map/ppermute | solution.py:427
  59.4 10.6 %all-to-all-start.2 = ((bf16[8,16,256]{2,1,0:T(8,128)(2,1)}), bf16[8,16,256]{2,1,0:T(8,128)(2,1)S(1)}, u32[]{:S(2)}, u32[]{:S(2)}) async-start(bf16[8,16,256]{2,1,0:T(8,128)(2,1)} %bitcast.6), calls=%async_computation.2 | async-start | bytes 131072 | tf_op jit(solution)/shard_map/all_to_all | solution.py:406
  70.7 13.4 %all-to-all-start.3 = ((bf16[16,16,256]{2,1,0:T(8,128)(2,1)}), bf16[16,16,256]{2,1,0:T(8,128)(2,1)S(1)}, u32[]{:S(2)}, u32[]{:S(2)}) async-start(bf16[16,16,256]{2,1,0:T(8,128)(2,1)} %broadcast_in_dim.8), calls=%async_computation.3 | async-start | bytes 262144 | tf_op jit(solution)/shard_map/all_to_all | solution.py:406
  84.1 1.6 copy-start.3
  87.6 5.4 %collective-permute-start.1 = (bf16[16,4096]{1,0:T(8,128)(2,1)S(1)}, bf16[16,4096]{1,0:T(8,128)(2,1)S(1)}, u32[]{:S(2)}, u32[]{:S(2)}) collective-permute-start(bf16[16,4096]{1,0:T(8,128)(2,1)S(1)} %bitcast.46), channel_id=1, source_target_pairs={{0,128},{128,0},{1,129},{129,1},{2,130},{130,2},{3,131},{131,3},{4... | collective-permute-start | bytes 393224 | tf_op jit(solution)/shard_map/ppermute | solution.py:427
  88.9 10.9 %all-to-all-start.4 = ((bf16[16,16,256]{2,1,0:T(8,128)(2,1)}), bf16[16,16,256]{2,1,0:T(8,128)(2,1)S(1)}, u32[]{:S(2)}, u32[]{:S(2)}) async-start(bf16[16,16,256]{2,1,0:T(8,128)(2,1)} %get-tuple-element.37), calls=%async_computation.4 | async-start | bytes 262144 | tf_op jit(solution)/shard_map/all_to_all | solution.py:406
  100.5 10.8 %all-to-all-start.5 = ((bf16[8,16,384]{2,1,0:T(8,128)(2,1)}), bf16[8,16,384]{2,1,0:T(8,128)(2,1)S(1)}, u32[]{:S(2)}, u32[]{:S(2)}) async-start(bf16[8,16,384]{2,1,0:T(8,128)(2,1)} %fusion.2), calls=%async_computation.5 | async-start | bytes 196608 | tf_op jit(solution)/shard_map/all_to_all | solution.py:406
  104.6 32.2 %all-gather.10.cloned.1.call-start = ((), (), s32[]{:S(2)}) async-start(), calls=%async_computation.11 | async-start | bytes 1310720 | tf_op jit(solution)/shard_map/all_gather | solution.py:473
  111.4 14.3 %copy-start.8 = (bf16[8,16,384]{2,1,0:T(8,128)(2,1)}, bf16[8,16,384]{2,1,0:T(8,128)(2,1)S(1)}, u32[]{:S(2)}) copy-start(bf16[8,16,384]{2,1,0:T(8,128)(2,1)S(1)} %all-to-all-done.5) | copy-start | bytes 294916
  112.9 23.9 %all-to-all-start.6 = ((bf16[16,8,3136]{2,1,0:T(8,128)(2,1)}), bf16[16,8,3136]{2,1,0:T(8,128)(2,1)S(1)}, u32[]{:S(2)}, u32[]{:S(2)}) async-start(bf16[16,8,3136]{2,1,0:T(8,128)(2,1)} %bitcast.11), calls=%async_computation.6 | async-start | bytes 1638400 | tf_op jit(solution)/shard_map/all_to_all | solution.py:406
  117.9 29.4 %collective-permute-start.5 = (bf16[3136,128]{1,0:T(8,128)(2,1)}, bf16[3136,128]{1,0:T(8,128)(2,1)}, u32[]{:S(2)}, u32[]{:S(2)}) collective-permute-start(bf16[3136,128]{1,0:T(8,128)(2,1)} %shard_map.89), channel_id=1, source_target_pairs={{0,1},{1,0},{2,3},{3,2},{4,5},{5,4},{6,7},{7,6},{8,9},{9,8},{10,11... | collective-permute-start | bytes 2408456 | tf_op jit(solution)/shard_map/ppermute | solution.py:491
  125.6 17.7 %slice-start = ((bf16[8,16,384]{2,1,0:T(8,128)(2,1)}), bf16[8,16,32]{2,1,0:T(8,128)(2,1)S(1)}, s32[]{:S(2)}) async-start(bf16[8,16,384]{2,1,0:T(8,128)(2,1)} %copy-done.8), calls=%async_computation.12 | async-start | bytes 65536 | tf_op jit(solution)/shard_map/slice | solution.py:482
  137.8 13.8 %all-to-all-start.7 = ((bf16[8,64,384]{2,1,0:T(8,128)(2,1)}), bf16[8,64,384]{2,1,0:T(8,128)(2,1)S(1)}, u32[]{:S(2)}, u32[]{:S(2)}) async-start(bf16[8,64,384]{2,1,0:T(8,128)(2,1)} %shard_map.91), calls=%async_computation.7 | async-start | bytes 786432 | tf_op jit(solution)/shard_map/all_to_all | solution.py:406
  147.3 2.8 %copy-start.6 = (bf16[128,4096]{1,0:T(8,128)(2,1)S(1)}, bf16[128,4096]{1,0:T(8,128)(2,1)}, u32[]{:S(2)}) copy-start(bf16[128,4096]{1,0:T(8,128)(2,1)} %all-gather.10.cloned.1.call-done) | copy-start | bytes 3145732
  151.6 1.7 copy-start.2
  156.0 4.3 %collective-permute-start.3 = (bf16[16,72,128]{2,1,0:T(8,128)(2,1)S(1)}, bf16[16,72,128]{2,1,0:T(8,128)(2,1)S(1)}, u32[]{:S(2)}, u32[]{:S(2)}) collective-permute-start(bf16[16,72,128]{2,1,0:T(8,128)(2,1)S(1)} %get-tuple-element.51), channel_id=1, source_target_pairs={{0,1},{1,0},{2,3},{3,2},{4,5},{5,4},{6,7},{7,6},{8,9},{9,8},{10,11... | collective-permute-start | bytes 884744 | tf_op jit(solution)/shard_map/ppermute | solution.py:495
  159.8 8.1 %collective-permute-start.4 = (f32[16,4096]{1,0:T(8,128)}, f32[16,4096]{1,0:T(8,128)S(1)}, u32[]{:S(2)}, u32[]{:S(2)}) collective-permute-start(f32[16,4096]{1,0:T(8,128)} %slice_select_fusion), channel_id=1, source_target_pairs={{0,1},{1,0},{2,3},{3,2},{4,5},{5,4},{6,7},{7,6},{8,9},{9,8},{10,11... | collective-permute-start | bytes 786440 | tf_op jit(solution)/shard_map/ppermute | solution.py:511
  161.1 16.4 %all-to-all-start.8 = ((bf16[16,72,128]{2,1,0:T(8,128)(2,1)}), bf16[16,72,128]{2,1,0:T(8,128)(2,1)S(1)}, u32[]{:S(2)}, u32[]{:S(2)}) async-start(bf16[16,72,128]{2,1,0:T(8,128)(2,1)} %add_convert_fusion), calls=%async_computation.8 | async-start | bytes 589824 | tf_op jit(solution)/shard_map/all_to_all | solution.py:406
  168.9 2.3 %copy-start.1 = (bf16[4608,512]{1,0:T(8,128)(2,1)S(1)}, bf16[4608,512]{1,0:T(8,128)(2,1)}, u32[]{:S(2)}) copy-start(bf16[4608,512]{1,0:T(8,128)(2,1)} %weight_ref.3) | copy-start | bytes 14155780
Sparse Core Ops, SparseCore 0:
  11.3 59.5 all-gather.7
  72.7 29.0 all-gather.5
  107.8 28.9 all-gather.9

commit v12 on v11

--- a/solution.py
+++ b/solution.py
@@ -187,39 +187,42 @@
     )(pre, dfeat)
 
 
-def fc7_kernel(known_ref, hidden_ref, pick_ref, seven_ref, terms_ref):
+def fc7_kernel(near_ref, far_ref, hidden_ref, pick_ref, seven_ref, terms_ref):
     count, mine, wide = hidden_ref.shape
-    lines, both, _ = known_ref.shape
+    lines, both, _ = near_ref.shape
     rows7, cols7 = count * wide, both // 2
-
-    def weight(k, start, size):
-        block = known_ref[:, k * cols7 : (k + 1) * cols7, start : start + size]
-        return block.reshape(lines * cols7, size)
-
+    cols = lines * cols7
+
+    def weight(ref, k, start, size):
+        return ref[:, k * cols7 : (k + 1) * cols7, start : start + size].reshape(cols, size)
+
+    parts = [(ref, h, k) for h, ref in enumerate((near_ref, far_ref)) for k in range(2)]
     sevens = []
-    for k in range(2):
-        y7_pre = jnp.zeros((lines * cols7, mine), F32)
+    for ref, h, k in parts:
+        y7_pre = jnp.zeros((cols, mine), F32)
         for g in range(count):
-            y7_pre += dot(weight(k, g * wide, wide), hidden_ref[g], ((1,), (1,)))
-        cot = dot(weight(k, rows7, pick_ref.shape[0]), pick_ref[...], ((1,), (0,)))
+            y7_pre += dot(weight(ref, k, g * wide, wide), hidden_ref[g], ((1,), (1,)))
+        cot = dot(weight(ref, k, rows7, pick_ref.shape[0]), pick_ref[...], ((1,), (0,)))
         sevens.append((cot * slope(y7_pre)).astype(BF))
-        seven_ref[:, k * mine : (k + 1) * mine] = sevens[k]
+        seven_ref[h * cols : (h + 1) * cols, k * mine : (k + 1) * mine] = sevens[-1]
     for g in range(count):
-        parts = [dot(sevens[k], weight(k, g * wide, wide), ((0,), (0,))) for k in range(2)]
-        terms_ref[g] = (parts[0] + parts[1]).astype(BF)
-
-
-def fc7_step(known, hidden, pick):
-    lines, both, _ = known.shape
+        total = jnp.zeros((mine, wide), F32)
+        for seven, (ref, _, k) in zip(sevens, parts):
+            total += dot(seven, weight(ref, k, g * wide, wide), ((0,), (0,)))
+        terms_ref[g] = total.astype(BF)
+
+
+def fc7_step(near, far, hidden, pick):
+    lines, both, _ = near.shape
     return pl.pallas_call(
         fc7_kernel,
         out_shape=[
-            jax.ShapeDtypeStruct((lines * both // 2, 2 * pick.shape[1]), BF),
+            jax.ShapeDtypeStruct((lines * both, 2 * pick.shape[1]), BF),
             jax.ShapeDtypeStruct(hidden.shape, BF),
         ],
         compiler_params=VMEM,
-        cost_estimate=cost(4 * known.size * pick.shape[1], known.size * 2),
-    )(known, hidden, pick)
+        cost_estimate=cost(8 * near.size * pick.shape[1], near.size * 4),
+    )(near, far, hidden, pick)
 
 
 def back_kernel(g_ref, weight_ref, out_ref):
@@ -443,8 +446,7 @@
         me_word = me.reshape(1).astype(jnp.int32)
 
         known = join(fc7_weight.T, cotangent.T)
-        known = lax.all_gather(known, gx + ("core",), axis=0, tiled=False)
-        known = known.reshape(nx, nc * cols7, rows7 + total)
+        known = lax.all_gather(paired(known, "core", pair), "y", axis=0, tiled=False)
         other6 = lax.ppermute(fc6_weight, "core", pair)
         conv_pre, feat = conv_forward(images, conv_weight, nx)
         slopes = turned_slope(conv_pre, cols).reshape(nx, part, cols)
@@ -455,7 +457,8 @@
         first = jnp.where(core == 0, fc6_weight, other6)
         second = jnp.where(core == 0, other6, fc6_weight)
         weight6 = jnp.concatenate([first, second], axis=1)
-        inputs, weight6 = lax.optimization_barrier((inputs, weight6))
+        inputs, weight6, known = lax.optimization_barrier((inputs, weight6, known))
+        known_far = lax.ppermute(known, "xh", across)
 
         h6_terms = dot(inputs, weight6, ((1,), (0,))).astype(BF).reshape(nx, mine, wide)
         h6_pre = swap(h6_terms, gx).astype(F32).sum(axis=0)
@@ -465,7 +468,7 @@
         place = lax.broadcasted_iota(jnp.int32, (total, mine), 1)
         source = (place % nx) * ny + (me * near + place // nx) * nc + core
         pick = (lax.broadcasted_iota(jnp.int32, (total, mine), 0) == source).astype(BF)
-        g_seven, dh6_terms = fc7_step(known, hidden, pick)
+        g_seven, dh6_terms = fc7_step(known, known_far, hidden, pick)
         dh6_terms, hidden = lax.optimization_barrier((dh6_terms, hidden))
         hidden = hidden.transpose(1, 0, 2).reshape(mine, rows7)
         hidden = paired(hidden, "xh", across)
@@ -474,7 +477,8 @@
         grad_hidden = dh6_terms.astype(F32).sum(axis=0)
         own_six = (grad_hidden * slope(h6_pre)).astype(BF)
 
-        columns = g_seven.reshape(nx, cols7, nc * mine)
+        columns = g_seven.reshape(nh, nv, cols7, nc * mine)
+        columns = jnp.where(high == 0, columns, columns[::-1]).reshape(nx, cols7, nc * mine)
         columns = jnp.pad(columns, ((0, 0), (0, mine - cols7), (0, LANES - nc * mine)))
         both = jnp.concatenate([jnp.broadcast_to(own_six, (nx, mine, wide)), columns], axis=2)
         both, gathered = lax.optimization_barrier((swap(both, gx), gathered))
@@ -498,8 +502,7 @@
         columns = columns.reshape(nh, nv, cols7, nc, mine).transpose(3, 2, 1, 0, 4)
         columns = columns.reshape(nc * cols7, group)
         terms7 = dot(columns, all_hidden, ((1,), (0,)))
-        own7 = jnp.where(core == 0, terms7[:cols7], terms7[cols7:])
-        sent7 = jnp.where(core == 0, terms7[cols7:], terms7[:cols7])
+        own7, sent7 = terms7[:cols7], terms7[cols7:]
         packed = swap(packed, "gz")
 
         runs = feats // part

time: 187 us -> 207 us (1.11)
  waiting for transfers between devices: 62.2 us -> 76.5 us
  starting transfers between devices: 63 us -> 67.1 us
    all_to_all x9, waiting for transfers between devices: 39.3 us -> 52.3 us  [swap(): return lax.all_to_all(value, axis, 0, 0, tiled=True)]
    ppermute x2 -> x3, starting transfers between devices: 2.54 us -> 7.21 us  [paired(): return jnp.concatenate([value, lax.ppermute(value, axis, way)], axis=0)]
    ppermute x1, starting transfers between devices: 3.33 us -> 0.01 us  [on_device(): other6 = lax.ppermute(fc6_weight, 'core', pair)]
    ppermute x2 -> x3, waiting for transfers between devices: 10.8 us -> 11.5 us  [paired(): return jnp.concatenate([value, lax.ppermute(value, axis, way)], axis=0)]
    unnamed x20 -> x18, local copies, waits for them, and re-layouts: 10.8 us -> 10.4 us
  transfers between devices with their start and end apart: 18 -> 20, of which waited for: 12 -> 12; matrix products, arithmetic and copies ran while one was open for 8% -> 8% of each run, Pallas kernels for 9% -> 9%
where the time goes in v12:
time: 207 us; the launch traced here: 205 us
  waiting for transfers between devices  76.5 us (37%)
  starting transfers between devices  67.1 us (32%)
  Pallas kernels  21.8 us (11%)
  local copies, waits for them, and re-layouts  15.4 us (7%)
  between operations  14.1 us (7%)
  other arithmetic  8.66 us (4%)
    all_to_all x9, waiting for transfers between devices, swap(): return lax.all_to_all(value, axis, 0, 0, tiled=True)  52.3 us
    all_to_all x9, starting transfers between devices, swap(): return lax.all_to_all(value, axis, 0, 0, tiled=True)  48.3 us
    ppermute x3, waiting for transfers between devices, paired(): return jnp.concatenate([value, lax.ppermute(value, axis, way)], axis=0)  11.5 us
    all_gather x1, waiting for transfers between devices, on_device(): lax.all_gather(hidden, 'y', axis=0, tiled=False).reshape(group, rows7)  11.3 us
    unnamed x18, local copies, waits for them, and re-layouts  10.4 us
    ppermute x1, starting transfers between devices, on_device(): lax.ppermute(sent6, 'core', pair)  7.41 us
    ppermute x3, starting transfers between devices, paired(): return jnp.concatenate([value, lax.ppermute(value, axis, way)], axis=0)  7.21 us
  transfers between devices with their start and end apart: 20, of which 12 were waited for; matrix products, arithmetic and copies ran while one was open for 8% of the time, Pallas kernels for 9%

profile of v12, /device:TPU:1, one launch (start us, length us, event | category | flops | bytes accessed | tf_op | source)
XLA Modules:
  0.0 204.8 jit_solution(18057415132385592625)
XLA Ops:
  7.2 1.6 shard_map.86
  8.8 3.2 %collective-permute-start.1 = (bf16[16,4352]{1,0:T(8,128)(2,1)}, bf16[16,4352]{1,0:T(8,128)(2,1)S(1)}, u32[]{:S(2)}, u32[]{:S(2)}) collective-permute-start(bf16[16,4352]{1,0:T(8,128)(2,1)} %shard_map.86), channel_id=1, source_target_pairs={{0,1},{1,0},{2,3},{3,2},{4,5},{5,4},{6,7},{7,6},{8,9},{9,8},{10,11... | collective-permute-start | bytes 417800 | tf_op jit(solution)/shard_map/ppermute | solution.py:430
  12.0 1.2 collective-permute-done.1
  13.2 1.6 pad_maximum_fusion.2
  14.9 2.3 %copy-done = bf16[4608,512]{1,0:T(8,128)(2,1)S(1)} copy-done((bf16[4608,512]{1,0:T(8,128)(2,1)S(1)}, bf16[4608,512]{1,0:T(8,128)(2,1)}, u32[]{:S(2)}) %copy-start) | copy-done | bytes 4718616
  17.2 0.9 copy-done.4
  18.2 3.0 %shard_map.84 = (f32[224,512]{1,0:T(8,128)S(1)}, bf16[8,16,256]{2,1,0:T(8,128)(2,1)}) custom-call(bf16[1,14,14,512]{3,2,1,0:T(8,128)(2,1)S(1)} %copy-done.4, bf16[4608,512]{1,0:T(8,128)(2,1)S(1)} %copy-done), custom_call_target="tpu_custom_call" | custom-call | flops 1056964608 | bytes 4718592 | tf_op jit(solution)/shard_map/pallas_call | solution.py:93
  21.2 5.1 %all-to-all-start = ((bf16[8,16,256]{2,1,0:T(8,128)(2,1)}), bf16[8,16,256]{2,1,0:T(8,128)(2,1)S(1)}, u32[]{:S(2)}, u32[]{:S(2)}) async-start(bf16[8,16,256]{2,1,0:T(8,128)(2,1)} %get-tuple-element.31), calls=%async_computation | async-start | bytes 131072 | tf_op jit(solution)/shard_map/all_to_all | solution.py:409
  26.2 6.8 %all-to-all-done.feat_ref = bf16[8,16,256]{2,1,0:T(8,128)(2,1)S(1)} async-done(((bf16[8,16,256]{2,1,0:T(8,128)(2,1)}), bf16[8,16,256]{2,1,0:T(8,128)(2,1)S(1)}, u32[]{:S(2)}, u32[]{:S(2)}) %all-to-all-start) | async-done | bytes 65568 | tf_op jit(solution)/shard_map/all_to_all | solution.py:409
  33.1 1.0 shard_map.85
  34.0 8.3 %all-to-all-start.1 = ((bf16[16,8,3136]{2,1,0:T(8,128)(2,1)}), bf16[16,8,3136]{2,1,0:T(8,128)(2,1)S(1)}, u32[]{:S(2)}, u32[]{:S(2)}) async-start(bf16[16,8,3136]{2,1,0:T(8,128)(2,1)} %shard_map.85), calls=%async_computation.1 | async-start | bytes 1638400 | tf_op jit(solution)/shard_map/all_to_all | solution.py:409
  42.4 1.1 collective-permute-start.4
  43.5 1.3 broadcast_select_fusion.1
  44.8 10.3 %collective-permute-done.4 = bf16[1,14,14,512]{3,2,1,0:T(8,128)(2,1)S(1)} collective-permute-done((bf16[1,14,14,512]{3,2,1,0:T(8,128)(2,1)S(1)}, bf16[1,14,14,512]{3,2,1,0:T(8,128)(2,1)S(1)}, u32[]{:S(2)}, u32[]{:S(2)}) %collective-permute-start.4) | collective-permute-done | bytes 200736 | tf_op jit(solution)/shard_map/ppermute | solution.py:430
  55.1 0.8 pad_maximum_fusion.1
  56.0 1.6 pad_maximum_fusion.weight_ref
  57.5 3.6 %all-to-all-done.1 = bf16[16,8,3136]{2,1,0:T(8,128)(2,1)S(1)} async-done(((bf16[16,8,3136]{2,1,0:T(8,128)(2,1)}), bf16[16,8,3136]{2,1,0:T(8,128)(2,1)S(1)}, u32[]{:S(2)}, u32[]{:S(2)}) %all-to-all-start.1) | async-done | bytes 802848 | tf_op jit(solution)/shard_map/all_to_all | solution.py:409
  61.1 1.0 collective-permute-start.2
  62.1 1.0 convolution_convert_fusion
  63.1 3.9 %all-to-all-start.2 = ((bf16[8,16,256]{2,1,0:T(8,128)(2,1)}), bf16[8,16,256]{2,1,0:T(8,128)(2,1)S(1)}, u32[]{:S(2)}, u32[]{:S(2)}) async-start(bf16[8,16,256]{2,1,0:T(8,128)(2,1)} %bitcast.6), calls=%async_computation.2 | async-start | bytes 131072 | tf_op jit(solution)/shard_map/all_to_all | solution.py:409
  67.0 19.1 %all-to-all-done.2 = bf16[8,16,256]{2,1,0:T(8,128)(2,1)S(1)} async-done(((bf16[8,16,256]{2,1,0:T(8,128)(2,1)}), bf16[8,16,256]{2,1,0:T(8,128)(2,1)S(1)}, u32[]{:S(2)}, u32[]{:S(2)}) %all-to-all-start.2) | async-done | bytes 65568 | tf_op jit(solution)/shard_map/all_to_all | solution.py:409
  86.2 0.7 broadcast_in_dim.8
  86.8 8.1 %all-to-all-start.3 = ((bf16[16,16,256]{2,1,0:T(8,128)(2,1)}), bf16[16,16,256]{2,1,0:T(8,128)(2,1)S(1)}, u32[]{:S(2)}, u32[]{:S(2)}) async-start(bf16[16,16,256]{2,1,0:T(8,128)(2,1)} %broadcast_in_dim.8), calls=%async_computation.3 | async-start | bytes 262144 | tf_op jit(solution)/shard_map/all_to_all | solution.py:409
  95.0 7.4 %all-to-all-done.3.hidden_ref = bf16[16,16,256]{2,1,0:T(8,128)(2,1)S(1)} async-done(((bf16[16,16,256]{2,1,0:T(8,128)(2,1)}), bf16[16,16,256]{2,1,0:T(8,128)(2,1)S(1)}, u32[]{:S(2)}, u32[]{:S(2)}) %all-to-all-start.3) | async-done | bytes 131104 | tf_op jit(solution)/shard_map/all_to_all | solution.py:409
  102.4 1.2 copy-done.3
  103.6 3.0 %shard_map.87 = (bf16[128,32]{1,0:T(8,128)(2,1)S(1)}, bf16[16,16,256]{2,1,0:T(8,128)(2,1)}) custom-call(bf16[4,32,4352]{2,1,0:T(8,128)(2,1)S(1)} %bitcast.41, bf16[4,32,4352]{2,1,0:T(8,128)(2,1)} %collective-permute-done.2.far_ref, bf16[16,16,256]{2,1,0:T(8,128)(2,1)S(1)} %all-to-all-done.3.hidden_ref, bf16[256,16]{1,0:T(8,128)(2,1)S(1)} %fusion.2.pick_ref), custom_call_target="tpu_custom_call" | custom-call | flops 71303168 | bytes 2228224 | tf_op jit(solution)/shard_map/pallas_call | solution.py:217
  106.7 2.9 %collective-permute-start.3 = (bf16[16,4096]{1,0:T(8,128)(2,1)S(1)}, bf16[16,4096]{1,0:T(8,128)(2,1)S(1)}, u32[]{:S(2)}, u32[]{:S(2)}) collective-permute-start(bf16[16,4096]{1,0:T(8,128)(2,1)S(1)} %bitcast.48), channel_id=1, source_target_pairs={{0,128},{128,0},{1,129},{129,1},{2,130},{130,2},{3,131},{131,3},{4... | collective-permute-start | bytes 393224 | tf_op jit(solution)/shard_map/ppermute | solution.py:430
  109.6 3.5 %all-to-all-start.4 = ((bf16[16,16,256]{2,1,0:T(8,128)(2,1)}), bf16[16,16,256]{2,1,0:T(8,128)(2,1)S(1)}, u32[]{:S(2)}, u32[]{:S(2)}) async-start(bf16[16,16,256]{2,1,0:T(8,128)(2,1)} %get-tuple-element.39), calls=%async_computation.4 | async-start | bytes 262144 | tf_op jit(solution)/shard_map/all_to_all | solution.py:409
  113.1 0.7 pad_maximum_fusion.3
  113.8 6.6 %all-to-all-done.4 = bf16[16,16,256]{2,1,0:T(8,128)(2,1)S(1)} async-done(((bf16[16,16,256]{2,1,0:T(8,128)(2,1)}), bf16[16,16,256]{2,1,0:T(8,128)(2,1)S(1)}, u32[]{:S(2)}, u32[]{:S(2)}) %all-to-all-start.4) | async-done | bytes 131104 | tf_op jit(solution)/shard_map/all_to_all | solution.py:409
  120.5 0.7 fusion.3
  121.2 3.4 %all-to-all-start.5 = ((bf16[8,16,384]{2,1,0:T(8,128)(2,1)}), bf16[8,16,384]{2,1,0:T(8,128)(2,1)S(1)}, u32[]{:S(2)}, u32[]{:S(2)}) async-start(bf16[8,16,384]{2,1,0:T(8,128)(2,1)} %fusion.3), calls=%async_computation.5 | async-start | bytes 196608 | tf_op jit(solution)/shard_map/all_to_all | solution.py:409
  124.6 0.7 all-gather.10.cloned.1.call-update
  125.4 6.0 %all-to-all-done.5 = bf16[8,16,384]{2,1,0:T(8,128)(2,1)S(1)} async-done(((bf16[8,16,384]{2,1,0:T(8,128)(2,1)}), bf16[8,16,384]{2,1,0:T(8,128)(2,1)S(1)}, u32[]{:S(2)}, u32[]{:S(2)}) %all-to-all-start.5) | async-done | bytes 98336 | tf_op jit(solution)/shard_map/all_to_all | solution.py:409
  131.4 1.6 shard_map.88
  132.9 3.6 %all-to-all-start.6 = ((bf16[16,8,3136]{2,1,0:T(8,128)(2,1)}), bf16[16,8,3136]{2,1,0:T(8,128)(2,1)S(1)}, u32[]{:S(2)}, u32[]{:S(2)}) async-start(bf16[16,8,3136]{2,1,0:T(8,128)(2,1)} %bitcast.12), calls=%async_computation.6 | async-start | bytes 1638400 | tf_op jit(solution)/shard_map/all_to_all | solution.py:409
  136.6 1.3 shard_map.89
  137.9 7.4 %collective-permute-start.7 = (bf16[3136,128]{1,0:T(8,128)(2,1)}, bf16[3136,128]{1,0:T(8,128)(2,1)}, u32[]{:S(2)}, u32[]{:S(2)}) collective-permute-start(bf16[3136,128]{1,0:T(8,128)(2,1)} %shard_map.89), channel_id=1, source_target_pairs={{0,1},{1,0},{2,3},{3,2},{4,5},{5,4},{6,7},{7,6},{8,9},{9,8},{10,11... | collective-permute-start | bytes 2408456 | tf_op jit(solution)/shard_map/ppermute | solution.py:495
  145.3 0.2 shard_map.90
  145.6 11.3 %all-gather.10.cloned.1.call-done = bf16[128,4096]{1,0:T(8,128)(2,1)} async-done(((bf16[32,4096]{1,0:T(8,128)(2,1)}), bf16[128,4096]{1,0:T(8,128)(2,1)}) %all-gather.10.cloned.1.call-update) | async-done | bytes 1048592 | tf_op jit(solution)/shard_map/all_gather | solution.py:476
  156.9 1.0 shard_map.91
  157.9 5.5 %all-to-all-start.7 = ((bf16[8,64,384]{2,1,0:T(8,128)(2,1)}), bf16[8,64,384]{2,1,0:T(8,128)(2,1)S(1)}, u32[]{:S(2)}, u32[]{:S(2)}) async-start(bf16[8,64,384]{2,1,0:T(8,128)(2,1)} %shard_map.91), calls=%async_computation.7 | async-start | bytes 786432 | tf_op jit(solution)/shard_map/all_to_all | solution.py:409
  163.5 0.1 fusion.20.spread_ref
  163.9 0.1 reshape.82
  164.0 3.7 %pad.18 = bf16[8,18,16,512]{3,2,1,0:T(8,128)(2,1)} pad(bf16[8,14,14,512]{3,2,1,0:T(8,128)(2,1)} %all-gather.6.cloned.1.call-done, bf16[]{:T(256)} %constant.124.clone.1), padding=0_0x1_3x1_1x0_0 | pad | bytes 3964930 | tf_op jit(solution)/shard_map/vmap(jit(_pad))/pad | solution.py:418
  167.7 2.7 %shard_map.93 = f32[3136,128]{1,0:T(8,128)} custom-call(s32[1]{0:T(128)} %bitcast.1.which_ref, bf16[128,3136]{1,0:T(8,128)(2,1)S(1)} %bitcast.36, bf16[128,256]{1,0:T(8,128)(2,1)S(1)} %bitcast.44, bf16[3136,128]{1,0:T(8,128)(2,1)} %collective-permute-done.7.more_ref), custom_call_target="tpu_custom_call" | custom-call | flops 1000 | bytes 1000 | tf_op jit(solution)/shard_map/pallas_call | solution.py:258
  170.4 1.3 all-to-all-done.7.packs_ref
  171.7 1.7 copy-done.2
  173.4 2.7 %shard_map.92 = (f32[16,72,128]{2,1,0:T(8,128)S(1)}, bf16[16,72,128]{2,1,0:T(8,128)(2,1)S(1)}) custom-call(s32[2]{0:T(128)S(1)} %pad_add_fusion.place_ref, bf16[8,288,512]{2,1,0:T(8,128)(2,1)S(1)} %bitcast.37, bf16[8,64,384]{2,1,0:T(8,128)(2,1)S(1)} %all-to-all-done.7.packs_ref, bf16[64,256]{1,0:T(8,128)(2,1)S(1)} %fusion.20.spread_ref), custom_call_target="tpu_custom_call" | custom-call | flops 1207959552 | bytes 2359296 | tf_op jit(solution)/shard_map/pallas_call | solution.py:341
  176.1 2.9 %collective-permute-start.5 = (bf16[16,72,128]{2,1,0:T(8,128)(2,1)S(1)}, bf16[16,72,128]{2,1,0:T(8,128)(2,1)S(1)}, u32[]{:S(2)}, u32[]{:S(2)}) collective-permute-start(bf16[16,72,128]{2,1,0:T(8,128)(2,1)S(1)} %get-tuple-element.53), channel_id=1, source_target_pairs={{0,1},{1,0},{2,3},{3,2},{4,5},{5,4},{6,7},{7,6},{8,9},{9,8},{10,11... | collective-permute-start | bytes 884744 | tf_op jit(solution)/shard_map/ppermute | solution.py:499
  179.0 0.3 fusion.25
  179.3 0.1 collective-permute-start.6
  179.4 0.1 slice.36
  179.5 0.1 convert_element_type.56
  179.7 0.5 collective-permute-done.5
  180.2 0.8 add_convert_fusion
  181.0 6.8 %all-to-all-start.8 = ((bf16[16,72,128]{2,1,0:T(8,128)(2,1)}), bf16[16,72,128]{2,1,0:T(8,128)(2,1)S(1)}, u32[]{:S(2)}, u32[]{:S(2)}) async-start(bf16[16,72,128]{2,1,0:T(8,128)(2,1)} %add_convert_fusion), calls=%async_computation.8 | async-start | bytes 589824 | tf_op jit(solution)/shard_map/all_to_all | solution.py:409
  187.8 0.7 fusion
  188.6 0.2 shard_map.94
  188.9 2.3 %copy-done.1 = bf16[4608,512]{1,0:T(8,128)(2,1)S(1)} copy-done((bf16[4608,512]{1,0:T(8,128)(2,1)S(1)}, bf16[4608,512]{1,0:T(8,128)(2,1)}, u32[]{:S(2)}) %copy-start.1) | copy-done | bytes 4718616
  191.2 3.5 %shard_map.95 = f32[1,14,14,512]{3,2,1,0:T(8,128)S(1)} custom-call(bf16[288,512]{1,0:T(8,128)(2,1)S(1)} %bitcast.39, bf16[4608,512]{1,0:T(8,128)(2,1)S(1)} %copy-done.1), custom_call_target="tpu_custom_call" | custom-call | flops 1000 | bytes 1000 | tf_op jit(solution)/shard_map/pallas_call | solution.py:382
  194.7 1.2 copy.23
  195.9 1.5 all-to-all-done.8
  197.5 0.7 copy.22
  (54 shorter events, 0.9 us)
Async XLA Ops:
  7.2 50.4 %all-gather.8.cloned.1.call-start = ((), (), s32[]{:S(2)}) async-start(), calls=%async_computation.10 | async-start | bytes 1392640 | tf_op jit(solution)/shard_map/all_gather | solution.py:449
  8.8 4.4 %collective-permute-start.1 = (bf16[16,4352]{1,0:T(8,128)(2,1)}, bf16[16,4352]{1,0:T(8,128)(2,1)S(1)}, u32[]{:S(2)}, u32[]{:S(2)}) collective-permute-start(bf16[16,4352]{1,0:T(8,128)(2,1)} %shard_map.86), channel_id=1, source_target_pairs={{0,1},{1,0},{2,3},{3,2},{4,5},{5,4},{6,7},{7,6},{8,9},{9,8},{10,11... | collective-permute-start | bytes 417800 | tf_op jit(solution)/shard_map/ppermute | solution.py:430
  12.0 21.0 %collective-permute-start = (bf16[3136,128]{1,0:T(8,128)(2,1)}, bf16[3136,128]{1,0:T(8,128)(2,1)S(1)}, u32[]{:S(2)}, u32[]{:S(2)}) collective-permute-start(bf16[3136,128]{1,0:T(8,128)(2,1)} %param.7), channel_id=1, source_target_pairs={{0,1},{1,0},{2,3},{3,2},{4,5},{5,4},{6,7},{7,6},{8,9},{9,8},{10,11... | collective-permute-start | bytes 2408456 | tf_op jit(solution)/shard_map/ppermute | solution.py:450
  14.9 2.3 %copy-start = (bf16[4608,512]{1,0:T(8,128)(2,1)S(1)}, bf16[4608,512]{1,0:T(8,128)(2,1)}, u32[]{:S(2)}) copy-start(bf16[4608,512]{1,0:T(8,128)(2,1)} %weight_ref.3) | copy-start | bytes 14155780
  17.2 0.9 copy-start.4
  21.1 21.2 %copy-start.5 = (bf16[1,14,14,512]{3,2,1,0:T(8,128)(2,1)S(1)}, bf16[1,14,14,512]{3,2,1,0:T(8,128)(2,1)}, u32[]{:S(2)}) copy-start(bf16[1,14,14,512]{3,2,1,0:T(8,128)(2,1)} %maps_ref.1) | copy-start | bytes 602116
  21.2 22.3 %copy-start.7 = (bf16[3136,128]{1,0:T(8,128)(2,1)S(1)}, bf16[3136,128]{1,0:T(8,128)(2,1)}, u32[]{:S(2)}) copy-start(bf16[3136,128]{1,0:T(8,128)(2,1)} %param.7) | copy-start | bytes 2408452
  21.2 11.9 %all-to-all-start = ((bf16[8,16,256]{2,1,0:T(8,128)(2,1)}), bf16[8,16,256]{2,1,0:T(8,128)(2,1)S(1)}, u32[]{:S(2)}, u32[]{:S(2)}) async-start(bf16[8,16,256]{2,1,0:T(8,128)(2,1)} %get-tuple-element.31), calls=%async_computation | async-start | bytes 131072 | tf_op jit(solution)/shard_map/all_to_all | solution.py:409
  34.0 27.1 %all-to-all-start.1 = ((bf16[16,8,3136]{2,1,0:T(8,128)(2,1)}), bf16[16,8,3136]{2,1,0:T(8,128)(2,1)S(1)}, u32[]{:S(2)}, u32[]{:S(2)}) async-start(bf16[16,8,3136]{2,1,0:T(8,128)(2,1)} %shard_map.85), calls=%async_computation.1 | async-start | bytes 1638400 | tf_op jit(solution)/shard_map/all_to_all | solution.py:409
  42.3 83.0 %all-gather.6.cloned.1.call-start = ((), (), s32[]{:S(2)}) async-start(), calls=%async_computation.9 | async-start | bytes 2293760 | tf_op jit(solution)/shard_map/all_gather | solution.py:455
  42.4 12.7 %collective-permute-start.4 = (bf16[1,14,14,512]{3,2,1,0:T(8,128)(2,1)S(1)}, bf16[1,14,14,512]{3,2,1,0:T(8,128)(2,1)S(1)}, u32[]{:S(2)}, u32[]{:S(2)}) collective-permute-start(bf16[1,14,14,512]{3,2,1,0:T(8,128)(2,1)S(1)} %copy-done.5), channel_id=1, source_target_pairs={{0,128},{128,0},{1,129},{129,1},{2,130},{130,2},{3,131},{131,3},{4... | collective-permute-start | bytes 602120 | tf_op jit(solution)/shard_map/ppermute | solution.py:430
  61.1 41.3 %collective-permute-start.2 = (bf16[4,32,4352]{2,1,0:T(8,128)(2,1)}, bf16[4,32,4352]{2,1,0:T(8,128)(2,1)}, u32[]{:S(2)}, u32[]{:S(2)}) collective-permute-start(bf16[4,32,4352]{2,1,0:T(8,128)(2,1)} %bitcast.40), channel_id=1, source_target_pairs={{0,128},{128,0},{1,129},{129,1},{2,130},{130,2},{3,131},{131,3},{4... | collective-permute-start | bytes 3342344 | tf_op jit(solution)/shard_map/ppermute | solution.py:461
  63.1 23.0 %all-to-all-start.2 = ((bf16[8,16,256]{2,1,0:T(8,128)(2,1)}), bf16[8,16,256]{2,1,0:T(8,128)(2,1)S(1)}, u32[]{:S(2)}, u32[]{:S(2)}) async-start(bf16[8,16,256]{2,1,0:T(8,128)(2,1)} %bitcast.6), calls=%async_computation.2 | async-start | bytes 131072 | tf_op jit(solution)/shard_map/all_to_all | solution.py:409
  86.8 15.5 %all-to-all-start.3 = ((bf16[16,16,256]{2,1,0:T(8,128)(2,1)}), bf16[16,16,256]{2,1,0:T(8,128)(2,1)S(1)}, u32[]{:S(2)}, u32[]{:S(2)}) async-start(bf16[16,16,256]{2,1,0:T(8,128)(2,1)} %broadcast_in_dim.8), calls=%async_computation.3 | async-start | bytes 262144 | tf_op jit(solution)/shard_map/all_to_all | solution.py:409
  102.4 1.2 copy-start.3
  106.7 6.4 %collective-permute-start.3 = (bf16[16,4096]{1,0:T(8,128)(2,1)S(1)}, bf16[16,4096]{1,0:T(8,128)(2,1)S(1)}, u32[]{:S(2)}, u32[]{:S(2)}) collective-permute-start(bf16[16,4096]{1,0:T(8,128)(2,1)S(1)} %bitcast.48), channel_id=1, source_target_pairs={{0,128},{128,0},{1,129},{129,1},{2,130},{130,2},{3,131},{131,3},{4... | collective-permute-start | bytes 393224 | tf_op jit(solution)/shard_map/ppermute | solution.py:430
  109.6 10.9 %all-to-all-start.4 = ((bf16[16,16,256]{2,1,0:T(8,128)(2,1)}), bf16[16,16,256]{2,1,0:T(8,128)(2,1)S(1)}, u32[]{:S(2)}, u32[]{:S(2)}) async-start(bf16[16,16,256]{2,1,0:T(8,128)(2,1)} %get-tuple-element.39), calls=%async_computation.4 | async-start | bytes 262144 | tf_op jit(solution)/shard_map/all_to_all | solution.py:409
  121.2 10.2 %all-to-all-start.5 = ((bf16[8,16,384]{2,1,0:T(8,128)(2,1)}), bf16[8,16,384]{2,1,0:T(8,128)(2,1)S(1)}, u32[]{:S(2)}, u32[]{:S(2)}) async-start(bf16[8,16,384]{2,1,0:T(8,128)(2,1)} %fusion.3), calls=%async_computation.5 | async-start | bytes 196608 | tf_op jit(solution)/shard_map/all_to_all | solution.py:409
  124.6 32.3 %all-gather.10.cloned.1.call-start = ((), (), s32[]{:S(2)}) async-start(), calls=%async_computation.11 | async-start | bytes 1310720 | tf_op jit(solution)/shard_map/all_gather | solution.py:476
  132.9 24.0 %all-to-all-start.6 = ((bf16[16,8,3136]{2,1,0:T(8,128)(2,1)}), bf16[16,8,3136]{2,1,0:T(8,128)(2,1)S(1)}, u32[]{:S(2)}, u32[]{:S(2)}) async-start(bf16[16,8,3136]{2,1,0:T(8,128)(2,1)} %bitcast.12), calls=%async_computation.6 | async-start | bytes 1638400 | tf_op jit(solution)/shard_map/all_to_all | solution.py:409
  137.9 29.8 %collective-permute-start.7 = (bf16[3136,128]{1,0:T(8,128)(2,1)}, bf16[3136,128]{1,0:T(8,128)(2,1)}, u32[]{:S(2)}, u32[]{:S(2)}) collective-permute-start(bf16[3136,128]{1,0:T(8,128)(2,1)} %shard_map.89), channel_id=1, source_target_pairs={{0,1},{1,0},{2,3},{3,2},{4,5},{5,4},{6,7},{7,6},{8,9},{9,8},{10,11... | collective-permute-start | bytes 2408456 | tf_op jit(solution)/shard_map/ppermute | solution.py:495
  157.9 13.8 %all-to-all-start.7 = ((bf16[8,64,384]{2,1,0:T(8,128)(2,1)}), bf16[8,64,384]{2,1,0:T(8,128)(2,1)S(1)}, u32[]{:S(2)}, u32[]{:S(2)}) async-start(bf16[8,64,384]{2,1,0:T(8,128)(2,1)} %shard_map.91), calls=%async_computation.7 | async-start | bytes 786432 | tf_op jit(solution)/shard_map/all_to_all | solution.py:409
  171.7 1.7 copy-start.2
  173.3 5.7 %copy-start.6 = (bf16[128,4096]{1,0:T(8,128)(2,1)S(1)}, bf16[128,4096]{1,0:T(8,128)(2,1)}, u32[]{:S(2)}) copy-start(bf16[128,4096]{1,0:T(8,128)(2,1)} %all-gather.10.cloned.1.call-done) | copy-start | bytes 3145732
  176.1 4.1 %collective-permute-start.5 = (bf16[16,72,128]{2,1,0:T(8,128)(2,1)S(1)}, bf16[16,72,128]{2,1,0:T(8,128)(2,1)S(1)}, u32[]{:S(2)}, u32[]{:S(2)}) collective-permute-start(bf16[16,72,128]{2,1,0:T(8,128)(2,1)S(1)} %get-tuple-element.53), channel_id=1, source_target_pairs={{0,1},{1,0},{2,3},{3,2},{4,5},{5,4},{6,7},{7,6},{8,9},{9,8},{10,11... | collective-permute-start | bytes 884744 | tf_op jit(solution)/shard_map/ppermute | solution.py:499
  179.3 8.5 %collective-permute-start.6 = (f32[16,4096]{1,0:T(8,128)S(1)}, f32[16,4096]{1,0:T(8,128)S(1)}, u32[]{:S(2)}, u32[]{:S(2)}) collective-permute-start(f32[16,4096]{1,0:T(8,128)S(1)} %slice.33), channel_id=1, source_target_pairs={{0,1},{1,0},{2,3},{3,2},{4,5},{5,4},{6,7},{7,6},{8,9},{9,8},{10,11... | collective-permute-start | bytes 786440 | tf_op jit(solution)/shard_map/ppermute | solution.py:514
  181.0 16.4 %all-to-all-start.8 = ((bf16[16,72,128]{2,1,0:T(8,128)(2,1)}), bf16[16,72,128]{2,1,0:T(8,128)(2,1)S(1)}, u32[]{:S(2)}, u32[]{:S(2)}) async-start(bf16[16,72,128]{2,1,0:T(8,128)(2,1)} %add_convert_fusion), calls=%async_computation.8 | async-start | bytes 589824 | tf_op jit(solution)/shard_map/all_to_all | solution.py:409
  188.8 2.3 %copy-start.1 = (bf16[4608,512]{1,0:T(8,128)(2,1)S(1)}, bf16[4608,512]{1,0:T(8,128)(2,1)}, u32[]{:S(2)}) copy-start(bf16[4608,512]{1,0:T(8,128)(2,1)} %weight_ref.3) | copy-start | bytes 14155780
Sparse Core Ops, SparseCore 0:
  15.0 26.6 all-gather.7
  56.1 31.0 all-gather.5
  127.8 29.0 all-gather.9

commit v13 on v11

--- a/solution.py
+++ b/solution.py
@@ -10,6 +10,7 @@
 LANES = 128
 LINE = 16
 VMEM = pltpu.CompilerParams(vmem_limit_bytes=20 * 2**20)
+WHOLE = pltpu.CompilerParams(vmem_limit_bytes=57 * 2**20)
 
 
 def activate(value):
@@ -33,7 +34,7 @@
 
 
 def forward_kernel(
-    maps_ref, weight_ref, pre_ref, feat_ref, held_ref, lines_ref, sums_ref, pool_ref, runs_ref, sems
+    image_ref, weight_ref, pre_ref, feat_ref, held_ref, maps_ref, lines_ref, sums_ref, pool_ref, runs_ref, sems
 ):
     pix, chans = pre_ref.shape
     _, height, width, depth = maps_ref.shape
@@ -47,9 +48,12 @@
         )
 
     order = [3 * row + col for col in range(3) for row in range(3)]
+    fetch = pltpu.make_async_copy(image_ref, maps_ref, sems.at[9])
+    fetch.start()
     for tap in order:
         load(tap).start()
     lines_ref[...] = jnp.zeros(lines_ref.shape, F32)
+    fetch.wait()
     for k in range(height):
         at = (k + 1) * LINE + 1
         lines_ref[at : at + width, :] = maps_ref[0, k].astype(F32)
@@ -93,7 +97,7 @@
     return pl.pallas_call(
         forward_kernel,
         in_specs=[
-            pl.BlockSpec(memory_space=pltpu.VMEM),
+            pl.BlockSpec(memory_space=pl.ANY),
             pl.BlockSpec(memory_space=pl.ANY),
         ],
         out_shape=[
@@ -102,27 +106,37 @@
         ],
         scratch_shapes=[
             pltpu.VMEM((3, 3 * depth, chans), BF),
+            pltpu.VMEM(maps.shape, BF),
             pltpu.VMEM((pix + 3 * LINE, depth), F32),
             pltpu.VMEM((3, pix + LINE, chans), F32),
             pltpu.VMEM((chans // LANES, pix // 2, LANES), F32),
             pltpu.VMEM((nx * rows, width), F32),
-            pltpu.SemaphoreType.DMA((9,)),
-        ],
-        compiler_params=VMEM,
+            pltpu.SemaphoreType.DMA((10,)),
+        ],
+        compiler_params=WHOLE,
         cost_estimate=cost(18 * pix * depth * chans, weight.size * 2, pix * chans),
     )(maps, weight)
 
 
-def join_kernel(left_ref, right_ref, out_ref):
-    cut = left_ref.shape[1]
-    out_ref[:, :cut] = left_ref[...]
-    out_ref[:, cut:] = right_ref[...]
+def join_kernel(left_ref, right_ref, out_ref, sems):
+    cut, more = left_ref.shape[1], right_ref.shape[1]
+    copies = [
+        pltpu.make_async_copy(left_ref, out_ref.at[:, pl.ds(0, cut)], sems.at[0]),
+        pltpu.make_async_copy(right_ref, out_ref.at[:, pl.ds(cut, more)], sems.at[1]),
+    ]
+    for copy in copies:
+        copy.start()
+    for copy in copies:
+        copy.wait()
 
 
 def join(left, right):
     rows, cut = left.shape
     return pl.pallas_call(
         join_kernel,
+        in_specs=[pl.BlockSpec(memory_space=pl.ANY)] * 2,
+        out_specs=pl.BlockSpec(memory_space=pl.ANY),
+        scratch_shapes=[pltpu.SemaphoreType.DMA((2,))],
         out_shape=jax.ShapeDtypeStruct((rows, cut + right.shape[1]), left.dtype),
         cost_estimate=cost(0, left.size * 4),
     )(left, right)

time: 187 us -> 188 us (level)
  Pallas kernels: 20.6 us -> 24.4 us
  local copies, waits for them, and re-layouts: 15.8 us -> 12.5 us
    pallas_call x2, Pallas kernels: 4.54 us -> 9.45 us  [the longest x1 5.34 us: join(): pl.pallas_call(join_kernel, in_specs=[pl.BlockSpec(memory_space=pl.ANY)]...]
    unnamed x20, local copies, waits for them, and re-layouts: 10.8 us -> 7.53 us
where the time goes in v13:
time: 188 us; the launch traced here: 186 us
  starting transfers between devices  63.4 us (34%)
  waiting for transfers between devices  63.1 us (34%)
  Pallas kernels  24.4 us (13%)
  between operations  14.1 us (8%)
  local copies, waits for them, and re-layouts  12.5 us (7%)
  other arithmetic  7.65 us (4%)
    all_to_all x9, starting transfers between devices, swap(): return lax.all_to_all(value, axis, 0, 0, tiled=True)  46.9 us
    all_to_all x9, waiting for transfers between devices, swap(): return lax.all_to_all(value, axis, 0, 0, tiled=True)  40.7 us
    all_gather x1, waiting for transfers between devices, on_device(): lax.all_gather(hidden, 'y', axis=0, tiled=False).reshape(group, rows7)  10.9 us
    ppermute x2, waiting for transfers between devices, paired(): return jnp.concatenate([value, lax.ppermute(value, axis, way)], axis=0)  9.98 us
    unnamed x20, local copies, waits for them, and re-layouts  7.53 us
    ppermute x1, starting transfers between devices, on_device(): lax.ppermute(sent6, 'core', pair)  7.29 us
    pallas_call x1, Pallas kernels, join(): pl.pallas_call(join_kernel, in_specs=[pl.BlockSpec(memory_space=pl.ANY)]...  5.34 us
    pallas_call x1, Pallas kernels, conv_forward(): pl.pallas_call(forward_kernel, in_specs=[pl.BlockSpec(memory_space=pl.ANY...  4.11 us
  transfers between devices with their start and end apart: 18, of which 12 were waited for; matrix products, arithmetic and copies ran while one was open for 8% of the time, Pallas kernels for 9%

profile of v13, /device:TPU:1, one launch (start us, length us, event | category | flops | bytes accessed | tf_op | source)
XLA Modules:
  0.0 186.5 jit_solution(9699242468441283420)
XLA Ops:
  7.2 5.3 %shard_map.84 = bf16[16,4352]{1,0:T(8,128)(2,1)} custom-call(bf16[16,4096]{1,0:T(8,128)(2,1)} %bitcast.50, bf16[16,256]{1,0:T(8,128)(2,1)} %bitcast.51), custom_call_target="tpu_custom_call" | custom-call | bytes 262144 | tf_op jit(solution)/shard_map/pallas_call | solution.py:135
  12.6 3.3 %collective-permute-start = (bf16[3136,128]{1,0:T(8,128)(2,1)}, bf16[3136,128]{1,0:T(8,128)(2,1)S(1)}, u32[]{:S(2)}, u32[]{:S(2)}) collective-permute-start(bf16[3136,128]{1,0:T(8,128)(2,1)} %param.7), channel_id=1, source_target_pairs={{0,1},{1,0},{2,3},{3,2},{4,5},{5,4},{6,7},{7,6},{8,9},{9,8},{10,11... | collective-permute-start | bytes 2408456 | tf_op jit(solution)/shard_map/ppermute | solution.py:462
  15.9 4.1 %shard_map.85 = (f32[224,512]{1,0:T(8,128)}, bf16[8,16,256]{2,1,0:T(8,128)(2,1)}) custom-call(bf16[1,14,14,512]{3,2,1,0:T(8,128)(2,1)} %image_ref.1, bf16[4608,512]{1,0:T(8,128)(2,1)} %weight_ref.3), custom_call_target="tpu_custom_call" | custom-call | flops 1056964608 | bytes 4718592 | tf_op jit(solution)/shard_map/pallas_call | solution.py:97
  20.1 5.1 %all-to-all-start = ((bf16[8,16,256]{2,1,0:T(8,128)(2,1)}), bf16[8,16,256]{2,1,0:T(8,128)(2,1)S(1)}, u32[]{:S(2)}, u32[]{:S(2)}) async-start(bf16[8,16,256]{2,1,0:T(8,128)(2,1)} %get-tuple-element.30), calls=%async_computation | async-start | bytes 131072 | tf_op jit(solution)/shard_map/all_to_all | solution.py:420
  25.1 6.7 %all-to-all-done.feat_ref = bf16[8,16,256]{2,1,0:T(8,128)(2,1)S(1)} async-done(((bf16[8,16,256]{2,1,0:T(8,128)(2,1)}), bf16[8,16,256]{2,1,0:T(8,128)(2,1)S(1)}, u32[]{:S(2)}, u32[]{:S(2)}) %all-to-all-start) | async-done | bytes 65568 | tf_op jit(solution)/shard_map/all_to_all | solution.py:420
  31.8 1.0 shard_map.86
  32.8 8.3 %all-to-all-start.1 = ((bf16[16,8,3136]{2,1,0:T(8,128)(2,1)}), bf16[16,8,3136]{2,1,0:T(8,128)(2,1)S(1)}, u32[]{:S(2)}, u32[]{:S(2)}) async-start(bf16[16,8,3136]{2,1,0:T(8,128)(2,1)} %shard_map.86), calls=%async_computation.1 | async-start | bytes 1638400 | tf_op jit(solution)/shard_map/all_to_all | solution.py:420
  41.2 1.2 collective-permute-start.2
  42.4 2.2 %broadcast_select_fusion.1 = (bf16[3136,128]{1,0:T(8,128)(2,1)S(1)}, bf16[3136,128]{1,0:T(8,128)(2,1)}) fusion(bf16[3136,128]{1,0:T(8,128)(2,1)S(1)} %copy-done.6, bf16[3136,128]{1,0:T(8,128)(2,1)} %copy-done.7, pred[]{:T(512)S(6)} %eq.20), kind=kLoop, calls=%fused_computation.3 | loop fusion | flops 802816 | bytes 3211265 | tf_op jit(solution)/shard_map/jit(_where)/select_n | solution.py:469
  44.6 9.4 %collective-permute-done.2 = bf16[1,14,14,512]{3,2,1,0:T(8,128)(2,1)S(1)} collective-permute-done((bf16[1,14,14,512]{3,2,1,0:T(8,128)(2,1)S(1)}, bf16[1,14,14,512]{3,2,1,0:T(8,128)(2,1)S(1)}, u32[]{:S(2)}, u32[]{:S(2)}) %collective-permute-start.2) | collective-permute-done | bytes 200736 | tf_op jit(solution)/shard_map/ppermute | solution.py:441
  54.0 0.8 pad_maximum_fusion.1
  54.9 1.3 pad_maximum_fusion.weight_ref
  56.2 3.9 %all-to-all-done.1 = bf16[16,8,3136]{2,1,0:T(8,128)(2,1)S(1)} async-done(((bf16[16,8,3136]{2,1,0:T(8,128)(2,1)}), bf16[16,8,3136]{2,1,0:T(8,128)(2,1)S(1)}, u32[]{:S(2)}, u32[]{:S(2)}) %all-to-all-start.1) | async-done | bytes 802848 | tf_op jit(solution)/shard_map/all_to_all | solution.py:420
  60.1 1.0 convolution_convert_fusion
  61.1 3.9 %all-to-all-start.2 = ((bf16[8,16,256]{2,1,0:T(8,128)(2,1)}), bf16[8,16,256]{2,1,0:T(8,128)(2,1)S(1)}, u32[]{:S(2)}, u32[]{:S(2)}) async-start(bf16[8,16,256]{2,1,0:T(8,128)(2,1)} %bitcast.6), calls=%async_computation.2 | async-start | bytes 131072 | tf_op jit(solution)/shard_map/all_to_all | solution.py:420
  65.0 6.7 %all-to-all-done.2 = bf16[8,16,256]{2,1,0:T(8,128)(2,1)S(1)} async-done(((bf16[8,16,256]{2,1,0:T(8,128)(2,1)}), bf16[8,16,256]{2,1,0:T(8,128)(2,1)S(1)}, u32[]{:S(2)}, u32[]{:S(2)}) %all-to-all-start.2) | async-done | bytes 65568 | tf_op jit(solution)/shard_map/all_to_all | solution.py:420
  71.8 0.7 broadcast_in_dim.8
  72.4 6.0 %all-to-all-start.3 = ((bf16[16,16,256]{2,1,0:T(8,128)(2,1)}), bf16[16,16,256]{2,1,0:T(8,128)(2,1)S(1)}, u32[]{:S(2)}, u32[]{:S(2)}) async-start(bf16[16,16,256]{2,1,0:T(8,128)(2,1)} %broadcast_in_dim.8), calls=%async_computation.3 | async-start | bytes 262144 | tf_op jit(solution)/shard_map/all_to_all | solution.py:420
  78.5 7.4 %all-to-all-done.3.hidden_ref = bf16[16,16,256]{2,1,0:T(8,128)(2,1)S(1)} async-done(((bf16[16,16,256]{2,1,0:T(8,128)(2,1)}), bf16[16,16,256]{2,1,0:T(8,128)(2,1)S(1)}, u32[]{:S(2)}, u32[]{:S(2)}) %all-to-all-start.3) | async-done | bytes 131104 | tf_op jit(solution)/shard_map/all_to_all | solution.py:420
  85.8 1.6 copy-done.2
  87.5 1.8 shard_map.87
  89.3 1.3 collective-permute-start.1
  90.6 3.5 %all-to-all-start.4 = ((bf16[16,16,256]{2,1,0:T(8,128)(2,1)}), bf16[16,16,256]{2,1,0:T(8,128)(2,1)S(1)}, u32[]{:S(2)}, u32[]{:S(2)}) async-start(bf16[16,16,256]{2,1,0:T(8,128)(2,1)} %get-tuple-element.37), calls=%async_computation.4 | async-start | bytes 262144 | tf_op jit(solution)/shard_map/all_to_all | solution.py:420
  94.1 0.6 collective-permute-done.1
  94.7 0.7 pad_maximum_fusion.2
  95.4 6.1 %all-to-all-done.4 = bf16[16,16,256]{2,1,0:T(8,128)(2,1)S(1)} async-done(((bf16[16,16,256]{2,1,0:T(8,128)(2,1)}), bf16[16,16,256]{2,1,0:T(8,128)(2,1)S(1)}, u32[]{:S(2)}, u32[]{:S(2)}) %all-to-all-start.4) | async-done | bytes 131104 | tf_op jit(solution)/shard_map/all_to_all | solution.py:420
  101.6 0.7 fusion.2
  102.2 4.0 %all-to-all-start.5 = ((bf16[8,16,384]{2,1,0:T(8,128)(2,1)}), bf16[8,16,384]{2,1,0:T(8,128)(2,1)S(1)}, u32[]{:S(2)}, u32[]{:S(2)}) async-start(bf16[8,16,384]{2,1,0:T(8,128)(2,1)} %fusion.2), calls=%async_computation.5 | async-start | bytes 196608 | tf_op jit(solution)/shard_map/all_to_all | solution.py:420
  106.3 0.7 all-gather.10.cloned.1.call-update
  107.0 6.0 %all-to-all-done.5 = bf16[8,16,384]{2,1,0:T(8,128)(2,1)S(1)} async-done(((bf16[8,16,384]{2,1,0:T(8,128)(2,1)}), bf16[8,16,384]{2,1,0:T(8,128)(2,1)S(1)}, u32[]{:S(2)}, u32[]{:S(2)}) %all-to-all-start.5) | async-done | bytes 98336 | tf_op jit(solution)/shard_map/all_to_all | solution.py:420
  113.0 1.6 shard_map.88
  114.6 3.8 %all-to-all-start.6 = ((bf16[16,8,3136]{2,1,0:T(8,128)(2,1)}), bf16[16,8,3136]{2,1,0:T(8,128)(2,1)S(1)}, u32[]{:S(2)}, u32[]{:S(2)}) async-start(bf16[16,8,3136]{2,1,0:T(8,128)(2,1)} %bitcast.11), calls=%async_computation.6 | async-start | bytes 1638400 | tf_op jit(solution)/shard_map/all_to_all | solution.py:420
  118.4 1.3 shard_map.89
  119.7 7.3 %collective-permute-start.5 = (bf16[3136,128]{1,0:T(8,128)(2,1)}, bf16[3136,128]{1,0:T(8,128)(2,1)S(1)}, u32[]{:S(2)}, u32[]{:S(2)}) collective-permute-start(bf16[3136,128]{1,0:T(8,128)(2,1)} %shard_map.89), channel_id=1, source_target_pairs={{0,1},{1,0},{2,3},{3,2},{4,5},{5,4},{6,7},{7,6},{8,9},{9,8},{10,11... | collective-permute-start | bytes 2408456 | tf_op jit(solution)/shard_map/ppermute | solution.py:505
  127.0 0.1 pad_add_fusion.place_ref
  127.1 0.2 shard_map.90
  127.3 0.1 fusion.19.spread_ref
  127.5 10.9 %all-gather.10.cloned.1.call-done = bf16[128,4096]{1,0:T(8,128)(2,1)} async-done(((bf16[32,4096]{1,0:T(8,128)(2,1)}), bf16[128,4096]{1,0:T(8,128)(2,1)}) %all-gather.10.cloned.1.call-update) | async-done | bytes 1048592 | tf_op jit(solution)/shard_map/all_gather | solution.py:487
  138.4 1.0 shard_map.91
  139.4 5.5 %all-to-all-start.7 = ((bf16[8,64,384]{2,1,0:T(8,128)(2,1)}), bf16[8,64,384]{2,1,0:T(8,128)(2,1)S(1)}, u32[]{:S(2)}, u32[]{:S(2)}) async-start(bf16[8,64,384]{2,1,0:T(8,128)(2,1)} %shard_map.91), calls=%async_computation.7 | async-start | bytes 786432 | tf_op jit(solution)/shard_map/all_to_all | solution.py:420
  145.0 0.1 reshape.81
  145.1 0.1 copy.21
  145.2 0.1 reshape.82
  145.3 3.7 %pad.18 = bf16[8,18,16,512]{3,2,1,0:T(8,128)(2,1)} pad(bf16[8,14,14,512]{3,2,1,0:T(8,128)(2,1)} %all-gather.6.cloned.1.call-done, bf16[]{:T(256)} %constant.124.clone.1), padding=0_0x1_3x1_1x0_0 | pad | bytes 3964930 | tf_op jit(solution)/shard_map/vmap(jit(_pad))/pad | solution.py:429
  149.0 1.6 shard_map.93
  150.5 0.3 fusion.24
  150.8 2.4 %all-to-all-done.7.packs_ref = bf16[8,64,384]{2,1,0:T(8,128)(2,1)S(1)} async-done(((bf16[8,64,384]{2,1,0:T(8,128)(2,1)}), bf16[8,64,384]{2,1,0:T(8,128)(2,1)S(1)}, u32[]{:S(2)}, u32[]{:S(2)}) %all-to-all-start.7) | async-done | bytes 393248 | tf_op jit(solution)/shard_map/all_to_all | solution.py:420
  153.2 1.7 copy-done.1
  154.9 2.7 %shard_map.92 = (f32[16,72,128]{2,1,0:T(8,128)S(1)}, bf16[16,72,128]{2,1,0:T(8,128)(2,1)S(1)}) custom-call(s32[2]{0:T(128)S(1)} %pad_add_fusion.place_ref, bf16[8,288,512]{2,1,0:T(8,128)(2,1)S(1)} %bitcast.36, bf16[8,64,384]{2,1,0:T(8,128)(2,1)S(1)} %all-to-all-done.7.packs_ref, bf16[64,256]{1,0:T(8,128)(2,1)S(1)} %fusion.19.spread_ref), custom_call_target="tpu_custom_call" | custom-call | flops 1207959552 | bytes 2359296 | tf_op jit(solution)/shard_map/pallas_call | solution.py:352
  157.6 3.1 %collective-permute-start.3 = (bf16[16,72,128]{2,1,0:T(8,128)(2,1)S(1)}, bf16[16,72,128]{2,1,0:T(8,128)(2,1)S(1)}, u32[]{:S(2)}, u32[]{:S(2)}) collective-permute-start(bf16[16,72,128]{2,1,0:T(8,128)(2,1)S(1)} %get-tuple-element.51), channel_id=1, source_target_pairs={{0,1},{1,0},{2,3},{3,2},{4,5},{5,4},{6,7},{7,6},{8,9},{9,8},{10,11... | collective-permute-start | bytes 884744 | tf_op jit(solution)/shard_map/ppermute | solution.py:509
  160.7 0.1 collective-permute-start.4
  160.8 0.1 slice.38
  160.9 0.1 convert_element_type.56
  161.1 0.8 collective-permute-done.3
  161.9 0.8 add_convert_fusion
  162.7 6.9 %all-to-all-start.8 = ((bf16[16,72,128]{2,1,0:T(8,128)(2,1)}), bf16[16,72,128]{2,1,0:T(8,128)(2,1)S(1)}, u32[]{:S(2)}, u32[]{:S(2)}) async-start(bf16[16,72,128]{2,1,0:T(8,128)(2,1)} %add_convert_fusion), calls=%async_computation.8 | async-start | bytes 589824 | tf_op jit(solution)/shard_map/all_to_all | solution.py:420
  169.5 0.7 add_bitcast_fusion
  170.3 0.2 shard_map.94
  170.6 2.3 %copy-done = bf16[4608,512]{1,0:T(8,128)(2,1)S(1)} copy-done((bf16[4608,512]{1,0:T(8,128)(2,1)S(1)}, bf16[4608,512]{1,0:T(8,128)(2,1)}, u32[]{:S(2)}) %copy-start) | copy-done | bytes 4718616
  172.9 3.5 %shard_map.95 = f32[1,14,14,512]{3,2,1,0:T(8,128)S(1)} custom-call(bf16[288,512]{1,0:T(8,128)(2,1)S(1)} %bitcast.39, bf16[4608,512]{1,0:T(8,128)(2,1)S(1)} %copy-done), custom_call_target="tpu_custom_call" | custom-call | flops 1000 | bytes 1000 | tf_op jit(solution)/shard_map/pallas_call | solution.py:393
  176.4 1.2 copy.23
  177.6 1.5 all-to-all-done.8
  179.1 0.1 fusion.23
  179.2 0.7 copy.22
  (51 shorter events, 0.6 us)
Async XLA Ops:
  7.2 78.7 %all-gather.8.cloned.1.call-start = ((), (), s32[]{:S(2)}) async-start(), calls=%async_computation.10 | async-start | bytes 2367488 | tf_op jit(solution)/shard_map/all_gather | solution.py:460
  12.6 19.2 %collective-permute-start = (bf16[3136,128]{1,0:T(8,128)(2,1)}, bf16[3136,128]{1,0:T(8,128)(2,1)S(1)}, u32[]{:S(2)}, u32[]{:S(2)}) collective-permute-start(bf16[3136,128]{1,0:T(8,128)(2,1)} %param.7), channel_id=1, source_target_pairs={{0,1},{1,0},{2,3},{3,2},{4,5},{5,4},{6,7},{7,6},{8,9},{9,8},{10,11... | collective-permute-start | bytes 2408456 | tf_op jit(solution)/shard_map/ppermute | solution.py:462
  20.0 21.2 %copy-start.5 = (bf16[1,14,14,512]{3,2,1,0:T(8,128)(2,1)S(1)}, bf16[1,14,14,512]{3,2,1,0:T(8,128)(2,1)}, u32[]{:S(2)}) copy-start(bf16[1,14,14,512]{3,2,1,0:T(8,128)(2,1)} %image_ref.1) | copy-start | bytes 602116
  20.0 22.4 %copy-start.6 = (bf16[3136,128]{1,0:T(8,128)(2,1)S(1)}, bf16[3136,128]{1,0:T(8,128)(2,1)}, u32[]{:S(2)}) copy-start(bf16[3136,128]{1,0:T(8,128)(2,1)} %param.7) | copy-start | bytes 2408452
  20.1 11.8 %all-to-all-start = ((bf16[8,16,256]{2,1,0:T(8,128)(2,1)}), bf16[8,16,256]{2,1,0:T(8,128)(2,1)S(1)}, u32[]{:S(2)}, u32[]{:S(2)}) async-start(bf16[8,16,256]{2,1,0:T(8,128)(2,1)} %get-tuple-element.30), calls=%async_computation | async-start | bytes 131072 | tf_op jit(solution)/shard_map/all_to_all | solution.py:420
  31.8 9.4 %copy-start.7 = (bf16[3136,128]{1,0:T(8,128)(2,1)}, bf16[3136,128]{1,0:T(8,128)(2,1)S(1)}, u32[]{:S(2)}) copy-start(bf16[3136,128]{1,0:T(8,128)(2,1)S(1)} %collective-permute-done) | copy-start | bytes 2408452
  32.8 27.3 %all-to-all-start.1 = ((bf16[16,8,3136]{2,1,0:T(8,128)(2,1)}), bf16[16,8,3136]{2,1,0:T(8,128)(2,1)S(1)}, u32[]{:S(2)}, u32[]{:S(2)}) async-start(bf16[16,8,3136]{2,1,0:T(8,128)(2,1)} %shard_map.86), calls=%async_computation.1 | async-start | bytes 1638400 | tf_op jit(solution)/shard_map/all_to_all | solution.py:420
  41.2 65.8 %all-gather.6.cloned.1.call-start = ((), (), s32[]{:S(2)}) async-start(), calls=%async_computation.9 | async-start | bytes 2293760 | tf_op jit(solution)/shard_map/all_gather | solution.py:467
  41.2 12.8 %collective-permute-start.2 = (bf16[1,14,14,512]{3,2,1,0:T(8,128)(2,1)S(1)}, bf16[1,14,14,512]{3,2,1,0:T(8,128)(2,1)S(1)}, u32[]{:S(2)}, u32[]{:S(2)}) collective-permute-start(bf16[1,14,14,512]{3,2,1,0:T(8,128)(2,1)S(1)} %copy-done.5), channel_id=1, source_target_pairs={{0,128},{128,0},{1,129},{129,1},{2,130},{130,2},{3,131},{131,3},{4... | collective-permute-start | bytes 602120 | tf_op jit(solution)/shard_map/ppermute | solution.py:441
  61.1 10.6 %all-to-all-start.2 = ((bf16[8,16,256]{2,1,0:T(8,128)(2,1)}), bf16[8,16,256]{2,1,0:T(8,128)(2,1)S(1)}, u32[]{:S(2)}, u32[]{:S(2)}) async-start(bf16[8,16,256]{2,1,0:T(8,128)(2,1)} %bitcast.6), calls=%async_computation.2 | async-start | bytes 131072 | tf_op jit(solution)/shard_map/all_to_all | solution.py:420
  72.4 13.4 %all-to-all-start.3 = ((bf16[16,16,256]{2,1,0:T(8,128)(2,1)}), bf16[16,16,256]{2,1,0:T(8,128)(2,1)S(1)}, u32[]{:S(2)}, u32[]{:S(2)}) async-start(bf16[16,16,256]{2,1,0:T(8,128)(2,1)} %broadcast_in_dim.8), calls=%async_computation.3 | async-start | bytes 262144 | tf_op jit(solution)/shard_map/all_to_all | solution.py:420
  85.8 1.6 copy-start.2
  89.3 5.4 %collective-permute-start.1 = (bf16[16,4096]{1,0:T(8,128)(2,1)S(1)}, bf16[16,4096]{1,0:T(8,128)(2,1)S(1)}, u32[]{:S(2)}, u32[]{:S(2)}) collective-permute-start(bf16[16,4096]{1,0:T(8,128)(2,1)S(1)} %bitcast.46), channel_id=1, source_target_pairs={{0,128},{128,0},{1,129},{129,1},{2,130},{130,2},{3,131},{131,3},{4... | collective-permute-start | bytes 393224 | tf_op jit(solution)/shard_map/ppermute | solution.py:441
  90.6 10.9 %all-to-all-start.4 = ((bf16[16,16,256]{2,1,0:T(8,128)(2,1)}), bf16[16,16,256]{2,1,0:T(8,128)(2,1)S(1)}, u32[]{:S(2)}, u32[]{:S(2)}) async-start(bf16[16,16,256]{2,1,0:T(8,128)(2,1)} %get-tuple-element.37), calls=%async_computation.4 | async-start | bytes 262144 | tf_op jit(solution)/shard_map/all_to_all | solution.py:420
  102.2 10.8 %all-to-all-start.5 = ((bf16[8,16,384]{2,1,0:T(8,128)(2,1)}), bf16[8,16,384]{2,1,0:T(8,128)(2,1)S(1)}, u32[]{:S(2)}, u32[]{:S(2)}) async-start(bf16[8,16,384]{2,1,0:T(8,128)(2,1)} %fusion.2), calls=%async_computation.5 | async-start | bytes 196608 | tf_op jit(solution)/shard_map/all_to_all | solution.py:420
  106.2 32.2 %all-gather.10.cloned.1.call-start = ((), (), s32[]{:S(2)}) async-start(), calls=%async_computation.11 | async-start | bytes 1310720 | tf_op jit(solution)/shard_map/all_gather | solution.py:487
  113.0 14.4 %copy-start.8 = (bf16[8,16,384]{2,1,0:T(8,128)(2,1)}, bf16[8,16,384]{2,1,0:T(8,128)(2,1)S(1)}, u32[]{:S(2)}) copy-start(bf16[8,16,384]{2,1,0:T(8,128)(2,1)S(1)} %all-to-all-done.5) | copy-start | bytes 294916
  114.6 12.5 %copy-start.3 = (f32[224,512]{1,0:T(8,128)S(1)}, f32[224,512]{1,0:T(8,128)}, u32[]{:S(2)}) copy-start(f32[224,512]{1,0:T(8,128)} %get-tuple-element.49.pre_ref) | copy-start | bytes 1376260
  114.6 23.8 %all-to-all-start.6 = ((bf16[16,8,3136]{2,1,0:T(8,128)(2,1)}), bf16[16,8,3136]{2,1,0:T(8,128)(2,1)S(1)}, u32[]{:S(2)}, u32[]{:S(2)}) async-start(bf16[16,8,3136]{2,1,0:T(8,128)(2,1)} %bitcast.11), calls=%async_computation.6 | async-start | bytes 1638400 | tf_op jit(solution)/shard_map/all_to_all | solution.py:420
  119.7 29.3 %collective-permute-start.5 = (bf16[3136,128]{1,0:T(8,128)(2,1)}, bf16[3136,128]{1,0:T(8,128)(2,1)S(1)}, u32[]{:S(2)}, u32[]{:S(2)}) collective-permute-start(bf16[3136,128]{1,0:T(8,128)(2,1)} %shard_map.89), channel_id=1, source_target_pairs={{0,1},{1,0},{2,3},{3,2},{4,5},{5,4},{6,7},{7,6},{8,9},{9,8},{10,11... | collective-permute-start | bytes 2408456 | tf_op jit(solution)/shard_map/ppermute | solution.py:505
  127.5 17.5 %slice-start = ((bf16[8,16,384]{2,1,0:T(8,128)(2,1)}), bf16[8,16,32]{2,1,0:T(8,128)(2,1)S(1)}, s32[]{:S(2)}) async-start(bf16[8,16,384]{2,1,0:T(8,128)(2,1)} %copy-done.8), calls=%async_computation.12 | async-start | bytes 65536 | tf_op jit(solution)/shard_map/slice | solution.py:496
  139.4 13.7 %all-to-all-start.7 = ((bf16[8,64,384]{2,1,0:T(8,128)(2,1)}), bf16[8,64,384]{2,1,0:T(8,128)(2,1)S(1)}, u32[]{:S(2)}, u32[]{:S(2)}) async-start(bf16[8,64,384]{2,1,0:T(8,128)(2,1)} %shard_map.91), calls=%async_computation.7 | async-start | bytes 786432 | tf_op jit(solution)/shard_map/all_to_all | solution.py:420
  149.0 1.6 copy-start.4
  153.2 1.7 copy-start.1
  157.6 4.3 %collective-permute-start.3 = (bf16[16,72,128]{2,1,0:T(8,128)(2,1)S(1)}, bf16[16,72,128]{2,1,0:T(8,128)(2,1)S(1)}, u32[]{:S(2)}, u32[]{:S(2)}) collective-permute-start(bf16[16,72,128]{2,1,0:T(8,128)(2,1)S(1)} %get-tuple-element.51), channel_id=1, source_target_pairs={{0,1},{1,0},{2,3},{3,2},{4,5},{5,4},{6,7},{7,6},{8,9},{9,8},{10,11... | collective-permute-start | bytes 884744 | tf_op jit(solution)/shard_map/ppermute | solution.py:509
  160.7 8.8 %collective-permute-start.4 = (f32[16,4096]{1,0:T(8,128)S(1)}, f32[16,4096]{1,0:T(8,128)S(1)}, u32[]{:S(2)}, u32[]{:S(2)}) collective-permute-start(f32[16,4096]{1,0:T(8,128)S(1)} %slice_select_fusion), channel_id=1, source_target_pairs={{0,1},{1,0},{2,3},{3,2},{4,5},{5,4},{6,7},{7,6},{8,9},{9,8},{10,11... | collective-permute-start | bytes 786440 | tf_op jit(solution)/shard_map/ppermute | solution.py:525
  162.7 16.4 %all-to-all-start.8 = ((bf16[16,72,128]{2,1,0:T(8,128)(2,1)}), bf16[16,72,128]{2,1,0:T(8,128)(2,1)S(1)}, u32[]{:S(2)}, u32[]{:S(2)}) async-start(bf16[16,72,128]{2,1,0:T(8,128)(2,1)} %add_convert_fusion), calls=%async_computation.8 | async-start | bytes 589824 | tf_op jit(solution)/shard_map/all_to_all | solution.py:420
  170.5 2.3 %copy-start = (bf16[4608,512]{1,0:T(8,128)(2,1)S(1)}, bf16[4608,512]{1,0:T(8,128)(2,1)}, u32[]{:S(2)}) copy-start(bf16[4608,512]{1,0:T(8,128)(2,1)} %weight_ref.3) | copy-start | bytes 14155780
Sparse Core Ops, SparseCore 0:
  12.7 59.7 all-gather.7
  74.3 29.0 all-gather.5
  109.5 28.9 all-gather.9

commit v14 on v11

--- a/solution.py
+++ b/solution.py
@@ -10,6 +10,7 @@
 LANES = 128
 LINE = 16
 VMEM = pltpu.CompilerParams(vmem_limit_bytes=20 * 2**20)
+WHOLE = pltpu.CompilerParams(vmem_limit_bytes=57 * 2**20)
 
 
 def activate(value):
@@ -33,7 +34,7 @@
 
 
 def forward_kernel(
-    maps_ref, weight_ref, pre_ref, feat_ref, held_ref, lines_ref, sums_ref, pool_ref, runs_ref, sems
+    image_ref, weight_ref, pre_ref, feat_ref, held_ref, maps_ref, lines_ref, sums_ref, pool_ref, runs_ref, sems
 ):
     pix, chans = pre_ref.shape
     _, height, width, depth = maps_ref.shape
@@ -47,9 +48,12 @@
         )
 
     order = [3 * row + col for col in range(3) for row in range(3)]
+    fetch = pltpu.make_async_copy(image_ref, maps_ref, sems.at[9])
+    fetch.start()
     for tap in order:
         load(tap).start()
     lines_ref[...] = jnp.zeros(lines_ref.shape, F32)
+    fetch.wait()
     for k in range(height):
         at = (k + 1) * LINE + 1
         lines_ref[at : at + width, :] = maps_ref[0, k].astype(F32)
@@ -93,7 +97,7 @@
     return pl.pallas_call(
         forward_kernel,
         in_specs=[
-            pl.BlockSpec(memory_space=pltpu.VMEM),
+            pl.BlockSpec(memory_space=pl.ANY),
             pl.BlockSpec(memory_space=pl.ANY),
         ],
         out_shape=[
@@ -102,13 +106,14 @@
         ],
         scratch_shapes=[
             pltpu.VMEM((3, 3 * depth, chans), BF),
+            pltpu.VMEM(maps.shape, BF),
             pltpu.VMEM((pix + 3 * LINE, depth), F32),
             pltpu.VMEM((3, pix + LINE, chans), F32),
             pltpu.VMEM((chans // LANES, pix // 2, LANES), F32),
             pltpu.VMEM((nx * rows, width), F32),
-            pltpu.SemaphoreType.DMA((9,)),
-        ],
-        compiler_params=VMEM,
+            pltpu.SemaphoreType.DMA((10,)),
+        ],
+        compiler_params=WHOLE,
         cost_estimate=cost(18 * pix * depth * chans, weight.size * 2, pix * chans),
     )(maps, weight)
 

time: 187 us -> 184 us (0.984)
  local copies, waits for them, and re-layouts: 15.8 us -> 12.7 us
    unnamed x20, local copies, waits for them, and re-layouts: 10.8 us -> 7.64 us
where the time goes in v14:
time: 184 us; the launch traced here: 183 us
  waiting for transfers between devices  63.3 us (34%)
  starting transfers between devices  63.1 us (34%)
  Pallas kernels  20.6 us (11%)
  between operations  14.1 us (8%)
  local copies, waits for them, and re-layouts  12.7 us (7%)
  other arithmetic  7.65 us (4%)
    all_to_all x9, starting transfers between devices, swap(): return lax.all_to_all(value, axis, 0, 0, tiled=True)  46.7 us
    all_to_all x9, waiting for transfers between devices, swap(): return lax.all_to_all(value, axis, 0, 0, tiled=True)  40.7 us
    all_gather x1, waiting for transfers between devices, on_device(): lax.all_gather(hidden, 'y', axis=0, tiled=False).reshape(group, rows7)  10.9 us
    ppermute x2, waiting for transfers between devices, paired(): return jnp.concatenate([value, lax.ppermute(value, axis, way)], axis=0)  10.2 us
    unnamed x20, local copies, waits for them, and re-layouts  7.64 us
    ppermute x1, starting transfers between devices, on_device(): lax.ppermute(sent6, 'core', pair)  7.3 us
    pallas_call x1, Pallas kernels, conv_forward(): pl.pallas_call(forward_kernel, in_specs=[pl.BlockSpec(memory_space=pl.ANY...  4.11 us
    pad x2, local copies, waits for them, and re-layouts, bordered(): padded = jnp.pad(maps, ((1, 3), (1, LINE - side - 1), (0, 0)))  3.75 us
  transfers between devices with their start and end apart: 18, of which 12 were waited for; matrix products, arithmetic and copies ran while one was open for 8% of the time, Pallas kernels for 9%

profile of v14, /device:TPU:1, one launch (start us, length us, event | category | flops | bytes accessed | tf_op | source)
XLA Modules:
  0.0 182.7 jit_solution(11836867098679935364)
XLA Ops:
  7.2 1.6 shard_map.84
  8.8 3.3 %collective-permute-start = (bf16[3136,128]{1,0:T(8,128)(2,1)}, bf16[3136,128]{1,0:T(8,128)(2,1)S(1)}, u32[]{:S(2)}, u32[]{:S(2)}) collective-permute-start(bf16[3136,128]{1,0:T(8,128)(2,1)} %param.7), channel_id=1, source_target_pairs={{0,1},{1,0},{2,3},{3,2},{4,5},{5,4},{6,7},{7,6},{8,9},{9,8},{10,11... | collective-permute-start | bytes 2408456 | tf_op jit(solution)/shard_map/ppermute | solution.py:453
  12.1 4.1 %shard_map.85 = (f32[224,512]{1,0:T(8,128)}, bf16[8,16,256]{2,1,0:T(8,128)(2,1)}) custom-call(bf16[1,14,14,512]{3,2,1,0:T(8,128)(2,1)} %image_ref.1, bf16[4608,512]{1,0:T(8,128)(2,1)} %weight_ref.3), custom_call_target="tpu_custom_call" | custom-call | flops 1056964608 | bytes 4718592 | tf_op jit(solution)/shard_map/pallas_call | solution.py:97
  16.3 5.1 %all-to-all-start = ((bf16[8,16,256]{2,1,0:T(8,128)(2,1)}), bf16[8,16,256]{2,1,0:T(8,128)(2,1)S(1)}, u32[]{:S(2)}, u32[]{:S(2)}) async-start(bf16[8,16,256]{2,1,0:T(8,128)(2,1)} %get-tuple-element.30), calls=%async_computation | async-start | bytes 131072 | tf_op jit(solution)/shard_map/all_to_all | solution.py:411
  21.4 6.7 %all-to-all-done.feat_ref = bf16[8,16,256]{2,1,0:T(8,128)(2,1)S(1)} async-done(((bf16[8,16,256]{2,1,0:T(8,128)(2,1)}), bf16[8,16,256]{2,1,0:T(8,128)(2,1)S(1)}, u32[]{:S(2)}, u32[]{:S(2)}) %all-to-all-start) | async-done | bytes 65568 | tf_op jit(solution)/shard_map/all_to_all | solution.py:411
  28.1 1.0 shard_map.86
  29.1 8.3 %all-to-all-start.1 = ((bf16[16,8,3136]{2,1,0:T(8,128)(2,1)}), bf16[16,8,3136]{2,1,0:T(8,128)(2,1)S(1)}, u32[]{:S(2)}, u32[]{:S(2)}) async-start(bf16[16,8,3136]{2,1,0:T(8,128)(2,1)} %shard_map.86), calls=%async_computation.1 | async-start | bytes 1638400 | tf_op jit(solution)/shard_map/all_to_all | solution.py:411
  37.5 1.2 collective-permute-start.2
  38.7 2.2 %broadcast_select_fusion.1 = (bf16[3136,128]{1,0:T(8,128)(2,1)S(1)}, bf16[3136,128]{1,0:T(8,128)(2,1)}) fusion(bf16[3136,128]{1,0:T(8,128)(2,1)S(1)} %copy-done.6, bf16[3136,128]{1,0:T(8,128)(2,1)} %copy-done.7, pred[]{:T(512)S(6)} %eq.20), kind=kLoop, calls=%fused_computation.3 | loop fusion | flops 802816 | bytes 3211265 | tf_op jit(solution)/shard_map/jit(_where)/select_n | solution.py:460
  40.8 9.5 %collective-permute-done.2 = bf16[1,14,14,512]{3,2,1,0:T(8,128)(2,1)S(1)} collective-permute-done((bf16[1,14,14,512]{3,2,1,0:T(8,128)(2,1)S(1)}, bf16[1,14,14,512]{3,2,1,0:T(8,128)(2,1)S(1)}, u32[]{:S(2)}, u32[]{:S(2)}) %collective-permute-start.2) | collective-permute-done | bytes 200736 | tf_op jit(solution)/shard_map/ppermute | solution.py:432
  50.3 0.8 pad_maximum_fusion.1
  51.2 1.3 pad_maximum_fusion.weight_ref
  52.5 3.9 %all-to-all-done.1 = bf16[16,8,3136]{2,1,0:T(8,128)(2,1)S(1)} async-done(((bf16[16,8,3136]{2,1,0:T(8,128)(2,1)}), bf16[16,8,3136]{2,1,0:T(8,128)(2,1)S(1)}, u32[]{:S(2)}, u32[]{:S(2)}) %all-to-all-start.1) | async-done | bytes 802848 | tf_op jit(solution)/shard_map/all_to_all | solution.py:411
  56.4 1.0 convolution_convert_fusion
  57.4 3.8 %all-to-all-start.2 = ((bf16[8,16,256]{2,1,0:T(8,128)(2,1)}), bf16[8,16,256]{2,1,0:T(8,128)(2,1)S(1)}, u32[]{:S(2)}, u32[]{:S(2)}) async-start(bf16[8,16,256]{2,1,0:T(8,128)(2,1)} %bitcast.6), calls=%async_computation.2 | async-start | bytes 131072 | tf_op jit(solution)/shard_map/all_to_all | solution.py:411
  61.3 6.8 %all-to-all-done.2 = bf16[8,16,256]{2,1,0:T(8,128)(2,1)S(1)} async-done(((bf16[8,16,256]{2,1,0:T(8,128)(2,1)}), bf16[8,16,256]{2,1,0:T(8,128)(2,1)S(1)}, u32[]{:S(2)}, u32[]{:S(2)}) %all-to-all-start.2) | async-done | bytes 65568 | tf_op jit(solution)/shard_map/all_to_all | solution.py:411
  68.1 0.7 broadcast_in_dim.8
  68.8 5.9 %all-to-all-start.3 = ((bf16[16,16,256]{2,1,0:T(8,128)(2,1)}), bf16[16,16,256]{2,1,0:T(8,128)(2,1)S(1)}, u32[]{:S(2)}, u32[]{:S(2)}) async-start(bf16[16,16,256]{2,1,0:T(8,128)(2,1)} %broadcast_in_dim.8), calls=%async_computation.3 | async-start | bytes 262144 | tf_op jit(solution)/shard_map/all_to_all | solution.py:411
  74.7 7.4 %all-to-all-done.3.hidden_ref = bf16[16,16,256]{2,1,0:T(8,128)(2,1)S(1)} async-done(((bf16[16,16,256]{2,1,0:T(8,128)(2,1)}), bf16[16,16,256]{2,1,0:T(8,128)(2,1)S(1)}, u32[]{:S(2)}, u32[]{:S(2)}) %all-to-all-start.3) | async-done | bytes 131104 | tf_op jit(solution)/shard_map/all_to_all | solution.py:411
  82.1 1.7 copy-done.2
  83.8 1.8 shard_map.87
  85.6 1.3 collective-permute-start.1
  86.9 3.5 %all-to-all-start.4 = ((bf16[16,16,256]{2,1,0:T(8,128)(2,1)}), bf16[16,16,256]{2,1,0:T(8,128)(2,1)S(1)}, u32[]{:S(2)}, u32[]{:S(2)}) async-start(bf16[16,16,256]{2,1,0:T(8,128)(2,1)} %get-tuple-element.37), calls=%async_computation.4 | async-start | bytes 262144 | tf_op jit(solution)/shard_map/all_to_all | solution.py:411
  90.4 0.7 collective-permute-done.1
  91.1 0.7 pad_maximum_fusion.2
  91.8 6.0 %all-to-all-done.4 = bf16[16,16,256]{2,1,0:T(8,128)(2,1)S(1)} async-done(((bf16[16,16,256]{2,1,0:T(8,128)(2,1)}), bf16[16,16,256]{2,1,0:T(8,128)(2,1)S(1)}, u32[]{:S(2)}, u32[]{:S(2)}) %all-to-all-start.4) | async-done | bytes 131104 | tf_op jit(solution)/shard_map/all_to_all | solution.py:411
  97.8 0.7 fusion.2
  98.5 4.0 %all-to-all-start.5 = ((bf16[8,16,384]{2,1,0:T(8,128)(2,1)}), bf16[8,16,384]{2,1,0:T(8,128)(2,1)S(1)}, u32[]{:S(2)}, u32[]{:S(2)}) async-start(bf16[8,16,384]{2,1,0:T(8,128)(2,1)} %fusion.2), calls=%async_computation.5 | async-start | bytes 196608 | tf_op jit(solution)/shard_map/all_to_all | solution.py:411
  102.5 0.7 all-gather.10.cloned.1.call-update
  103.2 6.0 %all-to-all-done.5 = bf16[8,16,384]{2,1,0:T(8,128)(2,1)S(1)} async-done(((bf16[8,16,384]{2,1,0:T(8,128)(2,1)}), bf16[8,16,384]{2,1,0:T(8,128)(2,1)S(1)}, u32[]{:S(2)}, u32[]{:S(2)}) %all-to-all-start.5) | async-done | bytes 98336 | tf_op jit(solution)/shard_map/all_to_all | solution.py:411
  109.3 1.6 shard_map.88
  110.8 3.8 %all-to-all-start.6 = ((bf16[16,8,3136]{2,1,0:T(8,128)(2,1)}), bf16[16,8,3136]{2,1,0:T(8,128)(2,1)S(1)}, u32[]{:S(2)}, u32[]{:S(2)}) async-start(bf16[16,8,3136]{2,1,0:T(8,128)(2,1)} %bitcast.11), calls=%async_computation.6 | async-start | bytes 1638400 | tf_op jit(solution)/shard_map/all_to_all | solution.py:411
  114.6 1.3 shard_map.89
  115.9 7.3 %collective-permute-start.5 = (bf16[3136,128]{1,0:T(8,128)(2,1)}, bf16[3136,128]{1,0:T(8,128)(2,1)S(1)}, u32[]{:S(2)}, u32[]{:S(2)}) collective-permute-start(bf16[3136,128]{1,0:T(8,128)(2,1)} %shard_map.89), channel_id=1, source_target_pairs={{0,1},{1,0},{2,3},{3,2},{4,5},{5,4},{6,7},{7,6},{8,9},{9,8},{10,11... | collective-permute-start | bytes 2408456 | tf_op jit(solution)/shard_map/ppermute | solution.py:496
  123.2 0.1 pad_add_fusion.place_ref
  123.3 0.2 shard_map.90
  123.6 0.1 fusion.19.spread_ref
  123.7 10.9 %all-gather.10.cloned.1.call-done = bf16[128,4096]{1,0:T(8,128)(2,1)} async-done(((bf16[32,4096]{1,0:T(8,128)(2,1)}), bf16[128,4096]{1,0:T(8,128)(2,1)}) %all-gather.10.cloned.1.call-update) | async-done | bytes 1048592 | tf_op jit(solution)/shard_map/all_gather | solution.py:478
  134.7 1.0 shard_map.91
  135.7 5.5 %all-to-all-start.7 = ((bf16[8,64,384]{2,1,0:T(8,128)(2,1)}), bf16[8,64,384]{2,1,0:T(8,128)(2,1)S(1)}, u32[]{:S(2)}, u32[]{:S(2)}) async-start(bf16[8,64,384]{2,1,0:T(8,128)(2,1)} %shard_map.91), calls=%async_computation.7 | async-start | bytes 786432 | tf_op jit(solution)/shard_map/all_to_all | solution.py:411
  141.2 0.1 reshape.81
  141.3 0.1 copy.21
  141.4 0.1 reshape.82
  141.5 3.7 %pad.18 = bf16[8,18,16,512]{3,2,1,0:T(8,128)(2,1)} pad(bf16[8,14,14,512]{3,2,1,0:T(8,128)(2,1)} %all-gather.6.cloned.1.call-done, bf16[]{:T(256)} %constant.124.clone.1), padding=0_0x1_3x1_1x0_0 | pad | bytes 3964930 | tf_op jit(solution)/shard_map/vmap(jit(_pad))/pad | solution.py:420
  145.2 1.6 shard_map.93
  146.8 0.3 fusion.24
  147.1 2.4 %all-to-all-done.7.packs_ref = bf16[8,64,384]{2,1,0:T(8,128)(2,1)S(1)} async-done(((bf16[8,64,384]{2,1,0:T(8,128)(2,1)}), bf16[8,64,384]{2,1,0:T(8,128)(2,1)S(1)}, u32[]{:S(2)}, u32[]{:S(2)}) %all-to-all-start.7) | async-done | bytes 393248 | tf_op jit(solution)/shard_map/all_to_all | solution.py:411
  149.4 1.7 copy-done.1
  151.1 2.7 %shard_map.92 = (f32[16,72,128]{2,1,0:T(8,128)S(1)}, bf16[16,72,128]{2,1,0:T(8,128)(2,1)S(1)}) custom-call(s32[2]{0:T(128)S(1)} %pad_add_fusion.place_ref, bf16[8,288,512]{2,1,0:T(8,128)(2,1)S(1)} %bitcast.36, bf16[8,64,384]{2,1,0:T(8,128)(2,1)S(1)} %all-to-all-done.7.packs_ref, bf16[64,256]{1,0:T(8,128)(2,1)S(1)} %fusion.19.spread_ref), custom_call_target="tpu_custom_call" | custom-call | flops 1207959552 | bytes 2359296 | tf_op jit(solution)/shard_map/pallas_call | solution.py:343
  153.8 3.1 %collective-permute-start.3 = (bf16[16,72,128]{2,1,0:T(8,128)(2,1)S(1)}, bf16[16,72,128]{2,1,0:T(8,128)(2,1)S(1)}, u32[]{:S(2)}, u32[]{:S(2)}) collective-permute-start(bf16[16,72,128]{2,1,0:T(8,128)(2,1)S(1)} %get-tuple-element.51), channel_id=1, source_target_pairs={{0,1},{1,0},{2,3},{3,2},{4,5},{5,4},{6,7},{7,6},{8,9},{9,8},{10,11... | collective-permute-start | bytes 884744 | tf_op jit(solution)/shard_map/ppermute | solution.py:500
  157.0 0.1 collective-permute-start.4
  157.1 0.1 slice.38
  157.2 0.1 convert_element_type.56
  157.3 0.8 collective-permute-done.3
  158.1 0.8 add_convert_fusion
  158.9 6.9 %all-to-all-start.8 = ((bf16[16,72,128]{2,1,0:T(8,128)(2,1)}), bf16[16,72,128]{2,1,0:T(8,128)(2,1)S(1)}, u32[]{:S(2)}, u32[]{:S(2)}) async-start(bf16[16,72,128]{2,1,0:T(8,128)(2,1)} %add_convert_fusion), calls=%async_computation.8 | async-start | bytes 589824 | tf_op jit(solution)/shard_map/all_to_all | solution.py:411
  165.8 0.7 add_bitcast_fusion
  166.5 0.2 shard_map.94
  166.8 2.3 %copy-done = bf16[4608,512]{1,0:T(8,128)(2,1)S(1)} copy-done((bf16[4608,512]{1,0:T(8,128)(2,1)S(1)}, bf16[4608,512]{1,0:T(8,128)(2,1)}, u32[]{:S(2)}) %copy-start) | copy-done | bytes 4718616
  169.1 3.5 %shard_map.95 = f32[1,14,14,512]{3,2,1,0:T(8,128)S(1)} custom-call(bf16[288,512]{1,0:T(8,128)(2,1)S(1)} %bitcast.39, bf16[4608,512]{1,0:T(8,128)(2,1)S(1)} %copy-done), custom_call_target="tpu_custom_call" | custom-call | flops 1000 | bytes 1000 | tf_op jit(solution)/shard_map/pallas_call | solution.py:384
  172.6 1.2 copy.23
  173.8 1.5 all-to-all-done.8
  175.4 0.1 fusion.23
  175.5 0.7 copy.22
  (51 shorter events, 0.6 us)
Async XLA Ops:
  7.2 74.9 %all-gather.8.cloned.1.call-start = ((), (), s32[]{:S(2)}) async-start(), calls=%async_computation.10 | async-start | bytes 2367488 | tf_op jit(solution)/shard_map/all_gather | solution.py:451
  8.8 19.2 %collective-permute-start = (bf16[3136,128]{1,0:T(8,128)(2,1)}, bf16[3136,128]{1,0:T(8,128)(2,1)S(1)}, u32[]{:S(2)}, u32[]{:S(2)}) collective-permute-start(bf16[3136,128]{1,0:T(8,128)(2,1)} %param.7), channel_id=1, source_target_pairs={{0,1},{1,0},{2,3},{3,2},{4,5},{5,4},{6,7},{7,6},{8,9},{9,8},{10,11... | collective-permute-start | bytes 2408456 | tf_op jit(solution)/shard_map/ppermute | solution.py:453
  16.3 21.2 %copy-start.5 = (bf16[1,14,14,512]{3,2,1,0:T(8,128)(2,1)S(1)}, bf16[1,14,14,512]{3,2,1,0:T(8,128)(2,1)}, u32[]{:S(2)}) copy-start(bf16[1,14,14,512]{3,2,1,0:T(8,128)(2,1)} %image_ref.1) | copy-start | bytes 602116
  16.3 22.4 %copy-start.6 = (bf16[3136,128]{1,0:T(8,128)(2,1)S(1)}, bf16[3136,128]{1,0:T(8,128)(2,1)}, u32[]{:S(2)}) copy-start(bf16[3136,128]{1,0:T(8,128)(2,1)} %param.7) | copy-start | bytes 2408452
  16.3 11.8 %all-to-all-start = ((bf16[8,16,256]{2,1,0:T(8,128)(2,1)}), bf16[8,16,256]{2,1,0:T(8,128)(2,1)S(1)}, u32[]{:S(2)}, u32[]{:S(2)}) async-start(bf16[8,16,256]{2,1,0:T(8,128)(2,1)} %get-tuple-element.30), calls=%async_computation | async-start | bytes 131072 | tf_op jit(solution)/shard_map/all_to_all | solution.py:411
  28.1 9.4 %copy-start.7 = (bf16[3136,128]{1,0:T(8,128)(2,1)}, bf16[3136,128]{1,0:T(8,128)(2,1)S(1)}, u32[]{:S(2)}) copy-start(bf16[3136,128]{1,0:T(8,128)(2,1)S(1)} %collective-permute-done) | copy-start | bytes 2408452
  29.1 27.3 %all-to-all-start.1 = ((bf16[16,8,3136]{2,1,0:T(8,128)(2,1)}), bf16[16,8,3136]{2,1,0:T(8,128)(2,1)S(1)}, u32[]{:S(2)}, u32[]{:S(2)}) async-start(bf16[16,8,3136]{2,1,0:T(8,128)(2,1)} %shard_map.86), calls=%async_computation.1 | async-start | bytes 1638400 | tf_op jit(solution)/shard_map/all_to_all | solution.py:411
  37.4 65.8 %all-gather.6.cloned.1.call-start = ((), (), s32[]{:S(2)}) async-start(), calls=%async_computation.9 | async-start | bytes 2293760 | tf_op jit(solution)/shard_map/all_gather | solution.py:458
  37.5 12.9 %collective-permute-start.2 = (bf16[1,14,14,512]{3,2,1,0:T(8,128)(2,1)S(1)}, bf16[1,14,14,512]{3,2,1,0:T(8,128)(2,1)S(1)}, u32[]{:S(2)}, u32[]{:S(2)}) collective-permute-start(bf16[1,14,14,512]{3,2,1,0:T(8,128)(2,1)S(1)} %copy-done.5), channel_id=1, source_target_pairs={{0,128},{128,0},{1,129},{129,1},{2,130},{130,2},{3,131},{131,3},{4... | collective-permute-start | bytes 602120 | tf_op jit(solution)/shard_map/ppermute | solution.py:432
  57.4 10.6 %all-to-all-start.2 = ((bf16[8,16,256]{2,1,0:T(8,128)(2,1)}), bf16[8,16,256]{2,1,0:T(8,128)(2,1)S(1)}, u32[]{:S(2)}, u32[]{:S(2)}) async-start(bf16[8,16,256]{2,1,0:T(8,128)(2,1)} %bitcast.6), calls=%async_computation.2 | async-start | bytes 131072 | tf_op jit(solution)/shard_map/all_to_all | solution.py:411
  68.8 13.3 %all-to-all-start.3 = ((bf16[16,16,256]{2,1,0:T(8,128)(2,1)}), bf16[16,16,256]{2,1,0:T(8,128)(2,1)S(1)}, u32[]{:S(2)}, u32[]{:S(2)}) async-start(bf16[16,16,256]{2,1,0:T(8,128)(2,1)} %broadcast_in_dim.8), calls=%async_computation.3 | async-start | bytes 262144 | tf_op jit(solution)/shard_map/all_to_all | solution.py:411
  82.1 1.7 copy-start.2
  85.6 5.5 %collective-permute-start.1 = (bf16[16,4096]{1,0:T(8,128)(2,1)S(1)}, bf16[16,4096]{1,0:T(8,128)(2,1)S(1)}, u32[]{:S(2)}, u32[]{:S(2)}) collective-permute-start(bf16[16,4096]{1,0:T(8,128)(2,1)S(1)} %bitcast.46), channel_id=1, source_target_pairs={{0,128},{128,0},{1,129},{129,1},{2,130},{130,2},{3,131},{131,3},{4... | collective-permute-start | bytes 393224 | tf_op jit(solution)/shard_map/ppermute | solution.py:432
  86.9 10.9 %all-to-all-start.4 = ((bf16[16,16,256]{2,1,0:T(8,128)(2,1)}), bf16[16,16,256]{2,1,0:T(8,128)(2,1)S(1)}, u32[]{:S(2)}, u32[]{:S(2)}) async-start(bf16[16,16,256]{2,1,0:T(8,128)(2,1)} %get-tuple-element.37), calls=%async_computation.4 | async-start | bytes 262144 | tf_op jit(solution)/shard_map/all_to_all | solution.py:411
  98.5 10.8 %all-to-all-start.5 = ((bf16[8,16,384]{2,1,0:T(8,128)(2,1)}), bf16[8,16,384]{2,1,0:T(8,128)(2,1)S(1)}, u32[]{:S(2)}, u32[]{:S(2)}) async-start(bf16[8,16,384]{2,1,0:T(8,128)(2,1)} %fusion.2), calls=%async_computation.5 | async-start | bytes 196608 | tf_op jit(solution)/shard_map/all_to_all | solution.py:411
  102.5 32.2 %all-gather.10.cloned.1.call-start = ((), (), s32[]{:S(2)}) async-start(), calls=%async_computation.11 | async-start | bytes 1310720 | tf_op jit(solution)/shard_map/all_gather | solution.py:478
  109.3 14.5 %copy-start.8 = (bf16[8,16,384]{2,1,0:T(8,128)(2,1)}, bf16[8,16,384]{2,1,0:T(8,128)(2,1)S(1)}, u32[]{:S(2)}) copy-start(bf16[8,16,384]{2,1,0:T(8,128)(2,1)S(1)} %all-to-all-done.5) | copy-start | bytes 294916
  110.8 12.5 %copy-start.3 = (f32[224,512]{1,0:T(8,128)S(1)}, f32[224,512]{1,0:T(8,128)}, u32[]{:S(2)}) copy-start(f32[224,512]{1,0:T(8,128)} %get-tuple-element.49.pre_ref) | copy-start | bytes 1376260
  110.8 23.8 %all-to-all-start.6 = ((bf16[16,8,3136]{2,1,0:T(8,128)(2,1)}), bf16[16,8,3136]{2,1,0:T(8,128)(2,1)S(1)}, u32[]{:S(2)}, u32[]{:S(2)}) async-start(bf16[16,8,3136]{2,1,0:T(8,128)(2,1)} %bitcast.11), calls=%async_computation.6 | async-start | bytes 1638400 | tf_op jit(solution)/shard_map/all_to_all | solution.py:411
  115.9 29.3 %collective-permute-start.5 = (bf16[3136,128]{1,0:T(8,128)(2,1)}, bf16[3136,128]{1,0:T(8,128)(2,1)S(1)}, u32[]{:S(2)}, u32[]{:S(2)}) collective-permute-start(bf16[3136,128]{1,0:T(8,128)(2,1)} %shard_map.89), channel_id=1, source_target_pairs={{0,1},{1,0},{2,3},{3,2},{4,5},{5,4},{6,7},{7,6},{8,9},{9,8},{10,11... | collective-permute-start | bytes 2408456 | tf_op jit(solution)/shard_map/ppermute | solution.py:496
  123.7 17.5 %slice-start = ((bf16[8,16,384]{2,1,0:T(8,128)(2,1)}), bf16[8,16,32]{2,1,0:T(8,128)(2,1)S(1)}, s32[]{:S(2)}) async-start(bf16[8,16,384]{2,1,0:T(8,128)(2,1)} %copy-done.8), calls=%async_computation.12 | async-start | bytes 65536 | tf_op jit(solution)/shard_map/slice | solution.py:487
  135.7 13.7 %all-to-all-start.7 = ((bf16[8,64,384]{2,1,0:T(8,128)(2,1)}), bf16[8,64,384]{2,1,0:T(8,128)(2,1)S(1)}, u32[]{:S(2)}, u32[]{:S(2)}) async-start(bf16[8,64,384]{2,1,0:T(8,128)(2,1)} %shard_map.91), calls=%async_computation.7 | async-start | bytes 786432 | tf_op jit(solution)/shard_map/all_to_all | solution.py:411
  145.2 1.6 copy-start.4
  149.4 1.7 copy-start.1
  153.8 4.3 %collective-permute-start.3 = (bf16[16,72,128]{2,1,0:T(8,128)(2,1)S(1)}, bf16[16,72,128]{2,1,0:T(8,128)(2,1)S(1)}, u32[]{:S(2)}, u32[]{:S(2)}) collective-permute-start(bf16[16,72,128]{2,1,0:T(8,128)(2,1)S(1)} %get-tuple-element.51), channel_id=1, source_target_pairs={{0,1},{1,0},{2,3},{3,2},{4,5},{5,4},{6,7},{7,6},{8,9},{9,8},{10,11... | collective-permute-start | bytes 884744 | tf_op jit(solution)/shard_map/ppermute | solution.py:500
  157.0 8.8 %collective-permute-start.4 = (f32[16,4096]{1,0:T(8,128)S(1)}, f32[16,4096]{1,0:T(8,128)S(1)}, u32[]{:S(2)}, u32[]{:S(2)}) collective-permute-start(f32[16,4096]{1,0:T(8,128)S(1)} %slice_select_fusion), channel_id=1, source_target_pairs={{0,1},{1,0},{2,3},{3,2},{4,5},{5,4},{6,7},{7,6},{8,9},{9,8},{10,11... | collective-permute-start | bytes 786440 | tf_op jit(solution)/shard_map/ppermute | solution.py:516
  158.9 16.4 %all-to-all-start.8 = ((bf16[16,72,128]{2,1,0:T(8,128)(2,1)}), bf16[16,72,128]{2,1,0:T(8,128)(2,1)S(1)}, u32[]{:S(2)}, u32[]{:S(2)}) async-start(bf16[16,72,128]{2,1,0:T(8,128)(2,1)} %add_convert_fusion), calls=%async_computation.8 | async-start | bytes 589824 | tf_op jit(solution)/shard_map/all_to_all | solution.py:411
  166.8 2.3 %copy-start = (bf16[4608,512]{1,0:T(8,128)(2,1)S(1)}, bf16[4608,512]{1,0:T(8,128)(2,1)}, u32[]{:S(2)}) copy-start(bf16[4608,512]{1,0:T(8,128)(2,1)} %weight_ref.3) | copy-start | bytes 14155780
Sparse Core Ops, SparseCore 0:
  11.3 57.9 all-gather.7
  71.1 29.8 all-gather.5
  105.7 28.9 all-gather.9
